TPU v7x, 32 devices: a whole 2x2x4 slice. The times are simulated.
32 devices in a mesh: dp: 4 (over z), ctx: 2 (over x), mp: 4 (over y, core).
Axes of the slice: x: 2, y: 2, z: 4, core: 2. Of those that a mesh axis runs over, the one named last changes fastest.
Arguments:
- tokens: bfloat16 [5632, 2304], P(('dp', 'ctx', 'mp')), may hold values from -6 to 6
- w_query: bfloat16 [2304, 2304], P(('dp', 'ctx'), 'mp'), may hold values from -0.125 to 0.125
- w_key: bfloat16 [2304, 2304], P(('dp', 'ctx'), 'mp'), may hold values from -0.125 to 0.125
- w_value: bfloat16 [2304, 2304], P(('dp', 'ctx'), 'mp'), may hold values from -0.125 to 0.125
- w_out: bfloat16 [2304, 2304], P('mp', ('dp', 'ctx')), may hold values from -3 to 3
- gain_attn: bfloat16 [2304], replicated, may hold values from 0.099609375 to 1.8984375
- w_gate: bfloat16 [2304, 5760], P(('dp', 'ctx'), 'mp'), may hold values from -0.125 to 0.125
- w_up: bfloat16 [2304, 5760], P(('dp', 'ctx'), 'mp'), may hold values from -0.125 to 0.125
- w_down: bfloat16 [5760, 2304], P('mp', ('dp', 'ctx')), may hold values from -0.625 to 0.625
- gain_mlp: bfloat16 [2304], replicated, may hold values from 0.099609375 to 1.8984375
- cotangent: bfloat16 [5632, 2304], P(('dp', 'ctx', 'mp')), may hold values from -6 to 6
- lineage: int32 [3, 5632], P(None, 'dp'), may hold values from 0 to 7, as said below
- padding: int32 [5632], P('dp'), may hold values from 0 to 1, as said below
- positions: int32 [5632], P('dp'), may hold values from 0 to 959, as said below
Outputs:
- output: bfloat16 [5632, 2304], P(('dp', 'ctx', 'mp'))
- input_grad: bfloat16 [5632, 2304], P(('dp', 'ctx', 'mp'))
- grad_query: float32 [2304, 2304], P(('dp', 'ctx'), 'mp')
- grad_key: float32 [2304, 2304], P(('dp', 'ctx'), 'mp')
- grad_value: float32 [2304, 2304], P(('dp', 'ctx'), 'mp')
- grad_out: float32 [2304, 2304], P('mp', ('dp', 'ctx'))
- grad_gain_attn: float32 [2304], replicated
- grad_gate: float32 [2304, 5760], P(('dp', 'ctx'), 'mp')
- grad_up: float32 [2304, 5760], P(('dp', 'ctx'), 'mp')
- grad_down: float32 [5760, 2304], P('mp', ('dp', 'ctx'))
- grad_gain_mlp: float32 [2304], replicated
Inputs may be any that keep to these rules, and one draw needn't show every extreme that they name: `lineage`: each tree's slot of 1408 tokens holds a trunk of 768 tokens first, two branches of 128 tokens whose parent is the trunk, two leaves of 64 tokens under each branch, and one run of 128 padding tokens; every segment lies in consecutive tokens after its parent. Within a tree the seven segments carry distinct numbers 0 to 6; padding tokens carry 7 in all three rows. The trunk's parent and grandparent are the trunk itself, a branch's grandparent is the trunk. Exactly 128 padding tokens in each tree's slot, in one run after the trunk. `positions`: trunk tokens count 0 to 767, branch tokens continue from 768, leaf tokens from 896; padding tokens count from 0.
All inputs are finite; a program needn't handle non-finite values.
Results may differ from a plain program's by a relative error of at most 0.019.
Values may be sent and summed in bfloat16 or wider, within the bound.
No kernel may reach another device: no remote copies, remote signals or barrier semaphores. Data moves between devices by JAX's collectives and lax.ppermute only.
A program may use at most 192 MiB of HBM per device.

v0:
```python
import math

import jax
import jax.numpy as jnp
from jax import lax
from jax.sharding import PartitionSpec as P

HEAD_DIM = 64


eps = 1e-05
branch_scale = 1.4 / math.sqrt(40.0)
rope_base = 10000.0
masked_value = -1e30


def normalize(field):
    return field * lax.rsqrt(jnp.mean(field * field, axis=-1, keepdims=True) + eps)


def norm_back(field, gain_f32, incoming):
    inverse = lax.rsqrt(jnp.mean(field * field, axis=-1, keepdims=True) + eps)
    scaled = gain_f32 * incoming
    along = jnp.mean(field * scaled, axis=-1, keepdims=True)
    return (
        inverse * scaled - field * inverse**3 * along,
        jnp.sum(incoming * field * inverse, axis=0),
    )


def rope_tables(places):
    half_dim = HEAD_DIM // 2
    inv_freq = rope_base ** (-2.0 * jnp.arange(half_dim, dtype=jnp.float32) / HEAD_DIM)
    angles = places.astype(jnp.float32)[:, None] * inv_freq[None, :]
    return (jnp.cos(angles)[:, None, :], jnp.sin(angles)[:, None, :])


def rotate(field, cosine_table, sine_table):
    half_dim = field.shape[-1] // 2
    first_half = field[..., :half_dim]
    second_half = field[..., half_dim:]
    return jnp.concatenate(
        [
            first_half * cosine_table - second_half * sine_table,
            second_half * cosine_table + first_half * sine_table,
        ],
        axis=-1,
    )


def shards(
    tokens,
    w_query,
    w_key,
    w_value,
    w_out,
    gain_attn,
    w_gate,
    w_up,
    w_down,
    gain_mlp,
    cotangent,
    lineage,
    padding,
    positions,
):
    row_count = tokens.shape[0]
    block_rows = row_count * lax.axis_size("mp")
    slot_len = lineage.shape[1]
    head_count = w_query.shape[1] // HEAD_DIM
    score_scale = HEAD_DIM ** (-0.5)
    q_start = lax.axis_index("ctx") * block_rows
    q_index = q_start + jnp.arange(block_rows, dtype=jnp.int32)
    k_index = jnp.arange(slot_len, dtype=jnp.int32)
    q_lineage = lax.dynamic_slice_in_dim(lineage, q_start, block_rows, 1)
    q_padding = lax.dynamic_slice_in_dim(padding, q_start, block_rows, 0)
    key_seg = lineage[0]
    related = (
        (key_seg[None, :] == q_lineage[0][:, None])
        | (key_seg[None, :] == q_lineage[1][:, None])
        | (key_seg[None, :] == q_lineage[2][:, None])
    )
    live_mask = (q_padding[:, None] == 0) & (padding[None, :] == 0)
    allowed = (k_index[None, :] == q_index[:, None]) | related & live_mask & (
        k_index[None, :] < q_index[:, None]
    )
    cosine_table, sine_table = rope_tables(
        lax.dynamic_slice_in_dim(positions, q_start, block_rows, 0)
    )
    gain_a = gain_attn.astype(jnp.float32)
    gain_m = gain_mlp.astype(jnp.float32)

    def gather_rows(field):
        return lax.all_gather(field, "mp", axis=0, tiled=True)

    def sum_rows(field):
        return lax.psum_scatter(field, "mp", scatter_dimension=0, tiled=True)

    def split_heads(field):
        return field.reshape(field.shape[0], head_count, HEAD_DIM).transpose(1, 0, 2)

    def join_heads(field):
        return field.transpose(1, 0, 2).reshape(field.shape[1], head_count * HEAD_DIM)

    def turn(field, sine_sign):
        turned = rotate(
            field.reshape(block_rows, head_count, HEAD_DIM), cosine_table, sine_sign * sine_table
        )
        return turned.reshape(block_rows, head_count * HEAD_DIM)

    def scores_of(query_head, key_head):
        raw = (
            jnp.einsum("qd,kd->qk", query_head, key_head, preferred_element_type=jnp.float32)
            * score_scale
        )
        return jnp.where(allowed, raw, masked_value)

    def head_forward(pieces):
        query_head, key_head, value_head = pieces
        scores = scores_of(query_head, key_head)
        row_max = jnp.max(scores, axis=1, keepdims=True)
        exp_scores = jnp.exp(scores - row_max)
        row_total = jnp.sum(exp_scores, axis=1, keepdims=True)
        probs = (exp_scores / row_total).astype(jnp.bfloat16)
        return (
            jnp.dot(probs, value_head, preferred_element_type=jnp.float32),
            (row_max + jnp.log(row_total))[:, 0],
        )

    def head_backward(pieces):
        query_head, key_head, value_head, d_head, log_total = pieces
        probs = jnp.exp(scores_of(query_head, key_head) - log_total[:, None])
        d_probs = jnp.einsum("qd,kd->qk", d_head, value_head, preferred_element_type=jnp.float32)
        centre = jnp.sum(probs * d_probs, axis=1, keepdims=True)
        d_scores = (probs * (d_probs - centre)).astype(jnp.bfloat16)
        d_query = jnp.dot(d_scores, key_head, preferred_element_type=jnp.float32) * score_scale
        d_key = (
            jnp.einsum("qk,qd->kd", d_scores, query_head, preferred_element_type=jnp.float32)
            * score_scale
        )
        d_value = jnp.einsum(
            "qk,qd->kd", probs.astype(jnp.bfloat16), d_head, preferred_element_type=jnp.float32
        )
        return (d_query, d_key, d_value)

    def attention_core(normed_rows):
        q_weight, k_weight, v_weight, o_weight = (
            lax.all_gather(w_query, ("dp", "ctx"), axis=0, tiled=True),
            lax.all_gather(w_key, ("dp", "ctx"), axis=0, tiled=True),
            lax.all_gather(w_value, ("dp", "ctx"), axis=0, tiled=True),
            lax.all_gather(w_out, ("dp", "ctx"), axis=1, tiled=True),
        )
        normed = gather_rows(normed_rows)
        query_rows = turn(
            jnp.dot(normed, q_weight, preferred_element_type=jnp.float32), 1.0
        ).astype(jnp.bfloat16)
        key_rows = turn(jnp.dot(normed, k_weight, preferred_element_type=jnp.float32), 1.0).astype(
            jnp.bfloat16
        )
        value_rows = jnp.dot(normed, v_weight, preferred_element_type=jnp.float32).astype(
            jnp.bfloat16
        )
        key_all, value_all = (
            lax.all_gather(key_rows, "ctx", axis=0, tiled=True),
            lax.all_gather(value_rows, "ctx", axis=0, tiled=True),
        )
        mixed_heads, log_total = lax.map(
            head_forward, (split_heads(query_rows), split_heads(key_all), split_heads(value_all))
        )
        mixed_heads = join_heads(mixed_heads).astype(jnp.bfloat16)
        return (
            q_weight,
            k_weight,
            v_weight,
            o_weight,
            normed,
            query_rows,
            key_all,
            value_all,
            mixed_heads,
            log_total,
        )

    def mlp_core(normed_rows):
        g_weight, u_weight, d_weight = (
            lax.all_gather(w_gate, ("dp", "ctx"), axis=0, tiled=True),
            lax.all_gather(w_up, ("dp", "ctx"), axis=0, tiled=True),
            lax.all_gather(w_down, ("dp", "ctx"), axis=1, tiled=True),
        )
        normed = gather_rows(normed_rows)
        gate_proj = jnp.dot(normed, g_weight, preferred_element_type=jnp.float32)
        up_proj = jnp.dot(normed, u_weight, preferred_element_type=jnp.float32)
        hidden = (jax.nn.silu(gate_proj) * up_proj).astype(jnp.bfloat16)
        return (g_weight, u_weight, d_weight, normed, gate_proj, up_proj, hidden)

    inputs = tokens.astype(jnp.float32)
    normed_a = (normalize(inputs) * gain_a).astype(jnp.bfloat16)
    saved_attn = attention_core(normed_a)
    residual = inputs + branch_scale * sum_rows(
        jnp.dot(saved_attn[8], saved_attn[3], preferred_element_type=jnp.float32)
    )
    normed_m = (normalize(residual) * gain_m).astype(jnp.bfloat16)
    saved_mlp = mlp_core(normed_m)
    output = residual + branch_scale * sum_rows(
        jnp.dot(saved_mlp[6], saved_mlp[2], preferred_element_type=jnp.float32)
    )
    normed_a, normed_m, output = lax.optimization_barrier((normed_a, normed_m, output))
    saved_attn = attention_core(normed_a)
    saved_mlp = mlp_core(normed_m)
    (
        q_weight,
        k_weight,
        v_weight,
        o_weight,
        normed_attn,
        query_rows,
        key_all,
        value_all,
        mixed_heads,
        log_total,
    ) = saved_attn
    g_weight, u_weight, d_weight, normed_mlp, gate_proj, up_proj, hidden = saved_mlp
    grad_rows = cotangent.astype(jnp.float32)
    d_mlp = gather_rows((branch_scale * grad_rows).astype(jnp.bfloat16))
    d_hidden = jnp.einsum("td,fd->tf", d_mlp, d_weight, preferred_element_type=jnp.float32)
    sigmoid_gate = jax.nn.sigmoid(gate_proj)
    d_gate = (d_hidden * up_proj * sigmoid_gate * (1.0 + gate_proj * (1.0 - sigmoid_gate))).astype(
        jnp.bfloat16
    )
    d_up = (d_hidden * jax.nn.silu(gate_proj)).astype(jnp.bfloat16)
    grad_down = jnp.einsum("tf,td->fd", hidden, d_mlp, preferred_element_type=jnp.float32)
    grad_gate = jnp.einsum("td,tf->df", normed_mlp, d_gate, preferred_element_type=jnp.float32)
    grad_up = jnp.einsum("td,tf->df", normed_mlp, d_up, preferred_element_type=jnp.float32)
    grad_gate, grad_up, grad_down = (
        lax.psum_scatter(
            grad_gate.astype(jnp.bfloat16), ("dp", "ctx"), scatter_dimension=0, tiled=True
        ).astype(jnp.float32),
        lax.psum_scatter(
            grad_up.astype(jnp.bfloat16), ("dp", "ctx"), scatter_dimension=0, tiled=True
        ).astype(jnp.float32),
        lax.psum_scatter(
            grad_down.astype(jnp.bfloat16), ("dp", "ctx"), scatter_dimension=1, tiled=True
        ).astype(jnp.float32),
    )
    d_normed_mlp = sum_rows(
        jnp.einsum("tf,df->td", d_gate, g_weight, preferred_element_type=jnp.float32)
        + jnp.einsum("tf,df->td", d_up, u_weight, preferred_element_type=jnp.float32)
    )
    back_mlp, gain_mlp_part = norm_back(residual, gain_m, d_normed_mlp)
    d_residual = grad_rows + back_mlp
    d_attn = gather_rows((branch_scale * d_residual).astype(jnp.bfloat16))
    d_mixed = jnp.einsum("td,hd->th", d_attn, o_weight, preferred_element_type=jnp.float32).astype(
        jnp.bfloat16
    )
    grad_out = jnp.einsum("th,td->hd", mixed_heads, d_attn, preferred_element_type=jnp.float32)
    d_query, d_key, d_value = lax.map(
        head_backward,
        (
            split_heads(query_rows),
            split_heads(key_all),
            split_heads(value_all),
            split_heads(d_mixed),
            log_total,
        ),
    )
    d_key, d_value = (
        lax.psum_scatter(join_heads(d_key), "ctx", scatter_dimension=0, tiled=True),
        lax.psum_scatter(join_heads(d_value), "ctx", scatter_dimension=0, tiled=True),
    )
    d_query = turn(join_heads(d_query), -1.0).astype(jnp.bfloat16)
    d_key = turn(d_key, -1.0).astype(jnp.bfloat16)
    d_value = d_value.astype(jnp.bfloat16)
    grad_query = jnp.einsum("td,th->dh", normed_attn, d_query, preferred_element_type=jnp.float32)
    grad_key = jnp.einsum("td,th->dh", normed_attn, d_key, preferred_element_type=jnp.float32)
    grad_value = jnp.einsum("td,th->dh", normed_attn, d_value, preferred_element_type=jnp.float32)
    grad_query, grad_key, grad_value, grad_out = (
        lax.psum_scatter(
            grad_query.astype(jnp.bfloat16), ("dp", "ctx"), scatter_dimension=0, tiled=True
        ).astype(jnp.float32),
        lax.psum_scatter(
            grad_key.astype(jnp.bfloat16), ("dp", "ctx"), scatter_dimension=0, tiled=True
        ).astype(jnp.float32),
        lax.psum_scatter(
            grad_value.astype(jnp.bfloat16), ("dp", "ctx"), scatter_dimension=0, tiled=True
        ).astype(jnp.float32),
        lax.psum_scatter(
            grad_out.astype(jnp.bfloat16), ("dp", "ctx"), scatter_dimension=1, tiled=True
        ).astype(jnp.float32),
    )
    d_normed_attn = sum_rows(
        jnp.einsum("th,dh->td", d_query, q_weight, preferred_element_type=jnp.float32)
        + jnp.einsum("th,dh->td", d_key, k_weight, preferred_element_type=jnp.float32)
        + jnp.einsum("th,dh->td", d_value, v_weight, preferred_element_type=jnp.float32)
    )
    back_attn, gain_attn_part = norm_back(inputs, gain_a, d_normed_attn)
    input_grad = d_residual + back_attn
    grad_gain_attn, grad_gain_mlp = lax.psum((gain_attn_part, gain_mlp_part), ("dp", "ctx", "mp"))
    return (
        output.astype(jnp.bfloat16),
        input_grad.astype(jnp.bfloat16),
        grad_query,
        grad_key,
        grad_value,
        grad_out,
        grad_gain_attn,
        grad_gate,
        grad_up,
        grad_down,
        grad_gain_mlp,
    )


def solution(mesh):
    placed = (
        P(("dp", "ctx", "mp"), None),
        P(("dp", "ctx"), "mp"),
        P(("dp", "ctx"), "mp"),
        P(("dp", "ctx"), "mp"),
        P("mp", ("dp", "ctx")),
        P(),
        P(("dp", "ctx"), "mp"),
        P(("dp", "ctx"), "mp"),
        P("mp", ("dp", "ctx")),
        P(),
        P(("dp", "ctx", "mp"), None),
        P(None, "dp"),
        P("dp"),
        P("dp"),
    )
    return jax.shard_map(
        shards,
        mesh=mesh,
        in_specs=placed,
        out_specs=(
            P(("dp", "ctx", "mp"), None),
            P(("dp", "ctx", "mp"), None),
            P(("dp", "ctx"), "mp"),
            P(("dp", "ctx"), "mp"),
            P(("dp", "ctx"), "mp"),
            P("mp", ("dp", "ctx")),
            P(),
            P(("dp", "ctx"), "mp"),
            P(("dp", "ctx"), "mp"),
            P("mp", ("dp", "ctx")),
            P(),
        ),
        check_vma=False,
    )
```

profile of v0, /device:TPU:0, one launch (start us, length us, event | category | flops | bytes accessed | tf_op | source)
XLA Modules:
  0.0 2162.2 jit_solution(4239237197776958745)
XLA Ops:
  16.1 55.2 %all-gather.26.cloned.1.call-done = bf16[2304,576]{1,0:T(8,128)(2,1)} async-done(((bf16[288,576]{1,0:T(8,128)(2,1)}), bf16[2304,576]{1,0:T(8,128)(2,1)}) %all-gather.26.cloned.1.call-update) | async-done | bytes 2654224 | tf_op jit(solution)/shard_map/all_gather | solution.py:149
  71.3 29.9 %all-gather.22.cloned.1.call-done = bf16[704,2304]{1,0:T(8,128)(2,1)} async-done(((bf16[176,2304]{1,0:T(8,128)(2,1)}), bf16[704,2304]{1,0:T(8,128)(2,1)}) %all-gather.22.cloned.1.call-update) | async-done | bytes 3244048 | tf_op jit(solution)/shard_map/all_gather | solution.py:94
  106.3 55.5 %all-gather.24.cloned.1.call-done = bf16[2304,576]{1,0:T(8,128)(2,1)} async-done(((bf16[288,576]{1,0:T(8,128)(2,1)}), bf16[2304,576]{1,0:T(8,128)(2,1)}) %all-gather.24.cloned.1.call-update) | async-done | bytes 2654224 | tf_op jit(solution)/shard_map/all_gather | solution.py:148
  168.6 52.3 %all-gather.28.cloned.1.call-done = bf16[2304,576]{1,0:T(8,128)(2,1)} async-done(((bf16[288,576]{1,0:T(8,128)(2,1)}), bf16[2304,576]{1,0:T(8,128)(2,1)}) %all-gather.28.cloned.1.call-update) | async-done | bytes 2654224 | tf_op jit(solution)/shard_map/all_gather | solution.py:150
  220.9 6.0 fusion.74
  229.2 21.7 %all-gather.48.cloned.1.call-done = bf16[2,704,576]{1,2,0:T(8,128)(2,1)} async-done(((bf16[1,704,576]{1,2,0:T(8,128)(2,1)}), bf16[2,704,576]{1,2,0:T(8,128)(2,1)}) %all-gather.48.cloned.1.call-update) | async-done | bytes 1622032 | tf_op jit(solution)/shard_map/all_gather | solution.py:164
  256.7 25.6 %all-gather.50.cloned.1.call-done = bf16[2,704,576]{1,2,0:T(8,128)(2,1)} async-done(((bf16[1,704,576]{1,2,0:T(8,128)(2,1)}), bf16[2,704,576]{1,2,0:T(8,128)(2,1)}) %all-gather.50.cloned.1.call-update) | async-done | bytes 1622032 | tf_op jit(solution)/shard_map/all_gather | solution.py:165
  288.1 54.9 %while.42 = (s32[]{:T(128)}, bf16[9,704,64]{1,2,0:T(8,128)(2,1)S(1)}, bf16[9,704,64]{1,2,0:T(8,128)(2,1)}, bf16[9,1408,64]{1,2,0:T(8,128)(2,1)}, bf16[9,1408,64]...) while((s32[]{:T(128)}, ...), condition=%wide.region_4.5_spmd.clone.clone, body=%wide.region_1.4_spmd.clone.sunk.clone | while | flops 272587392 | bytes 12587965 | solution.py:167
  343.1 7.4 fusion.85
  351.3 59.1 %reduce-scatter.18.cloned.1.call-done = f32[176,2304]{1,0:T(8,128)} async-done(((f32[704,2304]{1,0:T(8,128)}), f32[176,2304]{1,0:T(8,128)}) %reduce-scatter.18.cloned.1.call-update) | async-done | bytes 1622032 | tf_op jit(solution)/shard_map/reduce_scatter | solution.py:97
  414.8 106.8 %all-gather.34.cloned.1.call-done = bf16[2304,1440]{1,0:T(8,128)(2,1)} async-done(((bf16[288,1440]{1,0:T(8,128)(2,1)}), bf16[2304,1440]{1,0:T(8,128)(2,1)}) %all-gather.34.cloned.1.call-update) | async-done | bytes 6635536 | tf_op jit(solution)/shard_map/all_gather | solution.py:186
  521.6 29.4 %all-gather.32.cloned.1.call-done = bf16[704,2304]{1,0:T(8,128)(2,1)} async-done(((bf16[176,2304]{1,0:T(8,128)(2,1)}), bf16[704,2304]{1,0:T(8,128)(2,1)}) %all-gather.32.cloned.1.call-update) | async-done | bytes 3244048 | tf_op jit(solution)/shard_map/all_gather | solution.py:94
  551.0 9.8 fusion.86
  560.7 101.5 %all-gather.38.cloned.1.call-done = bf16[1440,2304]{0,1:T(8,128)(2,1)} async-done(((bf16[1440,288]{0,1:T(8,128)(2,1)}), bf16[1440,2304]{0,1:T(8,128)(2,1)}) %all-gather.38.cloned.1.call-update) | async-done | bytes 6635536 | tf_op jit(solution)/shard_map/all_gather | solution.py:188
  662.2 109.3 %all-gather.36.cloned.1.call-done = bf16[2304,1440]{1,0:T(8,128)(2,1)} async-done(((bf16[288,1440]{1,0:T(8,128)(2,1)}), bf16[2304,1440]{1,0:T(8,128)(2,1)}) %all-gather.36.cloned.1.call-update) | async-done | bytes 6635536 | tf_op jit(solution)/shard_map/all_gather | solution.py:187
  771.5 20.2 fusion.87
  791.8 58.0 %reduce-scatter.20.cloned.1.call-done = f32[176,2304]{1,0:T(8,128)} async-done(((f32[704,2304]{1,0:T(8,128)}), f32[176,2304]{1,0:T(8,128)}) %reduce-scatter.20.cloned.1.call-update) | async-done | bytes 1622032 | tf_op jit(solution)/shard_map/reduce_scatter | solution.py:97
  854.5 27.1 %all-gather.44.cloned.1.call-done = bf16[704,2304]{1,0:T(8,128)(2,1)} async-done(((bf16[176,2304]{1,0:T(8,128)(2,1)}), bf16[704,2304]{1,0:T(8,128)(2,1)}) %all-gather.44.cloned.1.call-update) | async-done | bytes 3244048 | tf_op jit(solution)/shard_map/all_gather | solution.py:94
  881.6 5.3 fusion.92
  891.1 6.6 fusion.75
  897.9 14.8 all-gather.42.cloned.1.call-done
  912.7 10.7 fusion.89
  923.4 8.8 fusion.88
  932.2 11.6 all-gather.40.cloned.1.call-done
  943.8 11.1 multiply_convert_fusion.2
  954.9 9.0 fusion.90
  963.9 10.4 convolution_add_fusion
  986.5 19.5 all-gather.54.cloned.1.call-done
  1016.5 51.9 %reduce-scatter.22.cloned.1.call-done = f32[176,2304]{1,0:T(8,128)} async-done(((f32[704,2304]{1,0:T(8,128)}), f32[176,2304]{1,0:T(8,128)}) %reduce-scatter.22.cloned.1.call-update) | async-done | bytes 1622032 | tf_op jit(solution)/shard_map/reduce_scatter | solution.py:97
  1073.2 57.6 %while.43 = (s32[]{:T(128)}, bf16[9,704,64]{1,2,0:T(8,128)(2,1)S(1)}, f32[9,704]{1,0:T(8,128)S(1)}, bf16[9,704,64]{2,1,0:T(8,128)(2,1)}, bf16[9,1408,64]{2,1,0:T...) while((s32[]{:T(128)}, ...), condition=%wide.region_13.14_spmd.clone.clone, body=%wide.region_10.13_spmd.clone.sunk.clone | while | flops 272588096 | bytes 13050057 | solution.py:167
  1137.1 109.8 %while.44 = (s32[]{:T(128)}, f32[9,704,64]{1,2,0:T(8,128)}, f32[9,1408,64]{1,2,0:T(8,128)}, f32[9,1408,64]{1,2,0:T(8,128)}, bf16[9,704,64]{2,1,0:T(8,128)(2,1)},...) while((s32[]{:T(128)}, f32[9,704,64]{1,2,0:T(8,128)}, ...), condition=%wide.region_16.17_spmd.clone.clone, body=%wide.region_14.16_spmd.clone.sunk.clone | while | flops 654347584 | bytes 32495072 | solution.py:256
  1256.9 10.8 convolution_convert_fusion.2
  1267.8 9.9 convolution_convert_fusion.1
  1277.7 11.5 convolution_convert_fusion
  1289.3 6.7 convolution_convert_fusion.3
  1308.7 7.2 convolution_convert_fusion.5
  1315.9 35.1 %reduce-scatter.42.cloned.1.call-done = f32[704,576]{1,0:T(8,128)} async-done(((f32[1408,576]{1,0:T(8,128)}), f32[704,576]{1,0:T(8,128)}) %reduce-scatter.42.cloned.1.call-update) | async-done | bytes 1622032
  1352.9 6.5 convolution_convert_fusion.4
  1367.0 5.5 add_add_fusion
  1372.6 111.6 %reduce-scatter.34.cloned.1.call-done = bf16[288,1440]{1,0:T(8,128)(2,1)} async-done(((bf16[2304,1440]{1,0:T(8,128)(2,1)}), bf16[288,1440]{1,0:T(8,128)(2,1)}) %reduce-scatter.34.cloned.1.call-update) | async-done | bytes 829456 | tf_op jit(solution)/shard_map/reduce_scatter | solution.py:235
  1486.8 129.1 %reduce-scatter.36.cloned.1.call-done = bf16[288,1440]{1,0:T(8,128)(2,1)} async-done(((bf16[2304,1440]{1,0:T(8,128)(2,1)}), bf16[288,1440]{1,0:T(8,128)(2,1)}) %reduce-scatter.36.cloned.1.call-update) | async-done | bytes 829456 | tf_op jit(solution)/shard_map/reduce_scatter | solution.py:238
  1618.4 129.6 %reduce-scatter.38.cloned.1.call-done = bf16[1440,288]{0,1:T(8,128)(2,1)} async-done(((bf16[1440,2304]{0,1:T(8,128)(2,1)}), bf16[1440,288]{0,1:T(8,128)(2,1)}) %reduce-scatter.38.cloned.1.call-update) | async-done | bytes 829456 | tf_op jit(solution)/shard_map/reduce_scatter | solution.py:241
  1750.7 72.4 %reduce-scatter.32.cloned.1.call-done = bf16[576,288]{0,1:T(8,128)(2,1)} async-done(((bf16[576,2304]{0,1:T(8,128)(2,1)}), bf16[576,288]{0,1:T(8,128)(2,1)}) %reduce-scatter.32.cloned.1.call-update) | async-done | bytes 331792 | tf_op jit(solution)/shard_map/reduce_scatter | solution.py:286
  1824.9 73.5 %reduce-scatter.26.cloned.1.call-done = bf16[288,576]{1,0:T(8,128)(2,1)} async-done(((bf16[2304,576]{1,0:T(8,128)(2,1)}), bf16[288,576]{1,0:T(8,128)(2,1)}) %reduce-scatter.26.cloned.1.call-update) | async-done | bytes 331792 | tf_op jit(solution)/shard_map/reduce_scatter | solution.py:277
  1900.3 73.3 %reduce-scatter.28.cloned.1.call-done = bf16[288,576]{1,0:T(8,128)(2,1)} async-done(((bf16[2304,576]{1,0:T(8,128)(2,1)}), bf16[288,576]{1,0:T(8,128)(2,1)}) %reduce-scatter.28.cloned.1.call-update) | async-done | bytes 331792 | tf_op jit(solution)/shard_map/reduce_scatter | solution.py:280
  1975.5 73.6 %reduce-scatter.30.cloned.1.call-done = bf16[288,576]{1,0:T(8,128)(2,1)} async-done(((bf16[2304,576]{1,0:T(8,128)(2,1)}), bf16[288,576]{1,0:T(8,128)(2,1)}) %reduce-scatter.30.cloned.1.call-update) | async-done | bytes 331792 | tf_op jit(solution)/shard_map/reduce_scatter | solution.py:283
  2051.0 59.4 %reduce-scatter.24.cloned.1.call-done = f32[176,2304]{1,0:T(8,128)} async-done(((f32[704,2304]{1,0:T(8,128)}), f32[176,2304]{1,0:T(8,128)}) %reduce-scatter.24.cloned.1.call-update) | async-done | bytes 1622032 | tf_op jit(solution)/shard_map/reduce_scatter | solution.py:97
  2112.4 39.9 %all-reduce = (f32[2304]{0:T(1024)}, f32[2304]{0:T(1024)}) all-reduce(f32[2304]{0:T(1024)S(1)} %get-tuple-element.381, f32[2304]{0:T(1024)S(1)} %copy-done.16), channel_id=1, replica_groups=mesh['dp'=4,'ctx'=2,'mp'=4] {'dp','ctx','mp'}, use_global_device_ids=true, to_apply=%region_26.27 | all-reduce | flops 4608 | bytes 36864 | tf_op jit(solution)/shard_map/psum | solution.py:297
  (337 shorter events, 355.8 us)
Async XLA Ops:
  7.2 7.7 copy-start.23
  7.2 64.1 %all-gather.26.cloned.1.call-start = ((), (), s32[]{:S(2)}) async-start(), calls=%async_computation.15 | async-start | bytes 3317760 | tf_op jit(solution)/shard_map/all_gather | solution.py:149
  7.9 93.3 %all-gather.22.cloned.1.call-start = ((), (), s32[]{:S(2)}) async-start(), calls=%async_computation.13 | async-start | bytes 4055040 | tf_op jit(solution)/shard_map/all_gather | solution.py:94
  13.5 148.3 %all-gather.24.cloned.1.call-start = ((), (), s32[]{:S(2)}) async-start(), calls=%async_computation.14 | async-start | bytes 3317760 | tf_op jit(solution)/shard_map/all_gather | solution.py:148
  14.3 206.6 %all-gather.28.cloned.1.call-start = ((), (), s32[]{:S(2)}) async-start(), calls=%async_computation.16 | async-start | bytes 3317760 | tf_op jit(solution)/shard_map/all_gather | solution.py:150
  14.8 236.1 %all-gather.48.cloned.1.call-start = ((), (), s32[]{:S(2)}) async-start(), calls=%async_computation.37 | async-start | bytes 2654208 | tf_op jit(solution)/shard_map/all_gather | solution.py:164
  16.1 150.9 %copy-start.12 = (f32[704,32]{0,1:T(8,128)}, f32[704,32]{0,1:T(8,128)S(1)}, u32[]{:S(2)}) copy-start(f32[704,32]{0,1:T(8,128)S(1)} %get-tuple-element.503) | copy-start | bytes 270340
  16.1 873.3 %copy-start.11 = (f32[704,32]{0,1:T(8,128)}, f32[704,32]{0,1:T(8,128)S(1)}, u32[]{:S(2)}) copy-start(f32[704,32]{0,1:T(8,128)S(1)} %get-tuple-element.504) | copy-start | bytes 270340
  168.5 59.5 %copy-start.17 = (s32[1408]{0:T(1024)S(1)}, s32[1408]{0:T(1024)}, u32[]{:S(2)}) copy-start(s32[1408]{0:T(1024)} %param.32) | copy-start | bytes 16900
  168.5 113.8 %all-gather.50.cloned.1.call-start = ((), (), s32[]{:S(2)}) async-start(), calls=%async_computation.38 | async-start | bytes 2654208 | tf_op jit(solution)/shard_map/all_gather | solution.py:165
  226.9 116.2 %all-gather.30.cloned.1.call-start = ((), (), s32[]{:S(2)}) async-start(), calls=%async_computation.17 | async-start | bytes 3317760 | tf_op jit(solution)/shard_map/all_gather | solution.py:151
  227.7 182.7 %reduce-scatter.18.cloned.1.call-start = ((), (), s32[]{:S(2)}) async-start(), calls=%async_computation.18 | async-start | bytes 8110080 | tf_op jit(solution)/shard_map/reduce_scatter | solution.py:97
  228.0 26.2 %copy-start.4 = (bf16[9,704,64]{1,2,0:T(8,128)(2,1)}, bf16[9,704,64]{1,2,0:T(8,128)(2,1)S(1)}, u32[]{:S(2)}) copy-start(bf16[9,704,64]{1,2,0:T(8,128)(2,1)S(1)} %fusion.82) | copy-start | bytes 2433028
  256.7 31.4 %copy-start.6 = (bf16[9,704,64]{1,2,0:T(8,128)(2,1)S(1)}, bf16[9,704,64]{1,2,0:T(8,128)(2,1)}, u32[]{:S(2)}) copy-start(bf16[9,704,64]{1,2,0:T(8,128)(2,1)} %copy-done.4) | copy-start | bytes 2433028
  350.5 59.9 %copy-start = (bf16[176,2304]{1,0:T(8,128)(2,1)S(1)}, bf16[176,2304]{1,0:T(8,128)(2,1)}, u32[]{:S(2)}) copy-start(bf16[176,2304]{1,0:T(8,128)(2,1)} %param.20) | copy-start | bytes 2433028
  350.5 171.1 %all-gather.34.cloned.1.call-start = ((), (), s32[]{:S(2)}) async-start(), calls=%async_computation.20 | async-start | bytes 7962624 | tf_op jit(solution)/shard_map/all_gather | solution.py:186
  351.2 199.7 %all-gather.32.cloned.1.call-start = ((), (), s32[]{:S(2)}) async-start(), calls=%async_computation.19 | async-start | bytes 4055040 | tf_op jit(solution)/shard_map/all_gather | solution.py:94
  413.3 249.0 %all-gather.38.cloned.1.call-start = ((), (), s32[]{:S(2)}) async-start(), calls=%async_computation.22 | async-start | bytes 7962624 | tf_op jit(solution)/shard_map/all_gather | solution.py:188
  414.0 357.5 %all-gather.36.cloned.1.call-start = ((), (), s32[]{:S(2)}) async-start(), calls=%async_computation.21 | async-start | bytes 7962624 | tf_op jit(solution)/shard_map/all_gather | solution.py:187
  414.6 435.2 %reduce-scatter.20.cloned.1.call-start = ((), (), s32[]{:S(2)}) async-start(), calls=%async_computation.23 | async-start | bytes 8110080 | tf_op jit(solution)/shard_map/reduce_scatter | solution.py:97
  791.8 61.2 %copy-start.7 = (bf16[176,2304]{1,0:T(8,128)(2,1)S(1)}, bf16[176,2304]{1,0:T(8,128)(2,1)}, u32[]{:S(2)}) copy-start(bf16[176,2304]{1,0:T(8,128)(2,1)} %param.30) | copy-start | bytes 2433028
  791.8 89.8 %all-gather.44.cloned.1.call-start = ((), (), s32[]{:S(2)}) async-start(), calls=%async_computation.27 | async-start | bytes 4055040 | tf_op jit(solution)/shard_map/all_gather | solution.py:94
  852.3 60.4 %all-gather.42.cloned.1.call-start = ((), (), s32[]{:S(2)}) async-start(), calls=%async_computation.25 | async-start | bytes 4055040 | tf_op jit(solution)/shard_map/all_gather | solution.py:94
  852.9 90.9 %all-gather.40.cloned.1.call-start = ((), (), s32[]{:S(2)}) async-start(), calls=%async_computation.24 | async-start | bytes 4055040 | tf_op jit(solution)/shard_map/all_gather | solution.py:94
  854.0 122.3 %all-gather.52.cloned.1.call-start = ((), (), s32[]{:S(2)}) async-start(), calls=%async_computation.39 | async-start | bytes 2654208 | tf_op jit(solution)/shard_map/all_gather | solution.py:164
  891.0 115.1 %all-gather.54.cloned.1.call-start = ((), (), s32[]{:S(2)}) async-start(), calls=%async_computation.40 | async-start | bytes 2654208 | tf_op jit(solution)/shard_map/all_gather | solution.py:165
  897.7 170.7 %reduce-scatter.22.cloned.1.call-start = ((), (), s32[]{:S(2)}) async-start(), calls=%async_computation.26 | async-start | bytes 8110080 | tf_op jit(solution)/shard_map/reduce_scatter | solution.py:97
  912.7 10.7 copy-start.26
  954.9 9.0 copy-start.30
  954.9 9.0 copy-start.29
  974.3 156.5 %all-gather.46.cloned.1.call-start = ((), (), s32[]{:S(2)}) async-start(), calls=%async_computation.28 | async-start | bytes 4055040 | tf_op jit(solution)/shard_map/all_gather | solution.py:94
  1011.8 59.1 %copy-start.8 = (bf16[176,2304]{1,0:T(8,128)(2,1)S(1)}, bf16[176,2304]{1,0:T(8,128)(2,1)}, u32[]{:S(2)}) copy-start(bf16[176,2304]{1,0:T(8,128)(2,1)} %param.30) | copy-start | bytes 2433028
  1073.1 227.2 %reduce-scatter.40.cloned.1.call-start = ((), (), s32[]{:S(2)}) async-start(), calls=%async_computation.41 | async-start | bytes 5406720
  1251.8 99.2 %reduce-scatter.42.cloned.1.call-start = ((), (), s32[]{:S(2)}) async-start(), calls=%async_computation.42 | async-start | bytes 5406720
  1256.8 227.4 %reduce-scatter.34.cloned.1.call-start = ((), (), s32[]{:S(2)}) async-start(), calls=%async_computation.34 | async-start | bytes 7962624 | tf_op jit(solution)/shard_map/reduce_scatter | solution.py:235
  1267.7 348.1 %reduce-scatter.36.cloned.1.call-start = ((), (), s32[]{:S(2)}) async-start(), calls=%async_computation.35 | async-start | bytes 7962624 | tf_op jit(solution)/shard_map/reduce_scatter | solution.py:238
  1277.7 470.4 %reduce-scatter.38.cloned.1.call-start = ((), (), s32[]{:S(2)}) async-start(), calls=%async_computation.36 | async-start | bytes 7962624 | tf_op jit(solution)/shard_map/reduce_scatter | solution.py:241
  1289.3 533.7 %reduce-scatter.32.cloned.1.call-start = ((), (), s32[]{:S(2)}) async-start(), calls=%async_computation.33 | async-start | bytes 3317760 | tf_op jit(solution)/shard_map/reduce_scatter | solution.py:286
  1296.0 602.4 %reduce-scatter.26.cloned.1.call-start = ((), (), s32[]{:S(2)}) async-start(), calls=%async_computation.30 | async-start | bytes 3317760 | tf_op jit(solution)/shard_map/reduce_scatter | solution.py:277
  1308.6 665.0 %reduce-scatter.28.cloned.1.call-start = ((), (), s32[]{:S(2)}) async-start(), calls=%async_computation.31 | async-start | bytes 3317760 | tf_op jit(solution)/shard_map/reduce_scatter | solution.py:280
  1315.9 733.3 %reduce-scatter.30.cloned.1.call-start = ((), (), s32[]{:S(2)}) async-start(), calls=%async_computation.32 | async-start | bytes 3317760 | tf_op jit(solution)/shard_map/reduce_scatter | solution.py:283
  1359.4 751.0 %reduce-scatter.24.cloned.1.call-start = ((), (), s32[]{:S(2)}) async-start(), calls=%async_computation.29 | async-start | bytes 8110080 | tf_op jit(solution)/shard_map/reduce_scatter | solution.py:97
  1618.4 492.0 %copy-start.1 = (bf16[176,2304]{1,0:T(8,128)(2,1)S(1)}, bf16[176,2304]{1,0:T(8,128)(2,1)}, u32[]{:S(2)}) copy-start(bf16[176,2304]{1,0:T(8,128)(2,1)} %param.20) | copy-start | bytes 2433028
  1618.4 492.0 %copy-start.15 = (f32[2304]{0:T(1024)S(1)}, f32[2304]{0:T(1024)}, u32[]{:S(2)}) copy-start(f32[2304]{0:T(1024)} %copy-done.14) | copy-start | bytes 27652
  1618.4 492.0 %copy-start.19 = (f32[176]{0:T(256)S(1)}, f32[176]{0:T(256)}, u32[]{:S(2)}) copy-start(f32[176]{0:T(256)} %copy-done.18) | copy-start | bytes 2116
  1750.7 361.7 %copy-start.16 = (f32[2304]{0:T(1024)S(1)}, f32[2304]{0:T(1024)}, u32[]{:S(2)}) copy-start(f32[2304]{0:T(1024)} %get-tuple-element.379) | copy-start | bytes 27652
  1750.7 401.6 %copy-start.2 = (f32[176,2304]{1,0:T(8,128)S(1)}, f32[176,2304]{1,0:T(8,128)}, u32[]{:S(2)}) copy-start(f32[176,2304]{1,0:T(8,128)} %get-tuple-element.471) | copy-start | bytes 4866052
  1750.7 401.6 %copy-start.22 = (f32[176]{0:T(256)S(1)}, f32[176]{0:T(256)}, u32[]{:S(2)}) copy-start(f32[176]{0:T(256)} %get-tuple-element.505) | copy-start | bytes 2116
  (13 other events, 38.3 us)
Sparse Core Ops, SparseCore 0:
  10.2 61.0 all-gather.25
  73.4 27.7 all-gather.21
  103.4 58.3 all-gather.23
  163.8 56.9 all-gather.27
  222.8 28.0 all-gather.47
  252.9 29.4 all-gather.49
  284.5 58.4 all-gather.29
  350.6 59.7 reduce-scatter.17
  412.8 108.7 all-gather.33
  523.6 27.2 all-gather.31
  553.4 108.7 all-gather.37
  664.5 106.9 all-gather.35
  791.9 57.8 reduce-scatter.19
  852.4 29.0 all-gather.43
  883.5 29.0 all-gather.41
  914.6 29.0 all-gather.39
  945.7 29.4 all-gather.51
  976.6 29.4 all-gather.53
  1008.6 59.6 reduce-scatter.21
  1073.2 29.0 all-gather.45
  1251.9 48.3 reduce-scatter.39
  1302.6 48.3 reduce-scatter.41
  1355.1 129.0 reduce-scatter.33
  1487.7 128.0 reduce-scatter.35
  1620.0 128.0 reduce-scatter.37
  1751.5 71.4 reduce-scatter.31
  1826.8 71.4 reduce-scatter.25
  1901.9 71.6 reduce-scatter.27
  1977.6 71.5 reduce-scatter.29
  2051.6 58.8 reduce-scatter.23
where the time goes:
time: 2170 us; the launch traced here: 2160 us
  waiting for transfers between devices  1600 us (74%)
  matrix products  397 us (18%)
  other arithmetic  59.4 us (3%)
  local copies, waits for them, and re-layouts  50.5 us (2%)
  blocking collectives  39.9 us (2%)
    reduce_scatter x4, waiting for transfers between devices, sum_rows(): return lax.psum_scatter(field, 'mp', scatter_dimension=0, tiled=True)  228 us
    reduce_scatter x1, waiting for transfers between devices, shards(): lax.psum_scatter(grad_down.astype(jnp.bfloat16), ('dp', 'ctx'), scatter_d...  130 us
    reduce_scatter x1, waiting for transfers between devices, shards(): lax.psum_scatter(grad_up.astype(jnp.bfloat16), ('dp', 'ctx'), scatter_dim...  129 us
    all_gather x6, waiting for transfers between devices, gather_rows(): return lax.all_gather(field, 'mp', axis=0, tiled=True)  113 us
    reduce_scatter x1, waiting for transfers between devices, shards(): lax.psum_scatter(grad_gate.astype(jnp.bfloat16), ('dp', 'ctx'), scatter_d...  112 us
    all_gather x1, waiting for transfers between devices, mlp_core(): lax.all_gather(w_up, ('dp', 'ctx'), axis=0, tiled=True)  109 us
    all_gather x1, waiting for transfers between devices, mlp_core(): lax.all_gather(w_gate, ('dp', 'ctx'), axis=0, tiled=True)  107 us
    dot_general x27, matrix products, scores_of(): jnp.einsum('qd,kd->qk', query_head, key_head, preferred_element_type=jnp....  102 us
  transfers between devices with their start and end apart: 30, of which 27 were waited for; matrix products, arithmetic and copies ran while one was open for 16% of the time, Pallas kernels for 0%

commit v1 on v0

v1 whole, which is shorter than its diff:
```python
import functools
import math

import jax
import jax.numpy as jnp
from jax import lax
from jax.experimental import pallas as pl
from jax.experimental.pallas import tpu as pltpu
from jax.sharding import PartitionSpec as P

HEAD_DIM = 64
LANES = 128
PAIRS = 2
TILE = 128

eps = 1e-05
branch_scale = 1.4 / math.sqrt(40.0)
rope_base = 10000.0
masked_value = -1e30

f32 = jnp.float32
bf16 = jnp.bfloat16

NN = (((1,), (0,)), ((), ()))
NT = (((1,), (1,)), ((), ()))
TN = (((0,), (0,)), ((), ()))


def dot(left, right, dims=NN):
    return lax.dot_general(left, right, dims, preferred_element_type=f32)


def normalize(field):
    return field * lax.rsqrt(jnp.mean(field * field, axis=-1, keepdims=True) + eps)


def norm_back(field, gain_f32, incoming):
    inverse = lax.rsqrt(jnp.mean(field * field, axis=-1, keepdims=True) + eps)
    scaled = gain_f32 * incoming
    along = jnp.mean(field * scaled, axis=-1, keepdims=True)
    return (
        inverse * scaled - field * inverse**3 * along,
        jnp.sum(incoming * field * inverse, axis=0),
    )


def flip_x(field):
    return lax.ppermute(field, "ctx", [(0, 1), (1, 0)])


def flip_y(field):
    return lax.ppermute(field, "mp", [(0, 2), (2, 0), (1, 3), (3, 1)])


def flip_core(field):
    return lax.ppermute(field, "mp", [(0, 1), (1, 0), (2, 3), (3, 2)])


def gather_rows(own):
    half = own.shape[0] // 2
    from_x, from_y = flip_x(own), flip_y(own)
    corner = jnp.concatenate([flip_y(from_x[:half]), flip_x(from_y[half:])], axis=0)
    near = jnp.concatenate([own, from_y, from_x, corner], axis=0)
    return jnp.concatenate([near, flip_core(near)], axis=0)


def sum_rows(left, right, dims):
    count = left.shape[0] // 2
    block = count // 4
    half = block // 2
    away = flip_core(dot(left[count:], right, dims).astype(bf16))
    total = dot(left[:count], right, dims) + away.astype(f32)
    total = total.reshape(2, 2, block, total.shape[-1])
    got_x = flip_x(total[1, :, :half].astype(bf16)).astype(f32)
    got_y = flip_y(total[:, 1, half:].astype(bf16)).astype(f32)
    upper = total[0, :, :half] + got_x
    lower = total[:, 0, half:] + got_y
    upper = upper[0] + flip_y(upper[1].astype(bf16)).astype(f32)
    lower = lower[0] + flip_x(lower[1].astype(bf16)).astype(f32)
    return jnp.concatenate([upper, lower], axis=0)


def sum_all(field):
    total = flip_core(field) + field
    total = flip_y(total) + total
    total = flip_x(total) + total
    count, step = lax.axis_size("dp"), 1
    if count & (count - 1):
        return lax.psum(total, "dp")
    while step < count:
        total = lax.ppermute(total, "dp", [(i, i ^ step) for i in range(count)]) + total
        step *= 2
    return total


def lane_mask(rows, upper):
    lane = lax.broadcasted_iota(jnp.int32, (rows, LANES), 1)
    return lane >= HEAD_DIM if upper else lane < HEAD_DIM


def swap_halves(field):
    lane = lax.broadcasted_iota(jnp.int32, field.shape, 1)
    return jnp.where(
        lane % HEAD_DIM < HEAD_DIM // 2,
        pltpu.roll(field, LANES - HEAD_DIM // 2, 1),
        pltpu.roll(field, HEAD_DIM // 2, 1),
    )


def two_heads(block):
    zero = jnp.zeros_like(block)
    return jnp.concatenate(
        [
            jnp.where(lane_mask(block.shape[0], False), block, zero),
            jnp.where(lane_mask(block.shape[0], True), block, zero),
        ],
        axis=0,
    )


def forward_kernel(
    info, qkv_ref, cos_ref, sin_ref, bias_ref, rot_ref, mixed_ref, lse_ref, s_ref, e_ref, vt_ref, o_ref
):
    slot = qkv_ref.shape[0]
    rows = slot // 8
    tiles = slot // TILE
    for n in range(8):
        here = pl.ds(n * rows, rows)
        there = pl.ds(pl.multiple_of(info[n] * rows, 16), rows)
        cosine, sine = cos_ref[here, :], sin_ref[here, :]
        for g in (0, 1, 2, 3, 6):
            lanes = pl.ds(g * LANES, LANES)
            field = qkv_ref[there, lanes]
            field = field * cosine + swap_halves(field) * sine
            if g < 2:
                field = field * (HEAD_DIM**-0.5)
            if g == 6:
                field = jnp.where(lane_mask(rows, False), field * (HEAD_DIM**-0.5), field)
            rot_ref[here, lanes] = field.astype(bf16)
        for g in (4, 5):
            lanes = pl.ds(g * LANES, LANES)
            rot_ref[here, lanes] = qkv_ref[there, lanes].astype(bf16)
        lanes = pl.ds(7 * LANES, LANES)
        field = qkv_ref[there, lanes]
        rot_ref[here, lanes] = jnp.where(lane_mask(rows, False), field, 0.0).astype(bf16)

    def softmax_block(count, width, keys, queries, biases):
        top = jnp.full((8, width), masked_value, f32)
        for t in range(count):
            scores = dot(keys(t), queries, NT) + biases(t)
            s_ref[pl.ds(t * TILE, TILE), pl.ds(0, width)] = scores
            top = jnp.maximum(top, jnp.max(scores.reshape(TILE // 8, 8, width), axis=0))
        top = jnp.max(top, axis=0, keepdims=True)
        total = jnp.zeros((8, width), f32)
        for t in range(count):
            weights = jnp.exp(s_ref[pl.ds(t * TILE, TILE), pl.ds(0, width)] - top)
            total = total + jnp.sum(weights.reshape(TILE // 8, 8, width), axis=0)
            e_ref[pl.ds(t * TILE, TILE), pl.ds(0, width)] = weights.astype(bf16)
        total = jnp.sum(total, axis=0, keepdims=True)
        depth = count * TILE
        product = dot(vt_ref[:, pl.ds(0, depth)], e_ref[pl.ds(0, depth), pl.ds(0, width)])
        return product / total, top + jnp.log(total)

    def pair(g, carry):
        q_lanes = pl.ds(pl.multiple_of(g * LANES, LANES), LANES)
        k_lanes = pl.ds(pl.multiple_of((PAIRS + g) * LANES, LANES), LANES)
        v_lanes = pl.ds(pl.multiple_of((2 * PAIRS + g) * LANES, LANES), LANES)
        o_lanes = pl.ds(pl.multiple_of((1 + g) * LANES, LANES), LANES)
        vt_ref[...] = rot_ref[:, v_lanes].T
        for i in range(tiles):
            cols = pl.ds(i * TILE, TILE)

            def biases(t):
                bias = bias_ref[pl.ds(t * TILE, TILE), cols]
                return jnp.concatenate([bias, bias], axis=1)

            product, log_total = softmax_block(
                i + 1,
                2 * TILE,
                lambda t: rot_ref[pl.ds(t * TILE, TILE), k_lanes],
                two_heads(rot_ref[cols, q_lanes]),
                biases,
            )
            lse_ref[g, :, pl.ds(i * 2 * TILE, 2 * TILE)] = jnp.broadcast_to(log_total, (8, 2 * TILE))
            out = jnp.concatenate([product[:HEAD_DIM, :TILE], product[HEAD_DIM:, TILE:]], axis=0)
            o_ref[cols, o_lanes] = out.T.astype(bf16)
        return carry

    lax.fori_loop(0, PAIRS, pair, 0)
    o_ref[:, pl.ds(0, LANES)] = jnp.zeros((slot, LANES), bf16)
    vt_ref[...] = rot_ref[:, pl.ds(7 * LANES, LANES)].T
    for j in range((tiles + 1) // 2):
        which = 2 * j + info[8]

        @pl.when(which < tiles)
        def _():
            cols = pl.ds(pl.multiple_of(which * TILE, TILE), TILE)
            queries = pltpu.roll(rot_ref[cols, pl.ds(6 * LANES, LANES)].astype(f32), HEAD_DIM, 1)
            queries = jnp.where(lane_mask(TILE, True), queries, 0.0).astype(bf16)
            product, log_total = softmax_block(
                min(2 * j + 2, tiles),
                TILE,
                lambda t: rot_ref[pl.ds(t * TILE, TILE), pl.ds(6 * LANES, LANES)],
                queries,
                lambda t: bias_ref[pl.ds(t * TILE, TILE), cols],
            )
            lse_ref[PAIRS, :, pl.ds(j * TILE, TILE)] = jnp.broadcast_to(log_total, (8, TILE))
            out = jnp.concatenate([jnp.zeros((HEAD_DIM, TILE), f32), product[:HEAD_DIM]], axis=0)
            o_ref[cols, pl.ds(0, LANES)] = out.T.astype(bf16)

    for n in range(8):
        there = pl.ds(pl.multiple_of(info[n] * rows, 16), rows)
        mixed_ref[there, :] = o_ref[pl.ds(n * rows, rows), :]


def backward_kernel(
    info, rot_ref, cos_ref, sin_ref, bias_ref, mixed_ref, dmix_ref, lse_ref, out_ref,
    d_ref, p_ref, ds_ref, kt_ref, dk_ref, dv_ref, dq_ref,
):
    slot = rot_ref.shape[0]
    rows = slot // 8
    tiles = slot // TILE
    for n in range(8):
        here = pl.ds(n * rows, rows)
        there = pl.ds(pl.multiple_of(info[n] * rows, 16), rows)
        d_rows = dmix_ref[there, :]
        d_ref[here, :] = d_rows
        p_ref[here, :] = d_rows.astype(f32) * mixed_ref[there, :].astype(f32)

    def row_sums(cols, lanes, upper):
        product = p_ref[cols, lanes]
        high = product.astype(bf16)
        low = (product - high.astype(f32)).astype(bf16)
        ones = jnp.where(lane_mask(8, upper), 1.0, 0.0).astype(bf16)
        return dot(ones, high, NT) + dot(ones, low, NT)

    def score_block(count, width, keys, values, queries, d_rows, biases, lse, centre):
        for t in range(count):
            here = pl.ds(t * TILE, TILE)
            probs = jnp.exp(dot(keys(t), queries, NT) + biases(t) - lse)
            d_probs = dot(values(t), d_rows, NT)
            d_scores = (probs * (d_probs - centre)).astype(bf16)
            ds_ref[here, pl.ds(0, width)] = d_scores
            dk_ref[here, :] += dot(d_scores, queries)
            dv_ref[here, :] += dot(probs.astype(bf16), d_rows)
        depth = count * TILE
        return dot(kt_ref[:, pl.ds(0, depth)], ds_ref[pl.ds(0, depth), pl.ds(0, width)]) * (HEAD_DIM**-0.5)

    def place(field_of, lanes, turned):
        for n in range(8):
            here = pl.ds(n * rows, rows)
            there = pl.ds(pl.multiple_of(info[n] * rows, 16), rows)
            field = field_of(here)
            if turned:
                field = field * cos_ref[here, :] - swap_halves(field) * sin_ref[here, :]
            out_ref[there, lanes] = field.astype(bf16)

    def pair(g, carry):
        q_lanes = pl.ds(pl.multiple_of(g * LANES, LANES), LANES)
        k_lanes = pl.ds(pl.multiple_of((PAIRS + g) * LANES, LANES), LANES)
        v_lanes = pl.ds(pl.multiple_of((2 * PAIRS + g) * LANES, LANES), LANES)
        o_lanes = pl.ds(pl.multiple_of((1 + g) * LANES, LANES), LANES)
        kt_ref[...] = rot_ref[:, k_lanes].T
        dk_ref[...] = jnp.zeros_like(dk_ref)
        dv_ref[...] = jnp.zeros_like(dv_ref)
        for i in range(tiles):
            cols = pl.ds(i * TILE, TILE)

            def biases(t):
                bias = bias_ref[pl.ds(t * TILE, TILE), cols]
                return jnp.concatenate([bias, bias], axis=1)

            centre = jnp.concatenate([row_sums(cols, o_lanes, False), row_sums(cols, o_lanes, True)], axis=1)
            d_query = score_block(
                i + 1,
                2 * TILE,
                lambda t: rot_ref[pl.ds(t * TILE, TILE), k_lanes],
                lambda t: rot_ref[pl.ds(t * TILE, TILE), v_lanes],
                two_heads(rot_ref[cols, q_lanes]),
                two_heads(d_ref[cols, o_lanes]),
                biases,
                lse_ref[g, pl.ds(0, 1), pl.ds(i * 2 * TILE, 2 * TILE)],
                centre[0:1],
            )
            out = jnp.concatenate([d_query[:HEAD_DIM, :TILE], d_query[HEAD_DIM:, TILE:]], axis=0)
            dq_ref[cols, :] = out.T
        place(lambda here: dq_ref[here, :], q_lanes, True)
        place(lambda here: dk_ref[here, :], k_lanes, True)
        place(lambda here: dv_ref[here, :], v_lanes, False)
        return carry

    lax.fori_loop(0, PAIRS, pair, 0)
    k_lanes, v_lanes = pl.ds(6 * LANES, LANES), pl.ds(7 * LANES, LANES)
    kt_ref[...] = rot_ref[:, k_lanes].T
    dk_ref[...] = jnp.zeros_like(dk_ref)
    dv_ref[...] = jnp.zeros_like(dv_ref)
    dq_ref[...] = jnp.zeros_like(dq_ref)
    for j in range((tiles + 1) // 2):
        which = 2 * j + info[8]

        @pl.when(which < tiles)
        def _():
            cols = pl.ds(pl.multiple_of(which * TILE, TILE), TILE)
            queries = pltpu.roll(rot_ref[cols, k_lanes].astype(f32), HEAD_DIM, 1)
            queries = jnp.where(lane_mask(TILE, True), queries, 0.0).astype(bf16)
            d_rows = pltpu.roll(d_ref[cols, pl.ds(0, LANES)].astype(f32), HEAD_DIM, 1)
            d_rows = jnp.where(lane_mask(TILE, False), d_rows, 0.0).astype(bf16)
            d_query = score_block(
                min(2 * j + 2, tiles),
                TILE,
                lambda t: rot_ref[pl.ds(t * TILE, TILE), k_lanes],
                lambda t: rot_ref[pl.ds(t * TILE, TILE), v_lanes],
                queries,
                d_rows,
                lambda t: bias_ref[pl.ds(t * TILE, TILE), cols],
                lse_ref[PAIRS, pl.ds(0, 1), pl.ds(j * TILE, TILE)],
                row_sums(cols, pl.ds(0, LANES), True)[0:1],
            )
            out = jnp.concatenate([d_query[HEAD_DIM:], jnp.zeros((HEAD_DIM, TILE), f32)], axis=0)
            dq_ref[cols, :] = out.T

    place(lambda here: dq_ref[here, :] + dk_ref[here, :], k_lanes, True)
    place(lambda here: dv_ref[here, :], v_lanes, False)


SMEM_SPEC = pl.BlockSpec(memory_space=pltpu.SMEM)
VMEM_SPEC = pl.BlockSpec(memory_space=pltpu.VMEM)


def attention_forward(info, qkv, cosine, sine, bias):
    slot = qkv.shape[0]
    pieces = slot // TILE
    return pl.pallas_call(
        forward_kernel,
        out_shape=(
            jax.ShapeDtypeStruct((slot, 8 * LANES), bf16),
            jax.ShapeDtypeStruct((slot, 3 * LANES), bf16),
            jax.ShapeDtypeStruct((PAIRS + 1, 8, pieces * 2 * TILE), f32),
        ),
        in_specs=[SMEM_SPEC] + [VMEM_SPEC] * 4,
        out_specs=(VMEM_SPEC,) * 3,
        scratch_shapes=[
            pltpu.VMEM((slot, 2 * TILE), f32),
            pltpu.VMEM((slot, 2 * TILE), bf16),
            pltpu.VMEM((LANES, slot), bf16),
            pltpu.VMEM((slot, 3 * LANES), bf16),
        ],
        compiler_params=pltpu.CompilerParams(vmem_limit_bytes=48 << 20),
        cost_estimate=pl.CostEstimate(
            flops=20 * slot * slot * 128, bytes_accessed=24 << 20, transcendentals=3 * slot * slot
        ),
        name="attention_forward",
    )(info, qkv, cosine, sine, bias)


def attention_backward(info, rotated, cosine, sine, bias, mixed, d_mixed, log_total):
    slot = rotated.shape[0]
    return pl.pallas_call(
        backward_kernel,
        out_shape=jax.ShapeDtypeStruct((slot, 8 * LANES), bf16),
        in_specs=[SMEM_SPEC] + [VMEM_SPEC] * 7,
        out_specs=VMEM_SPEC,
        scratch_shapes=[
            pltpu.VMEM((slot, 3 * LANES), bf16),
            pltpu.VMEM((slot, 3 * LANES), f32),
            pltpu.VMEM((slot, 2 * TILE), bf16),
            pltpu.VMEM((LANES, slot), bf16),
            pltpu.VMEM((slot, LANES), f32),
            pltpu.VMEM((slot, LANES), f32),
            pltpu.VMEM((slot, LANES), f32),
        ],
        compiler_params=pltpu.CompilerParams(vmem_limit_bytes=48 << 20),
        cost_estimate=pl.CostEstimate(
            flops=50 * slot * slot * 128, bytes_accessed=24 << 20, transcendentals=3 * slot * slot
        ),
        name="attention_backward",
    )(info, rotated, cosine, sine, bias, mixed, d_mixed, log_total)


def shards(
    tokens,
    w_query,
    w_key,
    w_value,
    w_out,
    gain_attn,
    w_gate,
    w_up,
    w_down,
    gain_mlp,
    cotangent,
    lineage,
    padding,
    positions,
):
    slot = lineage.shape[1]
    on_x, on_mp = lax.axis_index("ctx"), lax.axis_index("mp")
    on_y, on_core = on_mp // 2, on_mp % 2
    lower_x = on_x == 0
    heads = w_query.shape[1] // HEAD_DIM
    own_cols = heads // 2 * HEAD_DIM
    ff_half = w_gate.shape[1] // 2
    ff_pad = -(-ff_half // LANES) * LANES

    info = []
    for n in range(8):
        d_x, d_y, d_core = on_x ^ (n // 4), on_y ^ (n // 2 % 2), on_core ^ (n % 2)
        info.append(d_core * 4 + d_x * 2 + d_y)
    info = jnp.stack(info + [on_x] + [jnp.zeros_like(on_x)] * 7).astype(jnp.int32)

    gain_a = gain_attn.astype(f32)
    gain_m = gain_mlp.astype(f32)
    inputs = tokens.astype(f32)
    grad_rows = cotangent.astype(f32)

    def both_x(mine, theirs):
        got = flip_x(theirs)
        return jnp.where(lower_x, jnp.concatenate([mine, got], 0), jnp.concatenate([got, mine], 0))

    out_t = w_out.T
    a_cols = [w[:, :own_cols] for w in (w_query, w_key, w_value, out_t)]
    b_cols = [w[:, own_cols : 2 * own_cols] for w in (w_query, w_key, w_value, out_t)]
    s_cols = [w[:, 2 * own_cols :] for w in (w_query, w_key, w_value, out_t)]

    def pack(cols):
        return jnp.concatenate(cols[:3] + s_cols + cols[3:], axis=1)

    attn_a, attn_b = pack(a_cols), pack(b_cols)
    attn_part = both_x(jnp.where(lower_x, attn_a, attn_b), jnp.where(lower_x, attn_b, attn_a))

    def halves(weight):
        fill = ((0, 0), (0, ff_pad - ff_half))
        first, second = jnp.pad(weight[:, :ff_half], fill), jnp.pad(weight[:, ff_half:], fill)
        return jnp.where(lower_x, first, second), jnp.where(lower_x, second, first)

    gate_mine, gate_theirs = halves(w_gate)
    up_mine, up_theirs = halves(w_up)
    down_mine, down_theirs = halves(w_down.T)
    gu_part = both_x(
        jnp.concatenate([gate_mine, up_mine], 1), jnp.concatenate([gate_theirs, up_theirs], 1)
    )
    down_part = both_x(down_mine, down_theirs)

    attn_w = lax.all_gather(attn_part, "dp", axis=0, tiled=True)
    gu_w = lax.all_gather(gu_part, "dp", axis=0, tiled=True)
    down_w = lax.all_gather(down_part, "dp", axis=0, tiled=True)
    qkv_w = attn_w[:, : 8 * LANES]
    out_w = attn_w[:, 7 * LANES :]

    index = jnp.arange(slot, dtype=jnp.int32)
    own_seg = lineage[0]
    related = (
        (own_seg[:, None] == lineage[0][None, :])
        | (own_seg[:, None] == lineage[1][None, :])
        | (own_seg[:, None] == lineage[2][None, :])
    )
    live = padding == 0
    allowed = (index[:, None] == index[None, :]) | (
        related & live[:, None] & live[None, :] & (index[:, None] < index[None, :])
    )
    bias = jnp.where(allowed, 0.0, masked_value).astype(f32)
    half_dim = HEAD_DIM // 2
    inv_freq = rope_base ** (-2.0 * jnp.arange(half_dim, dtype=f32) / HEAD_DIM)
    angles = positions.astype(f32)[:, None] * inv_freq[None, :]
    cos, sin = jnp.cos(angles), jnp.sin(angles)
    cosine = jnp.concatenate([cos, cos, cos, cos], axis=1)
    sine = jnp.concatenate([-sin, sin, -sin, sin], axis=1)

    normed_a = gather_rows((normalize(inputs) * gain_a).astype(bf16))
    qkv = dot(normed_a, qkv_w)
    rotated, mixed, log_total = attention_forward(info, qkv, cosine, sine, bias)
    residual = inputs + branch_scale * sum_rows(mixed, out_w, NT)
    normed_m = gather_rows((normalize(residual) * gain_m).astype(bf16))
    gate_up = dot(normed_m, gu_w)
    gate, up = gate_up[:, :ff_pad], gate_up[:, ff_pad:]
    sigmoid_gate = jax.nn.sigmoid(gate)
    hidden = (gate * sigmoid_gate * up).astype(bf16)
    output = residual + branch_scale * sum_rows(hidden, down_w, NT)

    d_mlp = gather_rows((branch_scale * grad_rows).astype(bf16))
    grad_down = lax.psum_scatter(
        dot(d_mlp, hidden, TN).astype(bf16), "dp", scatter_dimension=0, tiled=True
    )
    d_hidden = dot(d_mlp, down_w)
    d_gate = (d_hidden * up * sigmoid_gate * (1.0 + gate * (1.0 - sigmoid_gate))).astype(bf16)
    d_up = (d_hidden * (gate * sigmoid_gate)).astype(bf16)
    d_gate_up = jnp.concatenate([d_gate, d_up], axis=1)
    d_normed_mlp = sum_rows(d_gate_up, gu_w, NT)
    grad_gu = lax.psum_scatter(
        dot(normed_m, d_gate_up, TN).astype(bf16), "dp", scatter_dimension=0, tiled=True
    )
    back_mlp, gain_mlp_part = norm_back(residual, gain_m, d_normed_mlp)
    d_residual = grad_rows + back_mlp

    d_attn = gather_rows((branch_scale * d_residual).astype(bf16))
    d_mixed = dot(d_attn, out_w).astype(bf16)
    grad_o = lax.psum_scatter(
        dot(d_attn, mixed, TN).astype(bf16), "dp", scatter_dimension=0, tiled=True
    )
    d_qkv = attention_backward(info, rotated, cosine, sine, bias, mixed, d_mixed, log_total)
    grad_qkv = lax.psum_scatter(
        dot(normed_a, d_qkv, TN).astype(bf16), "dp", scatter_dimension=0, tiled=True
    )
    d_normed_attn = sum_rows(d_qkv, qkv_w, NT)
    back_attn, gain_attn_part = norm_back(inputs, gain_a, d_normed_attn)
    input_grad = d_residual + back_attn
    gains = sum_all(jnp.stack([gain_attn_part, gain_mlp_part]))

    def rows_of_x(field):
        rows = field.shape[0] // 2
        mine = jnp.where(lower_x, field[:rows], field[rows:])
        got = flip_x(jnp.where(lower_x, field[rows:], field[:rows]))
        return mine.astype(f32), got.astype(f32)

    def join(mine, got):
        return jnp.where(lower_x, jnp.concatenate([mine, got], 1), jnp.concatenate([got, mine], 1))

    def join_heads(mine, got, at, shared_at):
        whole = join(mine[:, at : at + own_cols], got[:, at : at + own_cols])
        last = slice(shared_at, shared_at + HEAD_DIM)
        return jnp.concatenate([whole, mine[:, last] + got[:, last]], axis=1)

    mine, got = rows_of_x(grad_gu)
    grad_gate = join(mine[:, :ff_half], got[:, :ff_half])
    grad_up = join(mine[:, ff_pad : ff_pad + ff_half], got[:, ff_pad : ff_pad + ff_half])
    mine, got = rows_of_x(grad_down)
    grad_down = join(mine[:, :ff_half], got[:, :ff_half]).T
    mine, got = rows_of_x(grad_o)
    grad_out = join_heads(mine, got, LANES, HEAD_DIM).T
    mine, got = rows_of_x(grad_qkv)
    grad_query = join_heads(mine, got, 0, 6 * LANES)
    grad_key = join_heads(mine, got, 2 * LANES, 6 * LANES + HEAD_DIM)
    grad_value = join_heads(mine, got, 4 * LANES, 7 * LANES)

    return (
        output.astype(bf16),
        input_grad.astype(bf16),
        grad_query,
        grad_key,
        grad_value,
        grad_out,
        gains[0],
        grad_gate,
        grad_up,
        grad_down,
        gains[1],
    )


def solution(mesh):
    placed = (
        P(("dp", "ctx", "mp"), None),
        P(("dp", "ctx"), "mp"),
        P(("dp", "ctx"), "mp"),
        P(("dp", "ctx"), "mp"),
        P("mp", ("dp", "ctx")),
        P(),
        P(("dp", "ctx"), "mp"),
        P(("dp", "ctx"), "mp"),
        P("mp", ("dp", "ctx")),
        P(),
        P(("dp", "ctx", "mp"), None),
        P(None, "dp"),
        P("dp"),
        P("dp"),
    )
    return jax.shard_map(
        shards,
        mesh=mesh,
        in_specs=placed,
        out_specs=(
            P(("dp", "ctx", "mp"), None),
            P(("dp", "ctx", "mp"), None),
            P(("dp", "ctx"), "mp"),
            P(("dp", "ctx"), "mp"),
            P(("dp", "ctx"), "mp"),
            P("mp", ("dp", "ctx")),
            P(),
            P(("dp", "ctx"), "mp"),
            P(("dp", "ctx"), "mp"),
            P("mp", ("dp", "ctx")),
            P(),
        ),
        check_vma=False,
    )
```

time: 2170 us -> 836 us (0.39)
  waiting for transfers between devices: 1600 us -> 460 us
  matrix products: 397 us -> 141 us
  Pallas kernels: 0 us -> 66.6 us
  starting transfers between devices: 2.4 us -> 48.8 us
  blocking collectives: 39.9 us -> 0 us
    reduce_scatter x11 -> x4, waiting for transfers between devices: 891 us -> 67.7 us  [the longest x1 64 us: shards(): lax.psum_scatter(dot(normed_a, d_qkv, TN).astype(bf16), 'dp', scatter_dim...]
    all_gather x17 -> x3, waiting for transfers between devices: 660 us -> 137 us  [the longest x1 63 us: shards(): attn_w = lax.all_gather(attn_part, 'dp', axis=0, tiled=True)]
    dot_general x106 -> x16, matrix products: 397 us -> 141 us  [dot(): return lax.dot_general(left, right, dims, preferred_element_type=f32)]
    ppermute x0 -> x52, waiting for transfers between devices: none -> 255 us  [the longest x24 187 us: flip_x(): return lax.ppermute(field, 'ctx', [(0, 1), (1, 0)])]
    pallas_call x0 -> x2, Pallas kernels: none -> 66.6 us  [the longest x1 44.8 us: attention_backward(): pl.pallas_call(backward_kernel, out_shape=jax.ShapeDtypeStruct((slot, 8 *...]
    ppermute x0 -> x52, starting transfers between devices: none -> 47.8 us  [the longest x24 25.1 us: flip_x(): return lax.ppermute(field, 'ctx', [(0, 1), (1, 0)])]
    unnamed x32 -> x7, waiting for transfers between devices: 44.7 us -> 0.11 us
    psum x1 -> x0, blocking collectives: 39.9 us -> none  [shards(): lax.psum((gain_attn_part, gain_mlp_part), ('dp', 'ctx', 'mp'))]
  transfers between devices with their start and end apart: 30 -> 59, of which waited for: 27 -> 35; matrix products, arithmetic and copies ran while one was open for 16% -> 22% of each run, Pallas kernels for 0% -> 5%
where the time goes in v1:
time: 836 us; the launch traced here: 830 us
  waiting for transfers between devices  460 us (55%)
  matrix products  141 us (17%)
  Pallas kernels  66.6 us (8%)
  local copies, waits for them, and re-layouts  50.6 us (6%)
  starting transfers between devices  48.8 us (6%)
  other arithmetic  47.4 us (6%)
  between operations  15.6 us (2%)
    ppermute x24, waiting for transfers between devices, flip_x(): return lax.ppermute(field, 'ctx', [(0, 1), (1, 0)])  187 us
    dot_general x16, matrix products, dot(): return lax.dot_general(left, right, dims, preferred_element_type=f32)  141 us
    reduce_scatter x1, waiting for transfers between devices, shards(): lax.psum_scatter(dot(normed_a, d_qkv, TN).astype(bf16), 'dp', scatter_dim...  64 us
    all_gather x1, waiting for transfers between devices, shards(): attn_w = lax.all_gather(attn_part, 'dp', axis=0, tiled=True)  63 us
    all_gather x1, waiting for transfers between devices, shards(): down_w = lax.all_gather(down_part, 'dp', axis=0, tiled=True)  54.7 us
    ppermute x17, waiting for transfers between devices, flip_y(): return lax.ppermute(field, 'mp', [(0, 2), (2, 0), (1, 3), (3, 1)])  54.1 us
    pallas_call x1, Pallas kernels, attention_backward(): pl.pallas_call(backward_kernel, out_shape=jax.ShapeDtypeStruct((slot, 8 *...  44.8 us
    ppermute x24, starting transfers between devices, flip_x(): return lax.ppermute(field, 'ctx', [(0, 1), (1, 0)])  25.1 us
  transfers between devices with their start and end apart: 59, of which 35 were waited for; matrix products, arithmetic and copies ran while one was open for 22% of the time, Pallas kernels for 5%

profile of v1, /device:TPU:0, one launch (start us, length us, event | category | flops | bytes accessed | tf_op | source)
XLA Modules:
  0.0 830.1 jit_solution(6575918648026502700)
XLA Ops:
  17.0 16.5 %collective-permute-done.5 = bf16[288,1280]{1,0:T(8,128)(2,1)S(1)} collective-permute-done((bf16[288,1280]{1,0:T(8,128)(2,1)S(1)}, bf16[288,1280]{1,0:T(8,128)(2,1)S(1)}, u32[]{:S(2)}, u32[]{:S(2)}) %collective-permute-start.5) | collective-permute-done | bytes 737312 | tf_op jit(solution)/shard_map/ppermute | solution.py:48
  41.6 15.0 %collective-permute-done.1 = bf16[176,2304]{1,0:T(8,128)(2,1)S(1)} collective-permute-done((bf16[176,2304]{1,0:T(8,128)(2,1)S(1)}, bf16[176,2304]{1,0:T(8,128)(2,1)S(1)}, u32[]{:S(2)}, u32[]{:S(2)}) %collective-permute-start.1) | collective-permute-done | bytes 811040 | tf_op jit(solution)/shard_map/ppermute | solution.py:48
  62.4 4.0 collective-permute-done.2
  72.4 6.5 fusion.1.bias_ref
  78.8 3.9 constant_dynamic-update-slice_fusion.5
  82.7 63.0 %all-gather.4.cloned.1.call-done = bf16[2304,1280]{1,0:T(8,128)(2,1)} async-done(((bf16[576,1280]{1,0:T(8,128)(2,1)}), bf16[2304,1280]{1,0:T(8,128)(2,1)}) %all-gather.4.cloned.1.call-update) | async-done | bytes 5898256 | tf_op jit(solution)/shard_map/all_gather | solution.py:444
  145.7 12.0 %fusion.7.qkv_ref = f32[1408,1024]{1,0:T(8,128)} fusion(bf16[1408,2304]{1,0:T(8,128)(2,1)} %constant_dynamic-update-slice_fusion.5, bf16[2304,1280]{1,0:T(8,128)(2,1)} %all-gather.4.cloned.1.call-done), kind=kOutput, calls=%fused_computation.40 | convolution fusion | flops 6643777536 | bytes 16973824 | tf_op jit(solution)/shard_map/dot_general | solution.py:30
  157.7 21.9 %attention_forward.1 = (bf16[1408,1024]{1,0:T(8,128)(2,1)S(1)}, bf16[1408,384]{1,0:T(8,128)(2,1)S(1)}, f32[3,8,2816]{2,1,0:T(8,128)S(1)}) custom-call(s32[16]{0:T(128)S(1)} %stack.48.info, f32[1408,1024]{1,0:T(8,128)} %fusion.7.qkv_ref, f32[1408,128]{1,0:T(8,128)S(1)} %get-tuple-element.134.cos_ref, f32[1408,128]{1,0:T(8,128)S(1)} %get-tuple-element.135.sin_ref, ...), custom_call_target="tpu_custom_call" | custom-call | flops 5075107840 | bytes 25165824 | tf_op jit(solution)/shard_map/attention_forward/pallas_call | solution.py:333
  179.7 6.1 convolution_convert_fusion.4
  192.5 17.9 %collective-permute-done.16 = bf16[288,1536]{1,0:T(8,128)(2,1)S(1)} collective-permute-done((bf16[288,1536]{1,0:T(8,128)(2,1)S(1)}, bf16[288,1536]{1,0:T(8,128)(2,1)S(1)}, u32[]{:S(2)}, u32[]{:S(2)}) %collective-permute-start.16) | collective-permute-done | bytes 884768 | tf_op jit(solution)/shard_map/ppermute | solution.py:48
  212.4 4.4 convert_add_fusion.3
  220.1 7.8 collective-permute-done.24
  236.5 8.7 %collective-permute-done.7 = bf16[2,88,2304]{2,1,0:T(8,128)(2,1)S(1)} collective-permute-done((bf16[2,88,2304]{2,1,0:T(8,128)(2,1)S(1)}, bf16[2,88,2304]{2,1,0:T(8,128)(2,1)S(1)}, u32[]{:S(2)}, u32[]{:S(2)}) %collective-permute-start.7) | collective-permute-done | bytes 811040 | tf_op jit(solution)/shard_map/ppermute | solution.py:48
  247.8 8.5 %collective-permute-done.8 = bf16[88,2304]{1,0:T(8,128)(2,1)S(1)} collective-permute-done((bf16[88,2304]{1,0:T(8,128)(2,1)S(1)}, bf16[88,2304]{1,0:T(8,128)(2,1)S(1)}, u32[]{:S(2)}, u32[]{:S(2)}) %collective-permute-start.8) | collective-permute-done | bytes 405536 | tf_op jit(solution)/shard_map/ppermute | solution.py:52
  256.4 5.8 collective-permute-done.10
  268.6 16.2 %collective-permute-done.12 = bf16[176,2304]{1,0:T(8,128)(2,1)S(1)} collective-permute-done((bf16[176,2304]{1,0:T(8,128)(2,1)S(1)}, bf16[176,2304]{1,0:T(8,128)(2,1)S(1)}, u32[]{:S(2)}, u32[]{:S(2)}) %collective-permute-start.12) | collective-permute-done | bytes 811040 | tf_op jit(solution)/shard_map/ppermute | solution.py:48
  288.8 6.1 collective-permute-done.13
  297.4 12.0 %collective-permute-done.17 = bf16[288,768]{1,0:T(8,128)(2,1)S(1)} collective-permute-done((bf16[288,768]{1,0:T(8,128)(2,1)S(1)}, bf16[288,768]{1,0:T(8,128)(2,1)S(1)}, u32[]{:S(2)}, u32[]{:S(2)}) %collective-permute-start.17) | collective-permute-done | bytes 442400 | tf_op jit(solution)/shard_map/ppermute | solution.py:48
  314.8 3.9 constant_dynamic-update-slice_fusion.16
  318.7 19.4 %all-gather.6.cloned.1.call-done = bf16[2304,1536]{1,0:T(8,128)(2,1)} async-done(((bf16[576,1536]{1,0:T(8,128)(2,1)}), bf16[2304,1536]{1,0:T(8,128)(2,1)}) %all-gather.6.cloned.1.call-update) | async-done | bytes 7077904 | tf_op jit(solution)/shard_map/all_gather | solution.py:445
  338.0 15.8 %fusion.81 = f32[1408,1536]{1,0:T(8,128)} fusion(bf16[1408,2304]{1,0:T(8,128)(2,1)} %constant_dynamic-update-slice_fusion.16, bf16[2304,1536]{1,0:T(8,128)(2,1)} %all-gather.6.cloned.1.call-done), kind=kOutput, calls=%fused_computation.252 | convolution fusion | flops 9965666304 | bytes 22216704 | tf_op jit(solution)/shard_map/dot_general | solution.py:30
  353.8 54.7 %all-gather.8.cloned.1.call-done = bf16[2304,768]{1,0:T(8,128)(2,1)} async-done(((bf16[576,768]{1,0:T(8,128)(2,1)}), bf16[2304,768]{1,0:T(8,128)(2,1)}) %all-gather.8.cloned.1.call-update) | async-done | bytes 3538960 | tf_op jit(solution)/shard_map/all_gather | solution.py:446
  408.5 12.9 %multiply_convert_fusion = (bf16[1408,768]{1,0:T(8,128)(2,1)}, bf16[1408,768]{1,0:T(8,128)(2,1)}, bf16[1408,768]{1,0:T(8,128)(2,1)S(1)}) fusion(f32[1408,1536]{1,0:T(8,128)} %fusion.81, bf16[1408,2304]{1,0:T(8,128)(2,1)} %constant_dynamic-update-slice_fusion.27, bf16[2304,768]{1,0:T(8,128)(2,1)} %all-gather.8.cloned.1.call-done), kind=kOutput, calls=%fused_computation.25 | convolution fusion | flops 4999053312 | bytes 25165824 | tf_op jit(solution)/shard_map/dot_general | solution.py:30
  421.3 4.1 convolution_convert_fusion.3
  426.3 8.4 %convolution_convert_fusion.6 = bf16[704,2304]{1,0:T(8,128)(2,1)} fusion(bf16[2304,1536]{1,0:T(8,128)(2,1)S(1)} %copy-done.31, bf16[1408,768]{1,0:T(8,128)(2,1)} %get-tuple-element.36, bf16[1408,768]{1,0:T(8,128)(2,1)} %get-tuple-element.35), kind=kOutput, calls=%fused_computation.24 | convolution fusion | flops 4988780544 | bytes 14647296 | tf_op jit(solution)/shard_map/dot_general | solution.py:30
  434.7 7.5 convolution_convert_fusion.2
  442.7 6.0 convert_add_fusion.2
  452.0 9.3 %convert_add_fusion.1 = f32[704,2304]{1,0:T(8,128)S(1)} fusion(bf16[704,2304]{1,0:T(8,128)(2,1)} %collective-permute-done.28, bf16[2304,1536]{1,0:T(8,128)(2,1)} %all-gather.6.cloned.1.call-done, bf16[1408,768]{1,0:T(8,128)(2,1)} %get-tuple-element.36, bf16[1408,768]{1,0:T(8,128)(2,1)} %get-tuple-element.35), kind=kOutput, calls=%fused_computation.11 | convolution fusion | flops 4990402560 | bytes 21135360 | tf_op jit(solution)/shard_map/dot_general | solution.py:30
  462.7 7.0 collective-permute-done.19
  474.0 13.1 %collective-permute-done.29 = bf16[2,88,2304]{2,1,0:T(8,128)(2,1)S(1)} collective-permute-done((bf16[2,88,2304]{2,1,0:T(8,128)(2,1)S(1)}, bf16[2,88,2304]{2,1,0:T(8,128)(2,1)S(1)}, u32[]{:S(2)}, u32[]{:S(2)}) %collective-permute-start.29) | collective-permute-done | bytes 811040 | tf_op jit(solution)/shard_map/ppermute | solution.py:48
  491.4 6.1 collective-permute-done.20
  497.7 7.8 collective-permute-done.30
  510.9 17.4 %collective-permute-done.34 = bf16[176,2304]{1,0:T(8,128)(2,1)S(1)} collective-permute-done((bf16[176,2304]{1,0:T(8,128)(2,1)S(1)}, bf16[176,2304]{1,0:T(8,128)(2,1)S(1)}, u32[]{:S(2)}, u32[]{:S(2)}) %collective-permute-start.34) | collective-permute-done | bytes 811040 | tf_op jit(solution)/shard_map/ppermute | solution.py:48
  530.7 7.5 collective-permute-done.35
  539.7 5.8 collective-permute-done.37
  548.4 4.9 convolution_convert_fusion.7
  553.4 16.6 %convolution_convert_fusion = bf16[2304,1536]{1,0:T(8,128)(2,1)} fusion(bf16[1408,2304]{1,0:T(8,128)(2,1)} %constant_dynamic-update-slice_fusion.16, bf16[1408,768]{1,0:T(8,128)(2,1)} %get-tuple-element.35, bf16[1408,768]{1,0:T(8,128)(2,1)} %get-tuple-element.36), kind=kOutput, calls=%fused_computation | convolution fusion | flops 9977856000 | bytes 17891328 | tf_op jit(solution)/shard_map/dot_general | solution.py:30
  570.2 7.1 convolution_convert_fusion.8.dmix_ref
  577.3 44.8 %attention_backward.1 = bf16[1408,1024]{1,0:T(8,128)(2,1)} custom-call(s32[16]{0:T(128)S(1)} %stack.48.info, bf16[1408,1024]{1,0:T(8,128)(2,1)} %copy-done, f32[1408,128]{1,0:T(8,128)S(1)} %get-tuple-element.134.cos_ref, f32[1408,128]{1,0:T(8,128)S(1)} %get-tuple-element.135.sin_ref, f32[1408,1408]{1,0:T(8,128)} %fusion.1.bias_ref, ...), custom_call_target="tpu_custom_call" | custom-call | flops 12687769600 | bytes 25165824 | tf_op jit(solution)/shard_map/attention_backward/pallas_call | solution.py:358
  622.0 6.8 convolution_convert_fusion.5
  630.2 12.2 %convolution_convert_fusion.1 = bf16[2304,1024]{1,0:T(8,128)(2,1)} fusion(bf16[1408,2304]{1,0:T(8,128)(2,1)} %constant_dynamic-update-slice_fusion.5, bf16[1408,1024]{1,0:T(8,128)(2,1)} %attention_backward.1), kind=kOutput, calls=%fused_computation.14 | convolution fusion | flops 6646136832 | bytes 14090240 | tf_op jit(solution)/shard_map/dot_general | solution.py:30
  642.5 7.5 convert_add_fusion
  659.8 19.6 %collective-permute-done.44 = bf16[288,384]{1,0:T(8,128)(2,1)S(1)} collective-permute-done((bf16[288,384]{1,0:T(8,128)(2,1)S(1)}, bf16[288,384]{1,0:T(8,128)(2,1)S(1)}, u32[]{:S(2)}, u32[]{:S(2)}) %collective-permute-start.44) | collective-permute-done | bytes 221216 | tf_op jit(solution)/shard_map/ppermute | solution.py:48
  684.6 8.7 %collective-permute-done.40 = bf16[88,2304]{1,0:T(8,128)(2,1)S(1)} collective-permute-done((bf16[88,2304]{1,0:T(8,128)(2,1)S(1)}, bf16[88,2304]{1,0:T(8,128)(2,1)S(1)}, u32[]{:S(2)}, u32[]{:S(2)}) %collective-permute-start.40) | collective-permute-done | bytes 405536 | tf_op jit(solution)/shard_map/ppermute | solution.py:52
  703.4 7.3 collective-permute-done.48
  720.8 16.7 %collective-permute-done.50 = bf16[288,1536]{1,0:T(8,128)(2,1)S(1)} collective-permute-done((bf16[288,1536]{1,0:T(8,128)(2,1)S(1)}, bf16[288,1536]{1,0:T(8,128)(2,1)S(1)}, u32[]{:S(2)}, u32[]{:S(2)}) %collective-permute-start.50) | collective-permute-done | bytes 884768 | tf_op jit(solution)/shard_map/ppermute | solution.py:48
  738.9 64.0 %reduce-scatter.5.cloned.1.call-done = bf16[576,1024]{1,0:T(8,128)(2,1)} async-done(((bf16[2304,1024]{1,0:T(8,128)(2,1)}), bf16[576,1024]{1,0:T(8,128)(2,1)}) %reduce-scatter.5.cloned.1.call-update) | async-done | bytes 1179664 | tf_op jit(solution)/shard_map/reduce_scatter | solution.py:501
  809.6 9.9 %collective-permute-done.43 = bf16[288,1024]{1,0:T(8,128)(2,1)S(1)} collective-permute-done((bf16[288,1024]{1,0:T(8,128)(2,1)S(1)}, bf16[288,1024]{1,0:T(8,128)(2,1)S(1)}, u32[]{:S(2)}, u32[]{:S(2)}) %collective-permute-start.43) | collective-permute-done | bytes 589856 | tf_op jit(solution)/shard_map/ppermute | solution.py:48
  (311 shorter events, 145.7 us)
Async XLA Ops:
  7.2 138.6 %all-gather.4.cloned.1.call-start = ((), (), s32[]{:S(2)}) async-start(), calls=%async_computation.4 | async-start | bytes 7372800 | tf_op jit(solution)/shard_map/all_gather | solution.py:444
  14.0 19.5 %collective-permute-start.5 = (bf16[288,1280]{1,0:T(8,128)(2,1)S(1)}, bf16[288,1280]{1,0:T(8,128)(2,1)S(1)}, u32[]{:S(2)}, u32[]{:S(2)}) collective-permute-start(bf16[288,1280]{1,0:T(8,128)(2,1)S(1)} %get-tuple-element.55), channel_id=1, source_target_pairs={{0,4},{4,0},{1,5},{5,1},{2,6},{6,2},{3,7},{7,3},{8,12},{12,8},{9,1... | collective-permute-start | bytes 2211848 | tf_op jit(solution)/shard_map/ppermute | solution.py:48
  35.2 302.8 %all-gather.6.cloned.1.call-start = ((), (), s32[]{:S(2)}) async-start(), calls=%async_computation.5 | async-start | bytes 8847360 | tf_op jit(solution)/shard_map/all_gather | solution.py:445
  37.3 19.3 %collective-permute-start.1 = (bf16[176,2304]{1,0:T(8,128)(2,1)S(1)}, bf16[176,2304]{1,0:T(8,128)(2,1)S(1)}, u32[]{:S(2)}, u32[]{:S(2)}) collective-permute-start(bf16[176,2304]{1,0:T(8,128)(2,1)S(1)} %get-tuple-element.34), channel_id=1, source_target_pairs={{0,4},{4,0},{1,5},{5,1},{2,6},{6,2},{3,7},{7,3},{8,12},{12,8},{9,1... | collective-permute-start | bytes 2433032 | tf_op jit(solution)/shard_map/ppermute | solution.py:48
  39.1 19.1 %collective-permute-start = (bf16[176,2304]{1,0:T(8,128)(2,1)S(1)}, bf16[176,2304]{1,0:T(8,128)(2,1)S(1)}, u32[]{:S(2)}, u32[]{:S(2)}) collective-permute-start(bf16[176,2304]{1,0:T(8,128)(2,1)S(1)} %get-tuple-element.34), channel_id=1, source_target_pairs={{0,2},{2,0},{1,3},{3,1},{4,6},{6,4},{5,7},{7,5},{8,10},{10,8},{9,1... | collective-permute-start | bytes 2433032 | tf_op jit(solution)/shard_map/ppermute | solution.py:52
  68.4 10.5 %collective-permute-start.4 = (bf16[704,2304]{1,0:T(8,128)(2,1)}, bf16[704,2304]{1,0:T(8,128)(2,1)}, u32[]{:S(2)}, u32[]{:S(2)}) collective-permute-start(bf16[704,2304]{1,0:T(8,128)(2,1)} %get-tuple-element.107), channel_id=1, source_target_pairs={{0,1},{1,0},{2,3},{3,2},{4,5},{5,4},{6,7},{7,6},{8,9},{9,8},{10,11... | collective-permute-start | bytes 9732104 | tf_op jit(solution)/shard_map/ppermute | solution.py:56
  185.8 26.6 %collective-permute-start.6 = (bf16[704,2304]{1,0:T(8,128)(2,1)}, bf16[704,2304]{1,0:T(8,128)(2,1)}, u32[]{:S(2)}, u32[]{:S(2)}) collective-permute-start(bf16[704,2304]{1,0:T(8,128)(2,1)} %convolution_convert_fusion.4), channel_id=1, source_target_pairs={{0,1},{1,0},{2,3},{3,2},{4,5},{5,4},{6,7},{7,6},{8,9},{9,8},{10,11... | collective-permute-start | bytes 9732104 | tf_op jit(solution)/shard_map/ppermute | solution.py:56
  187.9 22.5 %collective-permute-start.16 = (bf16[288,1536]{1,0:T(8,128)(2,1)S(1)}, bf16[288,1536]{1,0:T(8,128)(2,1)S(1)}, u32[]{:S(2)}, u32[]{:S(2)}) collective-permute-start(bf16[288,1536]{1,0:T(8,128)(2,1)S(1)} %pad_maximum_fusion.4), channel_id=1, source_target_pairs={{0,4},{4,0},{1,5},{5,1},{2,6},{6,2},{3,7},{7,3},{8,12},{12,8},{9,1... | collective-permute-start | bytes 2654216 | tf_op jit(solution)/shard_map/ppermute | solution.py:48
  189.6 40.9 %collective-permute-start.23 = (bf16[176,2304]{1,0:T(8,128)(2,1)}, bf16[176,2304]{1,0:T(8,128)(2,1)}, u32[]{:S(2)}, u32[]{:S(2)}) collective-permute-start(bf16[176,2304]{1,0:T(8,128)(2,1)} %fusion.16), channel_id=1, source_target_pairs={{0,2},{2,0},{1,3},{3,1},{4,6},{6,4},{5,7},{7,5},{8,10},{10,8},{9,1... | collective-permute-start | bytes 2433032 | tf_op jit(solution)/shard_map/ppermute | solution.py:52
  191.0 36.9 %collective-permute-start.24 = (bf16[176,2304]{1,0:T(8,128)(2,1)}, bf16[176,2304]{1,0:T(8,128)(2,1)}, u32[]{:S(2)}, u32[]{:S(2)}) collective-permute-start(bf16[176,2304]{1,0:T(8,128)(2,1)} %fusion.16), channel_id=1, source_target_pairs={{0,4},{4,0},{1,5},{5,1},{2,6},{6,2},{3,7},{7,3},{8,12},{12,8},{9,1... | collective-permute-start | bytes 2433032 | tf_op jit(solution)/shard_map/ppermute | solution.py:48
  212.4 196.1 %all-gather.8.cloned.1.call-start = ((), (), s32[]{:S(2)}) async-start(), calls=%async_computation.6 | async-start | bytes 4423680 | tf_op jit(solution)/shard_map/all_gather | solution.py:446
  217.0 28.2 %collective-permute-start.7 = (bf16[2,88,2304]{2,1,0:T(8,128)(2,1)S(1)}, bf16[2,88,2304]{2,1,0:T(8,128)(2,1)S(1)}, u32[]{:S(2)}, u32[]{:S(2)}) collective-permute-start(bf16[2,88,2304]{2,1,0:T(8,128)(2,1)S(1)} %slice_bitcast_fusion.23), channel_id=1, source_target_pairs={{0,4},{4,0},{1,5},{5,1},{2,6},{6,2},{3,7},{7,3},{8,12},{12,8},{9,1... | collective-permute-start | bytes 2433032 | tf_op jit(solution)/shard_map/ppermute | solution.py:48
  217.6 27.6 %collective-permute-start.9 = (bf16[2,88,2304]{2,1,0:T(8,128)(2,1)S(1)}, bf16[2,88,2304]{2,1,0:T(8,128)(2,1)S(1)}, u32[]{:S(2)}, u32[]{:S(2)}) collective-permute-start(bf16[2,88,2304]{2,1,0:T(8,128)(2,1)S(1)} %slice_bitcast_fusion.21), channel_id=1, source_target_pairs={{0,2},{2,0},{1,3},{3,1},{4,6},{6,4},{5,7},{7,5},{8,10},{10,8},{9,1... | collective-permute-start | bytes 2433032 | tf_op jit(solution)/shard_map/ppermute | solution.py:52
  229.0 37.0 %collective-permute-start.25 = (bf16[88,2304]{1,0:T(8,128)(2,1)S(1)}, bf16[88,2304]{1,0:T(8,128)(2,1)S(1)}, u32[]{:S(2)}, u32[]{:S(2)}) collective-permute-start(bf16[88,2304]{1,0:T(8,128)(2,1)S(1)} %slice.487), channel_id=1, source_target_pairs={{0,2},{2,0},{1,3},{3,1},{4,6},{6,4},{5,7},{7,5},{8,10},{10,8},{9,1... | collective-permute-start | bytes 1216520 | tf_op jit(solution)/shard_map/ppermute | solution.py:52
  231.5 35.3 %collective-permute-start.26 = (bf16[88,2304]{1,0:T(8,128)(2,1)S(1)}, bf16[88,2304]{1,0:T(8,128)(2,1)S(1)}, u32[]{:S(2)}, u32[]{:S(2)}) collective-permute-start(bf16[88,2304]{1,0:T(8,128)(2,1)S(1)} %slice.488), channel_id=1, source_target_pairs={{0,4},{4,0},{1,5},{5,1},{2,6},{6,2},{3,7},{7,3},{8,12},{12,8},{9,1... | collective-permute-start | bytes 1216520 | tf_op jit(solution)/shard_map/ppermute | solution.py:48
  245.6 10.7 %collective-permute-start.8 = (bf16[88,2304]{1,0:T(8,128)(2,1)S(1)}, bf16[88,2304]{1,0:T(8,128)(2,1)S(1)}, u32[]{:S(2)}, u32[]{:S(2)}) collective-permute-start(bf16[88,2304]{1,0:T(8,128)(2,1)S(1)} %fusion.58), channel_id=1, source_target_pairs={{0,2},{2,0},{1,3},{3,1},{4,6},{6,4},{5,7},{7,5},{8,10},{10,8},{9,1... | collective-permute-start | bytes 1216520 | tf_op jit(solution)/shard_map/ppermute | solution.py:52
  247.2 14.9 %collective-permute-start.10 = (bf16[88,2304]{1,0:T(8,128)(2,1)S(1)}, bf16[88,2304]{1,0:T(8,128)(2,1)S(1)}, u32[]{:S(2)}, u32[]{:S(2)}) collective-permute-start(bf16[88,2304]{1,0:T(8,128)(2,1)S(1)} %fusion.59), channel_id=1, source_target_pairs={{0,4},{4,0},{1,5},{5,1},{2,6},{6,2},{3,7},{7,3},{8,12},{12,8},{9,1... | collective-permute-start | bytes 1216520 | tf_op jit(solution)/shard_map/ppermute | solution.py:48
  264.0 21.6 %collective-permute-start.11 = (bf16[176,2304]{1,0:T(8,128)(2,1)S(1)}, bf16[176,2304]{1,0:T(8,128)(2,1)S(1)}, u32[]{:S(2)}, u32[]{:S(2)}) collective-permute-start(bf16[176,2304]{1,0:T(8,128)(2,1)S(1)} %get-tuple-element.30), channel_id=1, source_target_pairs={{0,2},{2,0},{1,3},{3,1},{4,6},{6,4},{5,7},{7,5},{8,10},{10,8},{9,1... | collective-permute-start | bytes 2433032 | tf_op jit(solution)/shard_map/ppermute | solution.py:52
  265.4 19.5 %collective-permute-start.12 = (bf16[176,2304]{1,0:T(8,128)(2,1)S(1)}, bf16[176,2304]{1,0:T(8,128)(2,1)S(1)}, u32[]{:S(2)}, u32[]{:S(2)}) collective-permute-start(bf16[176,2304]{1,0:T(8,128)(2,1)S(1)} %get-tuple-element.30), channel_id=1, source_target_pairs={{0,4},{4,0},{1,5},{5,1},{2,6},{6,2},{3,7},{7,3},{8,12},{12,8},{9,1... | collective-permute-start | bytes 2433032 | tf_op jit(solution)/shard_map/ppermute | solution.py:48
  267.6 43.4 %collective-permute-start.27 = (bf16[704,2304]{1,0:T(8,128)(2,1)}, bf16[704,2304]{1,0:T(8,128)(2,1)}, u32[]{:S(2)}, u32[]{:S(2)}) collective-permute-start(bf16[704,2304]{1,0:T(8,128)(2,1)} %get-tuple-element.99), channel_id=1, source_target_pairs={{0,1},{1,0},{2,3},{3,2},{4,5},{5,4},{6,7},{7,6},{8,9},{9,8},{10,11... | collective-permute-start | bytes 9732104 | tf_op jit(solution)/shard_map/ppermute | solution.py:56
  285.6 10.3 %collective-permute-start.14 = (bf16[88,2304]{1,0:T(8,128)(2,1)S(1)}, bf16[88,2304]{1,0:T(8,128)(2,1)S(1)}, u32[]{:S(2)}, u32[]{:S(2)}) collective-permute-start(bf16[88,2304]{1,0:T(8,128)(2,1)S(1)} %slice.472), channel_id=1, source_target_pairs={{0,4},{4,0},{1,5},{5,1},{2,6},{6,2},{3,7},{7,3},{8,12},{12,8},{9,1... | collective-permute-start | bytes 1216520 | tf_op jit(solution)/shard_map/ppermute | solution.py:48
  296.9 17.9 %collective-permute-start.15 = (bf16[704,2304]{1,0:T(8,128)(2,1)}, bf16[704,2304]{1,0:T(8,128)(2,1)}, u32[]{:S(2)}, u32[]{:S(2)}) collective-permute-start(bf16[704,2304]{1,0:T(8,128)(2,1)} %get-tuple-element.103), channel_id=1, source_target_pairs={{0,1},{1,0},{2,3},{3,2},{4,5},{5,4},{6,7},{7,6},{8,9},{9,8},{10,11... | collective-permute-start | bytes 9732104 | tf_op jit(solution)/shard_map/ppermute | solution.py:56
  296.9 12.6 %collective-permute-start.17 = (bf16[288,768]{1,0:T(8,128)(2,1)S(1)}, bf16[288,768]{1,0:T(8,128)(2,1)S(1)}, u32[]{:S(2)}, u32[]{:S(2)}) collective-permute-start(bf16[288,768]{1,0:T(8,128)(2,1)S(1)} %copy-done.17), channel_id=1, source_target_pairs={{0,4},{4,0},{1,5},{5,1},{2,6},{6,2},{3,7},{7,3},{8,12},{12,8},{9,1... | collective-permute-start | bytes 1327112 | tf_op jit(solution)/shard_map/ppermute | solution.py:48
  310.7 318.2 %reduce-scatter.11.cloned.1.call-start = ((), (), s32[]{:S(2)}) async-start(), calls=%async_computation.10 | async-start | bytes 4423680 | tf_op jit(solution)/shard_map/reduce_scatter | solution.py:481
  425.5 17.2 %collective-permute-start.18 = (bf16[704,2304]{1,0:T(8,128)(2,1)}, bf16[704,2304]{1,0:T(8,128)(2,1)}, u32[]{:S(2)}, u32[]{:S(2)}) collective-permute-start(bf16[704,2304]{1,0:T(8,128)(2,1)} %convolution_convert_fusion.3), channel_id=1, source_target_pairs={{0,1},{1,0},{2,3},{3,2},{4,5},{5,4},{6,7},{7,6},{8,9},{9,8},{10,11... | collective-permute-start | bytes 9732104 | tf_op jit(solution)/shard_map/ppermute | solution.py:56
  434.7 17.3 %collective-permute-start.28 = (bf16[704,2304]{1,0:T(8,128)(2,1)}, bf16[704,2304]{1,0:T(8,128)(2,1)}, u32[]{:S(2)}, u32[]{:S(2)}) collective-permute-start(bf16[704,2304]{1,0:T(8,128)(2,1)} %convolution_convert_fusion.6), channel_id=1, source_target_pairs={{0,1},{1,0},{2,3},{3,2},{4,5},{5,4},{6,7},{7,6},{8,9},{9,8},{10,11... | collective-permute-start | bytes 9732104 | tf_op jit(solution)/shard_map/ppermute | solution.py:56
  442.2 214.5 %reduce-scatter.7.cloned.1.call-start = ((), (), s32[]{:S(2)}) async-start(), calls=%async_computation.8 | async-start | bytes 2211840 | tf_op jit(solution)/shard_map/reduce_scatter | solution.py:497
  448.8 20.9 %collective-permute-start.19 = (bf16[2,88,2304]{2,1,0:T(8,128)(2,1)S(1)}, bf16[2,88,2304]{2,1,0:T(8,128)(2,1)S(1)}, u32[]{:S(2)}, u32[]{:S(2)}) collective-permute-start(bf16[2,88,2304]{2,1,0:T(8,128)(2,1)S(1)} %slice_bitcast_fusion.19), channel_id=1, source_target_pairs={{0,4},{4,0},{1,5},{5,1},{2,6},{6,2},{3,7},{7,3},{8,12},{12,8},{9,1... | collective-permute-start | bytes 2433032 | tf_op jit(solution)/shard_map/ppermute | solution.py:48
  450.4 21.0 %collective-permute-start.21 = (bf16[2,88,2304]{2,1,0:T(8,128)(2,1)S(1)}, bf16[2,88,2304]{2,1,0:T(8,128)(2,1)S(1)}, u32[]{:S(2)}, u32[]{:S(2)}) collective-permute-start(bf16[2,88,2304]{2,1,0:T(8,128)(2,1)S(1)} %slice_bitcast_fusion.17), channel_id=1, source_target_pairs={{0,2},{2,0},{1,3},{3,1},{4,6},{6,4},{5,7},{7,5},{8,10},{10,8},{9,1... | collective-permute-start | bytes 2433032 | tf_op jit(solution)/shard_map/ppermute | solution.py:52
  461.4 25.7 %collective-permute-start.29 = (bf16[2,88,2304]{2,1,0:T(8,128)(2,1)S(1)}, bf16[2,88,2304]{2,1,0:T(8,128)(2,1)S(1)}, u32[]{:S(2)}, u32[]{:S(2)}) collective-permute-start(bf16[2,88,2304]{2,1,0:T(8,128)(2,1)S(1)} %slice_bitcast_fusion.15), channel_id=1, source_target_pairs={{0,4},{4,0},{1,5},{5,1},{2,6},{6,2},{3,7},{7,3},{8,12},{12,8},{9,1... | collective-permute-start | bytes 2433032 | tf_op jit(solution)/shard_map/ppermute | solution.py:48
  462.1 26.7 %collective-permute-start.31 = (bf16[2,88,2304]{2,1,0:T(8,128)(2,1)S(1)}, bf16[2,88,2304]{2,1,0:T(8,128)(2,1)S(1)}, u32[]{:S(2)}, u32[]{:S(2)}) collective-permute-start(bf16[2,88,2304]{2,1,0:T(8,128)(2,1)S(1)} %slice_bitcast_fusion.13), channel_id=1, source_target_pairs={{0,2},{2,0},{1,3},{3,1},{4,6},{6,4},{5,7},{7,5},{8,10},{10,8},{9,1... | collective-permute-start | bytes 2433032 | tf_op jit(solution)/shard_map/ppermute | solution.py:52
  471.8 25.7 %collective-permute-start.20 = (bf16[88,2304]{1,0:T(8,128)(2,1)S(1)}, bf16[88,2304]{1,0:T(8,128)(2,1)S(1)}, u32[]{:S(2)}, u32[]{:S(2)}) collective-permute-start(bf16[88,2304]{1,0:T(8,128)(2,1)S(1)} %fusion.60), channel_id=1, source_target_pairs={{0,2},{2,0},{1,3},{3,1},{4,6},{6,4},{5,7},{7,5},{8,10},{10,8},{9,1... | collective-permute-start | bytes 1216520 | tf_op jit(solution)/shard_map/ppermute | solution.py:52
  473.4 24.2 %collective-permute-start.22 = (bf16[88,2304]{1,0:T(8,128)(2,1)S(1)}, bf16[88,2304]{1,0:T(8,128)(2,1)S(1)}, u32[]{:S(2)}, u32[]{:S(2)}) collective-permute-start(bf16[88,2304]{1,0:T(8,128)(2,1)S(1)} %fusion.61), channel_id=1, source_target_pairs={{0,4},{4,0},{1,5},{5,1},{2,6},{6,2},{3,7},{7,3},{8,12},{12,8},{9,1... | collective-permute-start | bytes 1216520 | tf_op jit(solution)/shard_map/ppermute | solution.py:48
  489.2 16.3 %collective-permute-start.30 = (bf16[88,2304]{1,0:T(8,128)(2,1)S(1)}, bf16[88,2304]{1,0:T(8,128)(2,1)S(1)}, u32[]{:S(2)}, u32[]{:S(2)}) collective-permute-start(bf16[88,2304]{1,0:T(8,128)(2,1)S(1)} %fusion.62), channel_id=1, source_target_pairs={{0,2},{2,0},{1,3},{3,1},{4,6},{6,4},{5,7},{7,5},{8,10},{10,8},{9,1... | collective-permute-start | bytes 1216520 | tf_op jit(solution)/shard_map/ppermute | solution.py:52
  490.8 14.8 %collective-permute-start.32 = (bf16[88,2304]{1,0:T(8,128)(2,1)S(1)}, bf16[88,2304]{1,0:T(8,128)(2,1)S(1)}, u32[]{:S(2)}, u32[]{:S(2)}) collective-permute-start(bf16[88,2304]{1,0:T(8,128)(2,1)S(1)} %fusion.63), channel_id=1, source_target_pairs={{0,4},{4,0},{1,5},{5,1},{2,6},{6,2},{3,7},{7,3},{8,12},{12,8},{9,1... | collective-permute-start | bytes 1216520 | tf_op jit(solution)/shard_map/ppermute | solution.py:48
  508.8 19.5 %collective-permute-start.34 = (bf16[176,2304]{1,0:T(8,128)(2,1)S(1)}, bf16[176,2304]{1,0:T(8,128)(2,1)S(1)}, u32[]{:S(2)}, u32[]{:S(2)}) collective-permute-start(bf16[176,2304]{1,0:T(8,128)(2,1)S(1)} %get-tuple-element.27), channel_id=1, source_target_pairs={{0,4},{4,0},{1,5},{5,1},{2,6},{6,2},{3,7},{7,3},{8,12},{12,8},{9,1... | collective-permute-start | bytes 2433032 | tf_op jit(solution)/shard_map/ppermute | solution.py:48
  509.4 20.5 %collective-permute-start.33 = (bf16[176,2304]{1,0:T(8,128)(2,1)S(1)}, bf16[176,2304]{1,0:T(8,128)(2,1)S(1)}, u32[]{:S(2)}, u32[]{:S(2)}) collective-permute-start(bf16[176,2304]{1,0:T(8,128)(2,1)S(1)} %get-tuple-element.27), channel_id=1, source_target_pairs={{0,2},{2,0},{1,3},{3,1},{4,6},{6,4},{5,7},{7,5},{8,10},{10,8},{9,1... | collective-permute-start | bytes 2433032 | tf_op jit(solution)/shard_map/ppermute | solution.py:52
  553.3 161.0 %reduce-scatter.9.cloned.1.call-start = ((), (), s32[]{:S(2)}) async-start(), calls=%async_computation.9 | async-start | bytes 8847360 | tf_op jit(solution)/shard_map/reduce_scatter | solution.py:489
  570.0 232.9 %reduce-scatter.5.cloned.1.call-start = ((), (), s32[]{:S(2)}) async-start(), calls=%async_computation.7 | async-start | bytes 5898240 | tf_op jit(solution)/shard_map/reduce_scatter | solution.py:501
  628.8 13.7 %collective-permute-start.38 = (bf16[704,2304]{1,0:T(8,128)(2,1)}, bf16[704,2304]{1,0:T(8,128)(2,1)}, u32[]{:S(2)}, u32[]{:S(2)}) collective-permute-start(bf16[704,2304]{1,0:T(8,128)(2,1)} %convolution_convert_fusion.5), channel_id=1, source_target_pairs={{0,1},{1,0},{2,3},{3,2},{4,5},{5,4},{6,7},{7,6},{8,9},{9,8},{10,11... | collective-permute-start | bytes 9732104 | tf_op jit(solution)/shard_map/ppermute | solution.py:56
  630.2 26.5 %collective-permute-start.51 = (bf16[288,768]{1,0:T(8,128)(2,1)S(1)}, bf16[288,768]{1,0:T(8,128)(2,1)S(1)}, u32[]{:S(2)}, u32[]{:S(2)}) collective-permute-start(bf16[288,768]{1,0:T(8,128)(2,1)S(1)} %get-tuple-element.68), channel_id=1, source_target_pairs={{0,4},{4,0},{1,5},{5,1},{2,6},{6,2},{3,7},{7,3},{8,12},{12,8},{9,1... | collective-permute-start | bytes 1327112 | tf_op jit(solution)/shard_map/ppermute | solution.py:48
  654.0 25.4 %collective-permute-start.39 = (bf16[2,88,2304]{2,1,0:T(8,128)(2,1)}, bf16[2,88,2304]{2,1,0:T(8,128)(2,1)}, u32[]{:S(2)}, u32[]{:S(2)}) collective-permute-start(bf16[2,88,2304]{2,1,0:T(8,128)(2,1)} %slice_bitcast_fusion.11), channel_id=1, source_target_pairs={{0,4},{4,0},{1,5},{5,1},{2,6},{6,2},{3,7},{7,3},{8,12},{12,8},{9,1... | collective-permute-start | bytes 2433032 | tf_op jit(solution)/shard_map/ppermute | solution.py:48
  656.0 23.4 %collective-permute-start.41 = (bf16[2,88,2304]{2,1,0:T(8,128)(2,1)}, bf16[2,88,2304]{2,1,0:T(8,128)(2,1)}, u32[]{:S(2)}, u32[]{:S(2)}) collective-permute-start(bf16[2,88,2304]{2,1,0:T(8,128)(2,1)} %slice_bitcast_fusion.9), channel_id=1, source_target_pairs={{0,2},{2,0},{1,3},{3,1},{4,6},{6,4},{5,7},{7,5},{8,10},{10,8},{9,1... | collective-permute-start | bytes 2433032 | tf_op jit(solution)/shard_map/ppermute | solution.py:52
  657.8 21.5 %collective-permute-start.44 = (bf16[288,384]{1,0:T(8,128)(2,1)S(1)}, bf16[288,384]{1,0:T(8,128)(2,1)S(1)}, u32[]{:S(2)}, u32[]{:S(2)}) collective-permute-start(bf16[288,384]{1,0:T(8,128)(2,1)S(1)} %get-tuple-element.94), channel_id=1, source_target_pairs={{0,4},{4,0},{1,5},{5,1},{2,6},{6,2},{3,7},{7,3},{8,12},{12,8},{9,1... | collective-permute-start | bytes 663560 | tf_op jit(solution)/shard_map/ppermute | solution.py:48
  682.2 11.1 %collective-permute-start.40 = (bf16[88,2304]{1,0:T(8,128)(2,1)S(1)}, bf16[88,2304]{1,0:T(8,128)(2,1)S(1)}, u32[]{:S(2)}, u32[]{:S(2)}) collective-permute-start(bf16[88,2304]{1,0:T(8,128)(2,1)S(1)} %fusion.64), channel_id=1, source_target_pairs={{0,2},{2,0},{1,3},{3,1},{4,6},{6,4},{5,7},{7,5},{8,10},{10,8},{9,1... | collective-permute-start | bytes 1216520 | tf_op jit(solution)/shard_map/ppermute | solution.py:52
  682.8 10.8 %collective-permute-start.42 = (bf16[88,2304]{1,0:T(8,128)(2,1)S(1)}, bf16[88,2304]{1,0:T(8,128)(2,1)S(1)}, u32[]{:S(2)}, u32[]{:S(2)}) collective-permute-start(bf16[88,2304]{1,0:T(8,128)(2,1)S(1)} %fusion.65), channel_id=1, source_target_pairs={{0,4},{4,0},{1,5},{5,1},{2,6},{6,2},{3,7},{7,3},{8,12},{12,8},{9,1... | collective-permute-start | bytes 1216520 | tf_op jit(solution)/shard_map/ppermute | solution.py:48
  716.1 21.4 %collective-permute-start.50 = (bf16[288,1536]{1,0:T(8,128)(2,1)S(1)}, bf16[288,1536]{1,0:T(8,128)(2,1)S(1)}, u32[]{:S(2)}, u32[]{:S(2)}) collective-permute-start(bf16[288,1536]{1,0:T(8,128)(2,1)S(1)} %get-tuple-element.52), channel_id=1, source_target_pairs={{0,4},{4,0},{1,5},{5,1},{2,6},{6,2},{3,7},{7,3},{8,12},{12,8},{9,1... | collective-permute-start | bytes 2654216 | tf_op jit(solution)/shard_map/ppermute | solution.py:48
  804.4 15.2 %collective-permute-start.43 = (bf16[288,1024]{1,0:T(8,128)(2,1)S(1)}, bf16[288,1024]{1,0:T(8,128)(2,1)S(1)}, u32[]{:S(2)}, u32[]{:S(2)}) collective-permute-start(bf16[288,1024]{1,0:T(8,128)(2,1)S(1)} %get-tuple-element.66), channel_id=1, source_target_pairs={{0,4},{4,0},{1,5},{5,1},{2,6},{6,2},{3,7},{7,3},{8,12},{12,8},{9,1... | collective-permute-start | bytes 1769480 | tf_op jit(solution)/shard_map/ppermute | solution.py:48
  (49 other events, 525.0 us)
Sparse Core Ops, SparseCore 0:
  35.3 110.3 all-gather.3
  212.5 125.5 all-gather.5
  340.2 68.2 all-gather.7
  442.3 65.0 reduce-scatter.10
  553.4 35.4 reduce-scatter.6
  591.2 123.1 reduce-scatter.8
  716.8 86.0 reduce-scatter.4

commit v2 on v1

--- a/solution.py
+++ b/solution.py
@@ -28,6 +28,10 @@
 
 def dot(left, right, dims=NN):
     return lax.dot_general(left, right, dims, preferred_element_type=f32)
+
+
+def after(*fields):
+    return lax.optimization_barrier(fields)
 
 
 def normalize(field):
@@ -56,15 +60,22 @@
     return lax.ppermute(field, "mp", [(0, 1), (1, 0), (2, 3), (3, 2)])
 
 
-def gather_rows(own):
+def gather_near(own, other=None):
     half = own.shape[0] // 2
     from_x, from_y = flip_x(own), flip_y(own)
+    if other is not None:
+        from_x, from_y, other = after(from_x, from_y, other)
     corner = jnp.concatenate([flip_y(from_x[:half]), flip_x(from_y[half:])], axis=0)
     near = jnp.concatenate([own, from_y, from_x, corner], axis=0)
-    return jnp.concatenate([near, flip_core(near)], axis=0)
-
-
-def sum_rows(left, right, dims):
+    return near if other is None else (near, other)
+
+
+def gather_rows(own):
+    near = gather_near(own)
+    return near, flip_core(near)
+
+
+def sum_rows(left, right, dims, other=None):
     count = left.shape[0] // 2
     block = count // 4
     half = block // 2
@@ -75,9 +86,12 @@
     got_y = flip_y(total[:, 1, half:].astype(bf16)).astype(f32)
     upper = total[0, :, :half] + got_x
     lower = total[:, 0, half:] + got_y
+    if other is not None:
+        upper, other = after(upper, other)
     upper = upper[0] + flip_y(upper[1].astype(bf16)).astype(f32)
     lower = lower[0] + flip_x(lower[1].astype(bf16)).astype(f32)
-    return jnp.concatenate([upper, lower], axis=0)
+    total = jnp.concatenate([upper, lower], axis=0)
+    return total if other is None else (total, other)
 
 
 def sum_all(field):
@@ -214,18 +228,18 @@
 
 
 def backward_kernel(
-    info, rot_ref, cos_ref, sin_ref, bias_ref, mixed_ref, dmix_ref, lse_ref, out_ref,
+    info, rot_ref, cos_ref, sin_ref, bias_ref, mixed_ref, near_ref, far_ref, lse_ref, out_ref,
     d_ref, p_ref, ds_ref, kt_ref, dk_ref, dv_ref, dq_ref,
 ):
     slot = rot_ref.shape[0]
     rows = slot // 8
     tiles = slot // TILE
-    for n in range(8):
-        here = pl.ds(n * rows, rows)
-        there = pl.ds(pl.multiple_of(info[n] * rows, 16), rows)
-        d_rows = dmix_ref[there, :]
-        d_ref[here, :] = d_rows
-        p_ref[here, :] = d_rows.astype(f32) * mixed_ref[there, :].astype(f32)
+    for r in range(8):
+        here = pl.ds(r * rows, rows)
+        there = pl.ds(pl.multiple_of(info[9 + r] * rows, 16), rows)
+        d_rows = (near_ref if r < 4 else far_ref)[pl.ds(r % 4 * rows, rows), :]
+        d_ref[there, :] = d_rows
+        p_ref[there, :] = d_rows.astype(f32) * mixed_ref[here, :].astype(f32)
 
     def row_sums(cols, lanes, upper):
         product = p_ref[cols, lanes]
@@ -346,19 +360,17 @@
             pltpu.VMEM((slot, 3 * LANES), bf16),
         ],
         compiler_params=pltpu.CompilerParams(vmem_limit_bytes=48 << 20),
-        cost_estimate=pl.CostEstimate(
-            flops=20 * slot * slot * 128, bytes_accessed=24 << 20, transcendentals=3 * slot * slot
-        ),
+        cost_estimate=pl.CostEstimate(flops=0, bytes_accessed=1024, transcendentals=0),
         name="attention_forward",
     )(info, qkv, cosine, sine, bias)
 
 
-def attention_backward(info, rotated, cosine, sine, bias, mixed, d_mixed, log_total):
+def attention_backward(info, rotated, cosine, sine, bias, mixed, near, far, log_total):
     slot = rotated.shape[0]
     return pl.pallas_call(
         backward_kernel,
         out_shape=jax.ShapeDtypeStruct((slot, 8 * LANES), bf16),
-        in_specs=[SMEM_SPEC] + [VMEM_SPEC] * 7,
+        in_specs=[SMEM_SPEC] + [VMEM_SPEC] * 8,
         out_specs=VMEM_SPEC,
         scratch_shapes=[
             pltpu.VMEM((slot, 3 * LANES), bf16),
@@ -370,11 +382,144 @@
             pltpu.VMEM((slot, LANES), f32),
         ],
         compiler_params=pltpu.CompilerParams(vmem_limit_bytes=48 << 20),
-        cost_estimate=pl.CostEstimate(
-            flops=50 * slot * slot * 128, bytes_accessed=24 << 20, transcendentals=3 * slot * slot
+        cost_estimate=pl.CostEstimate(flops=0, bytes_accessed=1024, transcendentals=0),
+        name="attention_backward",
+    )(info, rotated, cosine, sine, bias, mixed, near, far, log_total)
+
+
+def whole(shape):
+    return pl.BlockSpec(shape, lambda i: (0,) * len(shape), pipeline_mode=pl.Buffered(1))
+
+
+FREE = pl.CostEstimate(flops=0, bytes_accessed=1024, transcendentals=0)
+ROOMY = pltpu.CompilerParams(vmem_limit_bytes=52 << 20)
+
+
+def gate_kernel(rows_ref, w_ref, *refs):
+    gate_up_ref, hidden_ref = refs[-2:]
+    width = hidden_ref.shape[1]
+    gate_up = dot(rows_ref[...], w_ref[...])
+    gate_up_ref[...] = gate_up
+    gate, up = gate_up[:, :width], gate_up[:, width:]
+    hidden_ref[...] = (gate * jax.nn.sigmoid(gate) * up).astype(bf16)
+
+
+def gate_half(rows, gu_w, width, earlier):
+    count, depth = rows.shape
+    tile = count // 4
+    at = 4 if earlier else 0
+    return pl.pallas_call(
+        gate_kernel,
+        grid=(4,),
+        out_shape=(
+            jax.ShapeDtypeStruct((2 * count, 2 * width), f32),
+            jax.ShapeDtypeStruct((2 * count, width), bf16),
         ),
-        name="attention_backward",
-    )(info, rotated, cosine, sine, bias, mixed, d_mixed, log_total)
+        in_specs=[pl.BlockSpec((tile, depth), lambda i: (i, 0)), whole((depth, 2 * width))]
+        + [pl.BlockSpec(memory_space=pl.ANY)] * len(earlier),
+        out_specs=(
+            pl.BlockSpec((tile, 2 * width), lambda i: (i + at, 0)),
+            pl.BlockSpec((tile, width), lambda i: (i + at, 0)),
+        ),
+        input_output_aliases={2: 0, 3: 1} if earlier else {},
+        compiler_params=ROOMY,
+        cost_estimate=FREE,
+        name="gate_half",
+    )(rows, gu_w, *earlier)
+
+
+def hidden_back_kernel(rows_ref, w_ref, gate_up_ref, out_ref):
+    width = w_ref.shape[1]
+    d_hidden = dot(rows_ref[...], w_ref[...])
+    gate, up = gate_up_ref[:, :width], gate_up_ref[:, width:]
+    sigmoid_gate = jax.nn.sigmoid(gate)
+    d_gate = d_hidden * up * sigmoid_gate * (1.0 + gate * (1.0 - sigmoid_gate))
+    out_ref[:, :width] = d_gate.astype(bf16)
+    out_ref[:, width:] = (d_hidden * (gate * sigmoid_gate)).astype(bf16)
+
+
+def hidden_back(rows, down_w, gate_up):
+    count, depth = rows.shape
+    width = gate_up.shape[1] // 2
+    tile = count // 8
+    return pl.pallas_call(
+        hidden_back_kernel,
+        grid=(8,),
+        out_shape=jax.ShapeDtypeStruct((count, 2 * width), bf16),
+        in_specs=[
+            pl.BlockSpec((tile, depth), lambda i: (i, 0)),
+            whole((depth, width)),
+            pl.BlockSpec((tile, 2 * width), lambda i: (i, 0)),
+        ],
+        out_specs=pl.BlockSpec((tile, 2 * width), lambda i: (i, 0)),
+        compiler_params=ROOMY,
+        cost_estimate=FREE,
+        name="hidden_back",
+    )(rows, down_w, gate_up)
+
+
+def rows_kernel(dims, rows_ref, w_ref, out_ref):
+    out_ref[...] = dot(rows_ref[...], w_ref[...], dims).astype(out_ref.dtype)
+
+
+def project(rows, weight, cols, kind):
+    count, depth = rows.shape
+    tile = count // 8
+    return pl.pallas_call(
+        functools.partial(rows_kernel, NN),
+        grid=(8,),
+        out_shape=jax.ShapeDtypeStruct((count, cols), kind),
+        in_specs=[
+            pl.BlockSpec((tile, depth), lambda i: (i, 0)),
+            pl.BlockSpec((depth, cols), lambda i: (0, 0), pipeline_mode=pl.Buffered(1)),
+        ],
+        out_specs=pl.BlockSpec((tile, cols), lambda i: (i, 0)),
+        compiler_params=ROOMY,
+        cost_estimate=FREE,
+        name="project",
+    )(rows, weight)
+
+
+def grads_kernel(place, *refs):
+    out_ref = refs[-1]
+    products = []
+    for near_ref, far_ref, right_ref in zip(refs[0:-1:3], refs[1:-1:3], refs[2:-1:3]):
+        left = jnp.concatenate([near_ref[...], far_ref[...]], axis=0)
+        products.append(dot(left, right_ref[...], TN))
+    place(out_ref, *products)
+
+
+def place_one(out_ref, product):
+    out_ref[...] = product.astype(bf16)
+
+
+def place_heads(out_ref, first, second):
+    start = first.shape[1] - LANES
+    out_ref[:, :start] = first[:, :start].astype(bf16)
+    out_ref[:, start : start + LANES] = (first[:, start:] + second[:, :LANES]).astype(bf16)
+    out_ref[:, start + LANES :] = second[:, LANES:].astype(bf16)
+
+
+def weight_grads(place, cols, *triples):
+    depth = triples[0][0].shape[1]
+    specs, operands = [], []
+    for near, far, right in triples:
+        specs += [
+            pl.BlockSpec((near.shape[0], 2 * LANES), lambda i: (0, i)),
+            pl.BlockSpec((far.shape[0], 2 * LANES), lambda i: (0, i)),
+            whole(right.shape),
+        ]
+        operands += [near, far, right]
+    return pl.pallas_call(
+        functools.partial(grads_kernel, place),
+        grid=(depth // (2 * LANES),),
+        out_shape=jax.ShapeDtypeStruct((depth, cols), bf16),
+        in_specs=specs,
+        out_specs=pl.BlockSpec((2 * LANES, cols), lambda i: (i, 0)),
+        compiler_params=ROOMY,
+        cost_estimate=FREE,
+        name="weight_grads",
+    )(*operands)
 
 
 def shards(
@@ -402,11 +547,13 @@
     ff_half = w_gate.shape[1] // 2
     ff_pad = -(-ff_half // LANES) * LANES
 
-    info = []
+    info, back = [], []
     for n in range(8):
         d_x, d_y, d_core = on_x ^ (n // 4), on_y ^ (n // 2 % 2), on_core ^ (n % 2)
         info.append(d_core * 4 + d_x * 2 + d_y)
-    info = jnp.stack(info + [on_x] + [jnp.zeros_like(on_x)] * 7).astype(jnp.int32)
+        from_x, from_y, from_core = on_x ^ (n // 2 % 2), on_y ^ (n % 2), on_core ^ (n // 4)
+        back.append(from_x * 4 + from_y * 2 + from_core)
+    info = jnp.stack(info + [on_x] + back).astype(jnp.int32)
 
     gain_a = gain_attn.astype(f32)
     gain_m = gain_mlp.astype(f32)
@@ -432,20 +579,6 @@
         fill = ((0, 0), (0, ff_pad - ff_half))
         first, second = jnp.pad(weight[:, :ff_half], fill), jnp.pad(weight[:, ff_half:], fill)
         return jnp.where(lower_x, first, second), jnp.where(lower_x, second, first)
-
-    gate_mine, gate_theirs = halves(w_gate)
-    up_mine, up_theirs = halves(w_up)
-    down_mine, down_theirs = halves(w_down.T)
-    gu_part = both_x(
-        jnp.concatenate([gate_mine, up_mine], 1), jnp.concatenate([gate_theirs, up_theirs], 1)
-    )
-    down_part = both_x(down_mine, down_theirs)
-
-    attn_w = lax.all_gather(attn_part, "dp", axis=0, tiled=True)
-    gu_w = lax.all_gather(gu_part, "dp", axis=0, tiled=True)
-    down_w = lax.all_gather(down_part, "dp", axis=0, tiled=True)
-    qkv_w = attn_w[:, : 8 * LANES]
-    out_w = attn_w[:, 7 * LANES :]
 
     index = jnp.arange(slot, dtype=jnp.int32)
     own_seg = lineage[0]
@@ -466,45 +599,62 @@
     cosine = jnp.concatenate([cos, cos, cos, cos], axis=1)
     sine = jnp.concatenate([-sin, sin, -sin, sin], axis=1)
 
-    normed_a = gather_rows((normalize(inputs) * gain_a).astype(bf16))
-    qkv = dot(normed_a, qkv_w)
+    attn_part, own_rows, grad_rows = after(attn_part, normalize(inputs) * gain_a, grad_rows)
+    near_a = gather_near(own_rows.astype(bf16))
+    near_a, w_gate, w_up, w_down, grad_rows = after(near_a, w_gate, w_up, w_down, grad_rows)
+    far_a = flip_core(near_a)
+    near_d, far_d = gather_rows((branch_scale * grad_rows).astype(bf16))
+    gate_mine, gate_theirs = halves(w_gate)
+    up_mine, up_theirs = halves(w_up)
+    down_mine, down_theirs = halves(w_down.T)
+    gu_part = both_x(
+        jnp.concatenate([gate_mine, up_mine], 1), jnp.concatenate([gate_theirs, up_theirs], 1)
+    )
+    down_part = both_x(down_mine, down_theirs)
+    normed_a = jnp.concatenate([near_a, far_a], axis=0)
+    d_mlp = jnp.concatenate([near_d, far_d], axis=0)
+    attn_w = lax.all_gather(attn_part, "dp", axis=0, tiled=True)
+    attn_w, normed_a, gu_part, down_part, d_mlp, bias, cosine, sine = after(
+        attn_w, normed_a, gu_part, down_part, d_mlp, bias, cosine, sine
+    )
+    gu_w = lax.all_gather(gu_part, "dp", axis=0, tiled=True)
+    down_w = lax.all_gather(down_part, "dp", axis=0, tiled=True)
+    qkv_w = attn_w[:, : 8 * LANES]
+    out_w = attn_w[:, 7 * LANES :]
+    qkv = project(normed_a, attn_w, 8 * LANES, f32)
     rotated, mixed, log_total = attention_forward(info, qkv, cosine, sine, bias)
-    residual = inputs + branch_scale * sum_rows(mixed, out_w, NT)
-    normed_m = gather_rows((normalize(residual) * gain_m).astype(bf16))
-    gate_up = dot(normed_m, gu_w)
-    gate, up = gate_up[:, :ff_pad], gate_up[:, ff_pad:]
-    sigmoid_gate = jax.nn.sigmoid(gate)
-    hidden = (gate * sigmoid_gate * up).astype(bf16)
-    output = residual + branch_scale * sum_rows(hidden, down_w, NT)
-
-    d_mlp = gather_rows((branch_scale * grad_rows).astype(bf16))
-    grad_down = lax.psum_scatter(
-        dot(d_mlp, hidden, TN).astype(bf16), "dp", scatter_dimension=0, tiled=True
-    )
-    d_hidden = dot(d_mlp, down_w)
-    d_gate = (d_hidden * up * sigmoid_gate * (1.0 + gate * (1.0 - sigmoid_gate))).astype(bf16)
-    d_up = (d_hidden * (gate * sigmoid_gate)).astype(bf16)
-    d_gate_up = jnp.concatenate([d_gate, d_up], axis=1)
-    d_normed_mlp = sum_rows(d_gate_up, gu_w, NT)
-    grad_gu = lax.psum_scatter(
-        dot(normed_m, d_gate_up, TN).astype(bf16), "dp", scatter_dimension=0, tiled=True
-    )
+    mixed_rows, gu_w = sum_rows(mixed, out_w, NT, gu_w)
+    residual = inputs + branch_scale * mixed_rows
+    near_m = gather_near((normalize(residual) * gain_m).astype(bf16))
+    far_m = flip_core(near_m)
+    gate_up, hidden = gate_half(far_m, gu_w, ff_pad, gate_half(near_m, gu_w, ff_pad, ()))
+
+    grad_down = weight_grads(place_one, ff_pad, (near_d, far_d, hidden))
+    gate_up, grad_down = after(gate_up, grad_down)
+    grad_down = lax.psum_scatter(grad_down, "dp", scatter_dimension=0, tiled=True)
+    d_gate_up = hidden_back(d_mlp, down_w, gate_up)
+    grad_gu = weight_grads(place_one, 2 * ff_pad, (near_m, far_m, d_gate_up))
+    d_gate_up, grad_gu = after(d_gate_up, grad_gu)
+    grad_gu = lax.psum_scatter(grad_gu, "dp", scatter_dimension=0, tiled=True)
+    d_normed_mlp, grad_down = sum_rows(d_gate_up, gu_w, NT, grad_down)
     back_mlp, gain_mlp_part = norm_back(residual, gain_m, d_normed_mlp)
     d_residual = grad_rows + back_mlp
 
-    d_attn = gather_rows((branch_scale * d_residual).astype(bf16))
-    d_mixed = dot(d_attn, out_w).astype(bf16)
-    grad_o = lax.psum_scatter(
-        dot(d_attn, mixed, TN).astype(bf16), "dp", scatter_dimension=0, tiled=True
-    )
-    d_qkv = attention_backward(info, rotated, cosine, sine, bias, mixed, d_mixed, log_total)
-    grad_qkv = lax.psum_scatter(
-        dot(normed_a, d_qkv, TN).astype(bf16), "dp", scatter_dimension=0, tiled=True
-    )
+    near_o, far_o = gather_rows((branch_scale * d_residual).astype(bf16))
+    d_mixed_near, d_mixed_far = dot(near_o, out_w).astype(bf16), dot(far_o, out_w).astype(bf16)
+    d_qkv = attention_backward(
+        info, rotated, cosine, sine, bias, mixed, d_mixed_near, d_mixed_far, log_total
+    )
+    grad_attn = weight_grads(
+        place_heads, 10 * LANES, (near_a, far_a, d_qkv), (near_o, far_o, mixed)
+    )
+    grad_attn, grad_gu, d_qkv, hidden = after(grad_attn, grad_gu, d_qkv, hidden)
+    grad_attn = lax.psum_scatter(grad_attn, "dp", scatter_dimension=0, tiled=True)
     d_normed_attn = sum_rows(d_qkv, qkv_w, NT)
     back_attn, gain_attn_part = norm_back(inputs, gain_a, d_normed_attn)
     input_grad = d_residual + back_attn
     gains = sum_all(jnp.stack([gain_attn_part, gain_mlp_part]))
+    output = residual + branch_scale * sum_rows(hidden, down_w, NT)
 
     def rows_of_x(field):
         rows = field.shape[0] // 2
@@ -525,12 +675,11 @@
     grad_up = join(mine[:, ff_pad : ff_pad + ff_half], got[:, ff_pad : ff_pad + ff_half])
     mine, got = rows_of_x(grad_down)
     grad_down = join(mine[:, :ff_half], got[:, :ff_half]).T
-    mine, got = rows_of_x(grad_o)
-    grad_out = join_heads(mine, got, LANES, HEAD_DIM).T
-    mine, got = rows_of_x(grad_qkv)
+    mine, got = rows_of_x(grad_attn)
     grad_query = join_heads(mine, got, 0, 6 * LANES)
     grad_key = join_heads(mine, got, 2 * LANES, 6 * LANES + HEAD_DIM)
     grad_value = join_heads(mine, got, 4 * LANES, 7 * LANES)
+    grad_out = join_heads(mine, got, 8 * LANES, 7 * LANES + HEAD_DIM).T
 
     return (
         output.astype(bf16),

time: 836 us -> 719 us (0.86)
  waiting for transfers between devices: 460 us -> 328 us
  Pallas kernels: 66.6 us -> 159 us
  matrix products: 141 us -> 50.2 us
    pallas_call x0 -> x7, Pallas kernels: none -> 93 us  [the longest x3 45.4 us: weight_grads(): pl.pallas_call(functools.partial(grads_kernel, place), grid=(depth // (2...]
    dot_general x16 -> x10, matrix products: 141 us -> 50.2 us  [dot(): return lax.dot_general(left, right, dims, preferred_element_type=f32)]
    all_gather x1, waiting for transfers between devices: 63 us -> 0.01 us  [shards(): attn_w = lax.all_gather(attn_part, 'dp', axis=0, tiled=True)]
    reduce_scatter x4 -> x3, waiting for transfers between devices: 67.7 us -> 6.31 us  [the longest x1 5.85 us: shards(): lax.psum_scatter(grad_attn, 'dp', scatter_dimension=0, tiled=True)]
    all_gather x1, waiting for transfers between devices: 54.7 us -> 1.77 us  [shards(): down_w = lax.all_gather(down_part, 'dp', axis=0, tiled=True)]
    all_gather x1, waiting for transfers between devices: 19.4 us -> 57.5 us  [shards(): gu_w = lax.all_gather(gu_part, 'dp', axis=0, tiled=True)]
    ppermute x24 -> x23, waiting for transfers between devices: 187 us -> 206 us  [flip_x(): return lax.ppermute(field, 'ctx', [(0, 1), (1, 0)])]
    ppermute x17, waiting for transfers between devices: 54.1 us -> 39.2 us  [flip_y(): return lax.ppermute(field, 'mp', [(0, 2), (2, 0), (1, 3), (3, 1)])]
  transfers between devices with their start and end apart: 59 -> 57, of which waited for: 35 -> 42; matrix products, arithmetic and copies ran while one was open for 22% -> 18% of each run, Pallas kernels for 5% -> 23%
where the time goes in v2:
time: 719 us; the launch traced here: 708 us
  waiting for transfers between devices  328 us (46%)
  Pallas kernels  159 us (22%)
  starting transfers between devices  56 us (8%)
  other arithmetic  55.2 us (8%)
  matrix products  50.2 us (7%)
  local copies, waits for them, and re-layouts  43.4 us (6%)
  between operations  15.4 us (2%)
    ppermute x23, waiting for transfers between devices, flip_x(): return lax.ppermute(field, 'ctx', [(0, 1), (1, 0)])  206 us
    all_gather x1, waiting for transfers between devices, shards(): gu_w = lax.all_gather(gu_part, 'dp', axis=0, tiled=True)  57.5 us
    dot_general x10, matrix products, dot(): return lax.dot_general(left, right, dims, preferred_element_type=f32)  50.2 us
    pallas_call x3, Pallas kernels, weight_grads(): pl.pallas_call(functools.partial(grads_kernel, place), grid=(depth // (2...  45.4 us
    pallas_call x1, Pallas kernels, attention_backward(): pl.pallas_call(backward_kernel, out_shape=jax.ShapeDtypeStruct((slot, 8 *...  44.4 us
    ppermute x17, waiting for transfers between devices, flip_y(): return lax.ppermute(field, 'mp', [(0, 2), (2, 0), (1, 3), (3, 1)])  39.2 us
    ppermute x23, starting transfers between devices, flip_x(): return lax.ppermute(field, 'ctx', [(0, 1), (1, 0)])  27.9 us
    ppermute x17, starting transfers between devices, flip_y(): return lax.ppermute(field, 'mp', [(0, 2), (2, 0), (1, 3), (3, 1)])  22.3 us
  transfers between devices with their start and end apart: 57, of which 42 were waited for; matrix products, arithmetic and copies ran while one was open for 18% of the time, Pallas kernels for 23%

profile of v2, /device:TPU:0, one launch (start us, length us, event | category | flops | bytes accessed | tf_op | source)
XLA Modules:
  0.0 708.0 jit_solution(5320976562566237247)
XLA Ops:
  16.3 3.0 collective-permute-start
  20.5 15.3 %collective-permute-done = bf16[288,1280]{1,0:T(8,128)(2,1)S(1)} collective-permute-done((bf16[288,1280]{1,0:T(8,128)(2,1)S(1)}, bf16[288,1280]{1,0:T(8,128)(2,1)S(1)}, u32[]{:S(2)}, u32[]{:S(2)}) %collective-permute-start) | collective-permute-done | bytes 737312 | tf_op jit(solution)/shard_map/ppermute | solution.py:52
  41.7 15.0 %collective-permute-done.2 = bf16[176,2304]{1,0:T(8,128)(2,1)S(1)} collective-permute-done((bf16[176,2304]{1,0:T(8,128)(2,1)S(1)}, bf16[176,2304]{1,0:T(8,128)(2,1)S(1)}, u32[]{:S(2)}, u32[]{:S(2)}) %collective-permute-start.2) | collective-permute-done | bytes 811040 | tf_op jit(solution)/shard_map/ppermute | solution.py:52
  63.9 2.6 collective-permute-done.3
  72.6 14.9 %collective-permute-done.9 = bf16[176,2304]{1,0:T(8,128)(2,1)S(1)} collective-permute-done((bf16[176,2304]{1,0:T(8,128)(2,1)S(1)}, bf16[176,2304]{1,0:T(8,128)(2,1)S(1)}, u32[]{:S(2)}, u32[]{:S(2)}) %collective-permute-start.9) | collective-permute-done | bytes 811040 | tf_op jit(solution)/shard_map/ppermute | solution.py:52
  92.9 4.3 collective-permute-done.10
  99.7 6.2 fusion.1.bias_ref
  109.4 2.6 fusion.64
  113.2 7.0 collective-permute-done.7
  121.4 17.4 %collective-permute-done.6 = bf16[288,1536]{1,0:T(8,128)(2,1)} collective-permute-done((bf16[288,1536]{1,0:T(8,128)(2,1)S(1)}, bf16[288,1536]{1,0:T(8,128)(2,1)}, u32[]{:S(2)}, u32[]{:S(2)}) %collective-permute-start.6) | collective-permute-done | bytes 884768 | tf_op jit(solution)/shard_map/ppermute | solution.py:52
  138.9 3.2 maximum_select_fusion
  142.1 6.0 pad_maximum_fusion.rows_ref
  148.1 3.9 constant_dynamic-update-slice_fusion.10.rows_ref
  152.3 13.2 %project.1.qkv_ref = f32[1408,1024]{1,0:T(8,128)} custom-call(bf16[1408,2304]{1,0:T(8,128)(2,1)} %pad_maximum_fusion.rows_ref, bf16[2304,1280]{1,0:T(8,128)(2,1)} %all-gather.4.cloned.1.call-done.w_ref), custom_call_target="tpu_custom_call" | custom-call | bytes 1024 | tf_op jit(solution)/shard_map/project/pallas_call | solution.py:468
  165.6 22.0 %attention_forward.1 = (bf16[1408,1024]{1,0:T(8,128)(2,1)S(1)}, bf16[1408,384]{1,0:T(8,128)(2,1)S(1)}, f32[3,8,2816]{2,1,0:T(8,128)S(1)}) custom-call(s32[17]{0:T(128)S(1)} %stack.80.info, f32[1408,1024]{1,0:T(8,128)} %project.1.qkv_ref, f32[1408,128]{1,0:T(8,128)S(1)} %get-tuple-element.56.cos_ref, f32[1408,128]{1,0:T(8,128)S(1)} %get-tuple-element.57.sin_ref, ...), custom_call_target="tpu_custom_call" | custom-call | bytes 1024 | tf_op jit(solution)/shard_map/attention_forward/pallas_call | solution.py:347
  189.6 5.8 collective-permute-done.13
  198.0 19.7 %collective-permute-done.14 = bf16[2,88,2304]{2,1,0:T(8,128)(2,1)S(1)} collective-permute-done((bf16[2,88,2304]{2,1,0:T(8,128)(2,1)S(1)}, bf16[2,88,2304]{2,1,0:T(8,128)(2,1)S(1)}, u32[]{:S(2)}, u32[]{:S(2)}) %collective-permute-start.14) | collective-permute-done | bytes 811040 | tf_op jit(solution)/shard_map/ppermute | solution.py:52
  222.2 57.5 %all-gather.6.cloned.1.call-done.w_ref = bf16[2304,1536]{1,0:T(8,128)(2,1)} async-done(((bf16[576,1536]{1,0:T(8,128)(2,1)}), bf16[2304,1536]{1,0:T(8,128)(2,1)}) %all-gather.6.cloned.1.call-update) | async-done | bytes 7077904 | tf_op jit(solution)/shard_map/all_gather | solution.py:620
  283.9 8.5 %collective-permute-done.15 = bf16[88,2304]{1,0:T(8,128)(2,1)S(1)} collective-permute-done((bf16[88,2304]{1,0:T(8,128)(2,1)S(1)}, bf16[88,2304]{1,0:T(8,128)(2,1)S(1)}, u32[]{:S(2)}, u32[]{:S(2)}) %collective-permute-start.15) | collective-permute-done | bytes 405536 | tf_op jit(solution)/shard_map/ppermute | solution.py:56
  298.6 16.5 %collective-permute-done.19 = bf16[176,2304]{1,0:T(8,128)(2,1)} collective-permute-done((bf16[176,2304]{1,0:T(8,128)(2,1)}, bf16[176,2304]{1,0:T(8,128)(2,1)}, u32[]{:S(2)}, u32[]{:S(2)}) %collective-permute-start.19) | collective-permute-done | bytes 811040 | tf_op jit(solution)/shard_map/ppermute | solution.py:52
  328.8 10.4 %gate_half.2 = (f32[1408,1536]{1,0:T(8,128)}, bf16[1408,768]{1,0:T(8,128)(2,1)}) custom-call(bf16[704,2304]{1,0:T(8,128)(2,1)} %constant_dynamic-update-slice_fusion.16.rows_ref.refs_0_, bf16[2304,1536]{1,0:T(8,128)(2,1)} %all-gather.6.cloned.1.call-done.w_ref), custom_call_target="tpu_custom_call" | custom-call | bytes 1024 | tf_op jit(solution)/shard_map/gate_half/pallas_call | solution.py:411
  340.9 10.4 %gate_half.3 = (f32[1408,1536]{1,0:T(8,128)}, bf16[1408,768]{1,0:T(8,128)(2,1)}) custom-call(bf16[704,2304]{1,0:T(8,128)(2,1)} %copy-done.9, bf16[2304,1536]{1,0:T(8,128)(2,1)} %all-gather.6.cloned.1.call-done.w_ref, f32[1408,1536]{1,0:T(8,128)} %get-tuple-element.66.refs_0_, ...), custom_call_target="tpu_custom_call", output_to_operand_aliasing={{0}: (2, {}), {1}: (3, {})} | custom-call | bytes 1024 | tf_op jit(solution)/shard_map/gate_half/pallas_call | solution.py:411
  351.3 11.8 %weight_grads.3 = bf16[2304,768]{1,0:T(8,128)(2,1)} custom-call(bf16[704,2304]{1,0:T(8,128)(2,1)} %get-tuple-element.142.refs_0_, bf16[704,2304]{1,0:T(8,128)(2,1)} %collective-permute-done.12.refs_1_, bf16[1408,768]{1,0:T(8,128)(2,1)} %get-tuple-element.76.refs_2_), custom_call_target="tpu_custom_call" | custom-call | bytes 1024 | tf_op jit(solution)/shard_map/weight_grads/pallas_call | solution.py:513
  365.0 13.6 %hidden_back.1.refs_2_ = bf16[1408,1536]{1,0:T(8,128)(2,1)} custom-call(bf16[1408,2304]{1,0:T(8,128)(2,1)} %constant_dynamic-update-slice_fusion.10.rows_ref, bf16[2304,768]{1,0:T(8,128)(2,1)} %all-gather.8.cloned.1.call-done.w_ref, f32[1408,1536]{1,0:T(8,128)} %get-tuple-element.70.gate_up_ref), custom_call_target="tpu_custom_call" | custom-call | bytes 1024 | tf_op jit(solution)/shard_map/hidden_back/pallas_call | solution.py:445
  378.6 16.4 %weight_grads.4 = bf16[2304,1536]{1,0:T(8,128)(2,1)} custom-call(bf16[704,2304]{1,0:T(8,128)(2,1)} %constant_dynamic-update-slice_fusion.16.rows_ref.refs_0_, bf16[704,2304]{1,0:T(8,128)(2,1)} %copy-done.9, bf16[1408,1536]{1,0:T(8,128)(2,1)} %hidden_back.1.refs_2_), custom_call_target="tpu_custom_call" | custom-call | bytes 1024 | tf_op jit(solution)/shard_map/weight_grads/pallas_call | solution.py:513
  395.0 10.0 %convolution_convert_fusion.3 = bf16[704,2304]{1,0:T(8,128)(2,1)} fusion(bf16[2304,1536]{1,0:T(8,128)(2,1)} %all-gather.6.cloned.1.call-done.w_ref, bf16[1408,1536]{1,0:T(8,128)(2,1)} %hidden_back.1.refs_2_), kind=kOutput, calls=%fused_computation.17 | convolution fusion | flops 4984455168 | bytes 12484608 | tf_op jit(solution)/shard_map/dot_general | solution.py:30
  405.3 5.8 collective-permute-done.23
  411.2 9.3 %convert_add_fusion.2 = f32[704,2304]{1,0:T(8,128)S(1)} fusion(bf16[704,2304]{1,0:T(8,128)(2,1)} %collective-permute-done.23, bf16[2304,1536]{1,0:T(8,128)(2,1)} %all-gather.6.cloned.1.call-done.w_ref, bf16[1408,1536]{1,0:T(8,128)(2,1)} %hidden_back.1.refs_2_), kind=kOutput, calls=%fused_computation.12 | convolution fusion | flops 4986077184 | bytes 18972672 | tf_op jit(solution)/shard_map/dot_general | solution.py:30
  423.9 16.9 %collective-permute-done.24 = bf16[2,88,2304]{2,1,0:T(8,128)(2,1)S(1)} collective-permute-done((bf16[2,88,2304]{2,1,0:T(8,128)(2,1)S(1)}, bf16[2,88,2304]{2,1,0:T(8,128)(2,1)S(1)}, u32[]{:S(2)}, u32[]{:S(2)}) %collective-permute-start.24) | collective-permute-done | bytes 811040 | tf_op jit(solution)/shard_map/ppermute | solution.py:52
  448.4 6.9 collective-permute-done.27
  463.4 15.3 %collective-permute-done.29 = bf16[176,2304]{1,0:T(8,128)(2,1)S(1)} collective-permute-done((bf16[176,2304]{1,0:T(8,128)(2,1)S(1)}, bf16[176,2304]{1,0:T(8,128)(2,1)S(1)}, u32[]{:S(2)}, u32[]{:S(2)}) %collective-permute-start.29) | collective-permute-done | bytes 811040 | tf_op jit(solution)/shard_map/ppermute | solution.py:52
  481.6 6.6 collective-permute-done.30
  496.1 44.4 %attention_backward.1.refs_2_ = bf16[1408,1024]{1,0:T(8,128)(2,1)} custom-call(s32[17]{0:T(128)S(1)} %stack.80.info, bf16[1408,1024]{1,0:T(8,128)(2,1)} %copy-done, f32[1408,128]{1,0:T(8,128)S(1)} %get-tuple-element.56.cos_ref, f32[1408,128]{1,0:T(8,128)S(1)} %get-tuple-element.57.sin_ref, f32[1408,1408]{1,0:T(8,128)} %fusion.1.bias_ref, ...), custom_call_target="tpu_custom_call" | custom-call | bytes 1024 | tf_op jit(solution)/shard_map/attention_backward/pallas_call | solution.py:370
  540.5 17.1 %weight_grads.5 = bf16[2304,1280]{1,0:T(8,128)(2,1)} custom-call(bf16[704,2304]{1,0:T(8,128)(2,1)} %constant_dynamic-update-slice_fusion.refs_0_, bf16[704,2304]{1,0:T(8,128)(2,1)} %collective-permute-done.5.refs_1_, bf16[1408,1024]{1,0:T(8,128)(2,1)} %attention_backward.1.refs_2_, bf16[704,2304]{1,0:T(8,128)(2,1)} %copy-done.15, ...), custom_call_target="tpu_custom_call" | custom-call | bytes 1024 | tf_op jit(solution)/shard_map/weight_grads/pallas_call | solution.py:513
  558.1 8.0 %convolution_convert_fusion.2 = bf16[704,2304]{1,0:T(8,128)(2,1)} fusion(bf16[2304,1280]{1,0:T(8,128)(2,1)} %all-gather.4.cloned.1.call-done.w_ref, bf16[1408,1024]{1,0:T(8,128)(2,1)} %attention_backward.1.refs_2_), kind=kOutput, calls=%fused_computation.16 | convolution fusion | flops 3323510784 | bytes 9404416 | tf_op jit(solution)/shard_map/dot_general | solution.py:30
  571.9 7.1 %convolution_convert_fusion = bf16[704,2304]{1,0:T(8,128)(2,1)} fusion(bf16[2304,768]{1,0:T(8,128)(2,1)} %all-gather.8.cloned.1.call-done.w_ref, bf16[1408,768]{1,0:T(8,128)(2,1)} %get-tuple-element.76.refs_2_), kind=kOutput, calls=%fused_computation.14 | convolution fusion | flops 2493038592 | bytes 7864320 | tf_op jit(solution)/shard_map/dot_general | solution.py:30
  579.4 13.4 %collective-permute-done.49 = bf16[288,1536]{1,0:T(8,128)(2,1)} collective-permute-done((bf16[288,1536]{1,0:T(8,128)(2,1)}, bf16[288,1536]{1,0:T(8,128)(2,1)}, u32[]{:S(2)}, u32[]{:S(2)}) %collective-permute-start.49) | collective-permute-done | bytes 884768 | tf_op jit(solution)/shard_map/ppermute | solution.py:52
  597.7 5.6 convert_add_fusion
  606.6 2.7 convert_add_fusion.1
  610.9 13.6 %collective-permute-done.39 = bf16[2,88,2304]{2,1,0:T(8,128)(2,1)S(1)} collective-permute-done((bf16[2,88,2304]{2,1,0:T(8,128)(2,1)S(1)}, bf16[2,88,2304]{2,1,0:T(8,128)(2,1)S(1)}, u32[]{:S(2)}, u32[]{:S(2)}) %collective-permute-start.39) | collective-permute-done | bytes 811040 | tf_op jit(solution)/shard_map/ppermute | solution.py:52
  628.9 12.9 %collective-permute-done.34 = bf16[2,88,2304]{2,1,0:T(8,128)(2,1)S(1)} collective-permute-done((bf16[2,88,2304]{2,1,0:T(8,128)(2,1)S(1)}, bf16[2,88,2304]{2,1,0:T(8,128)(2,1)S(1)}, u32[]{:S(2)}, u32[]{:S(2)}) %collective-permute-start.34) | collective-permute-done | bytes 811040 | tf_op jit(solution)/shard_map/ppermute | solution.py:52
  646.2 6.0 collective-permute-done.40
  657.3 2.4 collective-permute-done.45
  660.5 3.1 collective-permute-done.46
  665.2 2.8 collective-permute-done.47
  668.0 3.0 collective-permute-start.48
  671.0 5.8 reduce-scatter.8.cloned.1.call-done
  681.7 14.9 %collective-permute-done.43 = bf16[288,1280]{1,0:T(8,128)(2,1)S(1)} collective-permute-done((bf16[288,1280]{1,0:T(8,128)(2,1)S(1)}, bf16[288,1280]{1,0:T(8,128)(2,1)S(1)}, u32[]{:S(2)}, u32[]{:S(2)}) %collective-permute-start.43) | collective-permute-done | bytes 737312 | tf_op jit(solution)/shard_map/ppermute | solution.py:52
  (308 shorter events, 151.4 us)
Async XLA Ops:
  7.2 144.8 %all-gather.4.cloned.1.call-start = ((), (), s32[]{:S(2)}) async-start(), calls=%async_computation.3 | async-start | bytes 7372800 | tf_op jit(solution)/shard_map/all_gather | solution.py:616
  16.3 19.5 %collective-permute-start = (bf16[288,1280]{1,0:T(8,128)(2,1)S(1)}, bf16[288,1280]{1,0:T(8,128)(2,1)S(1)}, u32[]{:S(2)}, u32[]{:S(2)}) collective-permute-start(bf16[288,1280]{1,0:T(8,128)(2,1)S(1)} %get-tuple-element.122), channel_id=1, source_target_pairs={{0,4},{4,0},{1,5},{5,1},{2,6},{6,2},{3,7},{7,3},{8,12},{12,8},{9,1... | collective-permute-start | bytes 2211848 | tf_op jit(solution)/shard_map/ppermute | solution.py:52
  37.4 19.3 %collective-permute-start.2 = (bf16[176,2304]{1,0:T(8,128)(2,1)S(1)}, bf16[176,2304]{1,0:T(8,128)(2,1)S(1)}, u32[]{:S(2)}, u32[]{:S(2)}) collective-permute-start(bf16[176,2304]{1,0:T(8,128)(2,1)S(1)} %fusion.15), channel_id=1, source_target_pairs={{0,4},{4,0},{1,5},{5,1},{2,6},{6,2},{3,7},{7,3},{8,12},{12,8},{9,1... | collective-permute-start | bytes 2433032 | tf_op jit(solution)/shard_map/ppermute | solution.py:52
  39.2 19.1 %collective-permute-start.1 = (bf16[176,2304]{1,0:T(8,128)(2,1)S(1)}, bf16[176,2304]{1,0:T(8,128)(2,1)}, u32[]{:S(2)}, u32[]{:S(2)}) collective-permute-start(bf16[176,2304]{1,0:T(8,128)(2,1)S(1)} %fusion.15), channel_id=1, source_target_pairs={{0,2},{2,0},{1,3},{3,1},{4,6},{6,4},{5,7},{7,5},{8,10},{10,8},{9,1... | collective-permute-start | bytes 2433032 | tf_op jit(solution)/shard_map/ppermute | solution.py:56
  40.7 239.0 %all-gather.6.cloned.1.call-start = ((), (), s32[]{:S(2)}) async-start(), calls=%async_computation.4 | async-start | bytes 8847360 | tf_op jit(solution)/shard_map/all_gather | solution.py:620
  56.7 9.8 %collective-permute-start.3 = (bf16[88,2304]{1,0:T(8,128)(2,1)S(1)}, bf16[88,2304]{1,0:T(8,128)(2,1)S(1)}, u32[]{:S(2)}, u32[]{:S(2)}) collective-permute-start(bf16[88,2304]{1,0:T(8,128)(2,1)S(1)} %slice.441), channel_id=1, source_target_pairs={{0,2},{2,0},{1,3},{3,1},{4,6},{6,4},{5,7},{7,5},{8,10},{10,8},{9,1... | collective-permute-start | bytes 1216520 | tf_op jit(solution)/shard_map/ppermute | solution.py:56
  59.3 9.2 %collective-permute-start.4 = (bf16[88,2304]{1,0:T(8,128)(2,1)S(1)}, bf16[88,2304]{1,0:T(8,128)(2,1)S(1)}, u32[]{:S(2)}, u32[]{:S(2)}) collective-permute-start(bf16[88,2304]{1,0:T(8,128)(2,1)S(1)} %slice.442), channel_id=1, source_target_pairs={{0,4},{4,0},{1,5},{5,1},{2,6},{6,2},{3,7},{7,3},{8,12},{12,8},{9,1... | collective-permute-start | bytes 1216520 | tf_op jit(solution)/shard_map/ppermute | solution.py:52
  70.4 17.1 %collective-permute-start.9 = (bf16[176,2304]{1,0:T(8,128)(2,1)S(1)}, bf16[176,2304]{1,0:T(8,128)(2,1)S(1)}, u32[]{:S(2)}, u32[]{:S(2)}) collective-permute-start(bf16[176,2304]{1,0:T(8,128)(2,1)S(1)} %get-tuple-element.98), channel_id=1, source_target_pairs={{0,4},{4,0},{1,5},{5,1},{2,6},{6,2},{3,7},{7,3},{8,12},{12,8},{9,1... | collective-permute-start | bytes 2433032 | tf_op jit(solution)/shard_map/ppermute | solution.py:52
  71.9 19.0 %collective-permute-start.8 = (bf16[176,2304]{1,0:T(8,128)(2,1)S(1)}, bf16[176,2304]{1,0:T(8,128)(2,1)S(1)}, u32[]{:S(2)}, u32[]{:S(2)}) collective-permute-start(bf16[176,2304]{1,0:T(8,128)(2,1)S(1)} %get-tuple-element.98), channel_id=1, source_target_pairs={{0,2},{2,0},{1,3},{3,1},{4,6},{6,4},{5,7},{7,5},{8,10},{10,8},{9,1... | collective-permute-start | bytes 2433032 | tf_op jit(solution)/shard_map/ppermute | solution.py:56
  72.4 69.7 %collective-permute-start.5 = (bf16[704,2304]{1,0:T(8,128)(2,1)}, bf16[704,2304]{1,0:T(8,128)(2,1)}, u32[]{:S(2)}, u32[]{:S(2)}) collective-permute-start(bf16[704,2304]{1,0:T(8,128)(2,1)} %constant_dynamic-update-slice_fusion.refs_0_), channel_id=1, source_target_pairs={{0,1},{1,0},{2,3},{3,2},{4,5},{5,4},{6,7},{7,6},{8,9},{9,8},{10,11... | collective-permute-start | bytes 9732104 | tf_op jit(solution)/shard_map/ppermute | solution.py:60
  87.5 9.8 %collective-permute-start.10 = (bf16[88,2304]{1,0:T(8,128)(2,1)S(1)}, bf16[88,2304]{1,0:T(8,128)(2,1)S(1)}, u32[]{:S(2)}, u32[]{:S(2)}) collective-permute-start(bf16[88,2304]{1,0:T(8,128)(2,1)S(1)} %slice.445), channel_id=1, source_target_pairs={{0,2},{2,0},{1,3},{3,1},{4,6},{6,4},{5,7},{7,5},{8,10},{10,8},{9,1... | collective-permute-start | bytes 1216520 | tf_op jit(solution)/shard_map/ppermute | solution.py:56
  99.7 48.4 %collective-permute-start.12 = (bf16[704,2304]{1,0:T(8,128)(2,1)}, bf16[704,2304]{1,0:T(8,128)(2,1)}, u32[]{:S(2)}, u32[]{:S(2)}) collective-permute-start(bf16[704,2304]{1,0:T(8,128)(2,1)} %get-tuple-element.142.refs_0_), channel_id=1, source_target_pairs={{0,1},{1,0},{2,3},{3,2},{4,5},{5,4},{6,7},{7,6},{8,9},{9,8},{10,11... | collective-permute-start | bytes 9732104 | tf_op jit(solution)/shard_map/ppermute | solution.py:60
  107.2 13.0 %collective-permute-start.7 = (bf16[288,768]{1,0:T(8,128)(2,1)S(1)}, bf16[288,768]{1,0:T(8,128)(2,1)S(1)}, u32[]{:S(2)}, u32[]{:S(2)}) collective-permute-start(bf16[288,768]{1,0:T(8,128)(2,1)S(1)} %get-tuple-element.124), channel_id=1, source_target_pairs={{0,4},{4,0},{1,5},{5,1},{2,6},{6,2},{3,7},{7,3},{8,12},{12,8},{9,1... | collective-permute-start | bytes 1327112 | tf_op jit(solution)/shard_map/ppermute | solution.py:52
  107.3 31.5 %collective-permute-start.6 = (bf16[288,1536]{1,0:T(8,128)(2,1)S(1)}, bf16[288,1536]{1,0:T(8,128)(2,1)}, u32[]{:S(2)}, u32[]{:S(2)}) collective-permute-start(bf16[288,1536]{1,0:T(8,128)(2,1)S(1)} %pad_maximum_fusion.3), channel_id=1, source_target_pairs={{0,4},{4,0},{1,5},{5,1},{2,6},{6,2},{3,7},{7,3},{8,12},{12,8},{9,1... | collective-permute-start | bytes 2654216 | tf_op jit(solution)/shard_map/ppermute | solution.py:52
  152.0 213.0 %all-gather.8.cloned.1.call-start = ((), (), s32[]{:S(2)}) async-start(), calls=%async_computation.5 | async-start | bytes 4423680 | tf_op jit(solution)/shard_map/all_gather | solution.py:621
  197.5 20.2 %collective-permute-start.14 = (bf16[2,88,2304]{2,1,0:T(8,128)(2,1)S(1)}, bf16[2,88,2304]{2,1,0:T(8,128)(2,1)S(1)}, u32[]{:S(2)}, u32[]{:S(2)}) collective-permute-start(bf16[2,88,2304]{2,1,0:T(8,128)(2,1)S(1)} %slice_bitcast_fusion.21), channel_id=1, source_target_pairs={{0,4},{4,0},{1,5},{5,1},{2,6},{6,2},{3,7},{7,3},{8,12},{12,8},{9,1... | collective-permute-start | bytes 2433032 | tf_op jit(solution)/shard_map/ppermute | solution.py:52
  197.6 20.2 %collective-permute-start.16 = (bf16[2,88,2304]{2,1,0:T(8,128)(2,1)S(1)}, bf16[2,88,2304]{2,1,0:T(8,128)(2,1)S(1)}, u32[]{:S(2)}, u32[]{:S(2)}) collective-permute-start(bf16[2,88,2304]{2,1,0:T(8,128)(2,1)S(1)} %slice_bitcast_fusion.20), channel_id=1, source_target_pairs={{0,2},{2,0},{1,3},{3,1},{4,6},{6,4},{5,7},{7,5},{8,10},{10,8},{9,1... | collective-permute-start | bytes 2433032 | tf_op jit(solution)/shard_map/ppermute | solution.py:56
  220.4 62.2 %collective-permute-start.17 = (bf16[88,2304]{1,0:T(8,128)(2,1)S(1)}, bf16[88,2304]{1,0:T(8,128)(2,1)}, u32[]{:S(2)}, u32[]{:S(2)}) collective-permute-start(bf16[88,2304]{1,0:T(8,128)(2,1)S(1)} %fusion.57), channel_id=1, source_target_pairs={{0,4},{4,0},{1,5},{5,1},{2,6},{6,2},{3,7},{7,3},{8,12},{12,8},{9,1... | collective-permute-start | bytes 1216520 | tf_op jit(solution)/shard_map/ppermute | solution.py:52
  281.1 11.4 %collective-permute-start.15 = (bf16[88,2304]{1,0:T(8,128)(2,1)S(1)}, bf16[88,2304]{1,0:T(8,128)(2,1)S(1)}, u32[]{:S(2)}, u32[]{:S(2)}) collective-permute-start(bf16[88,2304]{1,0:T(8,128)(2,1)S(1)} %fusion.56), channel_id=1, source_target_pairs={{0,2},{2,0},{1,3},{3,1},{4,6},{6,4},{5,7},{7,5},{8,10},{10,8},{9,1... | collective-permute-start | bytes 1216520 | tf_op jit(solution)/shard_map/ppermute | solution.py:56
  295.5 19.5 %collective-permute-start.19 = (bf16[176,2304]{1,0:T(8,128)(2,1)}, bf16[176,2304]{1,0:T(8,128)(2,1)}, u32[]{:S(2)}, u32[]{:S(2)}) collective-permute-start(bf16[176,2304]{1,0:T(8,128)(2,1)} %get-tuple-element.94), channel_id=1, source_target_pairs={{0,4},{4,0},{1,5},{5,1},{2,6},{6,2},{3,7},{7,3},{8,12},{12,8},{9,1... | collective-permute-start | bytes 2433032 | tf_op jit(solution)/shard_map/ppermute | solution.py:52
  297.0 20.6 %collective-permute-start.18 = (bf16[176,2304]{1,0:T(8,128)(2,1)}, bf16[176,2304]{1,0:T(8,128)(2,1)}, u32[]{:S(2)}, u32[]{:S(2)}) collective-permute-start(bf16[176,2304]{1,0:T(8,128)(2,1)} %get-tuple-element.94), channel_id=1, source_target_pairs={{0,2},{2,0},{1,3},{3,1},{4,6},{6,4},{5,7},{7,5},{8,10},{10,8},{9,1... | collective-permute-start | bytes 2433032 | tf_op jit(solution)/shard_map/ppermute | solution.py:56
  298.5 146.9 %reduce-scatter.4.cloned.1.call-start = ((), (), s32[]{:S(2)}) async-start(), calls=%async_computation.6 | async-start | bytes 4423680 | tf_op jit(solution)/shard_map/reduce_scatter | solution.py:634
  316.1 9.6 %collective-permute-start.20 = (bf16[88,2304]{1,0:T(8,128)(2,1)S(1)}, bf16[88,2304]{1,0:T(8,128)(2,1)S(1)}, u32[]{:S(2)}, u32[]{:S(2)}) collective-permute-start(bf16[88,2304]{1,0:T(8,128)(2,1)S(1)} %slice.454), channel_id=1, source_target_pairs={{0,2},{2,0},{1,3},{3,1},{4,6},{6,4},{5,7},{7,5},{8,10},{10,8},{9,1... | collective-permute-start | bytes 1216520 | tf_op jit(solution)/shard_map/ppermute | solution.py:56
  318.7 9.4 %collective-permute-start.21 = (bf16[88,2304]{1,0:T(8,128)(2,1)S(1)}, bf16[88,2304]{1,0:T(8,128)(2,1)S(1)}, u32[]{:S(2)}, u32[]{:S(2)}) collective-permute-start(bf16[88,2304]{1,0:T(8,128)(2,1)S(1)} %slice.455), channel_id=1, source_target_pairs={{0,4},{4,0},{1,5},{5,1},{2,6},{6,2},{3,7},{7,3},{8,12},{12,8},{9,1... | collective-permute-start | bytes 1216520 | tf_op jit(solution)/shard_map/ppermute | solution.py:52
  328.8 10.4 %collective-permute-start.22 = (bf16[704,2304]{1,0:T(8,128)(2,1)}, bf16[704,2304]{1,0:T(8,128)(2,1)S(1)}, u32[]{:S(2)}, u32[]{:S(2)}) collective-permute-start(bf16[704,2304]{1,0:T(8,128)(2,1)} %constant_dynamic-update-slice_fusion.16.rows_ref.refs_0_), channel_id=1, source_target_pairs={{0,1},{1,0},{2,3},{3,2},{4,5},{5,4},{6,7},{7,6},{8,9},{9,8},{10,11... | collective-permute-start | bytes 9732104 | tf_op jit(solution)/shard_map/ppermute | solution.py:60
  363.2 195.0 %reduce-scatter.6.cloned.1.call-start = ((), (), s32[]{:S(2)}) async-start(), calls=%async_computation.7 | async-start | bytes 8847360 | tf_op jit(solution)/shard_map/reduce_scatter | solution.py:638
  405.1 271.7 %reduce-scatter.8.cloned.1.call-start = ((), (), s32[]{:S(2)}) async-start(), calls=%async_computation.8 | async-start | bytes 7372800 | tf_op jit(solution)/shard_map/reduce_scatter | solution.py:652
  420.7 20.2 %collective-permute-start.24 = (bf16[2,88,2304]{2,1,0:T(8,128)(2,1)S(1)}, bf16[2,88,2304]{2,1,0:T(8,128)(2,1)S(1)}, u32[]{:S(2)}, u32[]{:S(2)}) collective-permute-start(bf16[2,88,2304]{2,1,0:T(8,128)(2,1)S(1)} %slice_bitcast_fusion.18), channel_id=1, source_target_pairs={{0,4},{4,0},{1,5},{5,1},{2,6},{6,2},{3,7},{7,3},{8,12},{12,8},{9,1... | collective-permute-start | bytes 2433032 | tf_op jit(solution)/shard_map/ppermute | solution.py:52
  422.4 19.8 %collective-permute-start.26 = (bf16[2,88,2304]{2,1,0:T(8,128)(2,1)S(1)}, bf16[2,88,2304]{2,1,0:T(8,128)(2,1)S(1)}, u32[]{:S(2)}, u32[]{:S(2)}) collective-permute-start(bf16[2,88,2304]{2,1,0:T(8,128)(2,1)S(1)} %slice_bitcast_fusion.17), channel_id=1, source_target_pairs={{0,2},{2,0},{1,3},{3,1},{4,6},{6,4},{5,7},{7,5},{8,10},{10,8},{9,1... | collective-permute-start | bytes 2433032 | tf_op jit(solution)/shard_map/ppermute | solution.py:56
  444.9 10.4 %collective-permute-start.27 = (bf16[88,2304]{1,0:T(8,128)(2,1)S(1)}, bf16[88,2304]{1,0:T(8,128)(2,1)}, u32[]{:S(2)}, u32[]{:S(2)}) collective-permute-start(bf16[88,2304]{1,0:T(8,128)(2,1)S(1)} %fusion.59), channel_id=1, source_target_pairs={{0,4},{4,0},{1,5},{5,1},{2,6},{6,2},{3,7},{7,3},{8,12},{12,8},{9,1... | collective-permute-start | bytes 1216520 | tf_op jit(solution)/shard_map/ppermute | solution.py:52
  446.7 10.3 %collective-permute-start.25 = (bf16[88,2304]{1,0:T(8,128)(2,1)S(1)}, bf16[88,2304]{1,0:T(8,128)(2,1)S(1)}, u32[]{:S(2)}, u32[]{:S(2)}) collective-permute-start(bf16[88,2304]{1,0:T(8,128)(2,1)S(1)} %fusion.58), channel_id=1, source_target_pairs={{0,2},{2,0},{1,3},{3,1},{4,6},{6,4},{5,7},{7,5},{8,10},{10,8},{9,1... | collective-permute-start | bytes 1216520 | tf_op jit(solution)/shard_map/ppermute | solution.py:56
  460.7 18.1 %collective-permute-start.29 = (bf16[176,2304]{1,0:T(8,128)(2,1)S(1)}, bf16[176,2304]{1,0:T(8,128)(2,1)S(1)}, u32[]{:S(2)}, u32[]{:S(2)}) collective-permute-start(bf16[176,2304]{1,0:T(8,128)(2,1)S(1)} %get-tuple-element.91), channel_id=1, source_target_pairs={{0,4},{4,0},{1,5},{5,1},{2,6},{6,2},{3,7},{7,3},{8,12},{12,8},{9,1... | collective-permute-start | bytes 2433032 | tf_op jit(solution)/shard_map/ppermute | solution.py:52
  461.9 18.2 %collective-permute-start.28 = (bf16[176,2304]{1,0:T(8,128)(2,1)S(1)}, bf16[176,2304]{1,0:T(8,128)(2,1)S(1)}, u32[]{:S(2)}, u32[]{:S(2)}) collective-permute-start(bf16[176,2304]{1,0:T(8,128)(2,1)S(1)} %get-tuple-element.91), channel_id=1, source_target_pairs={{0,2},{2,0},{1,3},{3,1},{4,6},{6,4},{5,7},{7,5},{8,10},{10,8},{9,1... | collective-permute-start | bytes 2433032 | tf_op jit(solution)/shard_map/ppermute | solution.py:56
  478.8 9.4 %collective-permute-start.30 = (bf16[88,2304]{1,0:T(8,128)(2,1)S(1)}, bf16[88,2304]{1,0:T(8,128)(2,1)S(1)}, u32[]{:S(2)}, u32[]{:S(2)}) collective-permute-start(bf16[88,2304]{1,0:T(8,128)(2,1)S(1)} %slice.463), channel_id=1, source_target_pairs={{0,2},{2,0},{1,3},{3,1},{4,6},{6,4},{5,7},{7,5},{8,10},{10,8},{9,1... | collective-permute-start | bytes 1216520 | tf_op jit(solution)/shard_map/ppermute | solution.py:56
  489.6 76.7 %collective-permute-start.50 = (bf16[288,768]{1,0:T(8,128)(2,1)}, bf16[288,768]{1,0:T(8,128)(2,1)}, u32[]{:S(2)}, u32[]{:S(2)}) collective-permute-start(bf16[288,768]{1,0:T(8,128)(2,1)} %get-tuple-element.130), channel_id=1, source_target_pairs={{0,4},{4,0},{1,5},{5,1},{2,6},{6,2},{3,7},{7,3},{8,12},{12,8},{9,1... | collective-permute-start | bytes 1327112 | tf_op jit(solution)/shard_map/ppermute | solution.py:52
  566.1 31.5 %collective-permute-start.38 = (bf16[704,2304]{1,0:T(8,128)(2,1)}, bf16[704,2304]{1,0:T(8,128)(2,1)}, u32[]{:S(2)}, u32[]{:S(2)}) collective-permute-start(bf16[704,2304]{1,0:T(8,128)(2,1)} %convolution_convert_fusion.2), channel_id=1, source_target_pairs={{0,1},{1,0},{2,3},{3,2},{4,5},{5,4},{6,7},{7,6},{8,9},{9,8},{10,11... | collective-permute-start | bytes 9732104 | tf_op jit(solution)/shard_map/ppermute | solution.py:60
  570.4 22.4 %collective-permute-start.49 = (bf16[288,1536]{1,0:T(8,128)(2,1)}, bf16[288,1536]{1,0:T(8,128)(2,1)}, u32[]{:S(2)}, u32[]{:S(2)}) collective-permute-start(bf16[288,1536]{1,0:T(8,128)(2,1)} %get-tuple-element.114), channel_id=1, source_target_pairs={{0,4},{4,0},{1,5},{5,1},{2,6},{6,2},{3,7},{7,3},{8,12},{12,8},{9,1... | collective-permute-start | bytes 2654216 | tf_op jit(solution)/shard_map/ppermute | solution.py:52
  579.0 27.6 %collective-permute-start.33 = (bf16[704,2304]{1,0:T(8,128)(2,1)}, bf16[704,2304]{1,0:T(8,128)(2,1)S(1)}, u32[]{:S(2)}, u32[]{:S(2)}) collective-permute-start(bf16[704,2304]{1,0:T(8,128)(2,1)} %convolution_convert_fusion), channel_id=1, source_target_pairs={{0,1},{1,0},{2,3},{3,2},{4,5},{5,4},{6,7},{7,6},{8,9},{9,8},{10,11... | collective-permute-start | bytes 9732104 | tf_op jit(solution)/shard_map/ppermute | solution.py:60
  603.5 21.0 %collective-permute-start.39 = (bf16[2,88,2304]{2,1,0:T(8,128)(2,1)S(1)}, bf16[2,88,2304]{2,1,0:T(8,128)(2,1)S(1)}, u32[]{:S(2)}, u32[]{:S(2)}) collective-permute-start(bf16[2,88,2304]{2,1,0:T(8,128)(2,1)S(1)} %slice_bitcast_fusion.11), channel_id=1, source_target_pairs={{0,4},{4,0},{1,5},{5,1},{2,6},{6,2},{3,7},{7,3},{8,12},{12,8},{9,1... | collective-permute-start | bytes 2433032 | tf_op jit(solution)/shard_map/ppermute | solution.py:52
  605.1 21.1 %collective-permute-start.41 = (bf16[2,88,2304]{2,1,0:T(8,128)(2,1)S(1)}, bf16[2,88,2304]{2,1,0:T(8,128)(2,1)S(1)}, u32[]{:S(2)}, u32[]{:S(2)}) collective-permute-start(bf16[2,88,2304]{2,1,0:T(8,128)(2,1)S(1)} %slice_bitcast_fusion.9), channel_id=1, source_target_pairs={{0,2},{2,0},{1,3},{3,1},{4,6},{6,4},{5,7},{7,5},{8,10},{10,8},{9,1... | collective-permute-start | bytes 2433032 | tf_op jit(solution)/shard_map/ppermute | solution.py:56
  609.4 32.4 %collective-permute-start.34 = (bf16[2,88,2304]{2,1,0:T(8,128)(2,1)S(1)}, bf16[2,88,2304]{2,1,0:T(8,128)(2,1)S(1)}, u32[]{:S(2)}, u32[]{:S(2)}) collective-permute-start(bf16[2,88,2304]{2,1,0:T(8,128)(2,1)S(1)} %slice_bitcast_fusion.15), channel_id=1, source_target_pairs={{0,4},{4,0},{1,5},{5,1},{2,6},{6,2},{3,7},{7,3},{8,12},{12,8},{9,1... | collective-permute-start | bytes 2433032 | tf_op jit(solution)/shard_map/ppermute | solution.py:52
  610.2 33.4 %collective-permute-start.36 = (bf16[2,88,2304]{2,1,0:T(8,128)(2,1)S(1)}, bf16[2,88,2304]{2,1,0:T(8,128)(2,1)S(1)}, u32[]{:S(2)}, u32[]{:S(2)}) collective-permute-start(bf16[2,88,2304]{2,1,0:T(8,128)(2,1)S(1)} %slice_bitcast_fusion.13), channel_id=1, source_target_pairs={{0,2},{2,0},{1,3},{3,1},{4,6},{6,4},{5,7},{7,5},{8,10},{10,8},{9,1... | collective-permute-start | bytes 2433032 | tf_op jit(solution)/shard_map/ppermute | solution.py:56
  626.7 25.5 %collective-permute-start.40 = (bf16[88,2304]{1,0:T(8,128)(2,1)S(1)}, bf16[88,2304]{1,0:T(8,128)(2,1)S(1)}, u32[]{:S(2)}, u32[]{:S(2)}) collective-permute-start(bf16[88,2304]{1,0:T(8,128)(2,1)S(1)} %fusion.62), channel_id=1, source_target_pairs={{0,2},{2,0},{1,3},{3,1},{4,6},{6,4},{5,7},{7,5},{8,10},{10,8},{9,1... | collective-permute-start | bytes 1216520 | tf_op jit(solution)/shard_map/ppermute | solution.py:56
  628.3 24.0 %collective-permute-start.42 = (bf16[88,2304]{1,0:T(8,128)(2,1)S(1)}, bf16[88,2304]{1,0:T(8,128)(2,1)S(1)}, u32[]{:S(2)}, u32[]{:S(2)}) collective-permute-start(bf16[88,2304]{1,0:T(8,128)(2,1)S(1)} %fusion.63), channel_id=1, source_target_pairs={{0,4},{4,0},{1,5},{5,1},{2,6},{6,2},{3,7},{7,3},{8,12},{12,8},{9,1... | collective-permute-start | bytes 1216520 | tf_op jit(solution)/shard_map/ppermute | solution.py:52
  644.0 16.4 %collective-permute-start.35 = (bf16[88,2304]{1,0:T(8,128)(2,1)S(1)}, bf16[88,2304]{1,0:T(8,128)(2,1)S(1)}, u32[]{:S(2)}, u32[]{:S(2)}) collective-permute-start(bf16[88,2304]{1,0:T(8,128)(2,1)S(1)} %fusion.60), channel_id=1, source_target_pairs={{0,2},{2,0},{1,3},{3,1},{4,6},{6,4},{5,7},{7,5},{8,10},{10,8},{9,1... | collective-permute-start | bytes 1216520 | tf_op jit(solution)/shard_map/ppermute | solution.py:56
  645.6 19.6 %collective-permute-start.37 = (bf16[88,2304]{1,0:T(8,128)(2,1)S(1)}, bf16[88,2304]{1,0:T(8,128)(2,1)S(1)}, u32[]{:S(2)}, u32[]{:S(2)}) collective-permute-start(bf16[88,2304]{1,0:T(8,128)(2,1)S(1)} %fusion.61), channel_id=1, source_target_pairs={{0,4},{4,0},{1,5},{5,1},{2,6},{6,2},{3,7},{7,3},{8,12},{12,8},{9,1... | collective-permute-start | bytes 1216520 | tf_op jit(solution)/shard_map/ppermute | solution.py:52
  668.0 12.9 %collective-permute-start.48 = (f32[2,2304]{1,0:T(2,128)S(1)}, f32[2,2304]{1,0:T(2,128)S(1)}, u32[]{:S(2)}, u32[]{:S(2)}) collective-permute-start(f32[2,2304]{1,0:T(2,128)S(1)} %add.278), channel_id=1, source_target_pairs={{0,16},{8,24},{16,0},{24,8},{1,17},{9,25},{17,1},{25,9},{2,18},{10... | collective-permute-start | bytes 55304 | tf_op jit(solution)/shard_map/ppermute | solution.py:105
  678.3 18.3 %collective-permute-start.43 = (bf16[288,1280]{1,0:T(8,128)(2,1)S(1)}, bf16[288,1280]{1,0:T(8,128)(2,1)S(1)}, u32[]{:S(2)}, u32[]{:S(2)}) collective-permute-start(bf16[288,1280]{1,0:T(8,128)(2,1)S(1)} %get-tuple-element.120), channel_id=1, source_target_pairs={{0,4},{4,0},{1,5},{5,1},{2,6},{6,2},{3,7},{7,3},{8,12},{12,8},{9,1... | collective-permute-start | bytes 2211848 | tf_op jit(solution)/shard_map/ppermute | solution.py:52
  (52 other events, 492.3 us)
Sparse Core Ops, SparseCore 0:
  40.9 108.2 all-gather.3
  152.1 127.5 all-gather.5
  298.6 66.2 all-gather.7
  367.1 64.9 reduce-scatter.3
  434.3 123.7 reduce-scatter.5
  572.0 104.7 reduce-scatter.7

commit v3 on v2

--- a/solution.py
+++ b/solution.py
@@ -56,7 +56,11 @@
     return lax.ppermute(field, "mp", [(0, 2), (2, 0), (1, 3), (3, 1)])
 
 
-def flip_core(field):
+def flip_core(field, pieces=1):
+    if pieces > 1:
+        size = field.shape[0] // pieces
+        parts = [flip_core(field[i * size : (i + 1) * size]) for i in range(pieces)]
+        return jnp.concatenate(parts, axis=0)
     return lax.ppermute(field, "mp", [(0, 1), (1, 0), (2, 3), (3, 2)])
 
 
@@ -75,11 +79,11 @@
     return near, flip_core(near)
 
 
-def sum_rows(left, right, dims, other=None):
+def sum_rows(left, right, dims, other=None, pieces=1):
     count = left.shape[0] // 2
     block = count // 4
     half = block // 2
-    away = flip_core(dot(left[count:], right, dims).astype(bf16))
+    away = flip_core(dot(left[count:], right, dims).astype(bf16), pieces)
     total = dot(left[:count], right, dims) + away.astype(f32)
     total = total.reshape(2, 2, block, total.shape[-1])
     got_x = flip_x(total[1, :, :half].astype(bf16)).astype(f32)
@@ -458,26 +462,30 @@
     )(rows, down_w, gate_up)
 
 
-def rows_kernel(dims, rows_ref, w_ref, out_ref):
-    out_ref[...] = dot(rows_ref[...], w_ref[...], dims).astype(out_ref.dtype)
-
-
-def project(rows, weight, cols, kind):
+def rows_kernel(rows_ref, w_ref, *refs):
+    refs[-1][...] = dot(rows_ref[...], w_ref[...])
+
+
+def project_half(rows, weight, cols, earlier):
     count, depth = rows.shape
-    tile = count // 8
+    tile = count // 4
+    at = 0 if earlier is None else 4
+    earlier = () if earlier is None else (earlier,)
     return pl.pallas_call(
-        functools.partial(rows_kernel, NN),
-        grid=(8,),
-        out_shape=jax.ShapeDtypeStruct((count, cols), kind),
+        rows_kernel,
+        grid=(4,),
+        out_shape=jax.ShapeDtypeStruct((2 * count, cols), f32),
         in_specs=[
             pl.BlockSpec((tile, depth), lambda i: (i, 0)),
             pl.BlockSpec((depth, cols), lambda i: (0, 0), pipeline_mode=pl.Buffered(1)),
-        ],
-        out_specs=pl.BlockSpec((tile, cols), lambda i: (i, 0)),
+        ]
+        + [pl.BlockSpec(memory_space=pl.ANY)] * len(earlier),
+        out_specs=pl.BlockSpec((tile, cols), lambda i: (i + at, 0)),
+        input_output_aliases={2: 0} if earlier else {},
         compiler_params=ROOMY,
         cost_estimate=FREE,
-        name="project",
-    )(rows, weight)
+        name="project_half",
+    )(rows, weight, *earlier)
 
 
 def grads_kernel(place, *refs):
@@ -573,7 +581,7 @@
         return jnp.concatenate(cols[:3] + s_cols + cols[3:], axis=1)
 
     attn_a, attn_b = pack(a_cols), pack(b_cols)
-    attn_part = both_x(jnp.where(lower_x, attn_a, attn_b), jnp.where(lower_x, attn_b, attn_a))
+    attn_mine, attn_theirs = jnp.where(lower_x, attn_a, attn_b), jnp.where(lower_x, attn_b, attn_a)
 
     def halves(weight):
         fill = ((0, 0), (0, ff_pad - ff_half))
@@ -599,34 +607,51 @@
     cosine = jnp.concatenate([cos, cos, cos, cos], axis=1)
     sine = jnp.concatenate([-sin, sin, -sin, sin], axis=1)
 
-    attn_part, own_rows, grad_rows = after(attn_part, normalize(inputs) * gain_a, grad_rows)
-    near_a = gather_near(own_rows.astype(bf16))
-    near_a, w_gate, w_up, w_down, grad_rows = after(near_a, w_gate, w_up, w_down, grad_rows)
-    far_a = flip_core(near_a)
-    near_d, far_d = gather_rows((branch_scale * grad_rows).astype(bf16))
+    def rows_of_x(field):
+        rows = field.shape[0] // 2
+        mine = jnp.where(lower_x, field[:rows], field[rows:])
+        return mine, flip_x(jnp.where(lower_x, field[rows:], field[:rows]))
+
+    attn_got = flip_x(attn_theirs)
+    count, on_dp = lax.axis_size("dp"), lax.axis_index("dp")
+
+    def from_dp(field, k):
+        return lax.ppermute(field, "dp", [(i, i ^ k) for i in range(count)])
+
+    arrived = [from_dp(attn_mine, k) for k in range(1, count)]
+    _, own_rows = after(attn_got, (normalize(inputs) * gain_a).astype(bf16))
+    near_a, arrived[:2] = gather_near(own_rows, arrived[:2])
+    near_a, arrived[2:], w_gate, w_up = after(near_a, arrived[2:], w_gate, w_up)
     gate_mine, gate_theirs = halves(w_gate)
     up_mine, up_theirs = halves(w_up)
-    down_mine, down_theirs = halves(w_down.T)
     gu_part = both_x(
         jnp.concatenate([gate_mine, up_mine], 1), jnp.concatenate([gate_theirs, up_theirs], 1)
     )
-    down_part = both_x(down_mine, down_theirs)
-    normed_a = jnp.concatenate([near_a, far_a], axis=0)
-    d_mlp = jnp.concatenate([near_d, far_d], axis=0)
-    attn_w = lax.all_gather(attn_part, "dp", axis=0, tiled=True)
-    attn_w, normed_a, gu_part, down_part, d_mlp, bias, cosine, sine = after(
-        attn_w, normed_a, gu_part, down_part, d_mlp, bias, cosine, sine
-    )
+    block = (1, 1) + attn_mine.shape
+    attn_w = jnp.zeros((count, 2) + attn_mine.shape, bf16)
+    for k, field in enumerate([attn_mine] + arrived):
+        attn_w = lax.dynamic_update_slice(attn_w, field.reshape(block), (on_dp ^ k, on_x, 0, 0))
+    attn_all = lax.all_gather(attn_got, "dp", axis=0, tiled=False)
+    near_a, gu_part, attn_all, attn_w, bias, cosine, sine = after(
+        near_a, gu_part, attn_all, attn_w, bias, cosine, sine
+    )
+    far_a = flip_core(near_a)
+    attn_w = lax.dynamic_update_slice(attn_w, attn_all[:, None], (0, 1 - on_x, 0, 0))
+    attn_w = attn_w.reshape(count * 2 * attn_mine.shape[0], attn_mine.shape[1])
     gu_w = lax.all_gather(gu_part, "dp", axis=0, tiled=True)
-    down_w = lax.all_gather(down_part, "dp", axis=0, tiled=True)
     qkv_w = attn_w[:, : 8 * LANES]
     out_w = attn_w[:, 7 * LANES :]
-    qkv = project(normed_a, attn_w, 8 * LANES, f32)
+    qkv = project_half(far_a, attn_w, 8 * LANES, project_half(near_a, attn_w, 8 * LANES, None))
+    qkv, w_down, grad_rows = after(qkv, w_down, grad_rows)
+    near_d, far_d = gather_rows((branch_scale * grad_rows).astype(bf16))
+    d_mlp = jnp.concatenate([near_d, far_d], axis=0)
+    down_mine, down_theirs = halves(w_down.T)
+    down_part = both_x(down_mine, down_theirs)
     rotated, mixed, log_total = attention_forward(info, qkv, cosine, sine, bias)
-    mixed_rows, gu_w = sum_rows(mixed, out_w, NT, gu_w)
-    residual = inputs + branch_scale * mixed_rows
-    near_m = gather_near((normalize(residual) * gain_m).astype(bf16))
-    far_m = flip_core(near_m)
+    residual = inputs + branch_scale * sum_rows(mixed, out_w, NT, pieces=4)
+    near_m, (gu_w, d_mlp) = gather_near((normalize(residual) * gain_m).astype(bf16), (gu_w, d_mlp))
+    down_w = lax.all_gather(down_part, "dp", axis=0, tiled=True)
+    far_m = flip_core(near_m, 4)
     gate_up, hidden = gate_half(far_m, gu_w, ff_pad, gate_half(near_m, gu_w, ff_pad, ()))
 
     grad_down = weight_grads(place_one, ff_pad, (near_d, far_d, hidden))
@@ -650,27 +675,25 @@
     )
     grad_attn, grad_gu, d_qkv, hidden = after(grad_attn, grad_gu, d_qkv, hidden)
     grad_attn = lax.psum_scatter(grad_attn, "dp", scatter_dimension=0, tiled=True)
-    d_normed_attn = sum_rows(d_qkv, qkv_w, NT)
+    gu_mine, gu_got = rows_of_x(grad_gu)
+    gu_got, d_qkv, hidden = after(gu_got, d_qkv, hidden)
+    d_normed_attn = sum_rows(d_qkv, qkv_w, NT, pieces=4)
     back_attn, gain_attn_part = norm_back(inputs, gain_a, d_normed_attn)
     input_grad = d_residual + back_attn
-    gains = sum_all(jnp.stack([gain_attn_part, gain_mlp_part]))
-    output = residual + branch_scale * sum_rows(hidden, down_w, NT)
-
-    def rows_of_x(field):
-        rows = field.shape[0] // 2
-        mine = jnp.where(lower_x, field[:rows], field[rows:])
-        got = flip_x(jnp.where(lower_x, field[rows:], field[:rows]))
-        return mine.astype(f32), got.astype(f32)
+    gains, grad_attn = after(jnp.stack([gain_attn_part, gain_mlp_part]), grad_attn)
+    gains = sum_all(gains)
+    output = residual + branch_scale * sum_rows(hidden, down_w, NT, pieces=4)
 
     def join(mine, got):
+        mine, got = mine.astype(f32), got.astype(f32)
         return jnp.where(lower_x, jnp.concatenate([mine, got], 1), jnp.concatenate([got, mine], 1))
 
     def join_heads(mine, got, at, shared_at):
         whole = join(mine[:, at : at + own_cols], got[:, at : at + own_cols])
         last = slice(shared_at, shared_at + HEAD_DIM)
-        return jnp.concatenate([whole, mine[:, last] + got[:, last]], axis=1)
-
-    mine, got = rows_of_x(grad_gu)
+        return jnp.concatenate([whole, mine[:, last].astype(f32) + got[:, last].astype(f32)], axis=1)
+
+    mine, got = gu_mine, gu_got
     grad_gate = join(mine[:, :ff_half], got[:, :ff_half])
     grad_up = join(mine[:, ff_pad : ff_pad + ff_half], got[:, ff_pad : ff_pad + ff_half])
     mine, got = rows_of_x(grad_down)

time: 719 us -> 693 us (0.964)
  waiting for transfers between devices: 328 us -> 269 us
  local copies, waits for them, and re-layouts: 43.4 us -> 60.3 us
  starting transfers between devices: 56 us -> 64.6 us
    ppermute x23, waiting for transfers between devices: 206 us -> 137 us  [flip_x(): return lax.ppermute(field, 'ctx', [(0, 1), (1, 0)])]
    all_gather x1, waiting for transfers between devices: 57.5 us -> 0.01 us  [shards(): gu_w = lax.all_gather(gu_part, 'dp', axis=0, tiled=True)]
    all_gather x1, waiting for transfers between devices: 0.01 us -> 28.3 us  [shards(): attn_all = lax.all_gather(attn_got, 'dp', axis=0, tiled=False)]
    ppermute x0 -> x3, waiting for transfers between devices: none -> 21.5 us  [from_dp(): return lax.ppermute(field, 'dp', [(i, i ^ k) for i in range(count)])]
    all_gather x1, waiting for transfers between devices: 1.77 us -> 17.1 us  [shards(): down_w = lax.all_gather(down_part, 'dp', axis=0, tiled=True)]
    dynamic_update_slice x0 -> x4, local copies, waits for them, and re-layouts: none -> 9.81 us  [the longest x3 6.12 us: shards(): lax.dynamic_update_slice(attn_w, field.reshape(block), (on_dp ^ k, on_x,...]
    concatenate x2 -> x8, local copies, waits for them, and re-layouts: 1.62 us -> 9.13 us  [pack(): return jnp.concatenate(cols[:3] + s_cols + cols[3:], axis=1)]
    ppermute x9 -> x21, waiting for transfers between devices: 14.3 us -> 7.03 us  [flip_core(): return lax.ppermute(field, 'mp', [(0, 1), (1, 0), (2, 3), (3, 2)])]
  transfers between devices with their start and end apart: 57 -> 72, of which waited for: 42 -> 38; matrix products, arithmetic and copies ran while one was open for 18% -> 22% of each run, Pallas kernels for 23% -> 24%
where the time goes in v3:
time: 693 us; the launch traced here: 684 us
  waiting for transfers between devices  269 us (39%)
  Pallas kernels  162 us (23%)
  starting transfers between devices  64.6 us (9%)
  local copies, waits for them, and re-layouts  60.3 us (9%)
  matrix products  56.5 us (8%)
  other arithmetic  55.8 us (8%)
  between operations  15.8 us (2%)
    ppermute x23, waiting for transfers between devices, flip_x(): return lax.ppermute(field, 'ctx', [(0, 1), (1, 0)])  137 us
    dot_general x10, matrix products, dot(): return lax.dot_general(left, right, dims, preferred_element_type=f32)  56.5 us
    pallas_call x3, Pallas kernels, weight_grads(): pl.pallas_call(functools.partial(grads_kernel, place), grid=(depth // (2...  45.1 us
    pallas_call x1, Pallas kernels, attention_backward(): pl.pallas_call(backward_kernel, out_shape=jax.ShapeDtypeStruct((slot, 8 *...  44.7 us
    ppermute x17, waiting for transfers between devices, flip_y(): return lax.ppermute(field, 'mp', [(0, 2), (2, 0), (1, 3), (3, 1)])  44.3 us
    all_gather x1, waiting for transfers between devices, shards(): attn_all = lax.all_gather(attn_got, 'dp', axis=0, tiled=False)  28.3 us
    ppermute x23, starting transfers between devices, flip_x(): return lax.ppermute(field, 'ctx', [(0, 1), (1, 0)])  26.8 us
    unnamed x115, local copies, waits for them, and re-layouts  24.4 us
  transfers between devices with their start and end apart: 72, of which 38 were waited for; matrix products, arithmetic and copies ran while one was open for 22% of the time, Pallas kernels for 24%

profile of v3, /device:TPU:0, one launch (start us, length us, event | category | flops | bytes accessed | tf_op | source)
XLA Modules:
  0.0 684.0 jit_solution(11017110325595457732)
XLA Ops:
  15.2 3.0 collective-permute-start.3
  25.9 6.2 fusion.1.bias_ref
  32.1 3.0 broadcast_in_dim.12
  41.7 3.6 fusion.57
  45.4 3.9 pad_maximum_fusion.7
  50.2 21.5 %collective-permute-done.4 = bf16[288,1280]{1,0:T(8,128)(2,1)} collective-permute-done((bf16[288,1280]{1,0:T(8,128)(2,1)}, bf16[288,1280]{1,0:T(8,128)(2,1)}, u32[]{:S(2)}, u32[]{:S(2)}) %collective-permute-start.4) | collective-permute-done | bytes 737312 | tf_op jit(solution)/shard_map/ppermute | solution.py:619
  92.6 9.7 %collective-permute-done.8 = bf16[288,1536]{1,0:T(8,128)(2,1)S(1)} collective-permute-done((bf16[288,1536]{1,0:T(8,128)(2,1)S(1)}, bf16[288,1536]{1,0:T(8,128)(2,1)S(1)}, u32[]{:S(2)}, u32[]{:S(2)}) %collective-permute-start.8) | collective-permute-done | bytes 884768 | tf_op jit(solution)/shard_map/ppermute | solution.py:52
  104.2 28.3 %all-gather.9.cloned.1.call-done = bf16[1152,1280]{1,0:T(8,128)(2,1)} async-done(((bf16[288,1280]{1,0:T(8,128)(2,1)}), bf16[1152,1280]{1,0:T(8,128)(2,1)}) %all-gather.9.cloned.1.call-update) | async-done | bytes 2949136 | tf_op jit(solution)/shard_map/all_gather | solution.py:634
  135.4 3.7 bitcast_dynamic-update-slice_fusion
  139.1 8.0 %project_half.2.refs_0_ = f32[1408,1024]{1,0:T(8,128)} custom-call(bf16[704,2304]{1,0:T(8,128)(2,1)} %constant_dynamic-update-slice_fusion.rows_ref.refs_0_, bf16[2304,1280]{1,0:T(8,128)(2,1)} %bitcast.36.w_ref), custom_call_target="tpu_custom_call" | custom-call | bytes 1024 | tf_op jit(solution)/shard_map/project_half/pallas_call | solution.py:474
  147.1 8.2 %project_half.3.qkv_ref = f32[1408,1024]{1,0:T(8,128)} custom-call(bf16[704,2304]{1,0:T(8,128)(2,1)} %collective-permute-done.9.rows_ref.refs_1_, bf16[2304,1280]{1,0:T(8,128)(2,1)} %bitcast.36.w_ref, f32[1408,1024]{1,0:T(8,128)} %project_half.2.refs_0_), custom_call_target="tpu_custom_call", output_to_operand_aliasing={{}: (2, {})} | custom-call | bytes 1024 | tf_op jit(solution)/shard_map/project_half/pallas_call | solution.py:474
  159.1 21.7 %attention_forward.1 = (bf16[1408,1024]{1,0:T(8,128)(2,1)S(1)}, bf16[1408,384]{1,0:T(8,128)(2,1)S(1)}, f32[3,8,2816]{2,1,0:T(8,128)S(1)}) custom-call(s32[17]{0:T(128)S(1)} %stack.80.info, f32[1408,1024]{1,0:T(8,128)} %project_half.3.qkv_ref, f32[1408,128]{1,0:T(8,128)S(1)} %get-tuple-element.69.cos_ref, f32[1408,128]{1,0:T(8,128)S(1)} %get-tuple-element.70.sin_ref, ...), custom_call_target="tpu_custom_call" | custom-call | bytes 1024 | tf_op jit(solution)/shard_map/attention_forward/pallas_call | solution.py:351
  180.9 4.4 convolution_convert_fusion.1
  194.9 5.0 convert_add_fusion.3
  200.1 12.7 %collective-permute-done.20 = bf16[176,2304]{1,0:T(8,128)(2,1)S(1)} collective-permute-done((bf16[176,2304]{1,0:T(8,128)(2,1)}, bf16[176,2304]{1,0:T(8,128)(2,1)S(1)}, u32[]{:S(2)}, u32[]{:S(2)}) %collective-permute-start.20) | collective-permute-done | bytes 811040 | tf_op jit(solution)/shard_map/ppermute | solution.py:56
  217.7 3.7 collective-permute-done.22
  221.5 3.7 collective-permute-done.23
  225.3 14.5 %collective-permute-done.14 = bf16[2,88,2304]{2,1,0:T(8,128)(2,1)S(1)} collective-permute-done((bf16[2,88,2304]{2,1,0:T(8,128)(2,1)S(1)}, bf16[2,88,2304]{2,1,0:T(8,128)(2,1)S(1)}, u32[]{:S(2)}, u32[]{:S(2)}) %collective-permute-start.14) | collective-permute-done | bytes 811040 | tf_op jit(solution)/shard_map/ppermute | solution.py:52
  242.6 6.5 collective-permute-done.15
  258.2 15.5 %collective-permute-done.18 = bf16[176,2304]{1,0:T(8,128)(2,1)S(1)} collective-permute-done((bf16[176,2304]{1,0:T(8,128)(2,1)S(1)}, bf16[176,2304]{1,0:T(8,128)(2,1)S(1)}, u32[]{:S(2)}, u32[]{:S(2)}) %collective-permute-start.18) | collective-permute-done | bytes 811040 | tf_op jit(solution)/shard_map/ppermute | solution.py:52
  281.9 6.8 collective-permute-done.29
  290.7 10.6 %gate_half.2 = (f32[1408,1536]{1,0:T(8,128)}, bf16[1408,768]{1,0:T(8,128)(2,1)}) custom-call(bf16[704,2304]{1,0:T(8,128)(2,1)} %constant_dynamic-update-slice_fusion.20.rows_ref.refs_0_, bf16[2304,1536]{1,0:T(8,128)(2,1)} %all-gather.5.cloned.1.call-done.w_ref), custom_call_target="tpu_custom_call" | custom-call | bytes 1024 | tf_op jit(solution)/shard_map/gate_half/pallas_call | solution.py:415
  303.2 10.4 %gate_half.3 = (f32[1408,1536]{1,0:T(8,128)}, bf16[1408,768]{1,0:T(8,128)(2,1)}) custom-call(bf16[704,2304]{1,0:T(8,128)(2,1)} %copy-done.8, bf16[2304,1536]{1,0:T(8,128)(2,1)} %all-gather.5.cloned.1.call-done.w_ref, f32[1408,1536]{1,0:T(8,128)} %get-tuple-element.81.refs_0_, ...), custom_call_target="tpu_custom_call", output_to_operand_aliasing={{0}: (2, {}), {1}: (3, {})} | custom-call | bytes 1024 | tf_op jit(solution)/shard_map/gate_half/pallas_call | solution.py:415
  313.6 11.9 %weight_grads.3 = bf16[2304,768]{1,0:T(8,128)(2,1)} custom-call(bf16[704,2304]{1,0:T(8,128)(2,1)} %copy-done.18, bf16[704,2304]{1,0:T(8,128)(2,1)} %copy-done.11, bf16[1408,768]{1,0:T(8,128)(2,1)} %get-tuple-element.94.refs_2_), custom_call_target="tpu_custom_call" | custom-call | bytes 1024 | tf_op jit(solution)/shard_map/weight_grads/pallas_call | solution.py:521
  326.0 17.1 %all-gather.7.cloned.1.call-done.w_ref = bf16[2304,768]{1,0:T(8,128)(2,1)} async-done(((bf16[576,768]{1,0:T(8,128)(2,1)}), bf16[2304,768]{1,0:T(8,128)(2,1)}) %all-gather.7.cloned.1.call-update) | async-done | bytes 3538960 | tf_op jit(solution)/shard_map/all_gather | solution.py:653
  343.1 13.6 %hidden_back.1.refs_2_ = bf16[1408,1536]{1,0:T(8,128)(2,1)} custom-call(bf16[1408,2304]{1,0:T(8,128)(2,1)} %copy-done.14, bf16[2304,768]{1,0:T(8,128)(2,1)} %all-gather.7.cloned.1.call-done.w_ref, f32[1408,1536]{1,0:T(8,128)} %get-tuple-element.85.gate_up_ref), custom_call_target="tpu_custom_call" | custom-call | bytes 1024 | tf_op jit(solution)/shard_map/hidden_back/pallas_call | solution.py:449
  356.7 16.4 %weight_grads.4 = bf16[2304,1536]{1,0:T(8,128)(2,1)} custom-call(bf16[704,2304]{1,0:T(8,128)(2,1)} %constant_dynamic-update-slice_fusion.20.rows_ref.refs_0_, bf16[704,2304]{1,0:T(8,128)(2,1)} %copy-done.8, bf16[1408,1536]{1,0:T(8,128)(2,1)} %hidden_back.1.refs_2_), custom_call_target="tpu_custom_call" | custom-call | bytes 1024 | tf_op jit(solution)/shard_map/weight_grads/pallas_call | solution.py:521
  373.1 10.0 %convolution_convert_fusion.3 = bf16[704,2304]{1,0:T(8,128)(2,1)} fusion(bf16[2304,1536]{1,0:T(8,128)(2,1)} %all-gather.5.cloned.1.call-done.w_ref, bf16[1408,1536]{1,0:T(8,128)(2,1)} %hidden_back.1.refs_2_), kind=kOutput, calls=%fused_computation.16 | convolution fusion | flops 4984455168 | bytes 12484608 | tf_op jit(solution)/shard_map/dot_general | solution.py:30
  383.3 6.0 collective-permute-done.32
  389.2 9.3 %convert_add_fusion.2 = f32[704,2304]{1,0:T(8,128)S(1)} fusion(bf16[704,2304]{1,0:T(8,128)(2,1)} %collective-permute-done.32, bf16[2304,1536]{1,0:T(8,128)(2,1)} %all-gather.5.cloned.1.call-done.w_ref, bf16[1408,1536]{1,0:T(8,128)(2,1)} %hidden_back.1.refs_2_), kind=kOutput, calls=%fused_computation.11 | convolution fusion | flops 4986077184 | bytes 18972672 | tf_op jit(solution)/shard_map/dot_general | solution.py:30
  402.0 16.9 %collective-permute-done.33 = bf16[2,88,2304]{2,1,0:T(8,128)(2,1)S(1)} collective-permute-done((bf16[2,88,2304]{2,1,0:T(8,128)(2,1)S(1)}, bf16[2,88,2304]{2,1,0:T(8,128)(2,1)S(1)}, u32[]{:S(2)}, u32[]{:S(2)}) %collective-permute-start.33) | collective-permute-done | bytes 811040 | tf_op jit(solution)/shard_map/ppermute | solution.py:52
  426.6 6.9 %collective-permute-done.36 = bf16[88,2304]{1,0:T(8,128)(2,1)} collective-permute-done((bf16[88,2304]{1,0:T(8,128)(2,1)S(1)}, bf16[88,2304]{1,0:T(8,128)(2,1)}, u32[]{:S(2)}, u32[]{:S(2)}) %collective-permute-start.36) | collective-permute-done | bytes 405536 | tf_op jit(solution)/shard_map/ppermute | solution.py:52
  441.6 15.2 %collective-permute-done.38 = bf16[176,2304]{1,0:T(8,128)(2,1)S(1)} collective-permute-done((bf16[176,2304]{1,0:T(8,128)(2,1)S(1)}, bf16[176,2304]{1,0:T(8,128)(2,1)S(1)}, u32[]{:S(2)}, u32[]{:S(2)}) %collective-permute-start.38) | collective-permute-done | bytes 811040 | tf_op jit(solution)/shard_map/ppermute | solution.py:52
  459.8 6.6 collective-permute-done.39
  469.0 3.3 convolution_convert_fusion.5.near_ref
  472.5 4.5 convolution_convert_fusion.4.far_ref
  477.0 44.7 %attention_backward.1.refs_2_ = bf16[1408,1024]{1,0:T(8,128)(2,1)} custom-call(s32[17]{0:T(128)S(1)} %stack.80.info, bf16[1408,1024]{1,0:T(8,128)(2,1)} %copy-done, f32[1408,128]{1,0:T(8,128)S(1)} %get-tuple-element.69.cos_ref, f32[1408,128]{1,0:T(8,128)S(1)} %get-tuple-element.70.sin_ref, f32[1408,1408]{1,0:T(8,128)} %fusion.1.bias_ref, ...), custom_call_target="tpu_custom_call" | custom-call | bytes 1024 | tf_op jit(solution)/shard_map/attention_backward/pallas_call | solution.py:374
  521.6 16.8 %weight_grads.5 = bf16[2304,1280]{1,0:T(8,128)(2,1)} custom-call(bf16[704,2304]{1,0:T(8,128)(2,1)} %constant_dynamic-update-slice_fusion.rows_ref.refs_0_, bf16[704,2304]{1,0:T(8,128)(2,1)} %collective-permute-done.9.rows_ref.refs_1_, bf16[1408,1024]{1,0:T(8,128)(2,1)} %attention_backward.1.refs_2_, bf16[704,2304]{1,0:T(8,128)(2,1)} %copy-done.16, ...), custom_call_target="tpu_custom_call" | custom-call | bytes 1024 | tf_op jit(solution)/shard_map/weight_grads/pallas_call | solution.py:521
  544.2 18.9 %collective-permute-done.42 = bf16[288,1536]{1,0:T(8,128)(2,1)} collective-permute-done((bf16[288,1536]{1,0:T(8,128)(2,1)}, bf16[288,1536]{1,0:T(8,128)(2,1)}, u32[]{:S(2)}, u32[]{:S(2)}) %collective-permute-start.42) | collective-permute-done | bytes 884768 | tf_op jit(solution)/shard_map/ppermute | solution.py:52
  563.0 6.3 convolution_convert_fusion.2
  581.3 5.9 convert_add_fusion
  591.5 4.8 convert_add_fusion.1
  598.4 9.9 %collective-permute-done.55 = bf16[2,88,2304]{2,1,0:T(8,128)(2,1)S(1)} collective-permute-done((bf16[2,88,2304]{2,1,0:T(8,128)(2,1)S(1)}, bf16[2,88,2304]{2,1,0:T(8,128)(2,1)S(1)}, u32[]{:S(2)}, u32[]{:S(2)}) %collective-permute-start.55) | collective-permute-done | bytes 811040 | tf_op jit(solution)/shard_map/ppermute | solution.py:52
  612.9 12.7 %collective-permute-done.47 = bf16[2,88,2304]{2,1,0:T(8,128)(2,1)S(1)} collective-permute-done((bf16[2,88,2304]{2,1,0:T(8,128)(2,1)S(1)}, bf16[2,88,2304]{2,1,0:T(8,128)(2,1)S(1)}, u32[]{:S(2)}, u32[]{:S(2)}) %collective-permute-start.47) | collective-permute-done | bytes 811040 | tf_op jit(solution)/shard_map/ppermute | solution.py:52
  631.0 3.9 collective-permute-done.56
  637.2 10.8 %reduce-scatter.8.cloned.1.call-done = bf16[576,1280]{1,0:T(8,128)(2,1)} async-done(((bf16[2304,1280]{1,0:T(8,128)(2,1)}), bf16[576,1280]{1,0:T(8,128)(2,1)}) %reduce-scatter.8.cloned.1.call-update) | async-done | bytes 1474576 | tf_op jit(solution)/shard_map/reduce_scatter | solution.py:677
  661.1 3.0 collective-permute-start.64
  666.6 6.0 collective-permute-done.59
  (362 shorter events, 172.2 us)
Async XLA Ops:
  7.2 125.3 %all-gather.9.cloned.1.call-start = ((), (), s32[]{:S(2)}) async-start(), calls=%async_computation.8 | async-start | bytes 3686400 | tf_op jit(solution)/shard_map/all_gather | solution.py:634
  15.2 35.1 %collective-permute-start.3 = (bf16[288,1280]{1,0:T(8,128)(2,1)}, bf16[288,1280]{1,0:T(8,128)(2,1)}, u32[]{:S(2)}, u32[]{:S(2)}) collective-permute-start(bf16[288,1280]{1,0:T(8,128)(2,1)} %get-tuple-element.147), channel_id=1, source_target_pairs={{0,8},{8,0},{16,24},{24,16},{1,9},{9,1},{17,25},{25,17},{2,10},{10... | collective-permute-start | bytes 2211848 | tf_op jit(solution)/shard_map/ppermute | solution.py:619
  18.2 53.5 %collective-permute-start.4 = (bf16[288,1280]{1,0:T(8,128)(2,1)}, bf16[288,1280]{1,0:T(8,128)(2,1)}, u32[]{:S(2)}, u32[]{:S(2)}) collective-permute-start(bf16[288,1280]{1,0:T(8,128)(2,1)} %get-tuple-element.147), channel_id=1, source_target_pairs={{0,16},{8,24},{16,0},{24,8},{1,17},{9,25},{17,1},{25,9},{2,18},{10... | collective-permute-start | bytes 2211848 | tf_op jit(solution)/shard_map/ppermute | solution.py:619
  20.8 65.4 %collective-permute-start.7 = (bf16[288,1280]{1,0:T(8,128)(2,1)}, bf16[288,1280]{1,0:T(8,128)(2,1)}, u32[]{:S(2)}, u32[]{:S(2)}) collective-permute-start(bf16[288,1280]{1,0:T(8,128)(2,1)} %get-tuple-element.147), channel_id=1, source_target_pairs={{0,24},{8,16},{16,8},{24,0},{1,25},{9,17},{17,9},{25,1},{2,26},{10... | collective-permute-start | bytes 2211848 | tf_op jit(solution)/shard_map/ppermute | solution.py:619
  20.8 17.9 %collective-permute-start = (bf16[288,1280]{1,0:T(8,128)(2,1)}, bf16[288,1280]{1,0:T(8,128)(2,1)S(1)}, u32[]{:S(2)}, u32[]{:S(2)}) collective-permute-start(bf16[288,1280]{1,0:T(8,128)(2,1)} %get-tuple-element.148), channel_id=1, source_target_pairs={{0,4},{4,0},{1,5},{5,1},{2,6},{6,2},{3,7},{7,3},{8,12},{12,8},{9,1... | collective-permute-start | bytes 2211848 | tf_op jit(solution)/shard_map/ppermute | solution.py:52
  38.7 33.1 %collective-permute-start.1 = (bf16[176,2304]{1,0:T(8,128)(2,1)S(1)}, bf16[176,2304]{1,0:T(8,128)(2,1)}, u32[]{:S(2)}, u32[]{:S(2)}) collective-permute-start(bf16[176,2304]{1,0:T(8,128)(2,1)S(1)} %fusion.10), channel_id=1, source_target_pairs={{0,4},{4,0},{1,5},{5,1},{2,6},{6,2},{3,7},{7,3},{8,12},{12,8},{9,1... | collective-permute-start | bytes 2433032 | tf_op jit(solution)/shard_map/ppermute | solution.py:52
  40.1 31.6 %collective-permute-start.2 = (bf16[176,2304]{1,0:T(8,128)(2,1)S(1)}, bf16[176,2304]{1,0:T(8,128)(2,1)}, u32[]{:S(2)}, u32[]{:S(2)}) collective-permute-start(bf16[176,2304]{1,0:T(8,128)(2,1)S(1)} %fusion.10), channel_id=1, source_target_pairs={{0,2},{2,0},{1,3},{3,1},{4,6},{6,4},{5,7},{7,5},{8,10},{10,8},{9,1... | collective-permute-start | bytes 2433032 | tf_op jit(solution)/shard_map/ppermute | solution.py:56
  45.3 229.3 %all-gather.5.cloned.1.call-start = ((), (), s32[]{:S(2)}) async-start(), calls=%async_computation.3 | async-start | bytes 8847360 | tf_op jit(solution)/shard_map/all_gather | solution.py:641
  87.0 15.3 %collective-permute-start.8 = (bf16[288,1536]{1,0:T(8,128)(2,1)S(1)}, bf16[288,1536]{1,0:T(8,128)(2,1)S(1)}, u32[]{:S(2)}, u32[]{:S(2)}) collective-permute-start(bf16[288,1536]{1,0:T(8,128)(2,1)S(1)} %pad_maximum_fusion.2), channel_id=1, source_target_pairs={{0,4},{4,0},{1,5},{5,1},{2,6},{6,2},{3,7},{7,3},{8,12},{12,8},{9,1... | collective-permute-start | bytes 2654216 | tf_op jit(solution)/shard_map/ppermute | solution.py:52
  132.5 210.6 %all-gather.7.cloned.1.call-start = ((), (), s32[]{:S(2)}) async-start(), calls=%async_computation.4 | async-start | bytes 4423680 | tf_op jit(solution)/shard_map/all_gather | solution.py:653
  132.8 14.3 %collective-permute-start.9 = (bf16[704,2304]{1,0:T(8,128)(2,1)}, bf16[704,2304]{1,0:T(8,128)(2,1)}, u32[]{:S(2)}, u32[]{:S(2)}) collective-permute-start(bf16[704,2304]{1,0:T(8,128)(2,1)} %constant_dynamic-update-slice_fusion.rows_ref.refs_0_), channel_id=1, source_target_pairs={{0,1},{1,0},{2,3},{3,2},{4,5},{5,4},{6,7},{7,6},{8,9},{9,8},{10,11... | collective-permute-start | bytes 9732104 | tf_op jit(solution)/shard_map/ppermute | solution.py:64
  156.6 34.9 %collective-permute-start.21 = (bf16[176,2304]{1,0:T(8,128)(2,1)}, bf16[176,2304]{1,0:T(8,128)(2,1)}, u32[]{:S(2)}, u32[]{:S(2)}) collective-permute-start(bf16[176,2304]{1,0:T(8,128)(2,1)} %get-tuple-element.116), channel_id=1, source_target_pairs={{0,4},{4,0},{1,5},{5,1},{2,6},{6,2},{3,7},{7,3},{8,12},{12,8},{9,1... | collective-permute-start | bytes 2433032 | tf_op jit(solution)/shard_map/ppermute | solution.py:52
  158.4 29.2 %collective-permute-start.25 = (bf16[288,768]{1,0:T(8,128)(2,1)S(1)}, bf16[288,768]{1,0:T(8,128)(2,1)S(1)}, u32[]{:S(2)}, u32[]{:S(2)}) collective-permute-start(bf16[288,768]{1,0:T(8,128)(2,1)S(1)} %get-tuple-element.150), channel_id=1, source_target_pairs={{0,4},{4,0},{1,5},{5,1},{2,6},{6,2},{3,7},{7,3},{8,12},{12,8},{9,1... | collective-permute-start | bytes 1327112 | tf_op jit(solution)/shard_map/ppermute | solution.py:52
  191.5 232.0 %reduce-scatter.4.cloned.1.call-start = ((), (), s32[]{:S(2)}) async-start(), calls=%async_computation.5 | async-start | bytes 4423680 | tf_op jit(solution)/shard_map/reduce_scatter | solution.py:659
  191.5 21.2 %collective-permute-start.20 = (bf16[176,2304]{1,0:T(8,128)(2,1)}, bf16[176,2304]{1,0:T(8,128)(2,1)S(1)}, u32[]{:S(2)}, u32[]{:S(2)}) collective-permute-start(bf16[176,2304]{1,0:T(8,128)(2,1)} %get-tuple-element.116), channel_id=1, source_target_pairs={{0,2},{2,0},{1,3},{3,1},{4,6},{6,4},{5,7},{7,5},{8,10},{10,8},{9,1... | collective-permute-start | bytes 2433032 | tf_op jit(solution)/shard_map/ppermute | solution.py:56
  194.3 27.1 %collective-permute-start.22 = (bf16[88,2304]{1,0:T(8,128)(2,1)S(1)}, bf16[88,2304]{1,0:T(8,128)(2,1)S(1)}, u32[]{:S(2)}, u32[]{:S(2)}) collective-permute-start(bf16[88,2304]{1,0:T(8,128)(2,1)S(1)} %slice.494), channel_id=1, source_target_pairs={{0,2},{2,0},{1,3},{3,1},{4,6},{6,4},{5,7},{7,5},{8,10},{10,8},{9,1... | collective-permute-start | bytes 1216520 | tf_op jit(solution)/shard_map/ppermute | solution.py:56
  212.8 12.4 %collective-permute-start.23 = (bf16[88,2304]{1,0:T(8,128)(2,1)S(1)}, bf16[88,2304]{1,0:T(8,128)(2,1)S(1)}, u32[]{:S(2)}, u32[]{:S(2)}) collective-permute-start(bf16[88,2304]{1,0:T(8,128)(2,1)S(1)} %slice.495), channel_id=1, source_target_pairs={{0,4},{4,0},{1,5},{5,1},{2,6},{6,2},{3,7},{7,3},{8,12},{12,8},{9,1... | collective-permute-start | bytes 1216520 | tf_op jit(solution)/shard_map/ppermute | solution.py:52
  213.2 26.6 %collective-permute-start.14 = (bf16[2,88,2304]{2,1,0:T(8,128)(2,1)S(1)}, bf16[2,88,2304]{2,1,0:T(8,128)(2,1)S(1)}, u32[]{:S(2)}, u32[]{:S(2)}) collective-permute-start(bf16[2,88,2304]{2,1,0:T(8,128)(2,1)S(1)} %slice_bitcast_fusion.22), channel_id=1, source_target_pairs={{0,4},{4,0},{1,5},{5,1},{2,6},{6,2},{3,7},{7,3},{8,12},{12,8},{9,1... | collective-permute-start | bytes 2433032 | tf_op jit(solution)/shard_map/ppermute | solution.py:52
  214.9 25.0 %collective-permute-start.16 = (bf16[2,88,2304]{2,1,0:T(8,128)(2,1)S(1)}, bf16[2,88,2304]{2,1,0:T(8,128)(2,1)S(1)}, u32[]{:S(2)}, u32[]{:S(2)}) collective-permute-start(bf16[2,88,2304]{2,1,0:T(8,128)(2,1)S(1)} %slice_bitcast_fusion.20), channel_id=1, source_target_pairs={{0,2},{2,0},{1,3},{3,1},{4,6},{6,4},{5,7},{7,5},{8,10},{10,8},{9,1... | collective-permute-start | bytes 2433032 | tf_op jit(solution)/shard_map/ppermute | solution.py:56
  225.2 31.3 %collective-permute-start.24 = (bf16[704,2304]{1,0:T(8,128)(2,1)S(1)}, bf16[704,2304]{1,0:T(8,128)(2,1)S(1)}, u32[]{:S(2)}, u32[]{:S(2)}) collective-permute-start(bf16[704,2304]{1,0:T(8,128)(2,1)S(1)} %get-tuple-element.174.refs_0_), channel_id=1, source_target_pairs={{0,1},{1,0},{2,3},{3,2},{4,5},{5,4},{6,7},{7,6},{8,9},{9,8},{10,11... | collective-permute-start | bytes 9732104 | tf_op jit(solution)/shard_map/ppermute | solution.py:64
  253.2 20.5 %collective-permute-start.18 = (bf16[176,2304]{1,0:T(8,128)(2,1)S(1)}, bf16[176,2304]{1,0:T(8,128)(2,1)S(1)}, u32[]{:S(2)}, u32[]{:S(2)}) collective-permute-start(bf16[176,2304]{1,0:T(8,128)(2,1)S(1)} %get-tuple-element.114), channel_id=1, source_target_pairs={{0,4},{4,0},{1,5},{5,1},{2,6},{6,2},{3,7},{7,3},{8,12},{12,8},{9,1... | collective-permute-start | bytes 2433032 | tf_op jit(solution)/shard_map/ppermute | solution.py:52
  254.2 20.4 %collective-permute-start.19 = (bf16[176,2304]{1,0:T(8,128)(2,1)S(1)}, bf16[176,2304]{1,0:T(8,128)(2,1)}, u32[]{:S(2)}, u32[]{:S(2)}) collective-permute-start(bf16[176,2304]{1,0:T(8,128)(2,1)S(1)} %get-tuple-element.114), channel_id=1, source_target_pairs={{0,2},{2,0},{1,3},{3,1},{4,6},{6,4},{5,7},{7,5},{8,10},{10,8},{9,1... | collective-permute-start | bytes 2433032 | tf_op jit(solution)/shard_map/ppermute | solution.py:56
  275.7 25.6 %collective-permute-start.27 = (bf16[176,2304]{1,0:T(8,128)(2,1)}, bf16[176,2304]{1,0:T(8,128)(2,1)S(1)}, u32[]{:S(2)}, u32[]{:S(2)}) collective-permute-start(bf16[176,2304]{1,0:T(8,128)(2,1)} %collective-permute-done.19), channel_id=1, source_target_pairs={{0,1},{1,0},{2,3},{3,2},{4,5},{5,4},{6,7},{7,6},{8,9},{9,8},{10,11... | collective-permute-start | bytes 2433032 | tf_op jit(solution)/shard_map/ppermute | solution.py:64
  276.8 24.6 %collective-permute-start.28 = (bf16[176,2304]{1,0:T(8,128)(2,1)}, bf16[176,2304]{1,0:T(8,128)(2,1)S(1)}, u32[]{:S(2)}, u32[]{:S(2)}) collective-permute-start(bf16[176,2304]{1,0:T(8,128)(2,1)} %copy-done.24), channel_id=1, source_target_pairs={{0,1},{1,0},{2,3},{3,2},{4,5},{5,4},{6,7},{7,6},{8,9},{9,8},{10,11... | collective-permute-start | bytes 2433032 | tf_op jit(solution)/shard_map/ppermute | solution.py:64
  277.3 11.4 %collective-permute-start.29 = (bf16[88,2304]{1,0:T(8,128)(2,1)S(1)}, bf16[88,2304]{1,0:T(8,128)(2,1)S(1)}, u32[]{:S(2)}, u32[]{:S(2)}) collective-permute-start(bf16[88,2304]{1,0:T(8,128)(2,1)S(1)} %slice.405), channel_id=1, source_target_pairs={{0,2},{2,0},{1,3},{3,1},{4,6},{6,4},{5,7},{7,5},{8,10},{10,8},{9,1... | collective-permute-start | bytes 1216520 | tf_op jit(solution)/shard_map/ppermute | solution.py:56
  277.9 11.1 %collective-permute-start.30 = (bf16[88,2304]{1,0:T(8,128)(2,1)S(1)}, bf16[88,2304]{1,0:T(8,128)(2,1)S(1)}, u32[]{:S(2)}, u32[]{:S(2)}) collective-permute-start(bf16[88,2304]{1,0:T(8,128)(2,1)S(1)} %slice.406), channel_id=1, source_target_pairs={{0,4},{4,0},{1,5},{5,1},{2,6},{6,2},{3,7},{7,3},{8,12},{12,8},{9,1... | collective-permute-start | bytes 1216520 | tf_op jit(solution)/shard_map/ppermute | solution.py:52
  289.0 12.4 %collective-permute-start.31 = (bf16[176,2304]{1,0:T(8,128)(2,1)S(1)}, bf16[176,2304]{1,0:T(8,128)(2,1)S(1)}, u32[]{:S(2)}, u32[]{:S(2)}) collective-permute-start(bf16[176,2304]{1,0:T(8,128)(2,1)S(1)} %pad_maximum_fusion.3), channel_id=1, source_target_pairs={{0,1},{1,0},{2,3},{3,2},{4,5},{5,4},{6,7},{7,6},{8,9},{9,8},{10,11... | collective-permute-start | bytes 2433032 | tf_op jit(solution)/shard_map/ppermute | solution.py:64
  325.5 213.0 %reduce-scatter.6.cloned.1.call-start = ((), (), s32[]{:S(2)}) async-start(), calls=%async_computation.6 | async-start | bytes 8847360 | tf_op jit(solution)/shard_map/reduce_scatter | solution.py:663
  383.2 264.8 %reduce-scatter.8.cloned.1.call-start = ((), (), s32[]{:S(2)}) async-start(), calls=%async_computation.7 | async-start | bytes 7372800 | tf_op jit(solution)/shard_map/reduce_scatter | solution.py:677
  398.7 20.2 %collective-permute-start.33 = (bf16[2,88,2304]{2,1,0:T(8,128)(2,1)S(1)}, bf16[2,88,2304]{2,1,0:T(8,128)(2,1)S(1)}, u32[]{:S(2)}, u32[]{:S(2)}) collective-permute-start(bf16[2,88,2304]{2,1,0:T(8,128)(2,1)S(1)} %slice_bitcast_fusion.18), channel_id=1, source_target_pairs={{0,4},{4,0},{1,5},{5,1},{2,6},{6,2},{3,7},{7,3},{8,12},{12,8},{9,1... | collective-permute-start | bytes 2433032 | tf_op jit(solution)/shard_map/ppermute | solution.py:52
  400.5 19.8 %collective-permute-start.35 = (bf16[2,88,2304]{2,1,0:T(8,128)(2,1)S(1)}, bf16[2,88,2304]{2,1,0:T(8,128)(2,1)S(1)}, u32[]{:S(2)}, u32[]{:S(2)}) collective-permute-start(bf16[2,88,2304]{2,1,0:T(8,128)(2,1)S(1)} %slice_bitcast_fusion.17), channel_id=1, source_target_pairs={{0,2},{2,0},{1,3},{3,1},{4,6},{6,4},{5,7},{7,5},{8,10},{10,8},{9,1... | collective-permute-start | bytes 2433032 | tf_op jit(solution)/shard_map/ppermute | solution.py:56
  438.7 18.1 %collective-permute-start.38 = (bf16[176,2304]{1,0:T(8,128)(2,1)S(1)}, bf16[176,2304]{1,0:T(8,128)(2,1)S(1)}, u32[]{:S(2)}, u32[]{:S(2)}) collective-permute-start(bf16[176,2304]{1,0:T(8,128)(2,1)S(1)} %get-tuple-element.111), channel_id=1, source_target_pairs={{0,4},{4,0},{1,5},{5,1},{2,6},{6,2},{3,7},{7,3},{8,12},{12,8},{9,1... | collective-permute-start | bytes 2433032 | tf_op jit(solution)/shard_map/ppermute | solution.py:52
  440.1 18.4 %collective-permute-start.37 = (bf16[176,2304]{1,0:T(8,128)(2,1)S(1)}, bf16[176,2304]{1,0:T(8,128)(2,1)S(1)}, u32[]{:S(2)}, u32[]{:S(2)}) collective-permute-start(bf16[176,2304]{1,0:T(8,128)(2,1)S(1)} %get-tuple-element.111), channel_id=1, source_target_pairs={{0,2},{2,0},{1,3},{3,1},{4,6},{6,4},{5,7},{7,5},{8,10},{10,8},{9,1... | collective-permute-start | bytes 2433032 | tf_op jit(solution)/shard_map/ppermute | solution.py:56
  467.8 73.3 %collective-permute-start.65 = (bf16[288,768]{1,0:T(8,128)(2,1)}, bf16[288,768]{1,0:T(8,128)(2,1)}, u32[]{:S(2)}, u32[]{:S(2)}) collective-permute-start(bf16[288,768]{1,0:T(8,128)(2,1)} %get-tuple-element.156), channel_id=1, source_target_pairs={{0,4},{4,0},{1,5},{5,1},{2,6},{6,2},{3,7},{7,3},{8,12},{12,8},{9,1... | collective-permute-start | bytes 1327112 | tf_op jit(solution)/shard_map/ppermute | solution.py:52
  541.0 22.1 %collective-permute-start.42 = (bf16[288,1536]{1,0:T(8,128)(2,1)}, bf16[288,1536]{1,0:T(8,128)(2,1)}, u32[]{:S(2)}, u32[]{:S(2)}) collective-permute-start(bf16[288,1536]{1,0:T(8,128)(2,1)} %get-tuple-element.140), channel_id=1, source_target_pairs={{0,4},{4,0},{1,5},{5,1},{2,6},{6,2},{3,7},{7,3},{8,12},{12,8},{9,1... | collective-permute-start | bytes 2654216 | tf_op jit(solution)/shard_map/ppermute | solution.py:52
  569.7 11.1 %collective-permute-start.52 = (bf16[176,2304]{1,0:T(8,128)(2,1)S(1)}, bf16[176,2304]{1,0:T(8,128)(2,1)S(1)}, u32[]{:S(2)}, u32[]{:S(2)}) collective-permute-start(bf16[176,2304]{1,0:T(8,128)(2,1)S(1)} %get-tuple-element.130), channel_id=1, source_target_pairs={{0,1},{1,0},{2,3},{3,2},{4,5},{5,4},{6,7},{7,6},{8,9},{9,8},{10,11... | collective-permute-start | bytes 2433032 | tf_op jit(solution)/shard_map/ppermute | solution.py:64
  570.2 10.6 %collective-permute-start.53 = (bf16[176,2304]{1,0:T(8,128)(2,1)S(1)}, bf16[176,2304]{1,0:T(8,128)(2,1)S(1)}, u32[]{:S(2)}, u32[]{:S(2)}) collective-permute-start(bf16[176,2304]{1,0:T(8,128)(2,1)S(1)} %get-tuple-element.129), channel_id=1, source_target_pairs={{0,1},{1,0},{2,3},{3,2},{4,5},{5,4},{6,7},{7,6},{8,9},{9,8},{10,11... | collective-permute-start | bytes 2433032 | tf_op jit(solution)/shard_map/ppermute | solution.py:64
  570.3 11.0 %collective-permute-start.54 = (bf16[176,2304]{1,0:T(8,128)(2,1)S(1)}, bf16[176,2304]{1,0:T(8,128)(2,1)S(1)}, u32[]{:S(2)}, u32[]{:S(2)}) collective-permute-start(bf16[176,2304]{1,0:T(8,128)(2,1)S(1)} %get-tuple-element.128), channel_id=1, source_target_pairs={{0,1},{1,0},{2,3},{3,2},{4,5},{5,4},{6,7},{7,6},{8,9},{9,8},{10,11... | collective-permute-start | bytes 2433032 | tf_op jit(solution)/shard_map/ppermute | solution.py:64
  575.2 12.6 %collective-permute-start.43 = (bf16[176,2304]{1,0:T(8,128)(2,1)S(1)}, bf16[176,2304]{1,0:T(8,128)(2,1)S(1)}, u32[]{:S(2)}, u32[]{:S(2)}) collective-permute-start(bf16[176,2304]{1,0:T(8,128)(2,1)S(1)} %get-tuple-element.131), channel_id=1, source_target_pairs={{0,1},{1,0},{2,3},{3,2},{4,5},{5,4},{6,7},{7,6},{8,9},{9,8},{10,11... | collective-permute-start | bytes 2433032 | tf_op jit(solution)/shard_map/ppermute | solution.py:64
  587.3 21.0 %collective-permute-start.55 = (bf16[2,88,2304]{2,1,0:T(8,128)(2,1)S(1)}, bf16[2,88,2304]{2,1,0:T(8,128)(2,1)S(1)}, u32[]{:S(2)}, u32[]{:S(2)}) collective-permute-start(bf16[2,88,2304]{2,1,0:T(8,128)(2,1)S(1)} %slice_bitcast_fusion.11), channel_id=1, source_target_pairs={{0,4},{4,0},{1,5},{5,1},{2,6},{6,2},{3,7},{7,3},{8,12},{12,8},{9,1... | collective-permute-start | bytes 2433032 | tf_op jit(solution)/shard_map/ppermute | solution.py:52
  587.8 21.0 %collective-permute-start.57 = (bf16[2,88,2304]{2,1,0:T(8,128)(2,1)S(1)}, bf16[2,88,2304]{2,1,0:T(8,128)(2,1)S(1)}, u32[]{:S(2)}, u32[]{:S(2)}) collective-permute-start(bf16[2,88,2304]{2,1,0:T(8,128)(2,1)S(1)} %slice_bitcast_fusion.9), channel_id=1, source_target_pairs={{0,2},{2,0},{1,3},{3,1},{4,6},{6,4},{5,7},{7,5},{8,10},{10,8},{9,1... | collective-permute-start | bytes 2433032 | tf_op jit(solution)/shard_map/ppermute | solution.py:56
  596.3 29.3 %collective-permute-start.47 = (bf16[2,88,2304]{2,1,0:T(8,128)(2,1)S(1)}, bf16[2,88,2304]{2,1,0:T(8,128)(2,1)S(1)}, u32[]{:S(2)}, u32[]{:S(2)}) collective-permute-start(bf16[2,88,2304]{2,1,0:T(8,128)(2,1)S(1)} %slice_bitcast_fusion.15), channel_id=1, source_target_pairs={{0,4},{4,0},{1,5},{5,1},{2,6},{6,2},{3,7},{7,3},{8,12},{12,8},{9,1... | collective-permute-start | bytes 2433032 | tf_op jit(solution)/shard_map/ppermute | solution.py:52
  598.1 28.1 %collective-permute-start.49 = (bf16[2,88,2304]{2,1,0:T(8,128)(2,1)S(1)}, bf16[2,88,2304]{2,1,0:T(8,128)(2,1)S(1)}, u32[]{:S(2)}, u32[]{:S(2)}) collective-permute-start(bf16[2,88,2304]{2,1,0:T(8,128)(2,1)S(1)} %slice_bitcast_fusion.13), channel_id=1, source_target_pairs={{0,2},{2,0},{1,3},{3,1},{4,6},{6,4},{5,7},{7,5},{8,10},{10,8},{9,1... | collective-permute-start | bytes 2433032 | tf_op jit(solution)/shard_map/ppermute | solution.py:56
  609.3 25.6 %collective-permute-start.56 = (bf16[88,2304]{1,0:T(8,128)(2,1)S(1)}, bf16[88,2304]{1,0:T(8,128)(2,1)S(1)}, u32[]{:S(2)}, u32[]{:S(2)}) collective-permute-start(bf16[88,2304]{1,0:T(8,128)(2,1)S(1)} %fusion.55), channel_id=1, source_target_pairs={{0,2},{2,0},{1,3},{3,1},{4,6},{6,4},{5,7},{7,5},{8,10},{10,8},{9,1... | collective-permute-start | bytes 1216520 | tf_op jit(solution)/shard_map/ppermute | solution.py:56
  611.2 23.8 %collective-permute-start.58 = (bf16[88,2304]{1,0:T(8,128)(2,1)S(1)}, bf16[88,2304]{1,0:T(8,128)(2,1)S(1)}, u32[]{:S(2)}, u32[]{:S(2)}) collective-permute-start(bf16[88,2304]{1,0:T(8,128)(2,1)S(1)} %fusion.56), channel_id=1, source_target_pairs={{0,4},{4,0},{1,5},{5,1},{2,6},{6,2},{3,7},{7,3},{8,12},{12,8},{9,1... | collective-permute-start | bytes 1216520 | tf_op jit(solution)/shard_map/ppermute | solution.py:52
  627.4 20.6 %collective-permute-start.48 = (bf16[88,2304]{1,0:T(8,128)(2,1)}, bf16[88,2304]{1,0:T(8,128)(2,1)}, u32[]{:S(2)}, u32[]{:S(2)}) collective-permute-start(bf16[88,2304]{1,0:T(8,128)(2,1)} %fusion.53), channel_id=1, source_target_pairs={{0,2},{2,0},{1,3},{3,1},{4,6},{6,4},{5,7},{7,5},{8,10},{10,8},{9,1... | collective-permute-start | bytes 1216520 | tf_op jit(solution)/shard_map/ppermute | solution.py:56
  629.3 21.8 %collective-permute-start.50 = (bf16[88,2304]{1,0:T(8,128)(2,1)S(1)}, bf16[88,2304]{1,0:T(8,128)(2,1)}, u32[]{:S(2)}, u32[]{:S(2)}) collective-permute-start(bf16[88,2304]{1,0:T(8,128)(2,1)S(1)} %fusion.54), channel_id=1, source_target_pairs={{0,4},{4,0},{1,5},{5,1},{2,6},{6,2},{3,7},{7,3},{8,12},{12,8},{9,1... | collective-permute-start | bytes 1216520 | tf_op jit(solution)/shard_map/ppermute | solution.py:52
  655.0 17.6 %collective-permute-start.59 = (bf16[288,1280]{1,0:T(8,128)(2,1)S(1)}, bf16[288,1280]{1,0:T(8,128)(2,1)S(1)}, u32[]{:S(2)}, u32[]{:S(2)}) collective-permute-start(bf16[288,1280]{1,0:T(8,128)(2,1)S(1)} %get-tuple-element.146), channel_id=1, source_target_pairs={{0,4},{4,0},{1,5},{5,1},{2,6},{6,2},{3,7},{7,3},{8,12},{12,8},{9,1... | collective-permute-start | bytes 2211848 | tf_op jit(solution)/shard_map/ppermute | solution.py:52
  (73 other events, 582.1 us)
Sparse Core Ops, SparseCore 0:
  45.4 87.0 all-gather.8
  134.7 137.9 all-gather.4
  274.8 68.2 all-gather.6
  345.3 64.9 reduce-scatter.3
  412.4 123.7 reduce-scatter.5
  544.1 103.8 reduce-scatter.7

commit v4 on v3

--- a/solution.py
+++ b/solution.py
@@ -98,17 +98,17 @@
     return total if other is None else (total, other)
 
 
-def sum_all(field):
+def sum_all(field, other):
     total = flip_core(field) + field
     total = flip_y(total) + total
     total = flip_x(total) + total
     count, step = lax.axis_size("dp"), 1
-    if count & (count - 1):
-        return lax.psum(total, "dp")
     while step < count:
+        if 2 * step >= count:
+            total, other = after(total, other)
         total = lax.ppermute(total, "dp", [(i, i ^ step) for i in range(count)]) + total
         step *= 2
-    return total
+    return total, other
 
 
 def lane_mask(rows, upper):
@@ -253,16 +253,14 @@
         return dot(ones, high, NT) + dot(ones, low, NT)
 
     def score_block(count, width, keys, values, queries, d_rows, biases, lse, centre):
-        for t in range(count):
-            here = pl.ds(t * TILE, TILE)
-            probs = jnp.exp(dot(keys(t), queries, NT) + biases(t) - lse)
-            d_probs = dot(values(t), d_rows, NT)
-            d_scores = (probs * (d_probs - centre)).astype(bf16)
-            ds_ref[here, pl.ds(0, width)] = d_scores
-            dk_ref[here, :] += dot(d_scores, queries)
-            dv_ref[here, :] += dot(probs.astype(bf16), d_rows)
-        depth = count * TILE
-        return dot(kt_ref[:, pl.ds(0, depth)], ds_ref[pl.ds(0, depth), pl.ds(0, width)]) * (HEAD_DIM**-0.5)
+        here = pl.ds(0, count * TILE)
+        probs = jnp.exp(dot(keys(here), queries, NT) + biases(here) - lse)
+        d_probs = dot(values(here), d_rows, NT)
+        d_scores = (probs * (d_probs - centre)).astype(bf16)
+        ds_ref[here, pl.ds(0, width)] = d_scores
+        dk_ref[here, :] += dot(d_scores, queries)
+        dv_ref[here, :] += dot(probs.astype(bf16), d_rows)
+        return dot(kt_ref[:, here], ds_ref[here, pl.ds(0, width)]) * (HEAD_DIM**-0.5)
 
     def place(field_of, lanes, turned):
         for n in range(8):
@@ -284,16 +282,16 @@
         for i in range(tiles):
             cols = pl.ds(i * TILE, TILE)
 
-            def biases(t):
-                bias = bias_ref[pl.ds(t * TILE, TILE), cols]
+            def biases(here):
+                bias = bias_ref[here, cols]
                 return jnp.concatenate([bias, bias], axis=1)
 
             centre = jnp.concatenate([row_sums(cols, o_lanes, False), row_sums(cols, o_lanes, True)], axis=1)
             d_query = score_block(
                 i + 1,
                 2 * TILE,
-                lambda t: rot_ref[pl.ds(t * TILE, TILE), k_lanes],
-                lambda t: rot_ref[pl.ds(t * TILE, TILE), v_lanes],
+                lambda here: rot_ref[here, k_lanes],
+                lambda here: rot_ref[here, v_lanes],
                 two_heads(rot_ref[cols, q_lanes]),
                 two_heads(d_ref[cols, o_lanes]),
                 biases,
@@ -326,11 +324,11 @@
             d_query = score_block(
                 min(2 * j + 2, tiles),
                 TILE,
-                lambda t: rot_ref[pl.ds(t * TILE, TILE), k_lanes],
-                lambda t: rot_ref[pl.ds(t * TILE, TILE), v_lanes],
+                lambda here: rot_ref[here, k_lanes],
+                lambda here: rot_ref[here, v_lanes],
                 queries,
                 d_rows,
-                lambda t: bias_ref[pl.ds(t * TILE, TILE), cols],
+                lambda here: bias_ref[here, cols],
                 lse_ref[PAIRS, pl.ds(0, 1), pl.ds(j * TILE, TILE)],
                 row_sums(cols, pl.ds(0, LANES), True)[0:1],
             )
@@ -399,67 +397,93 @@
 ROOMY = pltpu.CompilerParams(vmem_limit_bytes=52 << 20)
 
 
-def gate_kernel(rows_ref, w_ref, *refs):
-    gate_up_ref, hidden_ref = refs[-2:]
-    width = hidden_ref.shape[1]
+def tail_lanes(shape, at, size):
+    lane = lax.broadcasted_iota(jnp.int32, shape, 1)
+    return (lane >= at) & (lane < at + size)
+
+
+def tail_parts(tail, size):
+    return pltpu.roll(tail, 2 * size, 1), pltpu.roll(tail, size, 1)
+
+
+def gate_kernel(size, rows_ref, w_ref, *refs):
+    gate_up_ref, main_ref, tail_ref = refs[-3:]
+    width = main_ref.shape[1]
     gate_up = dot(rows_ref[...], w_ref[...])
     gate_up_ref[...] = gate_up
-    gate, up = gate_up[:, :width], gate_up[:, width:]
-    hidden_ref[...] = (gate * jax.nn.sigmoid(gate) * up).astype(bf16)
-
-
-def gate_half(rows, gu_w, width, earlier):
+    gate, up = gate_up[:, :width], gate_up[:, width : 2 * width]
+    main_ref[...] = (gate * jax.nn.sigmoid(gate) * up).astype(bf16)
+    gate, up = tail_parts(gate_up[:, 2 * width :], size)
+    tail = gate * jax.nn.sigmoid(gate) * up
+    tail_ref[...] = jnp.where(tail_lanes(tail.shape, 2 * size, size), tail, 0.0).astype(bf16)
+
+
+def gate_half(rows, gu_w, width, size, earlier):
     count, depth = rows.shape
+    cols = gu_w.shape[1]
     tile = count // 4
     at = 4 if earlier else 0
+    widths = (cols, width, cols - 2 * width)
     return pl.pallas_call(
-        gate_kernel,
+        functools.partial(gate_kernel, size),
         grid=(4,),
-        out_shape=(
-            jax.ShapeDtypeStruct((2 * count, 2 * width), f32),
-            jax.ShapeDtypeStruct((2 * count, width), bf16),
+        out_shape=tuple(
+            jax.ShapeDtypeStruct((2 * count, w), kind) for w, kind in zip(widths, (f32, bf16, bf16))
         ),
-        in_specs=[pl.BlockSpec((tile, depth), lambda i: (i, 0)), whole((depth, 2 * width))]
+        in_specs=[pl.BlockSpec((tile, depth), lambda i: (i, 0)), whole((depth, cols))]
         + [pl.BlockSpec(memory_space=pl.ANY)] * len(earlier),
-        out_specs=(
-            pl.BlockSpec((tile, 2 * width), lambda i: (i + at, 0)),
-            pl.BlockSpec((tile, width), lambda i: (i + at, 0)),
-        ),
-        input_output_aliases={2: 0, 3: 1} if earlier else {},
+        out_specs=tuple(pl.BlockSpec((tile, w), lambda i: (i + at, 0)) for w in widths),
+        input_output_aliases={2: 0, 3: 1, 4: 2} if earlier else {},
         compiler_params=ROOMY,
         cost_estimate=FREE,
         name="gate_half",
     )(rows, gu_w, *earlier)
 
 
-def hidden_back_kernel(rows_ref, w_ref, gate_up_ref, out_ref):
-    width = w_ref.shape[1]
-    d_hidden = dot(rows_ref[...], w_ref[...])
-    gate, up = gate_up_ref[:, :width], gate_up_ref[:, width:]
+def gate_back(d_hidden, gate, up):
     sigmoid_gate = jax.nn.sigmoid(gate)
     d_gate = d_hidden * up * sigmoid_gate * (1.0 + gate * (1.0 - sigmoid_gate))
+    return d_gate, d_hidden * (gate * sigmoid_gate)
+
+
+def hidden_back_kernel(size, rows_ref, w_ref, tail_w_ref, gate_up_ref, out_ref):
+    width = w_ref.shape[1]
+    rows = rows_ref[...]
+    d_gate, d_up = gate_back(
+        dot(rows, w_ref[...]), gate_up_ref[:, :width], gate_up_ref[:, width : 2 * width]
+    )
     out_ref[:, :width] = d_gate.astype(bf16)
-    out_ref[:, width:] = (d_hidden * (gate * sigmoid_gate)).astype(bf16)
-
-
-def hidden_back(rows, down_w, gate_up):
+    out_ref[:, width : 2 * width] = d_up.astype(bf16)
+    gate, up = tail_parts(gate_up_ref[:, 2 * width :], size)
+    d_gate, d_up = gate_back(dot(rows, tail_w_ref[...]), gate, up)
+    lanes = d_gate.shape[1]
+    d_gate = pltpu.roll(d_gate, lanes - 2 * size, 1)
+    d_up = pltpu.roll(d_up, lanes - size, 1)
+    tail = jnp.where(tail_lanes(d_up.shape, size, size), d_up, 0.0)
+    tail = jnp.where(tail_lanes(d_up.shape, 0, size), d_gate, tail)
+    out_ref[:, 2 * width :] = tail.astype(bf16)
+
+
+def hidden_back(rows, down_w, gu_w, gate_up, size):
     count, depth = rows.shape
-    width = gate_up.shape[1] // 2
-    tile = count // 8
+    width, cols = down_w.shape[1], gate_up.shape[1]
+    tail = cols - 2 * width
+    tile = count // 4
     return pl.pallas_call(
-        hidden_back_kernel,
-        grid=(8,),
-        out_shape=jax.ShapeDtypeStruct((count, 2 * width), bf16),
+        functools.partial(hidden_back_kernel, size),
+        grid=(4,),
+        out_shape=jax.ShapeDtypeStruct((count, cols), bf16),
         in_specs=[
             pl.BlockSpec((tile, depth), lambda i: (i, 0)),
             whole((depth, width)),
-            pl.BlockSpec((tile, 2 * width), lambda i: (i, 0)),
+            pl.BlockSpec((depth, tail), lambda i: (0, 2 * width // tail), pipeline_mode=pl.Buffered(1)),
+            pl.BlockSpec((tile, cols), lambda i: (i, 0)),
         ],
-        out_specs=pl.BlockSpec((tile, 2 * width), lambda i: (i, 0)),
+        out_specs=pl.BlockSpec((tile, cols), lambda i: (i, 0)),
         compiler_params=ROOMY,
         cost_estimate=FREE,
         name="hidden_back",
-    )(rows, down_w, gate_up)
+    )(rows, down_w, gu_w, gate_up)
 
 
 def rows_kernel(rows_ref, w_ref, *refs):
@@ -501,6 +525,12 @@
     out_ref[...] = product.astype(bf16)
 
 
+def place_tail(out_ref, first, second):
+    start = first.shape[1] - second.shape[1]
+    out_ref[:, :start] = first[:, :start].astype(bf16)
+    out_ref[:, start:] = (first[:, start:] + second).astype(bf16)
+
+
 def place_heads(out_ref, first, second):
     start = first.shape[1] - LANES
     out_ref[:, :start] = first[:, :start].astype(bf16)
@@ -508,22 +538,22 @@
     out_ref[:, start + LANES :] = second[:, LANES:].astype(bf16)
 
 
-def weight_grads(place, cols, *triples):
+def weight_grads(place, cols, tile, *triples):
     depth = triples[0][0].shape[1]
     specs, operands = [], []
     for near, far, right in triples:
         specs += [
-            pl.BlockSpec((near.shape[0], 2 * LANES), lambda i: (0, i)),
-            pl.BlockSpec((far.shape[0], 2 * LANES), lambda i: (0, i)),
+            pl.BlockSpec((near.shape[0], tile), lambda i: (0, i)),
+            pl.BlockSpec((far.shape[0], tile), lambda i: (0, i)),
             whole(right.shape),
         ]
         operands += [near, far, right]
     return pl.pallas_call(
         functools.partial(grads_kernel, place),
-        grid=(depth // (2 * LANES),),
+        grid=(depth // tile,),
         out_shape=jax.ShapeDtypeStruct((depth, cols), bf16),
         in_specs=specs,
-        out_specs=pl.BlockSpec((2 * LANES, cols), lambda i: (i, 0)),
+        out_specs=pl.BlockSpec((tile, cols), lambda i: (i, 0)),
         compiler_params=ROOMY,
         cost_estimate=FREE,
         name="weight_grads",
@@ -553,7 +583,8 @@
     heads = w_query.shape[1] // HEAD_DIM
     own_cols = heads // 2 * HEAD_DIM
     ff_half = w_gate.shape[1] // 2
-    ff_pad = -(-ff_half // LANES) * LANES
+    ff_main = ff_half // LANES * LANES
+    ff_tail = ff_half - ff_main
 
     info, back = [], []
     for n in range(8):
@@ -584,9 +615,13 @@
     attn_mine, attn_theirs = jnp.where(lower_x, attn_a, attn_b), jnp.where(lower_x, attn_b, attn_a)
 
     def halves(weight):
-        fill = ((0, 0), (0, ff_pad - ff_half))
-        first, second = jnp.pad(weight[:, :ff_half], fill), jnp.pad(weight[:, ff_half:], fill)
+        first, second = weight[:, :ff_half], weight[:, ff_half:]
         return jnp.where(lower_x, first, second), jnp.where(lower_x, second, first)
+
+    def pack_hidden(gate, up, down):
+        fill = jnp.zeros((gate.shape[0], 2 * LANES - 3 * ff_tail), bf16)
+        tails = [w[:, ff_main:] for w in (gate, up, down)]
+        return jnp.concatenate([gate[:, :ff_main], up[:, :ff_main]] + tails + [fill], axis=1)
 
     index = jnp.arange(slot, dtype=jnp.int32)
     own_seg = lineage[0]
@@ -621,11 +656,12 @@
     arrived = [from_dp(attn_mine, k) for k in range(1, count)]
     _, own_rows = after(attn_got, (normalize(inputs) * gain_a).astype(bf16))
     near_a, arrived[:2] = gather_near(own_rows, arrived[:2])
-    near_a, arrived[2:], w_gate, w_up = after(near_a, arrived[2:], w_gate, w_up)
+    near_a, arrived[2:], w_gate, w_up, w_down = after(near_a, arrived[2:], w_gate, w_up, w_down)
     gate_mine, gate_theirs = halves(w_gate)
     up_mine, up_theirs = halves(w_up)
+    down_mine, down_theirs = halves(w_down.T)
     gu_part = both_x(
-        jnp.concatenate([gate_mine, up_mine], 1), jnp.concatenate([gate_theirs, up_theirs], 1)
+        pack_hidden(gate_mine, up_mine, down_mine), pack_hidden(gate_theirs, up_theirs, down_theirs)
     )
     block = (1, 1) + attn_mine.shape
     attn_w = jnp.zeros((count, 2) + attn_mine.shape, bf16)
@@ -642,23 +678,32 @@
     qkv_w = attn_w[:, : 8 * LANES]
     out_w = attn_w[:, 7 * LANES :]
     qkv = project_half(far_a, attn_w, 8 * LANES, project_half(near_a, attn_w, 8 * LANES, None))
-    qkv, w_down, grad_rows = after(qkv, w_down, grad_rows)
+    qkv, down_mine, down_theirs, grad_rows = after(
+        qkv, down_mine[:, :ff_main], down_theirs[:, :ff_main], grad_rows
+    )
     near_d, far_d = gather_rows((branch_scale * grad_rows).astype(bf16))
     d_mlp = jnp.concatenate([near_d, far_d], axis=0)
-    down_mine, down_theirs = halves(w_down.T)
     down_part = both_x(down_mine, down_theirs)
     rotated, mixed, log_total = attention_forward(info, qkv, cosine, sine, bias)
     residual = inputs + branch_scale * sum_rows(mixed, out_w, NT, pieces=4)
-    near_m, (gu_w, d_mlp) = gather_near((normalize(residual) * gain_m).astype(bf16), (gu_w, d_mlp))
+    own_m, gu_w, d_mlp = after((normalize(residual) * gain_m).astype(bf16), gu_w, d_mlp)
+    near_m = gather_near(own_m)
     down_w = lax.all_gather(down_part, "dp", axis=0, tiled=True)
     far_m = flip_core(near_m, 4)
-    gate_up, hidden = gate_half(far_m, gu_w, ff_pad, gate_half(near_m, gu_w, ff_pad, ()))
-
-    grad_down = weight_grads(place_one, ff_pad, (near_d, far_d, hidden))
+    earlier = gate_half(near_m, gu_w, ff_main, ff_tail, ())
+    gate_up, hidden, hidden_tail = gate_half(far_m, gu_w, ff_main, ff_tail, earlier)
+
+    grad_down = weight_grads(place_one, ff_main, 6 * LANES, (near_d, far_d, hidden))
     gate_up, grad_down = after(gate_up, grad_down)
     grad_down = lax.psum_scatter(grad_down, "dp", scatter_dimension=0, tiled=True)
-    d_gate_up = hidden_back(d_mlp, down_w, gate_up)
-    grad_gu = weight_grads(place_one, 2 * ff_pad, (near_m, far_m, d_gate_up))
+    d_gate_up = hidden_back(d_mlp, down_w, gu_w, gate_up, ff_tail)
+    grad_gu = weight_grads(
+        place_tail,
+        gate_up.shape[1],
+        3 * LANES,
+        (near_m, far_m, d_gate_up),
+        (near_d, far_d, hidden_tail),
+    )
     d_gate_up, grad_gu = after(d_gate_up, grad_gu)
     grad_gu = lax.psum_scatter(grad_gu, "dp", scatter_dimension=0, tiled=True)
     d_normed_mlp, grad_down = sum_rows(d_gate_up, gu_w, NT, grad_down)
@@ -671,17 +716,19 @@
         info, rotated, cosine, sine, bias, mixed, d_mixed_near, d_mixed_far, log_total
     )
     grad_attn = weight_grads(
-        place_heads, 10 * LANES, (near_a, far_a, d_qkv), (near_o, far_o, mixed)
+        place_heads, 10 * LANES, 3 * LANES, (near_a, far_a, d_qkv), (near_o, far_o, mixed)
     )
     grad_attn, grad_gu, d_qkv, hidden = after(grad_attn, grad_gu, d_qkv, hidden)
     grad_attn = lax.psum_scatter(grad_attn, "dp", scatter_dimension=0, tiled=True)
-    gu_mine, gu_got = rows_of_x(grad_gu)
-    gu_got, d_qkv, hidden = after(gu_got, d_qkv, hidden)
+    tail_mine, tail_got = rows_of_x(grad_gu[:, 2 * ff_main :])
+    tail_got, d_qkv, hidden = after(tail_got, d_qkv, hidden)
+    gu_mine, gu_got = rows_of_x(grad_gu[:, : 2 * ff_main])
     d_normed_attn = sum_rows(d_qkv, qkv_w, NT, pieces=4)
     back_attn, gain_attn_part = norm_back(inputs, gain_a, d_normed_attn)
     input_grad = d_residual + back_attn
-    gains, grad_attn = after(jnp.stack([gain_attn_part, gain_mlp_part]), grad_attn)
-    gains = sum_all(gains)
+    gains, grad_attn = sum_all(jnp.stack([gain_attn_part, gain_mlp_part]), grad_attn)
+    hidden = jnp.concatenate([hidden, hidden_tail], axis=1)
+    down_w = jnp.concatenate([down_w, gu_w[:, 2 * ff_main :]], axis=1)
     output = residual + branch_scale * sum_rows(hidden, down_w, NT, pieces=4)
 
     def join(mine, got):
@@ -693,11 +740,17 @@
         last = slice(shared_at, shared_at + HEAD_DIM)
         return jnp.concatenate([whole, mine[:, last].astype(f32) + got[:, last].astype(f32)], axis=1)
 
-    mine, got = gu_mine, gu_got
-    grad_gate = join(mine[:, :ff_half], got[:, :ff_half])
-    grad_up = join(mine[:, ff_pad : ff_pad + ff_half], got[:, ff_pad : ff_pad + ff_half])
-    mine, got = rows_of_x(grad_down)
-    grad_down = join(mine[:, :ff_half], got[:, :ff_half]).T
+    down_mine, down_got = rows_of_x(grad_down)
+
+    def join_hidden(mine, got, at):
+        last = slice(at * ff_tail, (at + 1) * ff_tail)
+        mine = jnp.concatenate([mine, tail_mine[:, last]], axis=1)
+        return join(mine, jnp.concatenate([got, tail_got[:, last]], axis=1))
+
+    grad_gate = join_hidden(gu_mine[:, :ff_main], gu_got[:, :ff_main], 0)
+    up_lanes = slice(ff_main, 2 * ff_main)
+    grad_up = join_hidden(gu_mine[:, up_lanes], gu_got[:, up_lanes], 1)
+    grad_down = join_hidden(down_mine, down_got, 2).T
     mine, got = rows_of_x(grad_attn)
     grad_query = join_heads(mine, got, 0, 6 * LANES)
     grad_key = join_heads(mine, got, 2 * LANES, 6 * LANES + HEAD_DIM)

time: 693 us -> 681 us (0.983)
  Pallas kernels: 162 us -> 141 us
  local copies, waits for them, and re-layouts: 60.3 us -> 70.6 us
    all_gather x1, waiting for transfers between devices: 0.01 us -> 20.8 us  [shards(): gu_w = lax.all_gather(gu_part, 'dp', axis=0, tiled=True)]
    pallas_call x1, Pallas kernels: 44.7 us -> 25.1 us  [attention_backward(): pl.pallas_call(backward_kernel, out_shape=jax.ShapeDtypeStruct((slot, 8 *...]
    all_gather x1, waiting for transfers between devices: 17.1 us -> 0.02 us  [shards(): down_w = lax.all_gather(down_part, 'dp', axis=0, tiled=True)]
    slice x3 -> x17, local copies, waits for them, and re-layouts: 0.58 us -> 9.4 us  [the longest x1 3.3 us: shards(): down_w = jnp.concatenate([down_w, gu_w[:, 2 * ff_main:]], axis=1)]
    ppermute x23 -> x24, waiting for transfers between devices: 137 us -> 132 us  [flip_x(): return lax.ppermute(field, 'ctx', [(0, 1), (1, 0)])]
    ppermute x23 -> x24, starting transfers between devices: 26.8 us -> 30.2 us  [flip_x(): return lax.ppermute(field, 'ctx', [(0, 1), (1, 0)])]
    unnamed x115 -> x107, local copies, waits for them, and re-layouts: 24.4 us -> 22.4 us
  transfers between devices with their start and end apart: 72 -> 73, of which waited for: 38 -> 38; matrix products, arithmetic and copies ran while one was open for 22% -> 24% of each run, Pallas kernels for 24% -> 21%
where the time goes in v4:
time: 681 us; the launch traced here: 673 us
  waiting for transfers between devices  265 us (39%)
  Pallas kernels  141 us (21%)
  local copies, waits for them, and re-layouts  70.6 us (10%)
  starting transfers between devices  65 us (10%)
  matrix products  58.6 us (9%)
  other arithmetic  56.9 us (8%)
  between operations  15.8 us (2%)
    ppermute x24, waiting for transfers between devices, flip_x(): return lax.ppermute(field, 'ctx', [(0, 1), (1, 0)])  132 us
    dot_general x10, matrix products, dot(): return lax.dot_general(left, right, dims, preferred_element_type=f32)  58.6 us
    ppermute x17, waiting for transfers between devices, flip_y(): return lax.ppermute(field, 'mp', [(0, 2), (2, 0), (1, 3), (3, 1)])  46.6 us
    pallas_call x3, Pallas kernels, weight_grads(): pl.pallas_call(functools.partial(grads_kernel, place), grid=(depth // til...  43.1 us
    ppermute x24, starting transfers between devices, flip_x(): return lax.ppermute(field, 'ctx', [(0, 1), (1, 0)])  30.2 us
    all_gather x1, waiting for transfers between devices, shards(): attn_all = lax.all_gather(attn_got, 'dp', axis=0, tiled=False)  25.2 us
    pallas_call x1, Pallas kernels, attention_backward(): pl.pallas_call(backward_kernel, out_shape=jax.ShapeDtypeStruct((slot, 8 *...  25.1 us
    unnamed x107, local copies, waits for them, and re-layouts  22.4 us
  transfers between devices with their start and end apart: 73, of which 38 were waited for; matrix products, arithmetic and copies ran while one was open for 24% of the time, Pallas kernels for 21%

profile of v4, /device:TPU:0, one launch (start us, length us, event | category | flops | bytes accessed | tf_op | source)
XLA Modules:
  0.0 672.8 jit_solution(11369923814602700390)
XLA Ops:
  25.9 6.2 fusion.1.bias_ref
  36.5 3.2 collective-permute-done
  42.7 3.6 fusion.57
  46.4 4.0 pad_maximum_fusion.11
  51.0 21.5 %collective-permute-done.4 = bf16[288,1280]{1,0:T(8,128)(2,1)} collective-permute-done((bf16[288,1280]{1,0:T(8,128)(2,1)}, bf16[288,1280]{1,0:T(8,128)(2,1)}, u32[]{:S(2)}, u32[]{:S(2)}) %collective-permute-start.4) | collective-permute-done | bytes 737312 | tf_op jit(solution)/shard_map/ppermute | solution.py:654
  97.2 7.9 %collective-permute-done.8 = bf16[288,1536]{1,0:T(8,128)(2,1)} collective-permute-done((bf16[288,1536]{1,0:T(8,128)(2,1)}, bf16[288,1536]{1,0:T(8,128)(2,1)}, u32[]{:S(2)}, u32[]{:S(2)}) %collective-permute-start.8) | collective-permute-done | bytes 884768 | tf_op jit(solution)/shard_map/ppermute | solution.py:52
  105.1 3.2 maximum_select_fusion
  108.3 25.2 %all-gather.9.cloned.1.call-done = bf16[1152,1280]{1,0:T(8,128)(2,1)} async-done(((bf16[288,1280]{1,0:T(8,128)(2,1)}), bf16[1152,1280]{1,0:T(8,128)(2,1)}) %all-gather.9.cloned.1.call-update) | async-done | bytes 2949136 | tf_op jit(solution)/shard_map/all_gather | solution.py:670
  136.5 3.7 bitcast_dynamic-update-slice_fusion
  140.2 8.0 %project_half.2.refs_0_ = f32[1408,1024]{1,0:T(8,128)} custom-call(bf16[704,2304]{1,0:T(8,128)(2,1)} %copy-done.14, bf16[2304,1280]{1,0:T(8,128)(2,1)} %bitcast.37.w_ref), custom_call_target="tpu_custom_call" | custom-call | bytes 1024 | tf_op jit(solution)/shard_map/project_half/pallas_call | solution.py:498
  148.2 8.0 %project_half.3.qkv_ref = f32[1408,1024]{1,0:T(8,128)} custom-call(bf16[704,2304]{1,0:T(8,128)(2,1)} %collective-permute-done.9.rows_ref.refs_1_, bf16[2304,1280]{1,0:T(8,128)(2,1)} %bitcast.37.w_ref, f32[1408,1024]{1,0:T(8,128)} %project_half.2.refs_0_), custom_call_target="tpu_custom_call", output_to_operand_aliasing={{}: (2, {})} | custom-call | bytes 1024 | tf_op jit(solution)/shard_map/project_half/pallas_call | solution.py:498
  159.6 22.4 %attention_forward.1 = (bf16[1408,1024]{1,0:T(8,128)(2,1)S(1)}, bf16[1408,384]{1,0:T(8,128)(2,1)S(1)}, f32[3,8,2816]{2,1,0:T(8,128)S(1)}) custom-call(s32[17]{0:T(128)S(1)} %stack.80.info, f32[1408,1024]{1,0:T(8,128)} %project_half.3.qkv_ref, f32[1408,128]{1,0:T(8,128)S(1)} %get-tuple-element.73.cos_ref, f32[1408,128]{1,0:T(8,128)S(1)} %get-tuple-element.74.sin_ref, ...), custom_call_target="tpu_custom_call" | custom-call | bytes 1024 | tf_op jit(solution)/shard_map/attention_forward/pallas_call | solution.py:349
  182.0 4.4 convolution_convert_fusion
  195.7 4.8 convert_add_fusion.3
  200.8 13.0 %collective-permute-done.18 = bf16[176,2304]{1,0:T(8,128)(2,1)S(1)} collective-permute-done((bf16[176,2304]{1,0:T(8,128)(2,1)}, bf16[176,2304]{1,0:T(8,128)(2,1)S(1)}, u32[]{:S(2)}, u32[]{:S(2)}) %collective-permute-start.18) | collective-permute-done | bytes 811040 | tf_op jit(solution)/shard_map/ppermute | solution.py:56
  227.0 13.8 %collective-permute-done.14 = bf16[2,88,2304]{2,1,0:T(8,128)(2,1)S(1)} collective-permute-done((bf16[2,88,2304]{2,1,0:T(8,128)(2,1)S(1)}, bf16[2,88,2304]{2,1,0:T(8,128)(2,1)S(1)}, u32[]{:S(2)}, u32[]{:S(2)}) %collective-permute-start.14) | collective-permute-done | bytes 811040 | tf_op jit(solution)/shard_map/ppermute | solution.py:52
  243.5 6.6 collective-permute-done.15
  257.9 20.8 %all-gather.5.cloned.1.call-done.w_ref.tail_w_ref = bf16[2304,1536]{1,0:T(8,128)(2,1)} async-done(((bf16[576,1536]{1,0:T(8,128)(2,1)}), bf16[2304,1536]{1,0:T(8,128)(2,1)}) %all-gather.5.cloned.1.call-update) | async-done | bytes 7077904 | tf_op jit(solution)/shard_map/all_gather | solution.py:677
  282.9 16.1 %collective-permute-done.27 = bf16[176,2304]{1,0:T(8,128)(2,1)S(1)} collective-permute-done((bf16[176,2304]{1,0:T(8,128)(2,1)}, bf16[176,2304]{1,0:T(8,128)(2,1)S(1)}, u32[]{:S(2)}, u32[]{:S(2)}) %collective-permute-start.27) | collective-permute-done | bytes 811040 | tf_op jit(solution)/shard_map/ppermute | solution.py:52
  302.8 6.9 %collective-permute-done.29 = bf16[88,2304]{1,0:T(8,128)(2,1)S(1)} collective-permute-done((bf16[88,2304]{1,0:T(8,128)(2,1)S(1)}, bf16[88,2304]{1,0:T(8,128)(2,1)S(1)}, u32[]{:S(2)}, u32[]{:S(2)}) %collective-permute-start.29) | collective-permute-done | bytes 405536 | tf_op jit(solution)/shard_map/ppermute | solution.py:56
  313.6 10.5 %gate_half.2 = (f32[1408,1536]{1,0:T(8,128)}, bf16[1408,640]{1,0:T(8,128)(2,1)}, bf16[1408,256]{1,0:T(8,128)(2,1)S(1)}) custom-call(bf16[704,2304]{1,0:T(8,128)(2,1)} %copy-done.12, bf16[2304,1536]{1,0:T(8,128)(2,1)} %all-gather.5.cloned.1.call-done.w_ref.tail_w_ref), custom_call_target="tpu_custom_call" | custom-call | bytes 1024 | tf_op jit(solution)/shard_map/gate_half/pallas_call | solution.py:427
  329.4 10.6 %gate_half.3 = (f32[1408,1536]{1,0:T(8,128)}, bf16[1408,640]{1,0:T(8,128)(2,1)}, bf16[1408,256]{1,0:T(8,128)(2,1)S(1)}) custom-call(bf16[704,2304]{1,0:T(8,128)(2,1)} %copy-done.13, bf16[2304,1536]{1,0:T(8,128)(2,1)} %all-gather.5.cloned.1.call-done.w_ref.tail_w_ref, ...), custom_call_target="tpu_custom_call", output_to_operand_aliasing={{0}: (2, {}), {1}: (3, {}), {2}: (4, {})} | custom-call | bytes 1024 | tf_op jit(solution)/shard_map/gate_half/pallas_call | solution.py:427
  341.5 8.5 %weight_grads.3 = bf16[2304,640]{1,0:T(8,128)(2,1)} custom-call(bf16[704,2304]{1,0:T(8,128)(2,1)} %copy-done.11, bf16[704,2304]{1,0:T(8,128)(2,1)} %copy-done.6, bf16[1408,640]{1,0:T(8,128)(2,1)S(1)} %copy-done), custom_call_target="tpu_custom_call" | custom-call | bytes 1024 | tf_op jit(solution)/shard_map/weight_grads/pallas_call | solution.py:551
  350.5 13.3 %hidden_back.1.refs_2_ = bf16[1408,1536]{1,0:T(8,128)(2,1)} custom-call(bf16[1408,2304]{1,0:T(8,128)(2,1)} %constant_dynamic-update-slice_fusion.10.rows_ref, bf16[2304,640]{1,0:T(8,128)(2,1)} %all-gather.7.cloned.1.call-done.w_ref, bf16[2304,1536]{1,0:T(8,128)(2,1)} %all-gather.5.cloned.1.call-done.w_ref.tail_w_ref, f32[1408,1536]{1,0:T(8,128)} %get-tuple-element.90.gate_up_ref), custom_call_target="tpu_custom_call" | custom-call | bytes 1024 | tf_op jit(solution)/shard_map/hidden_back/pallas_call | solution.py:472
  363.9 18.5 %weight_grads.4 = bf16[2304,1536]{1,0:T(8,128)(2,1)} custom-call(bf16[704,2304]{1,0:T(8,128)(2,1)} %copy-done.12, bf16[704,2304]{1,0:T(8,128)(2,1)} %copy-done.13, bf16[1408,1536]{1,0:T(8,128)(2,1)} %hidden_back.1.refs_2_, bf16[704,2304]{1,0:T(8,128)(2,1)} %copy-done.11, bf16[704,2304]{1,0:T(8,128)(2,1)} %copy-done.6, ...), custom_call_target="tpu_custom_call" | custom-call | bytes 1024 | tf_op jit(solution)/shard_map/weight_grads/pallas_call | solution.py:551
  382.4 9.9 %convolution_convert_fusion.3 = bf16[704,2304]{1,0:T(8,128)(2,1)} fusion(bf16[2304,1536]{1,0:T(8,128)(2,1)} %all-gather.5.cloned.1.call-done.w_ref.tail_w_ref, bf16[1408,1536]{1,0:T(8,128)(2,1)} %hidden_back.1.refs_2_), kind=kOutput, calls=%fused_computation.16 | convolution fusion | flops 4984455168 | bytes 12484608 | tf_op jit(solution)/shard_map/dot_general | solution.py:30
  393.1 5.7 collective-permute-done.32
  398.8 9.4 %convert_add_fusion.2 = f32[704,2304]{1,0:T(8,128)S(1)} fusion(bf16[704,2304]{1,0:T(8,128)(2,1)} %collective-permute-done.32, bf16[2304,1536]{1,0:T(8,128)(2,1)} %all-gather.5.cloned.1.call-done.w_ref.tail_w_ref, bf16[1408,1536]{1,0:T(8,128)(2,1)} %hidden_back.1.refs_2_), kind=kOutput, calls=%fused_computation.11 | convolution fusion | flops 4986077184 | bytes 18972672 | tf_op jit(solution)/shard_map/dot_general | solution.py:30
  410.2 18.6 %collective-permute-done.33 = bf16[2,88,2304]{2,1,0:T(8,128)(2,1)S(1)} collective-permute-done((bf16[2,88,2304]{2,1,0:T(8,128)(2,1)S(1)}, bf16[2,88,2304]{2,1,0:T(8,128)(2,1)S(1)}, u32[]{:S(2)}, u32[]{:S(2)}) %collective-permute-start.33) | collective-permute-done | bytes 811040 | tf_op jit(solution)/shard_map/ppermute | solution.py:52
  436.1 8.1 %collective-permute-done.36 = bf16[88,2304]{1,0:T(8,128)(2,1)} collective-permute-done((bf16[88,2304]{1,0:T(8,128)(2,1)}, bf16[88,2304]{1,0:T(8,128)(2,1)}, u32[]{:S(2)}, u32[]{:S(2)}) %collective-permute-start.36) | collective-permute-done | bytes 405536 | tf_op jit(solution)/shard_map/ppermute | solution.py:52
  451.0 16.4 %collective-permute-done.38 = bf16[176,2304]{1,0:T(8,128)(2,1)S(1)} collective-permute-done((bf16[176,2304]{1,0:T(8,128)(2,1)S(1)}, bf16[176,2304]{1,0:T(8,128)(2,1)S(1)}, u32[]{:S(2)}, u32[]{:S(2)}) %collective-permute-start.38) | collective-permute-done | bytes 811040 | tf_op jit(solution)/shard_map/ppermute | solution.py:52
  469.8 7.4 %collective-permute-done.39 = bf16[88,2304]{1,0:T(8,128)(2,1)S(1)} collective-permute-done((bf16[88,2304]{1,0:T(8,128)(2,1)S(1)}, bf16[88,2304]{1,0:T(8,128)(2,1)S(1)}, u32[]{:S(2)}, u32[]{:S(2)}) %collective-permute-start.39) | collective-permute-done | bytes 405536 | tf_op jit(solution)/shard_map/ppermute | solution.py:56
  477.4 3.3 slice.496
  482.3 3.3 convolution_convert_fusion.5.near_ref
  485.7 4.5 convolution_convert_fusion.4.far_ref
  490.2 25.1 %attention_backward.1.refs_2_ = bf16[1408,1024]{1,0:T(8,128)(2,1)} custom-call(s32[17]{0:T(128)S(1)} %stack.80.info, bf16[1408,1024]{1,0:T(8,128)(2,1)} %copy-done.2, f32[1408,128]{1,0:T(8,128)S(1)} %get-tuple-element.73.cos_ref, f32[1408,128]{1,0:T(8,128)S(1)} %get-tuple-element.74.sin_ref, f32[1408,1408]{1,0:T(8,128)} %fusion.1.bias_ref, ...), custom_call_target="tpu_custom_call" | custom-call | bytes 1024 | tf_op jit(solution)/shard_map/attention_backward/pallas_call | solution.py:372
  515.3 16.1 %weight_grads.5 = bf16[2304,1280]{1,0:T(8,128)(2,1)} custom-call(bf16[704,2304]{1,0:T(8,128)(2,1)} %copy-done.14, bf16[704,2304]{1,0:T(8,128)(2,1)} %collective-permute-done.9.rows_ref.refs_1_, bf16[1408,1024]{1,0:T(8,128)(2,1)} %attention_backward.1.refs_2_, bf16[704,2304]{1,0:T(8,128)(2,1)} %copy-done.19, bf16[704,2304]{1,0:T(8,128)(2,1)} %copy-done.23, ...), custom_call_target="tpu_custom_call" | custom-call | bytes 1024 | tf_op jit(solution)/shard_map/weight_grads/pallas_call | solution.py:551
  537.3 4.4 collective-permute-done.42
  541.7 7.2 %convolution_convert_fusion.1 = bf16[704,2304]{1,0:T(8,128)(2,1)S(1)} fusion(bf16[2304,1280]{1,0:T(8,128)(2,1)} %bitcast.37.w_ref, bf16[1408,1024]{1,0:T(8,128)(2,1)S(1)} %copy-done.17), kind=kOutput, calls=%fused_computation.14 | convolution fusion | flops 3323510784 | bytes 9404416 | tf_op jit(solution)/shard_map/dot_general | solution.py:30
  553.8 3.8 convolution_convert_fusion.2
  564.2 5.8 convert_add_fusion
  571.7 5.4 convert_add_fusion.1
  580.2 10.9 %collective-permute-done.55 = bf16[2,88,2304]{2,1,0:T(8,128)(2,1)S(1)} collective-permute-done((bf16[2,88,2304]{2,1,0:T(8,128)(2,1)S(1)}, bf16[2,88,2304]{2,1,0:T(8,128)(2,1)S(1)}, u32[]{:S(2)}, u32[]{:S(2)}) %collective-permute-start.55) | collective-permute-done | bytes 811040 | tf_op jit(solution)/shard_map/ppermute | solution.py:52
  595.2 13.3 %collective-permute-done.47 = bf16[2,88,2304]{2,1,0:T(8,128)(2,1)S(1)} collective-permute-done((bf16[2,88,2304]{2,1,0:T(8,128)(2,1)S(1)}, bf16[2,88,2304]{2,1,0:T(8,128)(2,1)S(1)}, u32[]{:S(2)}, u32[]{:S(2)}) %collective-permute-start.47) | collective-permute-done | bytes 811040 | tf_op jit(solution)/shard_map/ppermute | solution.py:52
  612.7 4.7 collective-permute-done.56
  622.2 3.7 collective-permute-done.60
  634.5 7.2 %reduce-scatter.8.cloned.1.call-done = bf16[576,1280]{1,0:T(8,128)(2,1)} async-done(((bf16[2304,1280]{1,0:T(8,128)(2,1)}), bf16[576,1280]{1,0:T(8,128)(2,1)}) %reduce-scatter.8.cloned.1.call-update) | async-done | bytes 1474576 | tf_op jit(solution)/shard_map/reduce_scatter | solution.py:722
  651.2 10.4 %collective-permute-done.63 = bf16[288,1280]{1,0:T(8,128)(2,1)S(1)} collective-permute-done((bf16[288,1280]{1,0:T(8,128)(2,1)S(1)}, bf16[288,1280]{1,0:T(8,128)(2,1)S(1)}, u32[]{:S(2)}, u32[]{:S(2)}) %collective-permute-start.63) | collective-permute-done | bytes 737312 | tf_op jit(solution)/shard_map/ppermute | solution.py:52
  (376 shorter events, 187.8 us)
Async XLA Ops:
  7.2 126.3 %all-gather.9.cloned.1.call-start = ((), (), s32[]{:S(2)}) async-start(), calls=%async_computation.8 | async-start | bytes 3686400 | tf_op jit(solution)/shard_map/all_gather | solution.py:670
  16.1 34.9 %collective-permute-start.3 = (bf16[288,1280]{1,0:T(8,128)(2,1)}, bf16[288,1280]{1,0:T(8,128)(2,1)}, u32[]{:S(2)}, u32[]{:S(2)}) collective-permute-start(bf16[288,1280]{1,0:T(8,128)(2,1)} %get-tuple-element.153), channel_id=1, source_target_pairs={{0,8},{8,0},{16,24},{24,16},{1,9},{9,1},{17,25},{25,17},{2,10},{10... | collective-permute-start | bytes 2211848 | tf_op jit(solution)/shard_map/ppermute | solution.py:654
  19.1 53.3 %collective-permute-start.4 = (bf16[288,1280]{1,0:T(8,128)(2,1)}, bf16[288,1280]{1,0:T(8,128)(2,1)}, u32[]{:S(2)}, u32[]{:S(2)}) collective-permute-start(bf16[288,1280]{1,0:T(8,128)(2,1)} %get-tuple-element.153), channel_id=1, source_target_pairs={{0,16},{8,24},{16,0},{24,8},{1,17},{9,25},{17,1},{25,9},{2,18},{10... | collective-permute-start | bytes 2211848 | tf_op jit(solution)/shard_map/ppermute | solution.py:654
  21.7 62.4 %collective-permute-start.7 = (bf16[288,1280]{1,0:T(8,128)(2,1)}, bf16[288,1280]{1,0:T(8,128)(2,1)}, u32[]{:S(2)}, u32[]{:S(2)}) collective-permute-start(bf16[288,1280]{1,0:T(8,128)(2,1)} %get-tuple-element.153), channel_id=1, source_target_pairs={{0,24},{8,16},{16,8},{24,0},{1,25},{9,17},{17,9},{25,1},{2,26},{10... | collective-permute-start | bytes 2211848 | tf_op jit(solution)/shard_map/ppermute | solution.py:654
  21.7 18.0 %collective-permute-start = (bf16[288,1280]{1,0:T(8,128)(2,1)}, bf16[288,1280]{1,0:T(8,128)(2,1)}, u32[]{:S(2)}, u32[]{:S(2)}) collective-permute-start(bf16[288,1280]{1,0:T(8,128)(2,1)} %get-tuple-element.154), channel_id=1, source_target_pairs={{0,4},{4,0},{1,5},{5,1},{2,6},{6,2},{3,7},{7,3},{8,12},{12,8},{9,1... | collective-permute-start | bytes 2211848 | tf_op jit(solution)/shard_map/ppermute | solution.py:52
  39.7 32.8 %collective-permute-start.1 = (bf16[176,2304]{1,0:T(8,128)(2,1)S(1)}, bf16[176,2304]{1,0:T(8,128)(2,1)}, u32[]{:S(2)}, u32[]{:S(2)}) collective-permute-start(bf16[176,2304]{1,0:T(8,128)(2,1)S(1)} %fusion.11), channel_id=1, source_target_pairs={{0,4},{4,0},{1,5},{5,1},{2,6},{6,2},{3,7},{7,3},{8,12},{12,8},{9,1... | collective-permute-start | bytes 2433032 | tf_op jit(solution)/shard_map/ppermute | solution.py:52
  41.2 31.3 %collective-permute-start.2 = (bf16[176,2304]{1,0:T(8,128)(2,1)S(1)}, bf16[176,2304]{1,0:T(8,128)(2,1)}, u32[]{:S(2)}, u32[]{:S(2)}) collective-permute-start(bf16[176,2304]{1,0:T(8,128)(2,1)S(1)} %fusion.11), channel_id=1, source_target_pairs={{0,2},{2,0},{1,3},{3,1},{4,6},{6,4},{5,7},{7,5},{8,10},{10,8},{9,1... | collective-permute-start | bytes 2433032 | tf_op jit(solution)/shard_map/ppermute | solution.py:56
  46.4 232.3 %all-gather.5.cloned.1.call-start = ((), (), s32[]{:S(2)}) async-start(), calls=%async_computation.3 | async-start | bytes 8847360 | tf_op jit(solution)/shard_map/all_gather | solution.py:677
  88.7 16.4 %collective-permute-start.8 = (bf16[288,1536]{1,0:T(8,128)(2,1)}, bf16[288,1536]{1,0:T(8,128)(2,1)}, u32[]{:S(2)}, u32[]{:S(2)}) collective-permute-start(bf16[288,1536]{1,0:T(8,128)(2,1)} %concatenate.198), channel_id=1, source_target_pairs={{0,4},{4,0},{1,5},{5,1},{2,6},{6,2},{3,7},{7,3},{8,12},{12,8},{9,1... | collective-permute-start | bytes 2654216 | tf_op jit(solution)/shard_map/ppermute | solution.py:52
  133.5 217.0 %all-gather.7.cloned.1.call-start = ((), (), s32[]{:S(2)}) async-start(), calls=%async_computation.4 | async-start | bytes 3686400 | tf_op jit(solution)/shard_map/all_gather | solution.py:691
  133.7 14.5 %collective-permute-start.9 = (bf16[704,2304]{1,0:T(8,128)(2,1)}, bf16[704,2304]{1,0:T(8,128)(2,1)}, u32[]{:S(2)}, u32[]{:S(2)}) collective-permute-start(bf16[704,2304]{1,0:T(8,128)(2,1)} %copy-done.14), channel_id=1, source_target_pairs={{0,1},{1,0},{2,3},{3,2},{4,5},{5,4},{6,7},{7,6},{8,9},{9,8},{10,11... | collective-permute-start | bytes 9732104 | tf_op jit(solution)/shard_map/ppermute | solution.py:64
  157.6 34.9 %collective-permute-start.19 = (bf16[176,2304]{1,0:T(8,128)(2,1)}, bf16[176,2304]{1,0:T(8,128)(2,1)}, u32[]{:S(2)}, u32[]{:S(2)}) collective-permute-start(bf16[176,2304]{1,0:T(8,128)(2,1)} %get-tuple-element.120), channel_id=1, source_target_pairs={{0,4},{4,0},{1,5},{5,1},{2,6},{6,2},{3,7},{7,3},{8,12},{12,8},{9,1... | collective-permute-start | bytes 2433032 | tf_op jit(solution)/shard_map/ppermute | solution.py:52
  159.0 29.7 %collective-permute-start.23 = (bf16[288,640]{1,0:T(8,128)(2,1)S(1)}, bf16[288,640]{1,0:T(8,128)(2,1)S(1)}, u32[]{:S(2)}, u32[]{:S(2)}) collective-permute-start(bf16[288,640]{1,0:T(8,128)(2,1)S(1)} %slice.575), channel_id=1, source_target_pairs={{0,4},{4,0},{1,5},{5,1},{2,6},{6,2},{3,7},{7,3},{8,12},{12,8},{9,1... | collective-permute-start | bytes 1105928 | tf_op jit(solution)/shard_map/ppermute | solution.py:52
  192.5 241.5 %reduce-scatter.4.cloned.1.call-start = ((), (), s32[]{:S(2)}) async-start(), calls=%async_computation.5 | async-start | bytes 3686400 | tf_op jit(solution)/shard_map/reduce_scatter | solution.py:698
  192.5 21.2 %collective-permute-start.18 = (bf16[176,2304]{1,0:T(8,128)(2,1)}, bf16[176,2304]{1,0:T(8,128)(2,1)S(1)}, u32[]{:S(2)}, u32[]{:S(2)}) collective-permute-start(bf16[176,2304]{1,0:T(8,128)(2,1)} %get-tuple-element.120), channel_id=1, source_target_pairs={{0,2},{2,0},{1,3},{3,1},{4,6},{6,4},{5,7},{7,5},{8,10},{10,8},{9,1... | collective-permute-start | bytes 2433032 | tf_op jit(solution)/shard_map/ppermute | solution.py:56
  195.2 27.2 %collective-permute-start.20 = (bf16[88,2304]{1,0:T(8,128)(2,1)S(1)}, bf16[88,2304]{1,0:T(8,128)(2,1)S(1)}, u32[]{:S(2)}, u32[]{:S(2)}) collective-permute-start(bf16[88,2304]{1,0:T(8,128)(2,1)S(1)} %slice.589), channel_id=1, source_target_pairs={{0,2},{2,0},{1,3},{3,1},{4,6},{6,4},{5,7},{7,5},{8,10},{10,8},{9,1... | collective-permute-start | bytes 1216520 | tf_op jit(solution)/shard_map/ppermute | solution.py:56
  213.8 12.4 %collective-permute-start.21 = (bf16[88,2304]{1,0:T(8,128)(2,1)S(1)}, bf16[88,2304]{1,0:T(8,128)(2,1)S(1)}, u32[]{:S(2)}, u32[]{:S(2)}) collective-permute-start(bf16[88,2304]{1,0:T(8,128)(2,1)S(1)} %slice.590), channel_id=1, source_target_pairs={{0,4},{4,0},{1,5},{5,1},{2,6},{6,2},{3,7},{7,3},{8,12},{12,8},{9,1... | collective-permute-start | bytes 1216520 | tf_op jit(solution)/shard_map/ppermute | solution.py:52
  214.5 26.4 %collective-permute-start.14 = (bf16[2,88,2304]{2,1,0:T(8,128)(2,1)S(1)}, bf16[2,88,2304]{2,1,0:T(8,128)(2,1)S(1)}, u32[]{:S(2)}, u32[]{:S(2)}) collective-permute-start(bf16[2,88,2304]{2,1,0:T(8,128)(2,1)S(1)} %slice_bitcast_fusion.22), channel_id=1, source_target_pairs={{0,4},{4,0},{1,5},{5,1},{2,6},{6,2},{3,7},{7,3},{8,12},{12,8},{9,1... | collective-permute-start | bytes 2433032 | tf_op jit(solution)/shard_map/ppermute | solution.py:52
  215.9 25.0 %collective-permute-start.16 = (bf16[2,88,2304]{2,1,0:T(8,128)(2,1)S(1)}, bf16[2,88,2304]{2,1,0:T(8,128)(2,1)S(1)}, u32[]{:S(2)}, u32[]{:S(2)}) collective-permute-start(bf16[2,88,2304]{2,1,0:T(8,128)(2,1)S(1)} %slice_bitcast_fusion.20), channel_id=1, source_target_pairs={{0,2},{2,0},{1,3},{3,1},{4,6},{6,4},{5,7},{7,5},{8,10},{10,8},{9,1... | collective-permute-start | bytes 2433032 | tf_op jit(solution)/shard_map/ppermute | solution.py:56
  227.0 27.3 %collective-permute-start.22 = (bf16[704,2304]{1,0:T(8,128)(2,1)S(1)}, bf16[704,2304]{1,0:T(8,128)(2,1)S(1)}, u32[]{:S(2)}, u32[]{:S(2)}) collective-permute-start(bf16[704,2304]{1,0:T(8,128)(2,1)S(1)} %get-tuple-element.179.refs_0_.refs_3_), channel_id=1, source_target_pairs={{0,1},{1,0},{2,3},{3,2},{4,5},{5,4},{6,7},{7,6},{8,9},{9,8},{10,11... | collective-permute-start | bytes 9732104 | tf_op jit(solution)/shard_map/ppermute | solution.py:64
  278.7 20.2 %collective-permute-start.27 = (bf16[176,2304]{1,0:T(8,128)(2,1)}, bf16[176,2304]{1,0:T(8,128)(2,1)S(1)}, u32[]{:S(2)}, u32[]{:S(2)}) collective-permute-start(bf16[176,2304]{1,0:T(8,128)(2,1)} %multiply_convert_fusion.2), channel_id=1, source_target_pairs={{0,4},{4,0},{1,5},{5,1},{2,6},{6,2},{3,7},{7,3},{8,12},{12,8},{9,1... | collective-permute-start | bytes 2433032 | tf_op jit(solution)/shard_map/ppermute | solution.py:52
  280.2 20.3 %collective-permute-start.25 = (bf16[176,2304]{1,0:T(8,128)(2,1)}, bf16[176,2304]{1,0:T(8,128)(2,1)S(1)}, u32[]{:S(2)}, u32[]{:S(2)}) collective-permute-start(bf16[176,2304]{1,0:T(8,128)(2,1)} %multiply_convert_fusion.2), channel_id=1, source_target_pairs={{0,2},{2,0},{1,3},{3,1},{4,6},{6,4},{5,7},{7,5},{8,10},{10,8},{9,1... | collective-permute-start | bytes 2433032 | tf_op jit(solution)/shard_map/ppermute | solution.py:56
  281.6 21.1 %collective-permute-start.24 = (bf16[176,2304]{1,0:T(8,128)(2,1)}, bf16[176,2304]{1,0:T(8,128)(2,1)S(1)}, u32[]{:S(2)}, u32[]{:S(2)}) collective-permute-start(bf16[176,2304]{1,0:T(8,128)(2,1)} %multiply_convert_fusion.2), channel_id=1, source_target_pairs={{0,1},{1,0},{2,3},{3,2},{4,5},{5,4},{6,7},{7,6},{8,9},{9,8},{10,11... | collective-permute-start | bytes 2433032 | tf_op jit(solution)/shard_map/ppermute | solution.py:64
  302.1 22.1 %collective-permute-start.26 = (bf16[176,2304]{1,0:T(8,128)(2,1)S(1)}, bf16[176,2304]{1,0:T(8,128)(2,1)}, u32[]{:S(2)}, u32[]{:S(2)}) collective-permute-start(bf16[176,2304]{1,0:T(8,128)(2,1)S(1)} %collective-permute-done.25), channel_id=1, source_target_pairs={{0,1},{1,0},{2,3},{3,2},{4,5},{5,4},{6,7},{7,6},{8,9},{9,8},{10,11... | collective-permute-start | bytes 2433032 | tf_op jit(solution)/shard_map/ppermute | solution.py:64
  302.1 23.3 %collective-permute-start.28 = (bf16[176,2304]{1,0:T(8,128)(2,1)S(1)}, bf16[176,2304]{1,0:T(8,128)(2,1)}, u32[]{:S(2)}, u32[]{:S(2)}) collective-permute-start(bf16[176,2304]{1,0:T(8,128)(2,1)S(1)} %collective-permute-done.27), channel_id=1, source_target_pairs={{0,1},{1,0},{2,3},{3,2},{4,5},{5,4},{6,7},{7,6},{8,9},{9,8},{10,11... | collective-permute-start | bytes 2433032 | tf_op jit(solution)/shard_map/ppermute | solution.py:64
  311.9 14.7 %collective-permute-start.31 = (bf16[176,2304]{1,0:T(8,128)(2,1)}, bf16[176,2304]{1,0:T(8,128)(2,1)}, u32[]{:S(2)}, u32[]{:S(2)}) collective-permute-start(bf16[176,2304]{1,0:T(8,128)(2,1)} %pad_maximum_fusion.7), channel_id=1, source_target_pairs={{0,1},{1,0},{2,3},{3,2},{4,5},{5,4},{6,7},{7,6},{8,9},{9,8},{10,11... | collective-permute-start | bytes 2433032 | tf_op jit(solution)/shard_map/ppermute | solution.py:64
  350.0 181.3 %reduce-scatter.6.cloned.1.call-start = ((), (), s32[]{:S(2)}) async-start(), calls=%async_computation.6 | async-start | bytes 8847360 | tf_op jit(solution)/shard_map/reduce_scatter | solution.py:708
  393.1 248.6 %reduce-scatter.8.cloned.1.call-start = ((), (), s32[]{:S(2)}) async-start(), calls=%async_computation.7 | async-start | bytes 7372800 | tf_op jit(solution)/shard_map/reduce_scatter | solution.py:722
  408.4 20.4 %collective-permute-start.33 = (bf16[2,88,2304]{2,1,0:T(8,128)(2,1)S(1)}, bf16[2,88,2304]{2,1,0:T(8,128)(2,1)S(1)}, u32[]{:S(2)}, u32[]{:S(2)}) collective-permute-start(bf16[2,88,2304]{2,1,0:T(8,128)(2,1)S(1)} %slice_bitcast_fusion.18), channel_id=1, source_target_pairs={{0,4},{4,0},{1,5},{5,1},{2,6},{6,2},{3,7},{7,3},{8,12},{12,8},{9,1... | collective-permute-start | bytes 2433032 | tf_op jit(solution)/shard_map/ppermute | solution.py:52
  409.7 20.0 %collective-permute-start.35 = (bf16[2,88,2304]{2,1,0:T(8,128)(2,1)S(1)}, bf16[2,88,2304]{2,1,0:T(8,128)(2,1)S(1)}, u32[]{:S(2)}, u32[]{:S(2)}) collective-permute-start(bf16[2,88,2304]{2,1,0:T(8,128)(2,1)S(1)} %slice_bitcast_fusion.17), channel_id=1, source_target_pairs={{0,2},{2,0},{1,3},{3,1},{4,6},{6,4},{5,7},{7,5},{8,10},{10,8},{9,1... | collective-permute-start | bytes 2433032 | tf_op jit(solution)/shard_map/ppermute | solution.py:56
  449.3 18.2 %collective-permute-start.38 = (bf16[176,2304]{1,0:T(8,128)(2,1)S(1)}, bf16[176,2304]{1,0:T(8,128)(2,1)S(1)}, u32[]{:S(2)}, u32[]{:S(2)}) collective-permute-start(bf16[176,2304]{1,0:T(8,128)(2,1)S(1)} %get-tuple-element.117), channel_id=1, source_target_pairs={{0,4},{4,0},{1,5},{5,1},{2,6},{6,2},{3,7},{7,3},{8,12},{12,8},{9,1... | collective-permute-start | bytes 2433032 | tf_op jit(solution)/shard_map/ppermute | solution.py:52
  450.5 18.7 %collective-permute-start.37 = (bf16[176,2304]{1,0:T(8,128)(2,1)S(1)}, bf16[176,2304]{1,0:T(8,128)(2,1)S(1)}, u32[]{:S(2)}, u32[]{:S(2)}) collective-permute-start(bf16[176,2304]{1,0:T(8,128)(2,1)S(1)} %get-tuple-element.117), channel_id=1, source_target_pairs={{0,2},{2,0},{1,3},{3,1},{4,6},{6,4},{5,7},{7,5},{8,10},{10,8},{9,1... | collective-permute-start | bytes 2433032 | tf_op jit(solution)/shard_map/ppermute | solution.py:56
  481.6 69.1 %collective-permute-start.66 = (bf16[288,640]{1,0:T(8,128)(2,1)}, bf16[288,640]{1,0:T(8,128)(2,1)}, u32[]{:S(2)}, u32[]{:S(2)}) collective-permute-start(bf16[288,640]{1,0:T(8,128)(2,1)} %get-tuple-element.166), channel_id=1, source_target_pairs={{0,4},{4,0},{1,5},{5,1},{2,6},{6,2},{3,7},{7,3},{8,12},{12,8},{9,1... | collective-permute-start | bytes 1105928 | tf_op jit(solution)/shard_map/ppermute | solution.py:52
  535.6 22.3 %collective-permute-start.65 = (bf16[288,1280]{1,0:T(8,128)(2,1)}, bf16[288,1280]{1,0:T(8,128)(2,1)}, u32[]{:S(2)}, u32[]{:S(2)}) collective-permute-start(bf16[288,1280]{1,0:T(8,128)(2,1)} %get-tuple-element.144), channel_id=1, source_target_pairs={{0,4},{4,0},{1,5},{5,1},{2,6},{6,2},{3,7},{7,3},{8,12},{12,8},{9,1... | collective-permute-start | bytes 2211848 | tf_op jit(solution)/shard_map/ppermute | solution.py:52
  549.1 14.5 %collective-permute-start.51 = (bf16[176,2304]{1,0:T(8,128)(2,1)S(1)}, bf16[176,2304]{1,0:T(8,128)(2,1)S(1)}, u32[]{:S(2)}, u32[]{:S(2)}) collective-permute-start(bf16[176,2304]{1,0:T(8,128)(2,1)S(1)} %get-tuple-element.131), channel_id=1, source_target_pairs={{0,1},{1,0},{2,3},{3,2},{4,5},{5,4},{6,7},{7,6},{8,9},{9,8},{10,11... | collective-permute-start | bytes 2433032 | tf_op jit(solution)/shard_map/ppermute | solution.py:64
  549.2 14.5 %collective-permute-start.52 = (bf16[176,2304]{1,0:T(8,128)(2,1)S(1)}, bf16[176,2304]{1,0:T(8,128)(2,1)S(1)}, u32[]{:S(2)}, u32[]{:S(2)}) collective-permute-start(bf16[176,2304]{1,0:T(8,128)(2,1)S(1)} %get-tuple-element.134), channel_id=1, source_target_pairs={{0,1},{1,0},{2,3},{3,2},{4,5},{5,4},{6,7},{7,6},{8,9},{9,8},{10,11... | collective-permute-start | bytes 2433032 | tf_op jit(solution)/shard_map/ppermute | solution.py:64
  549.7 14.5 %collective-permute-start.53 = (bf16[176,2304]{1,0:T(8,128)(2,1)S(1)}, bf16[176,2304]{1,0:T(8,128)(2,1)S(1)}, u32[]{:S(2)}, u32[]{:S(2)}) collective-permute-start(bf16[176,2304]{1,0:T(8,128)(2,1)S(1)} %get-tuple-element.133), channel_id=1, source_target_pairs={{0,1},{1,0},{2,3},{3,2},{4,5},{5,4},{6,7},{7,6},{8,9},{9,8},{10,11... | collective-permute-start | bytes 2433032 | tf_op jit(solution)/shard_map/ppermute | solution.py:64
  550.7 13.5 %collective-permute-start.54 = (bf16[176,2304]{1,0:T(8,128)(2,1)S(1)}, bf16[176,2304]{1,0:T(8,128)(2,1)S(1)}, u32[]{:S(2)}, u32[]{:S(2)}) collective-permute-start(bf16[176,2304]{1,0:T(8,128)(2,1)S(1)} %get-tuple-element.132), channel_id=1, source_target_pairs={{0,1},{1,0},{2,3},{3,2},{4,5},{5,4},{6,7},{7,6},{8,9},{9,8},{10,11... | collective-permute-start | bytes 2433032 | tf_op jit(solution)/shard_map/ppermute | solution.py:64
  557.9 12.5 %collective-permute-start.43 = (bf16[176,2304]{1,0:T(8,128)(2,1)S(1)}, bf16[176,2304]{1,0:T(8,128)(2,1)S(1)}, u32[]{:S(2)}, u32[]{:S(2)}) collective-permute-start(bf16[176,2304]{1,0:T(8,128)(2,1)S(1)} %get-tuple-element.135), channel_id=1, source_target_pairs={{0,1},{1,0},{2,3},{3,2},{4,5},{5,4},{6,7},{7,6},{8,9},{9,8},{10,11... | collective-permute-start | bytes 2433032 | tf_op jit(solution)/shard_map/ppermute | solution.py:64
  570.2 20.9 %collective-permute-start.55 = (bf16[2,88,2304]{2,1,0:T(8,128)(2,1)S(1)}, bf16[2,88,2304]{2,1,0:T(8,128)(2,1)S(1)}, u32[]{:S(2)}, u32[]{:S(2)}) collective-permute-start(bf16[2,88,2304]{2,1,0:T(8,128)(2,1)S(1)} %slice_bitcast_fusion.11), channel_id=1, source_target_pairs={{0,4},{4,0},{1,5},{5,1},{2,6},{6,2},{3,7},{7,3},{8,12},{12,8},{9,1... | collective-permute-start | bytes 2433032 | tf_op jit(solution)/shard_map/ppermute | solution.py:52
  570.4 20.9 %collective-permute-start.57 = (bf16[2,88,2304]{2,1,0:T(8,128)(2,1)S(1)}, bf16[2,88,2304]{2,1,0:T(8,128)(2,1)S(1)}, u32[]{:S(2)}, u32[]{:S(2)}) collective-permute-start(bf16[2,88,2304]{2,1,0:T(8,128)(2,1)S(1)} %slice_bitcast_fusion.9), channel_id=1, source_target_pairs={{0,2},{2,0},{1,3},{3,1},{4,6},{6,4},{5,7},{7,5},{8,10},{10,8},{9,1... | collective-permute-start | bytes 2433032 | tf_op jit(solution)/shard_map/ppermute | solution.py:56
  577.2 31.3 %collective-permute-start.47 = (bf16[2,88,2304]{2,1,0:T(8,128)(2,1)S(1)}, bf16[2,88,2304]{2,1,0:T(8,128)(2,1)S(1)}, u32[]{:S(2)}, u32[]{:S(2)}) collective-permute-start(bf16[2,88,2304]{2,1,0:T(8,128)(2,1)S(1)} %slice_bitcast_fusion.15), channel_id=1, source_target_pairs={{0,4},{4,0},{1,5},{5,1},{2,6},{6,2},{3,7},{7,3},{8,12},{12,8},{9,1... | collective-permute-start | bytes 2433032 | tf_op jit(solution)/shard_map/ppermute | solution.py:52
  579.4 29.3 %collective-permute-start.49 = (bf16[2,88,2304]{2,1,0:T(8,128)(2,1)S(1)}, bf16[2,88,2304]{2,1,0:T(8,128)(2,1)S(1)}, u32[]{:S(2)}, u32[]{:S(2)}) collective-permute-start(bf16[2,88,2304]{2,1,0:T(8,128)(2,1)S(1)} %slice_bitcast_fusion.13), channel_id=1, source_target_pairs={{0,2},{2,0},{1,3},{3,1},{4,6},{6,4},{5,7},{7,5},{8,10},{10,8},{9,1... | collective-permute-start | bytes 2433032 | tf_op jit(solution)/shard_map/ppermute | solution.py:56
  591.7 25.6 %collective-permute-start.56 = (bf16[88,2304]{1,0:T(8,128)(2,1)S(1)}, bf16[88,2304]{1,0:T(8,128)(2,1)S(1)}, u32[]{:S(2)}, u32[]{:S(2)}) collective-permute-start(bf16[88,2304]{1,0:T(8,128)(2,1)S(1)} %fusion.55), channel_id=1, source_target_pairs={{0,2},{2,0},{1,3},{3,1},{4,6},{6,4},{5,7},{7,5},{8,10},{10,8},{9,1... | collective-permute-start | bytes 1216520 | tf_op jit(solution)/shard_map/ppermute | solution.py:56
  593.1 24.3 %collective-permute-start.58 = (bf16[88,2304]{1,0:T(8,128)(2,1)S(1)}, bf16[88,2304]{1,0:T(8,128)(2,1)S(1)}, u32[]{:S(2)}, u32[]{:S(2)}) collective-permute-start(bf16[88,2304]{1,0:T(8,128)(2,1)S(1)} %fusion.56), channel_id=1, source_target_pairs={{0,4},{4,0},{1,5},{5,1},{2,6},{6,2},{3,7},{7,3},{8,12},{12,8},{9,1... | collective-permute-start | bytes 1216520 | tf_op jit(solution)/shard_map/ppermute | solution.py:52
  609.2 18.7 %collective-permute-start.48 = (bf16[88,2304]{1,0:T(8,128)(2,1)S(1)}, bf16[88,2304]{1,0:T(8,128)(2,1)S(1)}, u32[]{:S(2)}, u32[]{:S(2)}) collective-permute-start(bf16[88,2304]{1,0:T(8,128)(2,1)S(1)} %fusion.53), channel_id=1, source_target_pairs={{0,2},{2,0},{1,3},{3,1},{4,6},{6,4},{5,7},{7,5},{8,10},{10,8},{9,1... | collective-permute-start | bytes 1216520 | tf_op jit(solution)/shard_map/ppermute | solution.py:56
  610.6 20.1 %collective-permute-start.50 = (bf16[88,2304]{1,0:T(8,128)(2,1)S(1)}, bf16[88,2304]{1,0:T(8,128)(2,1)S(1)}, u32[]{:S(2)}, u32[]{:S(2)}) collective-permute-start(bf16[88,2304]{1,0:T(8,128)(2,1)S(1)} %fusion.54), channel_id=1, source_target_pairs={{0,4},{4,0},{1,5},{5,1},{2,6},{6,2},{3,7},{7,3},{8,12},{12,8},{9,1... | collective-permute-start | bytes 1216520 | tf_op jit(solution)/shard_map/ppermute | solution.py:52
  643.2 18.3 %collective-permute-start.63 = (bf16[288,1280]{1,0:T(8,128)(2,1)S(1)}, bf16[288,1280]{1,0:T(8,128)(2,1)S(1)}, u32[]{:S(2)}, u32[]{:S(2)}) collective-permute-start(bf16[288,1280]{1,0:T(8,128)(2,1)S(1)} %get-tuple-element.152), channel_id=1, source_target_pairs={{0,4},{4,0},{1,5},{5,1},{2,6},{6,2},{3,7},{7,3},{8,12},{12,8},{9,1... | collective-permute-start | bytes 2211848 | tf_op jit(solution)/shard_map/ppermute | solution.py:52
  (69 other events, 513.1 us)
Sparse Core Ops, SparseCore 0:
  46.5 86.9 all-gather.8
  135.6 143.0 all-gather.4
  280.8 58.4 all-gather.6
  350.2 54.6 reduce-scatter.3
  407.1 123.3 reduce-scatter.5
  537.2 104.4 reduce-scatter.7

commit v5 on v4

--- a/solution.py
+++ b/solution.py
@@ -406,38 +406,43 @@
     return pltpu.roll(tail, 2 * size, 1), pltpu.roll(tail, size, 1)
 
 
-def gate_kernel(size, rows_ref, w_ref, *refs):
+def gate_kernel(size, first_ref, second_ref, w_ref, *refs):
     gate_up_ref, main_ref, tail_ref = refs[-3:]
     width = main_ref.shape[1]
-    gate_up = dot(rows_ref[...], w_ref[...])
-    gate_up_ref[...] = gate_up
-    gate, up = gate_up[:, :width], gate_up[:, width : 2 * width]
-    main_ref[...] = (gate * jax.nn.sigmoid(gate) * up).astype(bf16)
-    gate, up = tail_parts(gate_up[:, 2 * width :], size)
-    tail = gate * jax.nn.sigmoid(gate) * up
-    tail_ref[...] = jnp.where(tail_lanes(tail.shape, 2 * size, size), tail, 0.0).astype(bf16)
-
-
-def gate_half(rows, gu_w, width, size, earlier):
-    count, depth = rows.shape
+
+    def project(rows):
+        gate_up = dot(rows, w_ref[...])
+        gate_up_ref[...] = gate_up
+        gate, up = gate_up[:, :width], gate_up[:, width : 2 * width]
+        main_ref[...] = (gate * jax.nn.sigmoid(gate) * up).astype(bf16)
+        gate, up = tail_parts(gate_up[:, 2 * width :], size)
+        tail = gate * jax.nn.sigmoid(gate) * up
+        tail_ref[...] = jnp.where(tail_lanes(tail.shape, 2 * size, size), tail, 0.0).astype(bf16)
+
+    pl.when(pl.program_id(0) == 0)(lambda: project(first_ref[...]))
+    pl.when(pl.program_id(0) == 1)(lambda: project(second_ref[...]))
+
+
+def gate_blocks(blocks, places, gu_w, width, size, earlier):
+    count, depth = blocks[0].shape
     cols = gu_w.shape[1]
-    tile = count // 4
-    at = 4 if earlier else 0
+    at, step = places[0], places[1] - places[0]
     widths = (cols, width, cols - 2 * width)
     return pl.pallas_call(
         functools.partial(gate_kernel, size),
-        grid=(4,),
+        grid=(2,),
         out_shape=tuple(
-            jax.ShapeDtypeStruct((2 * count, w), kind) for w, kind in zip(widths, (f32, bf16, bf16))
+            jax.ShapeDtypeStruct((8 * count, w), kind) for w, kind in zip(widths, (f32, bf16, bf16))
         ),
-        in_specs=[pl.BlockSpec((tile, depth), lambda i: (i, 0)), whole((depth, cols))]
+        in_specs=[whole((count, depth))] * 2
+        + [whole((depth, cols))]
         + [pl.BlockSpec(memory_space=pl.ANY)] * len(earlier),
-        out_specs=tuple(pl.BlockSpec((tile, w), lambda i: (i + at, 0)) for w in widths),
-        input_output_aliases={2: 0, 3: 1, 4: 2} if earlier else {},
+        out_specs=tuple(pl.BlockSpec((count, w), lambda i: (at + step * i, 0)) for w in widths),
+        input_output_aliases={3: 0, 4: 1, 5: 2} if earlier else {},
         compiler_params=ROOMY,
-        cost_estimate=FREE,
-        name="gate_half",
-    )(rows, gu_w, *earlier)
+        cost_estimate=pl.CostEstimate(flops=8 * count * depth * cols, bytes_accessed=1024, transcendentals=0),
+        name="gate_blocks",
+    )(*blocks, gu_w, *earlier)
 
 
 def gate_back(d_hidden, gate, up):
@@ -512,12 +517,13 @@
     )(rows, weight, *earlier)
 
 
-def grads_kernel(place, *refs):
+def grads_kernel(place, counts, *refs):
     out_ref = refs[-1]
-    products = []
-    for near_ref, far_ref, right_ref in zip(refs[0:-1:3], refs[1:-1:3], refs[2:-1:3]):
-        left = jnp.concatenate([near_ref[...], far_ref[...]], axis=0)
-        products.append(dot(left, right_ref[...], TN))
+    products, at = [], 0
+    for count in counts:
+        left = jnp.concatenate([ref[...] for ref in refs[at : at + count]], axis=0)
+        products.append(dot(left, refs[at + count][...], TN))
+        at += count + 1
     place(out_ref, *products)
 
 
@@ -538,18 +544,16 @@
     out_ref[:, start + LANES :] = second[:, LANES:].astype(bf16)
 
 
-def weight_grads(place, cols, tile, *triples):
-    depth = triples[0][0].shape[1]
+def weight_grads(place, cols, tile, *products):
+    depth = products[0][0][0].shape[1]
     specs, operands = [], []
-    for near, far, right in triples:
-        specs += [
-            pl.BlockSpec((near.shape[0], tile), lambda i: (0, i)),
-            pl.BlockSpec((far.shape[0], tile), lambda i: (0, i)),
-            whole(right.shape),
-        ]
-        operands += [near, far, right]
+    for pieces, right in products:
+        specs += [pl.BlockSpec((piece.shape[0], tile), lambda i: (0, i)) for piece in pieces]
+        specs += [whole(right.shape)]
+        operands += [*pieces, right]
+    counts = [len(pieces) for pieces, _ in products]
     return pl.pallas_call(
-        functools.partial(grads_kernel, place),
+        functools.partial(grads_kernel, place, counts),
         grid=(depth // tile,),
         out_shape=jax.ShapeDtypeStruct((depth, cols), bf16),
         in_specs=specs,
@@ -687,13 +691,22 @@
     rotated, mixed, log_total = attention_forward(info, qkv, cosine, sine, bias)
     residual = inputs + branch_scale * sum_rows(mixed, out_w, NT, pieces=4)
     own_m, gu_w, d_mlp = after((normalize(residual) * gain_m).astype(bf16), gu_w, d_mlp)
-    near_m = gather_near(own_m)
     down_w = lax.all_gather(down_part, "dp", axis=0, tiled=True)
-    far_m = flip_core(near_m, 4)
-    earlier = gate_half(near_m, gu_w, ff_main, ff_tail, ())
-    gate_up, hidden, hidden_tail = gate_half(far_m, gu_w, ff_main, ff_tail, earlier)
-
-    grad_down = weight_grads(place_one, ff_main, 6 * LANES, (near_d, far_d, hidden))
+    half = own_m.shape[0] // 2
+    from_x, from_y, own_c = flip_x(own_m), flip_y(own_m), flip_core(own_m)
+    gates = gate_blocks((own_m, own_c), (0, 4), gu_w, ff_main, ff_tail, ())
+    from_x, from_y, gates = after(from_x, from_y, gates)
+    corner = jnp.concatenate([flip_y(from_x[:half]), flip_x(from_y[half:])], axis=0)
+    y_c, x_c = flip_core(from_y), flip_core(from_x)
+    gates = gate_blocks((from_y, from_x), (1, 2), gu_w, ff_main, ff_tail, gates)
+    corner, gates = after(corner, gates)
+    corner_c = flip_core(corner)
+    gates = gate_blocks((y_c, x_c), (5, 6), gu_w, ff_main, ff_tail, gates)
+    gates = gate_blocks((corner, corner_c), (3, 7), gu_w, ff_main, ff_tail, gates)
+    gate_up, hidden, hidden_tail = gates
+    all_m = (own_m, from_y, from_x, corner, own_c, y_c, x_c, corner_c)
+
+    grad_down = weight_grads(place_one, ff_main, 6 * LANES, ((near_d, far_d), hidden))
     gate_up, grad_down = after(gate_up, grad_down)
     grad_down = lax.psum_scatter(grad_down, "dp", scatter_dimension=0, tiled=True)
     d_gate_up = hidden_back(d_mlp, down_w, gu_w, gate_up, ff_tail)
@@ -701,8 +714,8 @@
         place_tail,
         gate_up.shape[1],
         3 * LANES,
-        (near_m, far_m, d_gate_up),
-        (near_d, far_d, hidden_tail),
+        (all_m, d_gate_up),
+        ((near_d, far_d), hidden_tail),
     )
     d_gate_up, grad_gu = after(d_gate_up, grad_gu)
     grad_gu = lax.psum_scatter(grad_gu, "dp", scatter_dimension=0, tiled=True)
@@ -716,7 +729,7 @@
         info, rotated, cosine, sine, bias, mixed, d_mixed_near, d_mixed_far, log_total
     )
     grad_attn = weight_grads(
-        place_heads, 10 * LANES, 3 * LANES, (near_a, far_a, d_qkv), (near_o, far_o, mixed)
+        place_heads, 10 * LANES, 3 * LANES, ((near_a, far_a), d_qkv), ((near_o, far_o), mixed)
     )
     grad_attn, grad_gu, d_qkv, hidden = after(grad_attn, grad_gu, d_qkv, hidden)
     grad_attn = lax.psum_scatter(grad_attn, "dp", scatter_dimension=0, tiled=True)

time: 681 us -> 674 us (0.990)
  Pallas kernels: 141 us -> 150 us
  waiting for transfers between devices: 265 us -> 258 us
    pallas_call x5 -> x7, Pallas kernels: 64.2 us -> 73.3 us  [the longest x3 43.1 us: weight_grads(): pl.pallas_call(functools.partial(grads_kernel, place, counts), grid=(dept...]
    unnamed x107 -> x118, local copies, waits for them, and re-layouts: 22.4 us -> 18.8 us
  transfers between devices with their start and end apart: 73 -> 73, of which waited for: 38 -> 39; matrix products, arithmetic and copies ran while one was open for 24% -> 23% of each run, Pallas kernels for 21% -> 23%
where the time goes in v5:
time: 674 us; the launch traced here: 666 us
  waiting for transfers between devices  258 us (38%)
  Pallas kernels  150 us (22%)
  local copies, waits for them, and re-layouts  65 us (10%)
  starting transfers between devices  63.7 us (9%)
  matrix products  58.4 us (9%)
  other arithmetic  54.6 us (8%)
  between operations  15.8 us (2%)
    ppermute x24, waiting for transfers between devices, flip_x(): return lax.ppermute(field, 'ctx', [(0, 1), (1, 0)])  125 us
    dot_general x10, matrix products, dot(): return lax.dot_general(left, right, dims, preferred_element_type=f32)  58.4 us
    ppermute x17, waiting for transfers between devices, flip_y(): return lax.ppermute(field, 'mp', [(0, 2), (2, 0), (1, 3), (3, 1)])  43.6 us
    pallas_call x3, Pallas kernels, weight_grads(): pl.pallas_call(functools.partial(grads_kernel, place, counts), grid=(dept...  43.1 us
    pallas_call x4, Pallas kernels, gate_blocks(): pl.pallas_call(functools.partial(gate_kernel, size), grid=(2,), out_shape...  30.2 us
    ppermute x24, starting transfers between devices, flip_x(): return lax.ppermute(field, 'ctx', [(0, 1), (1, 0)])  27.2 us
    pallas_call x1, Pallas kernels, attention_backward(): pl.pallas_call(backward_kernel, out_shape=jax.ShapeDtypeStruct((slot, 8 *...  25.5 us
    all_gather x1, waiting for transfers between devices, shards(): attn_all = lax.all_gather(attn_got, 'dp', axis=0, tiled=False)  25.1 us
  transfers between devices with their start and end apart: 73, of which 39 were waited for; matrix products, arithmetic and copies ran while one was open for 23% of the time, Pallas kernels for 23%

profile of v5, /device:TPU:0, one launch (start us, length us, event | category | flops | bytes accessed | tf_op | source)
XLA Modules:
  0.0 666.1 jit_solution(8760187705448307654)
XLA Ops:
  25.9 6.2 fusion.1.bias_ref
  36.5 3.2 collective-permute-done
  42.7 3.6 fusion.56
  46.4 4.0 pad_maximum_fusion.9
  51.0 21.5 %collective-permute-done.4 = bf16[288,1280]{1,0:T(8,128)(2,1)} collective-permute-done((bf16[288,1280]{1,0:T(8,128)(2,1)}, bf16[288,1280]{1,0:T(8,128)(2,1)}, u32[]{:S(2)}, u32[]{:S(2)}) %collective-permute-start.4) | collective-permute-done | bytes 737312 | tf_op jit(solution)/shard_map/ppermute | solution.py:658
  97.3 7.9 %collective-permute-done.8 = bf16[288,1536]{1,0:T(8,128)(2,1)} collective-permute-done((bf16[288,1536]{1,0:T(8,128)(2,1)}, bf16[288,1536]{1,0:T(8,128)(2,1)}, u32[]{:S(2)}, u32[]{:S(2)}) %collective-permute-start.8) | collective-permute-done | bytes 884768 | tf_op jit(solution)/shard_map/ppermute | solution.py:52
  105.1 3.2 maximum_select_fusion
  108.4 25.1 %all-gather.9.cloned.1.call-done = bf16[1152,1280]{1,0:T(8,128)(2,1)} async-done(((bf16[288,1280]{1,0:T(8,128)(2,1)}), bf16[1152,1280]{1,0:T(8,128)(2,1)}) %all-gather.9.cloned.1.call-update) | async-done | bytes 2949136 | tf_op jit(solution)/shard_map/all_gather | solution.py:674
  136.6 3.6 bitcast_dynamic-update-slice_fusion
  140.2 8.0 %project_half.2.refs_0_ = f32[1408,1024]{1,0:T(8,128)} custom-call(bf16[704,2304]{1,0:T(8,128)(2,1)} %copy-done.19, bf16[2304,1280]{1,0:T(8,128)(2,1)} %bitcast.37.w_ref), custom_call_target="tpu_custom_call" | custom-call | bytes 1024 | tf_op jit(solution)/shard_map/project_half/pallas_call | solution.py:503
  148.2 8.0 %project_half.3.qkv_ref = f32[1408,1024]{1,0:T(8,128)} custom-call(bf16[704,2304]{1,0:T(8,128)(2,1)} %collective-permute-done.9.rows_ref.refs_1_, bf16[2304,1280]{1,0:T(8,128)(2,1)} %bitcast.37.w_ref, f32[1408,1024]{1,0:T(8,128)} %project_half.2.refs_0_), custom_call_target="tpu_custom_call", output_to_operand_aliasing={{}: (2, {})} | custom-call | bytes 1024 | tf_op jit(solution)/shard_map/project_half/pallas_call | solution.py:503
  159.6 22.2 %attention_forward.1 = (bf16[1408,1024]{1,0:T(8,128)(2,1)S(1)}, bf16[1408,384]{1,0:T(8,128)(2,1)S(1)}, f32[3,8,2816]{2,1,0:T(8,128)S(1)}) custom-call(s32[17]{0:T(128)S(1)} %stack.80.info, f32[1408,1024]{1,0:T(8,128)} %project_half.3.qkv_ref, f32[1408,128]{1,0:T(8,128)S(1)} %get-tuple-element.88.cos_ref, f32[1408,128]{1,0:T(8,128)S(1)} %get-tuple-element.89.sin_ref, ...), custom_call_target="tpu_custom_call" | custom-call | bytes 1024 | tf_op jit(solution)/shard_map/attention_forward/pallas_call | solution.py:349
  181.8 4.7 convolution_convert_fusion
  196.2 4.8 convert_add_fusion.3
  201.3 12.9 %collective-permute-done.18 = bf16[176,2304]{1,0:T(8,128)(2,1)S(1)} collective-permute-done((bf16[176,2304]{1,0:T(8,128)(2,1)}, bf16[176,2304]{1,0:T(8,128)(2,1)S(1)}, u32[]{:S(2)}, u32[]{:S(2)}) %collective-permute-start.18) | collective-permute-done | bytes 811040 | tf_op jit(solution)/shard_map/ppermute | solution.py:56
  227.4 13.9 %collective-permute-done.14 = bf16[2,88,2304]{2,1,0:T(8,128)(2,1)S(1)} collective-permute-done((bf16[2,88,2304]{2,1,0:T(8,128)(2,1)S(1)}, bf16[2,88,2304]{2,1,0:T(8,128)(2,1)S(1)}, u32[]{:S(2)}, u32[]{:S(2)}) %collective-permute-start.14) | collective-permute-done | bytes 811040 | tf_op jit(solution)/shard_map/ppermute | solution.py:52
  244.1 6.5 collective-permute-done.15
  257.6 21.2 %all-gather.5.cloned.1.call-done.w_ref.tail_w_ref = bf16[2304,1536]{1,0:T(8,128)(2,1)} async-done(((bf16[576,1536]{1,0:T(8,128)(2,1)}), bf16[2304,1536]{1,0:T(8,128)(2,1)}) %all-gather.5.cloned.1.call-update) | async-done | bytes 7077904 | tf_op jit(solution)/shard_map/all_gather | solution.py:681
  282.7 7.6 %gate_blocks.4 = (f32[1408,1536]{1,0:T(8,128)}, bf16[1408,640]{1,0:T(8,128)(2,1)}, bf16[1408,256]{1,0:T(8,128)(2,1)S(1)}) custom-call(bf16[176,2304]{1,0:T(8,128)(2,1)S(1)} %multiply_convert_fusion.2.first_ref.refs_0_, bf16[176,2304]{1,0:T(8,128)(2,1)} %copy-done.39, bf16[2304,1536]{1,0:T(8,128)(2,1)} %all-gather.5.cloned.1.call-done.w_ref.tail_w_ref), custom_call_target="tpu_custom_call" | custom-call | flops 4982833152 | bytes 1024 | tf_op jit(solution)/shard_map/gate_blocks/pallas_call | solution.py:431
  290.2 9.0 %collective-permute-done.24.second_ref.refs_2_ = bf16[176,2304]{1,0:T(8,128)(2,1)S(1)} collective-permute-done((bf16[176,2304]{1,0:T(8,128)(2,1)S(1)}, bf16[176,2304]{1,0:T(8,128)(2,1)S(1)}, u32[]{:S(2)}, u32[]{:S(2)}) %collective-permute-start.24) | collective-permute-done | bytes 811040 | tf_op jit(solution)/shard_map/ppermute | solution.py:52
  303.2 7.5 %gate_blocks.5 = (f32[1408,1536]{1,0:T(8,128)}, bf16[1408,640]{1,0:T(8,128)(2,1)}, bf16[1408,256]{1,0:T(8,128)(2,1)S(1)}) custom-call(bf16[176,2304]{1,0:T(8,128)(2,1)S(1)} %collective-permute-done.25.first_ref.refs_1_, bf16[176,2304]{1,0:T(8,128)(2,1)} %copy-done.24, ...), custom_call_target="tpu_custom_call", output_to_operand_aliasing={{0}: (3, {}), {1}: (4, {}), {2}: (5, {})} | custom-call | flops 4982833152 | bytes 1024 | tf_op jit(solution)/shard_map/gate_blocks/pallas_call | solution.py:431
  314.9 7.5 %gate_blocks.6 = (f32[1408,1536]{1,0:T(8,128)}, bf16[1408,640]{1,0:T(8,128)(2,1)}, bf16[1408,256]{1,0:T(8,128)(2,1)S(1)}) custom-call(bf16[176,2304]{1,0:T(8,128)(2,1)S(1)} %collective-permute-done.30.first_ref.refs_5_, bf16[176,2304]{1,0:T(8,128)(2,1)} %copy-done.27, ...), custom_call_target="tpu_custom_call", output_to_operand_aliasing={{0}: (3, {}), {1}: (4, {}), {2}: (5, {})} | custom-call | flops 4982833152 | bytes 1024 | tf_op jit(solution)/shard_map/gate_blocks/pallas_call | solution.py:431
  323.3 7.6 %gate_blocks.7 = (f32[1408,1536]{1,0:T(8,128)}, bf16[1408,640]{1,0:T(8,128)(2,1)}, bf16[1408,256]{1,0:T(8,128)(2,1)S(1)}) custom-call(bf16[176,2304]{1,0:T(8,128)(2,1)S(1)} %pad_maximum_fusion.5.first_ref.refs_3_, bf16[176,2304]{1,0:T(8,128)(2,1)} %copy-done.28, ...), custom_call_target="tpu_custom_call", output_to_operand_aliasing={{0}: (3, {}), {1}: (4, {}), {2}: (5, {})} | custom-call | flops 4982833152 | bytes 1024 | tf_op jit(solution)/shard_map/gate_blocks/pallas_call | solution.py:431
  332.4 8.5 %weight_grads.3 = bf16[2304,640]{1,0:T(8,128)(2,1)} custom-call(bf16[704,2304]{1,0:T(8,128)(2,1)} %copy-done.18, bf16[704,2304]{1,0:T(8,128)(2,1)} %copy-done.13, bf16[1408,640]{1,0:T(8,128)(2,1)S(1)} %copy-done), custom_call_target="tpu_custom_call" | custom-call | bytes 1024 | tf_op jit(solution)/shard_map/weight_grads/pallas_call | solution.py:555
  341.1 13.1 %hidden_back.1.refs_8_ = bf16[1408,1536]{1,0:T(8,128)(2,1)} custom-call(bf16[1408,2304]{1,0:T(8,128)(2,1)} %constant_dynamic-update-slice_fusion.10.rows_ref, bf16[2304,640]{1,0:T(8,128)(2,1)} %all-gather.7.cloned.1.call-done.w_ref, bf16[2304,1536]{1,0:T(8,128)(2,1)} %all-gather.5.cloned.1.call-done.w_ref.tail_w_ref, f32[1408,1536]{1,0:T(8,128)} %get-tuple-element.120.gate_up_ref), custom_call_target="tpu_custom_call" | custom-call | bytes 1024 | tf_op jit(solution)/shard_map/hidden_back/pallas_call | solution.py:477
  354.2 18.5 %weight_grads.4 = bf16[2304,1536]{1,0:T(8,128)(2,1)} custom-call(bf16[176,2304]{1,0:T(8,128)(2,1)S(1)} %copy-done.7, bf16[176,2304]{1,0:T(8,128)(2,1)} %copy-done.3, bf16[176,2304]{1,0:T(8,128)(2,1)} %copy-done.24, bf16[176,2304]{1,0:T(8,128)(2,1)} %copy-done.2, bf16[176,2304]{1,0:T(8,128)(2,1)} %copy-done.39, bf16[176,2304]{1,0:T(8,128)(2,1)} %copy-done.8, ...), custom_call_target="tpu_custom_call" | custom-call | bytes 1024 | tf_op jit(solution)/shard_map/weight_grads/pallas_call | solution.py:555
  372.7 10.0 %convolution_convert_fusion.3 = bf16[704,2304]{1,0:T(8,128)(2,1)} fusion(bf16[2304,1536]{1,0:T(8,128)(2,1)} %all-gather.5.cloned.1.call-done.w_ref.tail_w_ref, bf16[1408,1536]{1,0:T(8,128)(2,1)} %hidden_back.1.refs_8_), kind=kOutput, calls=%fused_computation.16 | convolution fusion | flops 4984455168 | bytes 12484608 | tf_op jit(solution)/shard_map/dot_general | solution.py:30
  383.2 5.7 collective-permute-done.32
  388.9 9.3 %convert_add_fusion.2 = f32[704,2304]{1,0:T(8,128)S(1)} fusion(bf16[704,2304]{1,0:T(8,128)(2,1)} %collective-permute-done.32, bf16[2304,1536]{1,0:T(8,128)(2,1)} %all-gather.5.cloned.1.call-done.w_ref.tail_w_ref, bf16[1408,1536]{1,0:T(8,128)(2,1)} %hidden_back.1.refs_8_), kind=kOutput, calls=%fused_computation.11 | convolution fusion | flops 4986077184 | bytes 18972672 | tf_op jit(solution)/shard_map/dot_general | solution.py:30
  400.2 18.6 %collective-permute-done.33 = bf16[2,88,2304]{2,1,0:T(8,128)(2,1)S(1)} collective-permute-done((bf16[2,88,2304]{2,1,0:T(8,128)(2,1)S(1)}, bf16[2,88,2304]{2,1,0:T(8,128)(2,1)S(1)}, u32[]{:S(2)}, u32[]{:S(2)}) %collective-permute-start.33) | collective-permute-done | bytes 811040 | tf_op jit(solution)/shard_map/ppermute | solution.py:52
  425.5 7.1 %collective-permute-done.36 = bf16[88,2304]{1,0:T(8,128)(2,1)S(1)} collective-permute-done((bf16[88,2304]{1,0:T(8,128)(2,1)S(1)}, bf16[88,2304]{1,0:T(8,128)(2,1)S(1)}, u32[]{:S(2)}, u32[]{:S(2)}) %collective-permute-start.36) | collective-permute-done | bytes 405536 | tf_op jit(solution)/shard_map/ppermute | solution.py:52
  440.0 16.9 %collective-permute-done.38 = bf16[176,2304]{1,0:T(8,128)(2,1)S(1)} collective-permute-done((bf16[176,2304]{1,0:T(8,128)(2,1)S(1)}, bf16[176,2304]{1,0:T(8,128)(2,1)S(1)}, u32[]{:S(2)}, u32[]{:S(2)}) %collective-permute-start.38) | collective-permute-done | bytes 811040 | tf_op jit(solution)/shard_map/ppermute | solution.py:52
  459.8 6.1 collective-permute-done.39
  466.3 3.3 slice.496
  471.9 3.3 convolution_convert_fusion.5.near_ref
  475.2 4.5 convolution_convert_fusion.4.far_ref
  479.8 25.5 %attention_backward.1.refs_2_ = bf16[1408,1024]{1,0:T(8,128)(2,1)} custom-call(s32[17]{0:T(128)S(1)} %stack.80.info, bf16[1408,1024]{1,0:T(8,128)(2,1)} %copy-done.9, f32[1408,128]{1,0:T(8,128)S(1)} %get-tuple-element.88.cos_ref, f32[1408,128]{1,0:T(8,128)S(1)} %get-tuple-element.89.sin_ref, f32[1408,1408]{1,0:T(8,128)} %fusion.1.bias_ref, ...), custom_call_target="tpu_custom_call" | custom-call | bytes 1024 | tf_op jit(solution)/shard_map/attention_backward/pallas_call | solution.py:372
  505.3 16.0 %weight_grads.5 = bf16[2304,1280]{1,0:T(8,128)(2,1)} custom-call(bf16[704,2304]{1,0:T(8,128)(2,1)} %copy-done.19, bf16[704,2304]{1,0:T(8,128)(2,1)} %collective-permute-done.9.rows_ref.refs_1_, bf16[1408,1024]{1,0:T(8,128)(2,1)} %attention_backward.1.refs_2_, bf16[704,2304]{1,0:T(8,128)(2,1)} %copy-done.25, bf16[704,2304]{1,0:T(8,128)(2,1)} %copy-done.31, ...), custom_call_target="tpu_custom_call" | custom-call | bytes 1024 | tf_op jit(solution)/shard_map/weight_grads/pallas_call | solution.py:555
  529.7 4.5 collective-permute-done.42
  534.3 6.7 %convolution_convert_fusion.1 = bf16[704,2304]{1,0:T(8,128)(2,1)S(1)} fusion(bf16[2304,1280]{1,0:T(8,128)(2,1)} %bitcast.37.w_ref, bf16[1408,1024]{1,0:T(8,128)(2,1)S(1)} %copy-done.22), kind=kOutput, calls=%fused_computation.14 | convolution fusion | flops 3323510784 | bytes 9404416 | tf_op jit(solution)/shard_map/dot_general | solution.py:30
  545.5 3.9 convolution_convert_fusion.2
  555.7 5.9 convert_add_fusion
  564.5 5.3 convert_add_fusion.1
  571.6 11.1 %collective-permute-done.55 = bf16[2,88,2304]{2,1,0:T(8,128)(2,1)S(1)} collective-permute-done((bf16[2,88,2304]{2,1,0:T(8,128)(2,1)S(1)}, bf16[2,88,2304]{2,1,0:T(8,128)(2,1)S(1)}, u32[]{:S(2)}, u32[]{:S(2)}) %collective-permute-start.55) | collective-permute-done | bytes 811040 | tf_op jit(solution)/shard_map/ppermute | solution.py:52
  586.6 13.4 %collective-permute-done.47 = bf16[2,88,2304]{2,1,0:T(8,128)(2,1)S(1)} collective-permute-done((bf16[2,88,2304]{2,1,0:T(8,128)(2,1)S(1)}, bf16[2,88,2304]{2,1,0:T(8,128)(2,1)S(1)}, u32[]{:S(2)}, u32[]{:S(2)}) %collective-permute-start.47) | collective-permute-done | bytes 811040 | tf_op jit(solution)/shard_map/ppermute | solution.py:52
  604.1 6.0 collective-permute-done.56
  626.2 8.8 %reduce-scatter.8.cloned.1.call-done = bf16[576,1280]{1,0:T(8,128)(2,1)} async-done(((bf16[2304,1280]{1,0:T(8,128)(2,1)}), bf16[576,1280]{1,0:T(8,128)(2,1)}) %reduce-scatter.8.cloned.1.call-update) | async-done | bytes 1474576 | tf_op jit(solution)/shard_map/reduce_scatter | solution.py:735
  644.5 10.4 %collective-permute-done.63 = bf16[288,1280]{1,0:T(8,128)(2,1)S(1)} collective-permute-done((bf16[288,1280]{1,0:T(8,128)(2,1)S(1)}, bf16[288,1280]{1,0:T(8,128)(2,1)S(1)}, u32[]{:S(2)}, u32[]{:S(2)}) %collective-permute-start.63) | collective-permute-done | bytes 737312 | tf_op jit(solution)/shard_map/ppermute | solution.py:52
  (387 shorter events, 187.8 us)
Async XLA Ops:
  7.2 126.3 %all-gather.9.cloned.1.call-start = ((), (), s32[]{:S(2)}) async-start(), calls=%async_computation.8 | async-start | bytes 3686400 | tf_op jit(solution)/shard_map/all_gather | solution.py:674
  16.1 34.9 %collective-permute-start.3 = (bf16[288,1280]{1,0:T(8,128)(2,1)}, bf16[288,1280]{1,0:T(8,128)(2,1)}, u32[]{:S(2)}, u32[]{:S(2)}) collective-permute-start(bf16[288,1280]{1,0:T(8,128)(2,1)} %get-tuple-element.183), channel_id=1, source_target_pairs={{0,8},{8,0},{16,24},{24,16},{1,9},{9,1},{17,25},{25,17},{2,10},{10... | collective-permute-start | bytes 2211848 | tf_op jit(solution)/shard_map/ppermute | solution.py:658
  19.1 53.3 %collective-permute-start.4 = (bf16[288,1280]{1,0:T(8,128)(2,1)}, bf16[288,1280]{1,0:T(8,128)(2,1)}, u32[]{:S(2)}, u32[]{:S(2)}) collective-permute-start(bf16[288,1280]{1,0:T(8,128)(2,1)} %get-tuple-element.183), channel_id=1, source_target_pairs={{0,16},{8,24},{16,0},{24,8},{1,17},{9,25},{17,1},{25,9},{2,18},{10... | collective-permute-start | bytes 2211848 | tf_op jit(solution)/shard_map/ppermute | solution.py:658
  21.7 62.4 %collective-permute-start.7 = (bf16[288,1280]{1,0:T(8,128)(2,1)}, bf16[288,1280]{1,0:T(8,128)(2,1)}, u32[]{:S(2)}, u32[]{:S(2)}) collective-permute-start(bf16[288,1280]{1,0:T(8,128)(2,1)} %get-tuple-element.183), channel_id=1, source_target_pairs={{0,24},{8,16},{16,8},{24,0},{1,25},{9,17},{17,9},{25,1},{2,26},{10... | collective-permute-start | bytes 2211848 | tf_op jit(solution)/shard_map/ppermute | solution.py:658
  21.7 18.0 %collective-permute-start = (bf16[288,1280]{1,0:T(8,128)(2,1)}, bf16[288,1280]{1,0:T(8,128)(2,1)}, u32[]{:S(2)}, u32[]{:S(2)}) collective-permute-start(bf16[288,1280]{1,0:T(8,128)(2,1)} %get-tuple-element.184), channel_id=1, source_target_pairs={{0,4},{4,0},{1,5},{5,1},{2,6},{6,2},{3,7},{7,3},{8,12},{12,8},{9,1... | collective-permute-start | bytes 2211848 | tf_op jit(solution)/shard_map/ppermute | solution.py:52
  39.7 32.8 %collective-permute-start.1 = (bf16[176,2304]{1,0:T(8,128)(2,1)S(1)}, bf16[176,2304]{1,0:T(8,128)(2,1)}, u32[]{:S(2)}, u32[]{:S(2)}) collective-permute-start(bf16[176,2304]{1,0:T(8,128)(2,1)S(1)} %fusion.10), channel_id=1, source_target_pairs={{0,4},{4,0},{1,5},{5,1},{2,6},{6,2},{3,7},{7,3},{8,12},{12,8},{9,1... | collective-permute-start | bytes 2433032 | tf_op jit(solution)/shard_map/ppermute | solution.py:52
  41.2 31.3 %collective-permute-start.2 = (bf16[176,2304]{1,0:T(8,128)(2,1)S(1)}, bf16[176,2304]{1,0:T(8,128)(2,1)}, u32[]{:S(2)}, u32[]{:S(2)}) collective-permute-start(bf16[176,2304]{1,0:T(8,128)(2,1)S(1)} %fusion.10), channel_id=1, source_target_pairs={{0,2},{2,0},{1,3},{3,1},{4,6},{6,4},{5,7},{7,5},{8,10},{10,8},{9,1... | collective-permute-start | bytes 2433032 | tf_op jit(solution)/shard_map/ppermute | solution.py:56
  46.4 232.4 %all-gather.5.cloned.1.call-start = ((), (), s32[]{:S(2)}) async-start(), calls=%async_computation.3 | async-start | bytes 8847360 | tf_op jit(solution)/shard_map/all_gather | solution.py:681
  88.8 16.4 %collective-permute-start.8 = (bf16[288,1536]{1,0:T(8,128)(2,1)}, bf16[288,1536]{1,0:T(8,128)(2,1)}, u32[]{:S(2)}, u32[]{:S(2)}) collective-permute-start(bf16[288,1536]{1,0:T(8,128)(2,1)} %concatenate.191), channel_id=1, source_target_pairs={{0,4},{4,0},{1,5},{5,1},{2,6},{6,2},{3,7},{7,3},{8,12},{12,8},{9,1... | collective-permute-start | bytes 2654216 | tf_op jit(solution)/shard_map/ppermute | solution.py:52
  133.5 207.5 %all-gather.7.cloned.1.call-start = ((), (), s32[]{:S(2)}) async-start(), calls=%async_computation.4 | async-start | bytes 3686400 | tf_op jit(solution)/shard_map/all_gather | solution.py:694
  133.7 14.4 %collective-permute-start.9 = (bf16[704,2304]{1,0:T(8,128)(2,1)}, bf16[704,2304]{1,0:T(8,128)(2,1)}, u32[]{:S(2)}, u32[]{:S(2)}) collective-permute-start(bf16[704,2304]{1,0:T(8,128)(2,1)} %copy-done.19), channel_id=1, source_target_pairs={{0,1},{1,0},{2,3},{3,2},{4,5},{5,4},{6,7},{7,6},{8,9},{9,8},{10,11... | collective-permute-start | bytes 9732104 | tf_op jit(solution)/shard_map/ppermute | solution.py:64
  157.5 35.5 %collective-permute-start.19 = (bf16[176,2304]{1,0:T(8,128)(2,1)}, bf16[176,2304]{1,0:T(8,128)(2,1)}, u32[]{:S(2)}, u32[]{:S(2)}) collective-permute-start(bf16[176,2304]{1,0:T(8,128)(2,1)} %get-tuple-element.150), channel_id=1, source_target_pairs={{0,4},{4,0},{1,5},{5,1},{2,6},{6,2},{3,7},{7,3},{8,12},{12,8},{9,1... | collective-permute-start | bytes 2433032 | tf_op jit(solution)/shard_map/ppermute | solution.py:52
  159.1 29.7 %collective-permute-start.23 = (bf16[288,640]{1,0:T(8,128)(2,1)S(1)}, bf16[288,640]{1,0:T(8,128)(2,1)S(1)}, u32[]{:S(2)}, u32[]{:S(2)}) collective-permute-start(bf16[288,640]{1,0:T(8,128)(2,1)S(1)} %slice.575), channel_id=1, source_target_pairs={{0,4},{4,0},{1,5},{5,1},{2,6},{6,2},{3,7},{7,3},{8,12},{12,8},{9,1... | collective-permute-start | bytes 1105928 | tf_op jit(solution)/shard_map/ppermute | solution.py:52
  192.6 230.8 %reduce-scatter.4.cloned.1.call-start = ((), (), s32[]{:S(2)}) async-start(), calls=%async_computation.5 | async-start | bytes 3686400 | tf_op jit(solution)/shard_map/reduce_scatter | solution.py:711
  193.0 21.2 %collective-permute-start.18 = (bf16[176,2304]{1,0:T(8,128)(2,1)}, bf16[176,2304]{1,0:T(8,128)(2,1)S(1)}, u32[]{:S(2)}, u32[]{:S(2)}) collective-permute-start(bf16[176,2304]{1,0:T(8,128)(2,1)} %get-tuple-element.150), channel_id=1, source_target_pairs={{0,2},{2,0},{1,3},{3,1},{4,6},{6,4},{5,7},{7,5},{8,10},{10,8},{9,1... | collective-permute-start | bytes 2433032 | tf_op jit(solution)/shard_map/ppermute | solution.py:56
  195.7 27.2 %collective-permute-start.20 = (bf16[88,2304]{1,0:T(8,128)(2,1)S(1)}, bf16[88,2304]{1,0:T(8,128)(2,1)S(1)}, u32[]{:S(2)}, u32[]{:S(2)}) collective-permute-start(bf16[88,2304]{1,0:T(8,128)(2,1)S(1)} %slice.589), channel_id=1, source_target_pairs={{0,2},{2,0},{1,3},{3,1},{4,6},{6,4},{5,7},{7,5},{8,10},{10,8},{9,1... | collective-permute-start | bytes 1216520 | tf_op jit(solution)/shard_map/ppermute | solution.py:56
  214.3 12.4 %collective-permute-start.21 = (bf16[88,2304]{1,0:T(8,128)(2,1)S(1)}, bf16[88,2304]{1,0:T(8,128)(2,1)S(1)}, u32[]{:S(2)}, u32[]{:S(2)}) collective-permute-start(bf16[88,2304]{1,0:T(8,128)(2,1)S(1)} %slice.590), channel_id=1, source_target_pairs={{0,4},{4,0},{1,5},{5,1},{2,6},{6,2},{3,7},{7,3},{8,12},{12,8},{9,1... | collective-permute-start | bytes 1216520 | tf_op jit(solution)/shard_map/ppermute | solution.py:52
  215.0 26.3 %collective-permute-start.14 = (bf16[2,88,2304]{2,1,0:T(8,128)(2,1)S(1)}, bf16[2,88,2304]{2,1,0:T(8,128)(2,1)S(1)}, u32[]{:S(2)}, u32[]{:S(2)}) collective-permute-start(bf16[2,88,2304]{2,1,0:T(8,128)(2,1)S(1)} %slice_bitcast_fusion.22), channel_id=1, source_target_pairs={{0,4},{4,0},{1,5},{5,1},{2,6},{6,2},{3,7},{7,3},{8,12},{12,8},{9,1... | collective-permute-start | bytes 2433032 | tf_op jit(solution)/shard_map/ppermute | solution.py:52
  216.4 25.0 %collective-permute-start.16 = (bf16[2,88,2304]{2,1,0:T(8,128)(2,1)S(1)}, bf16[2,88,2304]{2,1,0:T(8,128)(2,1)S(1)}, u32[]{:S(2)}, u32[]{:S(2)}) collective-permute-start(bf16[2,88,2304]{2,1,0:T(8,128)(2,1)S(1)} %slice_bitcast_fusion.20), channel_id=1, source_target_pairs={{0,2},{2,0},{1,3},{3,1},{4,6},{6,4},{5,7},{7,5},{8,10},{10,8},{9,1... | collective-permute-start | bytes 2433032 | tf_op jit(solution)/shard_map/ppermute | solution.py:56
  227.4 26.4 %collective-permute-start.22 = (bf16[704,2304]{1,0:T(8,128)(2,1)S(1)}, bf16[704,2304]{1,0:T(8,128)(2,1)S(1)}, u32[]{:S(2)}, u32[]{:S(2)}) collective-permute-start(bf16[704,2304]{1,0:T(8,128)(2,1)S(1)} %get-tuple-element.209.refs_0_.refs_9_), channel_id=1, source_target_pairs={{0,1},{1,0},{2,3},{3,2},{4,5},{5,4},{6,7},{7,6},{8,9},{9,8},{10,11... | collective-permute-start | bytes 9732104 | tf_op jit(solution)/shard_map/ppermute | solution.py:64
  278.8 20.4 %collective-permute-start.24 = (bf16[176,2304]{1,0:T(8,128)(2,1)S(1)}, bf16[176,2304]{1,0:T(8,128)(2,1)S(1)}, u32[]{:S(2)}, u32[]{:S(2)}) collective-permute-start(bf16[176,2304]{1,0:T(8,128)(2,1)S(1)} %multiply_convert_fusion.2.first_ref.refs_0_), channel_id=1, source_target_pairs={{0,4},{4,0},{1,5},{5,1},{2,6},{6,2},{3,7},{7,3},{8,12},{12,8},{9,1... | collective-permute-start | bytes 2433032 | tf_op jit(solution)/shard_map/ppermute | solution.py:52
  280.3 20.1 %collective-permute-start.25 = (bf16[176,2304]{1,0:T(8,128)(2,1)S(1)}, bf16[176,2304]{1,0:T(8,128)(2,1)S(1)}, u32[]{:S(2)}, u32[]{:S(2)}) collective-permute-start(bf16[176,2304]{1,0:T(8,128)(2,1)S(1)} %multiply_convert_fusion.2.first_ref.refs_0_), channel_id=1, source_target_pairs={{0,2},{2,0},{1,3},{3,1},{4,6},{6,4},{5,7},{7,5},{8,10},{10,8},{9,1... | collective-permute-start | bytes 2433032 | tf_op jit(solution)/shard_map/ppermute | solution.py:56
  300.5 13.4 %collective-permute-start.30 = (bf16[176,2304]{1,0:T(8,128)(2,1)S(1)}, bf16[176,2304]{1,0:T(8,128)(2,1)S(1)}, u32[]{:S(2)}, u32[]{:S(2)}) collective-permute-start(bf16[176,2304]{1,0:T(8,128)(2,1)S(1)} %collective-permute-done.25.first_ref.refs_1_), channel_id=1, source_target_pairs={{0,1},{1,0},{2,3},{3,2},{4,5},{5,4},{6,7},{7,6},{8,9},{9,8},{10,11... | collective-permute-start | bytes 2433032 | tf_op jit(solution)/shard_map/ppermute | solution.py:64
  300.6 13.3 %collective-permute-start.31 = (bf16[176,2304]{1,0:T(8,128)(2,1)S(1)}, bf16[176,2304]{1,0:T(8,128)(2,1)S(1)}, u32[]{:S(2)}, u32[]{:S(2)}) collective-permute-start(bf16[176,2304]{1,0:T(8,128)(2,1)S(1)} %collective-permute-done.24.second_ref.refs_2_), channel_id=1, source_target_pairs={{0,1},{1,0},{2,3},{3,2},{4,5},{5,4},{6,7},{7,6},{8,9},{9,8},{10,11... | collective-permute-start | bytes 2433032 | tf_op jit(solution)/shard_map/ppermute | solution.py:64
  301.1 11.4 %collective-permute-start.27 = (bf16[88,2304]{1,0:T(8,128)(2,1)S(1)}, bf16[88,2304]{1,0:T(8,128)(2,1)S(1)}, u32[]{:S(2)}, u32[]{:S(2)}) collective-permute-start(bf16[88,2304]{1,0:T(8,128)(2,1)S(1)} %slice.479), channel_id=1, source_target_pairs={{0,2},{2,0},{1,3},{3,1},{4,6},{6,4},{5,7},{7,5},{8,10},{10,8},{9,1... | collective-permute-start | bytes 1216520 | tf_op jit(solution)/shard_map/ppermute | solution.py:56
  302.6 11.1 %collective-permute-start.28 = (bf16[88,2304]{1,0:T(8,128)(2,1)S(1)}, bf16[88,2304]{1,0:T(8,128)(2,1)S(1)}, u32[]{:S(2)}, u32[]{:S(2)}) collective-permute-start(bf16[88,2304]{1,0:T(8,128)(2,1)S(1)} %slice.480), channel_id=1, source_target_pairs={{0,4},{4,0},{1,5},{5,1},{2,6},{6,2},{3,7},{7,3},{8,12},{12,8},{9,1... | collective-permute-start | bytes 1216520 | tf_op jit(solution)/shard_map/ppermute | solution.py:52
  341.0 182.2 %reduce-scatter.6.cloned.1.call-start = ((), (), s32[]{:S(2)}) async-start(), calls=%async_computation.6 | async-start | bytes 8847360 | tf_op jit(solution)/shard_map/reduce_scatter | solution.py:721
  383.2 251.8 %reduce-scatter.8.cloned.1.call-start = ((), (), s32[]{:S(2)}) async-start(), calls=%async_computation.7 | async-start | bytes 7372800 | tf_op jit(solution)/shard_map/reduce_scatter | solution.py:735
  398.4 20.4 %collective-permute-start.33 = (bf16[2,88,2304]{2,1,0:T(8,128)(2,1)S(1)}, bf16[2,88,2304]{2,1,0:T(8,128)(2,1)S(1)}, u32[]{:S(2)}, u32[]{:S(2)}) collective-permute-start(bf16[2,88,2304]{2,1,0:T(8,128)(2,1)S(1)} %slice_bitcast_fusion.18), channel_id=1, source_target_pairs={{0,4},{4,0},{1,5},{5,1},{2,6},{6,2},{3,7},{7,3},{8,12},{12,8},{9,1... | collective-permute-start | bytes 2433032 | tf_op jit(solution)/shard_map/ppermute | solution.py:52
  399.3 20.0 %collective-permute-start.35 = (bf16[2,88,2304]{2,1,0:T(8,128)(2,1)S(1)}, bf16[2,88,2304]{2,1,0:T(8,128)(2,1)S(1)}, u32[]{:S(2)}, u32[]{:S(2)}) collective-permute-start(bf16[2,88,2304]{2,1,0:T(8,128)(2,1)S(1)} %slice_bitcast_fusion.17), channel_id=1, source_target_pairs={{0,2},{2,0},{1,3},{3,1},{4,6},{6,4},{5,7},{7,5},{8,10},{10,8},{9,1... | collective-permute-start | bytes 2433032 | tf_op jit(solution)/shard_map/ppermute | solution.py:56
  438.7 18.2 %collective-permute-start.38 = (bf16[176,2304]{1,0:T(8,128)(2,1)S(1)}, bf16[176,2304]{1,0:T(8,128)(2,1)S(1)}, u32[]{:S(2)}, u32[]{:S(2)}) collective-permute-start(bf16[176,2304]{1,0:T(8,128)(2,1)S(1)} %get-tuple-element.147), channel_id=1, source_target_pairs={{0,4},{4,0},{1,5},{5,1},{2,6},{6,2},{3,7},{7,3},{8,12},{12,8},{9,1... | collective-permute-start | bytes 2433032 | tf_op jit(solution)/shard_map/ppermute | solution.py:52
  439.3 18.3 %collective-permute-start.37 = (bf16[176,2304]{1,0:T(8,128)(2,1)S(1)}, bf16[176,2304]{1,0:T(8,128)(2,1)S(1)}, u32[]{:S(2)}, u32[]{:S(2)}) collective-permute-start(bf16[176,2304]{1,0:T(8,128)(2,1)S(1)} %get-tuple-element.147), channel_id=1, source_target_pairs={{0,2},{2,0},{1,3},{3,1},{4,6},{6,4},{5,7},{7,5},{8,10},{10,8},{9,1... | collective-permute-start | bytes 2433032 | tf_op jit(solution)/shard_map/ppermute | solution.py:56
  470.4 72.4 %collective-permute-start.66 = (bf16[288,640]{1,0:T(8,128)(2,1)}, bf16[288,640]{1,0:T(8,128)(2,1)S(1)}, u32[]{:S(2)}, u32[]{:S(2)}) collective-permute-start(bf16[288,640]{1,0:T(8,128)(2,1)} %get-tuple-element.196), channel_id=1, source_target_pairs={{0,4},{4,0},{1,5},{5,1},{2,6},{6,2},{3,7},{7,3},{8,12},{12,8},{9,1... | collective-permute-start | bytes 1105928 | tf_op jit(solution)/shard_map/ppermute | solution.py:52
  528.9 20.7 %collective-permute-start.65 = (bf16[288,1280]{1,0:T(8,128)(2,1)}, bf16[288,1280]{1,0:T(8,128)(2,1)}, u32[]{:S(2)}, u32[]{:S(2)}) collective-permute-start(bf16[288,1280]{1,0:T(8,128)(2,1)} %get-tuple-element.174), channel_id=1, source_target_pairs={{0,4},{4,0},{1,5},{5,1},{2,6},{6,2},{3,7},{7,3},{8,12},{12,8},{9,1... | collective-permute-start | bytes 2211848 | tf_op jit(solution)/shard_map/ppermute | solution.py:52
  541.2 13.5 %collective-permute-start.51 = (bf16[176,2304]{1,0:T(8,128)(2,1)S(1)}, bf16[176,2304]{1,0:T(8,128)(2,1)S(1)}, u32[]{:S(2)}, u32[]{:S(2)}) collective-permute-start(bf16[176,2304]{1,0:T(8,128)(2,1)S(1)} %get-tuple-element.161), channel_id=1, source_target_pairs={{0,1},{1,0},{2,3},{3,2},{4,5},{5,4},{6,7},{7,6},{8,9},{9,8},{10,11... | collective-permute-start | bytes 2433032 | tf_op jit(solution)/shard_map/ppermute | solution.py:64
  541.3 13.9 %collective-permute-start.52 = (bf16[176,2304]{1,0:T(8,128)(2,1)S(1)}, bf16[176,2304]{1,0:T(8,128)(2,1)S(1)}, u32[]{:S(2)}, u32[]{:S(2)}) collective-permute-start(bf16[176,2304]{1,0:T(8,128)(2,1)S(1)} %get-tuple-element.164), channel_id=1, source_target_pairs={{0,1},{1,0},{2,3},{3,2},{4,5},{5,4},{6,7},{7,6},{8,9},{9,8},{10,11... | collective-permute-start | bytes 2433032 | tf_op jit(solution)/shard_map/ppermute | solution.py:64
  541.8 13.5 %collective-permute-start.53 = (bf16[176,2304]{1,0:T(8,128)(2,1)S(1)}, bf16[176,2304]{1,0:T(8,128)(2,1)S(1)}, u32[]{:S(2)}, u32[]{:S(2)}) collective-permute-start(bf16[176,2304]{1,0:T(8,128)(2,1)S(1)} %get-tuple-element.163), channel_id=1, source_target_pairs={{0,1},{1,0},{2,3},{3,2},{4,5},{5,4},{6,7},{7,6},{8,9},{9,8},{10,11... | collective-permute-start | bytes 2433032 | tf_op jit(solution)/shard_map/ppermute | solution.py:64
  542.8 12.9 %collective-permute-start.54 = (bf16[176,2304]{1,0:T(8,128)(2,1)S(1)}, bf16[176,2304]{1,0:T(8,128)(2,1)S(1)}, u32[]{:S(2)}, u32[]{:S(2)}) collective-permute-start(bf16[176,2304]{1,0:T(8,128)(2,1)S(1)} %get-tuple-element.162), channel_id=1, source_target_pairs={{0,1},{1,0},{2,3},{3,2},{4,5},{5,4},{6,7},{7,6},{8,9},{9,8},{10,11... | collective-permute-start | bytes 2433032 | tf_op jit(solution)/shard_map/ppermute | solution.py:64
  549.6 13.3 %collective-permute-start.43 = (bf16[176,2304]{1,0:T(8,128)(2,1)S(1)}, bf16[176,2304]{1,0:T(8,128)(2,1)S(1)}, u32[]{:S(2)}, u32[]{:S(2)}) collective-permute-start(bf16[176,2304]{1,0:T(8,128)(2,1)S(1)} %get-tuple-element.165), channel_id=1, source_target_pairs={{0,1},{1,0},{2,3},{3,2},{4,5},{5,4},{6,7},{7,6},{8,9},{9,8},{10,11... | collective-permute-start | bytes 2433032 | tf_op jit(solution)/shard_map/ppermute | solution.py:64
  561.6 21.0 %collective-permute-start.55 = (bf16[2,88,2304]{2,1,0:T(8,128)(2,1)S(1)}, bf16[2,88,2304]{2,1,0:T(8,128)(2,1)S(1)}, u32[]{:S(2)}, u32[]{:S(2)}) collective-permute-start(bf16[2,88,2304]{2,1,0:T(8,128)(2,1)S(1)} %slice_bitcast_fusion.11), channel_id=1, source_target_pairs={{0,4},{4,0},{1,5},{5,1},{2,6},{6,2},{3,7},{7,3},{8,12},{12,8},{9,1... | collective-permute-start | bytes 2433032 | tf_op jit(solution)/shard_map/ppermute | solution.py:52
  563.0 21.0 %collective-permute-start.57 = (bf16[2,88,2304]{2,1,0:T(8,128)(2,1)S(1)}, bf16[2,88,2304]{2,1,0:T(8,128)(2,1)S(1)}, u32[]{:S(2)}, u32[]{:S(2)}) collective-permute-start(bf16[2,88,2304]{2,1,0:T(8,128)(2,1)S(1)} %slice_bitcast_fusion.9), channel_id=1, source_target_pairs={{0,2},{2,0},{1,3},{3,1},{4,6},{6,4},{5,7},{7,5},{8,10},{10,8},{9,1... | collective-permute-start | bytes 2433032 | tf_op jit(solution)/shard_map/ppermute | solution.py:56
  569.9 30.1 %collective-permute-start.47 = (bf16[2,88,2304]{2,1,0:T(8,128)(2,1)S(1)}, bf16[2,88,2304]{2,1,0:T(8,128)(2,1)S(1)}, u32[]{:S(2)}, u32[]{:S(2)}) collective-permute-start(bf16[2,88,2304]{2,1,0:T(8,128)(2,1)S(1)} %slice_bitcast_fusion.15), channel_id=1, source_target_pairs={{0,4},{4,0},{1,5},{5,1},{2,6},{6,2},{3,7},{7,3},{8,12},{12,8},{9,1... | collective-permute-start | bytes 2433032 | tf_op jit(solution)/shard_map/ppermute | solution.py:52
  570.6 30.7 %collective-permute-start.49 = (bf16[2,88,2304]{2,1,0:T(8,128)(2,1)S(1)}, bf16[2,88,2304]{2,1,0:T(8,128)(2,1)S(1)}, u32[]{:S(2)}, u32[]{:S(2)}) collective-permute-start(bf16[2,88,2304]{2,1,0:T(8,128)(2,1)S(1)} %slice_bitcast_fusion.13), channel_id=1, source_target_pairs={{0,2},{2,0},{1,3},{3,1},{4,6},{6,4},{5,7},{7,5},{8,10},{10,8},{9,1... | collective-permute-start | bytes 2433032 | tf_op jit(solution)/shard_map/ppermute | solution.py:56
  584.4 25.6 %collective-permute-start.56 = (bf16[88,2304]{1,0:T(8,128)(2,1)S(1)}, bf16[88,2304]{1,0:T(8,128)(2,1)S(1)}, u32[]{:S(2)}, u32[]{:S(2)}) collective-permute-start(bf16[88,2304]{1,0:T(8,128)(2,1)S(1)} %fusion.54), channel_id=1, source_target_pairs={{0,2},{2,0},{1,3},{3,1},{4,6},{6,4},{5,7},{7,5},{8,10},{10,8},{9,1... | collective-permute-start | bytes 1216520 | tf_op jit(solution)/shard_map/ppermute | solution.py:56
  586.0 24.2 %collective-permute-start.58 = (bf16[88,2304]{1,0:T(8,128)(2,1)S(1)}, bf16[88,2304]{1,0:T(8,128)(2,1)S(1)}, u32[]{:S(2)}, u32[]{:S(2)}) collective-permute-start(bf16[88,2304]{1,0:T(8,128)(2,1)S(1)} %fusion.55), channel_id=1, source_target_pairs={{0,4},{4,0},{1,5},{5,1},{2,6},{6,2},{3,7},{7,3},{8,12},{12,8},{9,1... | collective-permute-start | bytes 1216520 | tf_op jit(solution)/shard_map/ppermute | solution.py:52
  601.8 17.1 %collective-permute-start.48 = (bf16[88,2304]{1,0:T(8,128)(2,1)S(1)}, bf16[88,2304]{1,0:T(8,128)(2,1)S(1)}, u32[]{:S(2)}, u32[]{:S(2)}) collective-permute-start(bf16[88,2304]{1,0:T(8,128)(2,1)S(1)} %fusion.52), channel_id=1, source_target_pairs={{0,2},{2,0},{1,3},{3,1},{4,6},{6,4},{5,7},{7,5},{8,10},{10,8},{9,1... | collective-permute-start | bytes 1216520 | tf_op jit(solution)/shard_map/ppermute | solution.py:56
  603.4 19.9 %collective-permute-start.50 = (bf16[88,2304]{1,0:T(8,128)(2,1)S(1)}, bf16[88,2304]{1,0:T(8,128)(2,1)S(1)}, u32[]{:S(2)}, u32[]{:S(2)}) collective-permute-start(bf16[88,2304]{1,0:T(8,128)(2,1)S(1)} %fusion.53), channel_id=1, source_target_pairs={{0,4},{4,0},{1,5},{5,1},{2,6},{6,2},{3,7},{7,3},{8,12},{12,8},{9,1... | collective-permute-start | bytes 1216520 | tf_op jit(solution)/shard_map/ppermute | solution.py:52
  636.5 18.3 %collective-permute-start.63 = (bf16[288,1280]{1,0:T(8,128)(2,1)S(1)}, bf16[288,1280]{1,0:T(8,128)(2,1)S(1)}, u32[]{:S(2)}, u32[]{:S(2)}) collective-permute-start(bf16[288,1280]{1,0:T(8,128)(2,1)S(1)} %get-tuple-element.182), channel_id=1, source_target_pairs={{0,4},{4,0},{1,5},{5,1},{2,6},{6,2},{3,7},{7,3},{8,12},{12,8},{9,1... | collective-permute-start | bytes 2211848 | tf_op jit(solution)/shard_map/ppermute | solution.py:52
  (78 other events, 601.4 us)
Sparse Core Ops, SparseCore 0:
  46.5 86.9 all-gather.8
  135.6 143.0 all-gather.4
  280.9 58.4 all-gather.6
  341.6 55.8 reduce-scatter.3
  399.8 123.3 reduce-scatter.5
  529.6 105.2 reduce-scatter.7

commit v6 on v5

--- a/solution.py
+++ b/solution.py
@@ -339,6 +339,7 @@
     place(lambda here: dv_ref[here, :], v_lanes, False)
 
 
+FREE = pl.CostEstimate(flops=0, bytes_accessed=1024, transcendentals=0)
 SMEM_SPEC = pl.BlockSpec(memory_space=pltpu.SMEM)
 VMEM_SPEC = pl.BlockSpec(memory_space=pltpu.VMEM)
 
@@ -389,11 +390,42 @@
     )(info, rotated, cosine, sine, bias, mixed, near, far, log_total)
 
 
+def pack_kernel(info, q_ref, k_ref, v_ref, o_ref, mine_ref, theirs_ref):
+    count, cols = q_ref.shape
+    own = cols // (2 * HEAD_DIM) * HEAD_DIM
+    fields = [q_ref[...], k_ref[...], v_ref[...], o_ref[...].astype(f32).T.astype(bf16)]
+    lower = info[8] == 0
+    for n, field in enumerate(fields):
+        lanes = pl.ds((n if n < 3 else 3 + 1) * own, own)
+        first, second = field[:, :own], field[:, own : 2 * own]
+        mine_ref[:, lanes] = jnp.where(lower, first, second)
+        theirs_ref[:, lanes] = jnp.where(lower, second, first)
+    for n in range(2):
+        left, right = fields[2 * n][:, 2 * own :], fields[2 * n + 1][:, 2 * own :]
+        shared = jnp.concatenate([left.astype(f32), right.astype(f32)], axis=1).astype(bf16)
+        lanes = pl.ds(3 * own + n * LANES, LANES)
+        mine_ref[:, lanes] = shared
+        theirs_ref[:, lanes] = shared
+
+
+def pack_heads(info, w_query, w_key, w_value, w_out):
+    count, cols = w_query.shape
+    shape = jax.ShapeDtypeStruct((count, 10 * LANES), bf16)
+    return pl.pallas_call(
+        pack_kernel,
+        out_shape=(shape, shape),
+        in_specs=[SMEM_SPEC] + [VMEM_SPEC] * 4,
+        out_specs=(VMEM_SPEC, VMEM_SPEC),
+        compiler_params=pltpu.CompilerParams(vmem_limit_bytes=24 << 20),
+        cost_estimate=FREE,
+        name="pack_heads",
+    )(info, w_query, w_key, w_value, w_out)
+
+
 def whole(shape):
     return pl.BlockSpec(shape, lambda i: (0,) * len(shape), pipeline_mode=pl.Buffered(1))
 
 
-FREE = pl.CostEstimate(flops=0, bytes_accessed=1024, transcendentals=0)
 ROOMY = pltpu.CompilerParams(vmem_limit_bytes=52 << 20)
 
 
@@ -473,10 +505,10 @@
     count, depth = rows.shape
     width, cols = down_w.shape[1], gate_up.shape[1]
     tail = cols - 2 * width
-    tile = count // 4
+    tile = count // 2
     return pl.pallas_call(
         functools.partial(hidden_back_kernel, size),
-        grid=(4,),
+        grid=(2,),
         out_shape=jax.ShapeDtypeStruct((count, cols), bf16),
         in_specs=[
             pl.BlockSpec((tile, depth), lambda i: (i, 0)),
@@ -607,16 +639,7 @@
         got = flip_x(theirs)
         return jnp.where(lower_x, jnp.concatenate([mine, got], 0), jnp.concatenate([got, mine], 0))
 
-    out_t = w_out.T
-    a_cols = [w[:, :own_cols] for w in (w_query, w_key, w_value, out_t)]
-    b_cols = [w[:, own_cols : 2 * own_cols] for w in (w_query, w_key, w_value, out_t)]
-    s_cols = [w[:, 2 * own_cols :] for w in (w_query, w_key, w_value, out_t)]
-
-    def pack(cols):
-        return jnp.concatenate(cols[:3] + s_cols + cols[3:], axis=1)
-
-    attn_a, attn_b = pack(a_cols), pack(b_cols)
-    attn_mine, attn_theirs = jnp.where(lower_x, attn_a, attn_b), jnp.where(lower_x, attn_b, attn_a)
+    attn_mine, attn_theirs = pack_heads(info, w_query, w_key, w_value, w_out)
 
     def halves(weight):
         first, second = weight[:, :ff_half], weight[:, ff_half:]

time: 674 us -> 668 us (level)
    concatenate x8 -> x0, local copies, waits for them, and re-layouts: 9.13 us -> none  [pack(): return jnp.concatenate(cols[:3] + s_cols + cols[3:], axis=1)]
    unnamed x118 -> x115, local copies, waits for them, and re-layouts: 18.8 us -> 25.6 us
    pallas_call x1 -> x2, Pallas kernels: 13.1 us -> 14.9 us  [the longest x1 14.1 us: hidden_back(): pl.pallas_call(functools.partial(hidden_back_kernel, size), grid=(2,), ou...]
  transfers between devices with their start and end apart: 73 -> 73, of which waited for: 39 -> 38; matrix products, arithmetic and copies ran while one was open for 23% -> 23% of each run, Pallas kernels for 23% -> 23%
where the time goes in v6:
time: 668 us; the launch traced here: 660 us
  waiting for transfers between devices  257 us (38%)
  Pallas kernels  152 us (23%)
  local copies, waits for them, and re-layouts  63.3 us (9%)
  starting transfers between devices  61.5 us (9%)
  matrix products  58.4 us (9%)
  other arithmetic  52.4 us (8%)
  between operations  15.7 us (2%)
    ppermute x24, waiting for transfers between devices, flip_x(): return lax.ppermute(field, 'ctx', [(0, 1), (1, 0)])  125 us
    dot_general x10, matrix products, dot(): return lax.dot_general(left, right, dims, preferred_element_type=f32)  58.4 us
    ppermute x17, waiting for transfers between devices, flip_y(): return lax.ppermute(field, 'mp', [(0, 2), (2, 0), (1, 3), (3, 1)])  44.8 us
    pallas_call x3, Pallas kernels, weight_grads(): pl.pallas_call(functools.partial(grads_kernel, place, counts), grid=(dept...  43.1 us
    pallas_call x4, Pallas kernels, gate_blocks(): pl.pallas_call(functools.partial(gate_kernel, size), grid=(2,), out_shape...  30.2 us
    pallas_call x1, Pallas kernels, attention_backward(): pl.pallas_call(backward_kernel, out_shape=jax.ShapeDtypeStruct((slot, 8 *...  25.7 us
    ppermute x24, starting transfers between devices, flip_x(): return lax.ppermute(field, 'ctx', [(0, 1), (1, 0)])  25.7 us
    unnamed x115, local copies, waits for them, and re-layouts  25.6 us
  transfers between devices with their start and end apart: 73, of which 38 were waited for; matrix products, arithmetic and copies ran while one was open for 23% of the time, Pallas kernels for 23%

profile of v6, /device:TPU:0, one launch (start us, length us, event | category | flops | bytes accessed | tf_op | source)
XLA Modules:
  0.0 660.5 jit_solution(5788971415990387640)
XLA Ops:
  21.3 3.8 fusion.56
  25.1 6.2 fusion.1.bias_ref
  42.9 4.5 pad_maximum_fusion.9
  48.3 20.7 %collective-permute-done.4 = bf16[288,1280]{1,0:T(8,128)(2,1)} collective-permute-done((bf16[288,1280]{1,0:T(8,128)(2,1)S(1)}, bf16[288,1280]{1,0:T(8,128)(2,1)}, u32[]{:S(2)}, u32[]{:S(2)}) %collective-permute-start.4) | collective-permute-done | bytes 737312 | tf_op jit(solution)/shard_map/ppermute | solution.py:681
  93.4 7.5 %collective-permute-done.8 = bf16[288,1536]{1,0:T(8,128)(2,1)} collective-permute-done((bf16[288,1536]{1,0:T(8,128)(2,1)}, bf16[288,1536]{1,0:T(8,128)(2,1)}, u32[]{:S(2)}, u32[]{:S(2)}) %collective-permute-start.8) | collective-permute-done | bytes 884768 | tf_op jit(solution)/shard_map/ppermute | solution.py:52
  100.9 3.2 maximum_select_fusion
  104.1 25.6 %all-gather.9.cloned.1.call-done = bf16[1152,1280]{1,0:T(8,128)(2,1)} async-done(((bf16[288,1280]{1,0:T(8,128)(2,1)}), bf16[1152,1280]{1,0:T(8,128)(2,1)}) %all-gather.9.cloned.1.call-update) | async-done | bytes 2949136 | tf_op jit(solution)/shard_map/all_gather | solution.py:697
  132.6 3.7 bitcast_dynamic-update-slice_fusion
  136.3 8.0 %project_half.2.refs_0_ = f32[1408,1024]{1,0:T(8,128)} custom-call(bf16[704,2304]{1,0:T(8,128)(2,1)} %constant_dynamic-update-slice_fusion.rows_ref.refs_0_, bf16[2304,1280]{1,0:T(8,128)(2,1)} %bitcast.24.w_ref), custom_call_target="tpu_custom_call" | custom-call | bytes 1024 | tf_op jit(solution)/shard_map/project_half/pallas_call | solution.py:535
  144.3 8.0 %project_half.3.qkv_ref = f32[1408,1024]{1,0:T(8,128)} custom-call(bf16[704,2304]{1,0:T(8,128)(2,1)} %collective-permute-done.9.rows_ref.refs_1_, bf16[2304,1280]{1,0:T(8,128)(2,1)} %bitcast.24.w_ref, f32[1408,1024]{1,0:T(8,128)} %project_half.2.refs_0_), custom_call_target="tpu_custom_call", output_to_operand_aliasing={{}: (2, {})} | custom-call | bytes 1024 | tf_op jit(solution)/shard_map/project_half/pallas_call | solution.py:535
  155.7 22.2 %attention_forward.1 = (bf16[1408,1024]{1,0:T(8,128)(2,1)S(1)}, bf16[1408,384]{1,0:T(8,128)(2,1)S(1)}, f32[3,8,2816]{2,1,0:T(8,128)S(1)}) custom-call(s32[17]{0:T(128)S(1)} %stack.80.info, f32[1408,1024]{1,0:T(8,128)} %project_half.3.qkv_ref, f32[1408,128]{1,0:T(8,128)S(1)} %get-tuple-element.92.cos_ref, f32[1408,128]{1,0:T(8,128)S(1)} %get-tuple-element.93.sin_ref, ...), custom_call_target="tpu_custom_call" | custom-call | bytes 1024 | tf_op jit(solution)/shard_map/attention_forward/pallas_call | solution.py:350
  177.9 4.7 convolution_convert_fusion
  192.4 4.8 convert_add_fusion.3
  197.4 13.0 %collective-permute-done.18 = bf16[176,2304]{1,0:T(8,128)(2,1)S(1)} collective-permute-done((bf16[176,2304]{1,0:T(8,128)(2,1)}, bf16[176,2304]{1,0:T(8,128)(2,1)S(1)}, u32[]{:S(2)}, u32[]{:S(2)}) %collective-permute-start.18) | collective-permute-done | bytes 811040 | tf_op jit(solution)/shard_map/ppermute | solution.py:56
  223.6 13.9 %collective-permute-done.14 = bf16[2,88,2304]{2,1,0:T(8,128)(2,1)S(1)} collective-permute-done((bf16[2,88,2304]{2,1,0:T(8,128)(2,1)S(1)}, bf16[2,88,2304]{2,1,0:T(8,128)(2,1)S(1)}, u32[]{:S(2)}, u32[]{:S(2)}) %collective-permute-start.14) | collective-permute-done | bytes 811040 | tf_op jit(solution)/shard_map/ppermute | solution.py:52
  240.2 6.6 collective-permute-done.15
  253.7 21.1 %all-gather.5.cloned.1.call-done.w_ref.tail_w_ref = bf16[2304,1536]{1,0:T(8,128)(2,1)} async-done(((bf16[576,1536]{1,0:T(8,128)(2,1)}), bf16[2304,1536]{1,0:T(8,128)(2,1)}) %all-gather.5.cloned.1.call-update) | async-done | bytes 7077904 | tf_op jit(solution)/shard_map/all_gather | solution.py:704
  278.7 7.6 %gate_blocks.4 = (f32[1408,1536]{1,0:T(8,128)}, bf16[1408,640]{1,0:T(8,128)(2,1)}, bf16[1408,256]{1,0:T(8,128)(2,1)S(1)}) custom-call(bf16[176,2304]{1,0:T(8,128)(2,1)S(1)} %multiply_convert_fusion.2.first_ref.refs_0_, bf16[176,2304]{1,0:T(8,128)(2,1)} %copy-done.39, bf16[2304,1536]{1,0:T(8,128)(2,1)} %all-gather.5.cloned.1.call-done.w_ref.tail_w_ref), custom_call_target="tpu_custom_call" | custom-call | flops 4982833152 | bytes 1024 | tf_op jit(solution)/shard_map/gate_blocks/pallas_call | solution.py:463
  286.3 9.0 %collective-permute-done.24.second_ref.refs_2_ = bf16[176,2304]{1,0:T(8,128)(2,1)S(1)} collective-permute-done((bf16[176,2304]{1,0:T(8,128)(2,1)S(1)}, bf16[176,2304]{1,0:T(8,128)(2,1)S(1)}, u32[]{:S(2)}, u32[]{:S(2)}) %collective-permute-start.24) | collective-permute-done | bytes 811040 | tf_op jit(solution)/shard_map/ppermute | solution.py:52
  299.2 7.5 %gate_blocks.5 = (f32[1408,1536]{1,0:T(8,128)}, bf16[1408,640]{1,0:T(8,128)(2,1)}, bf16[1408,256]{1,0:T(8,128)(2,1)S(1)}) custom-call(bf16[176,2304]{1,0:T(8,128)(2,1)S(1)} %collective-permute-done.25.first_ref.refs_1_, bf16[176,2304]{1,0:T(8,128)(2,1)} %copy-done.26, ...), custom_call_target="tpu_custom_call", output_to_operand_aliasing={{0}: (3, {}), {1}: (4, {}), {2}: (5, {})} | custom-call | flops 4982833152 | bytes 1024 | tf_op jit(solution)/shard_map/gate_blocks/pallas_call | solution.py:463
  311.0 7.6 %gate_blocks.6 = (f32[1408,1536]{1,0:T(8,128)}, bf16[1408,640]{1,0:T(8,128)(2,1)}, bf16[1408,256]{1,0:T(8,128)(2,1)S(1)}) custom-call(bf16[176,2304]{1,0:T(8,128)(2,1)S(1)} %collective-permute-done.30.first_ref.refs_5_, bf16[176,2304]{1,0:T(8,128)(2,1)} %copy-done.29, ...), custom_call_target="tpu_custom_call", output_to_operand_aliasing={{0}: (3, {}), {1}: (4, {}), {2}: (5, {})} | custom-call | flops 4982833152 | bytes 1024 | tf_op jit(solution)/shard_map/gate_blocks/pallas_call | solution.py:463
  319.5 7.5 %gate_blocks.7 = (f32[1408,1536]{1,0:T(8,128)}, bf16[1408,640]{1,0:T(8,128)(2,1)}, bf16[1408,256]{1,0:T(8,128)(2,1)S(1)}) custom-call(bf16[176,2304]{1,0:T(8,128)(2,1)S(1)} %pad_maximum_fusion.5.first_ref.refs_3_, bf16[176,2304]{1,0:T(8,128)(2,1)} %copy-done.30, ...), custom_call_target="tpu_custom_call", output_to_operand_aliasing={{0}: (3, {}), {1}: (4, {}), {2}: (5, {})} | custom-call | flops 4982833152 | bytes 1024 | tf_op jit(solution)/shard_map/gate_blocks/pallas_call | solution.py:463
  328.5 8.5 %weight_grads.3 = bf16[2304,640]{1,0:T(8,128)(2,1)} custom-call(bf16[704,2304]{1,0:T(8,128)(2,1)} %copy-done.21, bf16[704,2304]{1,0:T(8,128)(2,1)} %copy-done.16, bf16[1408,640]{1,0:T(8,128)(2,1)S(1)} %copy-done), custom_call_target="tpu_custom_call" | custom-call | bytes 1024 | tf_op jit(solution)/shard_map/weight_grads/pallas_call | solution.py:587
  337.1 14.1 %hidden_back.1.refs_8_ = bf16[1408,1536]{1,0:T(8,128)(2,1)} custom-call(bf16[1408,2304]{1,0:T(8,128)(2,1)} %constant_dynamic-update-slice_fusion.10.rows_ref, bf16[2304,640]{1,0:T(8,128)(2,1)} %all-gather.7.cloned.1.call-done.w_ref, bf16[2304,1536]{1,0:T(8,128)(2,1)} %all-gather.5.cloned.1.call-done.w_ref.tail_w_ref, f32[1408,1536]{1,0:T(8,128)} %get-tuple-element.124.gate_up_ref), custom_call_target="tpu_custom_call" | custom-call | bytes 1024 | tf_op jit(solution)/shard_map/hidden_back/pallas_call | solution.py:509
  351.3 18.5 %weight_grads.4 = bf16[2304,1536]{1,0:T(8,128)(2,1)} custom-call(bf16[176,2304]{1,0:T(8,128)(2,1)S(1)} %copy-done.7, bf16[176,2304]{1,0:T(8,128)(2,1)} %copy-done.3, bf16[176,2304]{1,0:T(8,128)(2,1)} %copy-done.26, bf16[176,2304]{1,0:T(8,128)(2,1)} %copy-done.2, bf16[176,2304]{1,0:T(8,128)(2,1)} %copy-done.39, bf16[176,2304]{1,0:T(8,128)(2,1)} %copy-done.8, ...), custom_call_target="tpu_custom_call" | custom-call | bytes 1024 | tf_op jit(solution)/shard_map/weight_grads/pallas_call | solution.py:587
  369.8 10.0 %convolution_convert_fusion.3 = bf16[704,2304]{1,0:T(8,128)(2,1)} fusion(bf16[2304,1536]{1,0:T(8,128)(2,1)} %all-gather.5.cloned.1.call-done.w_ref.tail_w_ref, bf16[1408,1536]{1,0:T(8,128)(2,1)} %hidden_back.1.refs_8_), kind=kOutput, calls=%fused_computation.16 | convolution fusion | flops 4984455168 | bytes 12484608 | tf_op jit(solution)/shard_map/dot_general | solution.py:30
  380.3 5.7 collective-permute-done.32
  385.9 9.5 %convert_add_fusion.2 = f32[704,2304]{1,0:T(8,128)S(1)} fusion(bf16[704,2304]{1,0:T(8,128)(2,1)} %collective-permute-done.32, bf16[2304,1536]{1,0:T(8,128)(2,1)} %all-gather.5.cloned.1.call-done.w_ref.tail_w_ref, bf16[1408,1536]{1,0:T(8,128)(2,1)} %hidden_back.1.refs_8_), kind=kOutput, calls=%fused_computation.11 | convolution fusion | flops 4986077184 | bytes 18972672 | tf_op jit(solution)/shard_map/dot_general | solution.py:30
  396.9 19.2 %collective-permute-done.33 = bf16[2,88,2304]{2,1,0:T(8,128)(2,1)S(1)} collective-permute-done((bf16[2,88,2304]{2,1,0:T(8,128)(2,1)S(1)}, bf16[2,88,2304]{2,1,0:T(8,128)(2,1)S(1)}, u32[]{:S(2)}, u32[]{:S(2)}) %collective-permute-start.33) | collective-permute-done | bytes 811040 | tf_op jit(solution)/shard_map/ppermute | solution.py:52
  422.5 7.5 %collective-permute-done.36 = bf16[88,2304]{1,0:T(8,128)(2,1)S(1)} collective-permute-done((bf16[88,2304]{1,0:T(8,128)(2,1)S(1)}, bf16[88,2304]{1,0:T(8,128)(2,1)S(1)}, u32[]{:S(2)}, u32[]{:S(2)}) %collective-permute-start.36) | collective-permute-done | bytes 405536 | tf_op jit(solution)/shard_map/ppermute | solution.py:52
  437.0 17.4 %collective-permute-done.38 = bf16[176,2304]{1,0:T(8,128)(2,1)S(1)} collective-permute-done((bf16[176,2304]{1,0:T(8,128)(2,1)S(1)}, bf16[176,2304]{1,0:T(8,128)(2,1)S(1)}, u32[]{:S(2)}, u32[]{:S(2)}) %collective-permute-start.38) | collective-permute-done | bytes 811040 | tf_op jit(solution)/shard_map/ppermute | solution.py:52
  456.8 6.7 %collective-permute-done.39 = bf16[88,2304]{1,0:T(8,128)(2,1)S(1)} collective-permute-done((bf16[88,2304]{1,0:T(8,128)(2,1)S(1)}, bf16[88,2304]{1,0:T(8,128)(2,1)S(1)}, u32[]{:S(2)}, u32[]{:S(2)}) %collective-permute-start.39) | collective-permute-done | bytes 405536 | tf_op jit(solution)/shard_map/ppermute | solution.py:56
  463.7 3.3 slice.448
  469.1 3.3 convolution_convert_fusion.5.near_ref
  472.4 4.5 convolution_convert_fusion.4.far_ref
  477.0 25.7 %attention_backward.1.refs_2_ = bf16[1408,1024]{1,0:T(8,128)(2,1)} custom-call(s32[17]{0:T(128)S(1)} %stack.80.info, bf16[1408,1024]{1,0:T(8,128)(2,1)} %copy-done.9, f32[1408,128]{1,0:T(8,128)S(1)} %get-tuple-element.92.cos_ref, f32[1408,128]{1,0:T(8,128)S(1)} %get-tuple-element.93.sin_ref, f32[1408,1408]{1,0:T(8,128)} %fusion.1.bias_ref, ...), custom_call_target="tpu_custom_call" | custom-call | bytes 1024 | tf_op jit(solution)/shard_map/attention_backward/pallas_call | solution.py:373
  502.7 16.0 %weight_grads.5 = bf16[2304,1280]{1,0:T(8,128)(2,1)} custom-call(bf16[704,2304]{1,0:T(8,128)(2,1)} %constant_dynamic-update-slice_fusion.rows_ref.refs_0_, bf16[704,2304]{1,0:T(8,128)(2,1)} %collective-permute-done.9.rows_ref.refs_1_, bf16[1408,1024]{1,0:T(8,128)(2,1)} %attention_backward.1.refs_2_, bf16[704,2304]{1,0:T(8,128)(2,1)} %copy-done.27, ...), custom_call_target="tpu_custom_call" | custom-call | bytes 1024 | tf_op jit(solution)/shard_map/weight_grads/pallas_call | solution.py:587
  524.3 4.3 collective-permute-done.42
  528.6 6.5 convolution_convert_fusion.1
  540.0 3.8 convolution_convert_fusion.2
  550.4 5.8 convert_add_fusion
  559.3 5.3 convert_add_fusion.1
  566.3 11.0 %collective-permute-done.55 = bf16[2,88,2304]{2,1,0:T(8,128)(2,1)S(1)} collective-permute-done((bf16[2,88,2304]{2,1,0:T(8,128)(2,1)S(1)}, bf16[2,88,2304]{2,1,0:T(8,128)(2,1)S(1)}, u32[]{:S(2)}, u32[]{:S(2)}) %collective-permute-start.55) | collective-permute-done | bytes 811040 | tf_op jit(solution)/shard_map/ppermute | solution.py:52
  581.4 13.3 %collective-permute-done.47 = bf16[2,88,2304]{2,1,0:T(8,128)(2,1)S(1)} collective-permute-done((bf16[2,88,2304]{2,1,0:T(8,128)(2,1)S(1)}, bf16[2,88,2304]{2,1,0:T(8,128)(2,1)S(1)}, u32[]{:S(2)}, u32[]{:S(2)}) %collective-permute-start.47) | collective-permute-done | bytes 811040 | tf_op jit(solution)/shard_map/ppermute | solution.py:52
  598.8 6.0 collective-permute-done.56
  609.9 3.2 collective-permute-done.60
  621.4 8.1 %reduce-scatter.8.cloned.1.call-done = bf16[576,1280]{1,0:T(8,128)(2,1)} async-done(((bf16[2304,1280]{1,0:T(8,128)(2,1)}), bf16[576,1280]{1,0:T(8,128)(2,1)}) %reduce-scatter.8.cloned.1.call-update) | async-done | bytes 1474576 | tf_op jit(solution)/shard_map/reduce_scatter | solution.py:758
  638.9 10.4 %collective-permute-done.63 = bf16[288,1280]{1,0:T(8,128)(2,1)S(1)} collective-permute-done((bf16[288,1280]{1,0:T(8,128)(2,1)S(1)}, bf16[288,1280]{1,0:T(8,128)(2,1)S(1)}, u32[]{:S(2)}, u32[]{:S(2)}) %collective-permute-start.63) | collective-permute-done | bytes 737312 | tf_op jit(solution)/shard_map/ppermute | solution.py:52
  (375 shorter events, 180.5 us)
Async XLA Ops:
  7.2 122.4 %all-gather.9.cloned.1.call-start = ((), (), s32[]{:S(2)}) async-start(), calls=%async_computation.8 | async-start | bytes 3686400 | tf_op jit(solution)/shard_map/all_gather | solution.py:697
  12.5 35.9 %collective-permute-start.3 = (bf16[288,1280]{1,0:T(8,128)(2,1)S(1)}, bf16[288,1280]{1,0:T(8,128)(2,1)}, u32[]{:S(2)}, u32[]{:S(2)}) collective-permute-start(bf16[288,1280]{1,0:T(8,128)(2,1)S(1)} %get-tuple-element.78), channel_id=1, source_target_pairs={{0,8},{8,0},{16,24},{24,16},{1,9},{9,1},{17,25},{25,17},{2,10},{10... | collective-permute-start | bytes 2211848 | tf_op jit(solution)/shard_map/ppermute | solution.py:681
  15.5 53.5 %collective-permute-start.4 = (bf16[288,1280]{1,0:T(8,128)(2,1)S(1)}, bf16[288,1280]{1,0:T(8,128)(2,1)}, u32[]{:S(2)}, u32[]{:S(2)}) collective-permute-start(bf16[288,1280]{1,0:T(8,128)(2,1)S(1)} %get-tuple-element.78), channel_id=1, source_target_pairs={{0,16},{8,24},{16,0},{24,8},{1,17},{9,25},{17,1},{25,9},{2,18},{10... | collective-permute-start | bytes 2211848 | tf_op jit(solution)/shard_map/ppermute | solution.py:681
  18.1 63.9 %collective-permute-start.7 = (bf16[288,1280]{1,0:T(8,128)(2,1)S(1)}, bf16[288,1280]{1,0:T(8,128)(2,1)}, u32[]{:S(2)}, u32[]{:S(2)}) collective-permute-start(bf16[288,1280]{1,0:T(8,128)(2,1)S(1)} %get-tuple-element.78), channel_id=1, source_target_pairs={{0,24},{8,16},{16,8},{24,0},{1,25},{9,17},{17,9},{25,1},{2,26},{10... | collective-permute-start | bytes 2211848 | tf_op jit(solution)/shard_map/ppermute | solution.py:681
  18.1 17.8 %collective-permute-start = (bf16[288,1280]{1,0:T(8,128)(2,1)S(1)}, bf16[288,1280]{1,0:T(8,128)(2,1)}, u32[]{:S(2)}, u32[]{:S(2)}) collective-permute-start(bf16[288,1280]{1,0:T(8,128)(2,1)S(1)} %get-tuple-element.76), channel_id=1, source_target_pairs={{0,4},{4,0},{1,5},{5,1},{2,6},{6,2},{3,7},{7,3},{8,12},{12,8},{9,1... | collective-permute-start | bytes 2211848 | tf_op jit(solution)/shard_map/ppermute | solution.py:52
  35.9 33.1 %collective-permute-start.1 = (bf16[176,2304]{1,0:T(8,128)(2,1)}, bf16[176,2304]{1,0:T(8,128)(2,1)}, u32[]{:S(2)}, u32[]{:S(2)}) collective-permute-start(bf16[176,2304]{1,0:T(8,128)(2,1)} %fusion.10), channel_id=1, source_target_pairs={{0,4},{4,0},{1,5},{5,1},{2,6},{6,2},{3,7},{7,3},{8,12},{12,8},{9,1... | collective-permute-start | bytes 2433032 | tf_op jit(solution)/shard_map/ppermute | solution.py:52
  37.4 31.6 %collective-permute-start.2 = (bf16[176,2304]{1,0:T(8,128)(2,1)}, bf16[176,2304]{1,0:T(8,128)(2,1)}, u32[]{:S(2)}, u32[]{:S(2)}) collective-permute-start(bf16[176,2304]{1,0:T(8,128)(2,1)} %fusion.10), channel_id=1, source_target_pairs={{0,2},{2,0},{1,3},{3,1},{4,6},{6,4},{5,7},{7,5},{8,10},{10,8},{9,1... | collective-permute-start | bytes 2433032 | tf_op jit(solution)/shard_map/ppermute | solution.py:56
  42.9 232.0 %all-gather.5.cloned.1.call-start = ((), (), s32[]{:S(2)}) async-start(), calls=%async_computation.3 | async-start | bytes 8847360 | tf_op jit(solution)/shard_map/all_gather | solution.py:704
  86.4 14.5 %collective-permute-start.8 = (bf16[288,1536]{1,0:T(8,128)(2,1)}, bf16[288,1536]{1,0:T(8,128)(2,1)}, u32[]{:S(2)}, u32[]{:S(2)}) collective-permute-start(bf16[288,1536]{1,0:T(8,128)(2,1)} %concatenate.141), channel_id=1, source_target_pairs={{0,4},{4,0},{1,5},{5,1},{2,6},{6,2},{3,7},{7,3},{8,12},{12,8},{9,1... | collective-permute-start | bytes 2654216 | tf_op jit(solution)/shard_map/ppermute | solution.py:52
  129.7 207.5 %all-gather.7.cloned.1.call-start = ((), (), s32[]{:S(2)}) async-start(), calls=%async_computation.4 | async-start | bytes 3686400 | tf_op jit(solution)/shard_map/all_gather | solution.py:717
  129.9 14.4 %collective-permute-start.9 = (bf16[704,2304]{1,0:T(8,128)(2,1)}, bf16[704,2304]{1,0:T(8,128)(2,1)}, u32[]{:S(2)}, u32[]{:S(2)}) collective-permute-start(bf16[704,2304]{1,0:T(8,128)(2,1)} %constant_dynamic-update-slice_fusion.rows_ref.refs_0_), channel_id=1, source_target_pairs={{0,1},{1,0},{2,3},{3,2},{4,5},{5,4},{6,7},{7,6},{8,9},{9,8},{10,11... | collective-permute-start | bytes 9732104 | tf_op jit(solution)/shard_map/ppermute | solution.py:64
  153.7 35.5 %collective-permute-start.19 = (bf16[176,2304]{1,0:T(8,128)(2,1)}, bf16[176,2304]{1,0:T(8,128)(2,1)}, u32[]{:S(2)}, u32[]{:S(2)}) collective-permute-start(bf16[176,2304]{1,0:T(8,128)(2,1)} %get-tuple-element.154), channel_id=1, source_target_pairs={{0,4},{4,0},{1,5},{5,1},{2,6},{6,2},{3,7},{7,3},{8,12},{12,8},{9,1... | collective-permute-start | bytes 2433032 | tf_op jit(solution)/shard_map/ppermute | solution.py:52
  155.1 29.9 %collective-permute-start.23 = (bf16[288,640]{1,0:T(8,128)(2,1)S(1)}, bf16[288,640]{1,0:T(8,128)(2,1)S(1)}, u32[]{:S(2)}, u32[]{:S(2)}) collective-permute-start(bf16[288,640]{1,0:T(8,128)(2,1)S(1)} %slice.524), channel_id=1, source_target_pairs={{0,4},{4,0},{1,5},{5,1},{2,6},{6,2},{3,7},{7,3},{8,12},{12,8},{9,1... | collective-permute-start | bytes 1105928 | tf_op jit(solution)/shard_map/ppermute | solution.py:52
  188.7 231.9 %reduce-scatter.4.cloned.1.call-start = ((), (), s32[]{:S(2)}) async-start(), calls=%async_computation.5 | async-start | bytes 3686400 | tf_op jit(solution)/shard_map/reduce_scatter | solution.py:734
  189.2 21.2 %collective-permute-start.18 = (bf16[176,2304]{1,0:T(8,128)(2,1)}, bf16[176,2304]{1,0:T(8,128)(2,1)S(1)}, u32[]{:S(2)}, u32[]{:S(2)}) collective-permute-start(bf16[176,2304]{1,0:T(8,128)(2,1)} %get-tuple-element.154), channel_id=1, source_target_pairs={{0,2},{2,0},{1,3},{3,1},{4,6},{6,4},{5,7},{7,5},{8,10},{10,8},{9,1... | collective-permute-start | bytes 2433032 | tf_op jit(solution)/shard_map/ppermute | solution.py:56
  191.9 27.2 %collective-permute-start.20 = (bf16[88,2304]{1,0:T(8,128)(2,1)S(1)}, bf16[88,2304]{1,0:T(8,128)(2,1)S(1)}, u32[]{:S(2)}, u32[]{:S(2)}) collective-permute-start(bf16[88,2304]{1,0:T(8,128)(2,1)S(1)} %slice.538), channel_id=1, source_target_pairs={{0,2},{2,0},{1,3},{3,1},{4,6},{6,4},{5,7},{7,5},{8,10},{10,8},{9,1... | collective-permute-start | bytes 1216520 | tf_op jit(solution)/shard_map/ppermute | solution.py:56
  210.4 12.4 %collective-permute-start.21 = (bf16[88,2304]{1,0:T(8,128)(2,1)S(1)}, bf16[88,2304]{1,0:T(8,128)(2,1)S(1)}, u32[]{:S(2)}, u32[]{:S(2)}) collective-permute-start(bf16[88,2304]{1,0:T(8,128)(2,1)S(1)} %slice.539), channel_id=1, source_target_pairs={{0,4},{4,0},{1,5},{5,1},{2,6},{6,2},{3,7},{7,3},{8,12},{12,8},{9,1... | collective-permute-start | bytes 1216520 | tf_op jit(solution)/shard_map/ppermute | solution.py:52
  211.1 26.4 %collective-permute-start.14 = (bf16[2,88,2304]{2,1,0:T(8,128)(2,1)S(1)}, bf16[2,88,2304]{2,1,0:T(8,128)(2,1)S(1)}, u32[]{:S(2)}, u32[]{:S(2)}) collective-permute-start(bf16[2,88,2304]{2,1,0:T(8,128)(2,1)S(1)} %slice_bitcast_fusion.22), channel_id=1, source_target_pairs={{0,4},{4,0},{1,5},{5,1},{2,6},{6,2},{3,7},{7,3},{8,12},{12,8},{9,1... | collective-permute-start | bytes 2433032 | tf_op jit(solution)/shard_map/ppermute | solution.py:52
  212.5 25.0 %collective-permute-start.16 = (bf16[2,88,2304]{2,1,0:T(8,128)(2,1)S(1)}, bf16[2,88,2304]{2,1,0:T(8,128)(2,1)S(1)}, u32[]{:S(2)}, u32[]{:S(2)}) collective-permute-start(bf16[2,88,2304]{2,1,0:T(8,128)(2,1)S(1)} %slice_bitcast_fusion.20), channel_id=1, source_target_pairs={{0,2},{2,0},{1,3},{3,1},{4,6},{6,4},{5,7},{7,5},{8,10},{10,8},{9,1... | collective-permute-start | bytes 2433032 | tf_op jit(solution)/shard_map/ppermute | solution.py:56
  223.6 26.5 %collective-permute-start.22 = (bf16[704,2304]{1,0:T(8,128)(2,1)S(1)}, bf16[704,2304]{1,0:T(8,128)(2,1)S(1)}, u32[]{:S(2)}, u32[]{:S(2)}) collective-permute-start(bf16[704,2304]{1,0:T(8,128)(2,1)S(1)} %get-tuple-element.211.refs_0_.refs_9_), channel_id=1, source_target_pairs={{0,1},{1,0},{2,3},{3,2},{4,5},{5,4},{6,7},{7,6},{8,9},{9,8},{10,11... | collective-permute-start | bytes 9732104 | tf_op jit(solution)/shard_map/ppermute | solution.py:64
  274.9 20.4 %collective-permute-start.24 = (bf16[176,2304]{1,0:T(8,128)(2,1)S(1)}, bf16[176,2304]{1,0:T(8,128)(2,1)S(1)}, u32[]{:S(2)}, u32[]{:S(2)}) collective-permute-start(bf16[176,2304]{1,0:T(8,128)(2,1)S(1)} %multiply_convert_fusion.2.first_ref.refs_0_), channel_id=1, source_target_pairs={{0,4},{4,0},{1,5},{5,1},{2,6},{6,2},{3,7},{7,3},{8,12},{12,8},{9,1... | collective-permute-start | bytes 2433032 | tf_op jit(solution)/shard_map/ppermute | solution.py:52
  276.3 20.1 %collective-permute-start.25 = (bf16[176,2304]{1,0:T(8,128)(2,1)S(1)}, bf16[176,2304]{1,0:T(8,128)(2,1)S(1)}, u32[]{:S(2)}, u32[]{:S(2)}) collective-permute-start(bf16[176,2304]{1,0:T(8,128)(2,1)S(1)} %multiply_convert_fusion.2.first_ref.refs_0_), channel_id=1, source_target_pairs={{0,2},{2,0},{1,3},{3,1},{4,6},{6,4},{5,7},{7,5},{8,10},{10,8},{9,1... | collective-permute-start | bytes 2433032 | tf_op jit(solution)/shard_map/ppermute | solution.py:56
  296.5 13.4 %collective-permute-start.30 = (bf16[176,2304]{1,0:T(8,128)(2,1)S(1)}, bf16[176,2304]{1,0:T(8,128)(2,1)S(1)}, u32[]{:S(2)}, u32[]{:S(2)}) collective-permute-start(bf16[176,2304]{1,0:T(8,128)(2,1)S(1)} %collective-permute-done.25.first_ref.refs_1_), channel_id=1, source_target_pairs={{0,1},{1,0},{2,3},{3,2},{4,5},{5,4},{6,7},{7,6},{8,9},{9,8},{10,11... | collective-permute-start | bytes 2433032 | tf_op jit(solution)/shard_map/ppermute | solution.py:64
  296.6 13.3 %collective-permute-start.31 = (bf16[176,2304]{1,0:T(8,128)(2,1)S(1)}, bf16[176,2304]{1,0:T(8,128)(2,1)S(1)}, u32[]{:S(2)}, u32[]{:S(2)}) collective-permute-start(bf16[176,2304]{1,0:T(8,128)(2,1)S(1)} %collective-permute-done.24.second_ref.refs_2_), channel_id=1, source_target_pairs={{0,1},{1,0},{2,3},{3,2},{4,5},{5,4},{6,7},{7,6},{8,9},{9,8},{10,11... | collective-permute-start | bytes 2433032 | tf_op jit(solution)/shard_map/ppermute | solution.py:64
  297.2 11.4 %collective-permute-start.27 = (bf16[88,2304]{1,0:T(8,128)(2,1)S(1)}, bf16[88,2304]{1,0:T(8,128)(2,1)S(1)}, u32[]{:S(2)}, u32[]{:S(2)}) collective-permute-start(bf16[88,2304]{1,0:T(8,128)(2,1)S(1)} %slice.431), channel_id=1, source_target_pairs={{0,2},{2,0},{1,3},{3,1},{4,6},{6,4},{5,7},{7,5},{8,10},{10,8},{9,1... | collective-permute-start | bytes 1216520 | tf_op jit(solution)/shard_map/ppermute | solution.py:56
  298.7 11.1 %collective-permute-start.28 = (bf16[88,2304]{1,0:T(8,128)(2,1)S(1)}, bf16[88,2304]{1,0:T(8,128)(2,1)S(1)}, u32[]{:S(2)}, u32[]{:S(2)}) collective-permute-start(bf16[88,2304]{1,0:T(8,128)(2,1)S(1)} %slice.432), channel_id=1, source_target_pairs={{0,4},{4,0},{1,5},{5,1},{2,6},{6,2},{3,7},{7,3},{8,12},{12,8},{9,1... | collective-permute-start | bytes 1216520 | tf_op jit(solution)/shard_map/ppermute | solution.py:52
  337.1 182.2 %reduce-scatter.6.cloned.1.call-start = ((), (), s32[]{:S(2)}) async-start(), calls=%async_computation.6 | async-start | bytes 8847360 | tf_op jit(solution)/shard_map/reduce_scatter | solution.py:744
  380.2 249.3 %reduce-scatter.8.cloned.1.call-start = ((), (), s32[]{:S(2)}) async-start(), calls=%async_computation.7 | async-start | bytes 7372800 | tf_op jit(solution)/shard_map/reduce_scatter | solution.py:758
  395.7 20.5 %collective-permute-start.33 = (bf16[2,88,2304]{2,1,0:T(8,128)(2,1)S(1)}, bf16[2,88,2304]{2,1,0:T(8,128)(2,1)S(1)}, u32[]{:S(2)}, u32[]{:S(2)}) collective-permute-start(bf16[2,88,2304]{2,1,0:T(8,128)(2,1)S(1)} %slice_bitcast_fusion.18), channel_id=1, source_target_pairs={{0,4},{4,0},{1,5},{5,1},{2,6},{6,2},{3,7},{7,3},{8,12},{12,8},{9,1... | collective-permute-start | bytes 2433032 | tf_op jit(solution)/shard_map/ppermute | solution.py:52
  396.3 20.0 %collective-permute-start.35 = (bf16[2,88,2304]{2,1,0:T(8,128)(2,1)S(1)}, bf16[2,88,2304]{2,1,0:T(8,128)(2,1)S(1)}, u32[]{:S(2)}, u32[]{:S(2)}) collective-permute-start(bf16[2,88,2304]{2,1,0:T(8,128)(2,1)S(1)} %slice_bitcast_fusion.17), channel_id=1, source_target_pairs={{0,2},{2,0},{1,3},{3,1},{4,6},{6,4},{5,7},{7,5},{8,10},{10,8},{9,1... | collective-permute-start | bytes 2433032 | tf_op jit(solution)/shard_map/ppermute | solution.py:56
  436.0 18.3 %collective-permute-start.38 = (bf16[176,2304]{1,0:T(8,128)(2,1)S(1)}, bf16[176,2304]{1,0:T(8,128)(2,1)S(1)}, u32[]{:S(2)}, u32[]{:S(2)}) collective-permute-start(bf16[176,2304]{1,0:T(8,128)(2,1)S(1)} %get-tuple-element.151), channel_id=1, source_target_pairs={{0,4},{4,0},{1,5},{5,1},{2,6},{6,2},{3,7},{7,3},{8,12},{12,8},{9,1... | collective-permute-start | bytes 2433032 | tf_op jit(solution)/shard_map/ppermute | solution.py:52
  436.6 18.4 %collective-permute-start.37 = (bf16[176,2304]{1,0:T(8,128)(2,1)S(1)}, bf16[176,2304]{1,0:T(8,128)(2,1)S(1)}, u32[]{:S(2)}, u32[]{:S(2)}) collective-permute-start(bf16[176,2304]{1,0:T(8,128)(2,1)S(1)} %get-tuple-element.151), channel_id=1, source_target_pairs={{0,2},{2,0},{1,3},{3,1},{4,6},{6,4},{5,7},{7,5},{8,10},{10,8},{9,1... | collective-permute-start | bytes 2433032 | tf_op jit(solution)/shard_map/ppermute | solution.py:56
  467.8 69.1 %collective-permute-start.66 = (bf16[288,640]{1,0:T(8,128)(2,1)}, bf16[288,640]{1,0:T(8,128)(2,1)}, u32[]{:S(2)}, u32[]{:S(2)}) collective-permute-start(bf16[288,640]{1,0:T(8,128)(2,1)} %get-tuple-element.198), channel_id=1, source_target_pairs={{0,4},{4,0},{1,5},{5,1},{2,6},{6,2},{3,7},{7,3},{8,12},{12,8},{9,1... | collective-permute-start | bytes 1105928 | tf_op jit(solution)/shard_map/ppermute | solution.py:52
  523.4 20.7 %collective-permute-start.65 = (bf16[288,1280]{1,0:T(8,128)(2,1)S(1)}, bf16[288,1280]{1,0:T(8,128)(2,1)}, u32[]{:S(2)}, u32[]{:S(2)}) collective-permute-start(bf16[288,1280]{1,0:T(8,128)(2,1)S(1)} %get-tuple-element.178), channel_id=1, source_target_pairs={{0,4},{4,0},{1,5},{5,1},{2,6},{6,2},{3,7},{7,3},{8,12},{12,8},{9,1... | collective-permute-start | bytes 2211848 | tf_op jit(solution)/shard_map/ppermute | solution.py:52
  535.3 14.5 %collective-permute-start.51 = (bf16[176,2304]{1,0:T(8,128)(2,1)S(1)}, bf16[176,2304]{1,0:T(8,128)(2,1)S(1)}, u32[]{:S(2)}, u32[]{:S(2)}) collective-permute-start(bf16[176,2304]{1,0:T(8,128)(2,1)S(1)} %get-tuple-element.165), channel_id=1, source_target_pairs={{0,1},{1,0},{2,3},{3,2},{4,5},{5,4},{6,7},{7,6},{8,9},{9,8},{10,11... | collective-permute-start | bytes 2433032 | tf_op jit(solution)/shard_map/ppermute | solution.py:64
  535.4 14.5 %collective-permute-start.52 = (bf16[176,2304]{1,0:T(8,128)(2,1)S(1)}, bf16[176,2304]{1,0:T(8,128)(2,1)S(1)}, u32[]{:S(2)}, u32[]{:S(2)}) collective-permute-start(bf16[176,2304]{1,0:T(8,128)(2,1)S(1)} %get-tuple-element.168), channel_id=1, source_target_pairs={{0,1},{1,0},{2,3},{3,2},{4,5},{5,4},{6,7},{7,6},{8,9},{9,8},{10,11... | collective-permute-start | bytes 2433032 | tf_op jit(solution)/shard_map/ppermute | solution.py:64
  535.9 14.5 %collective-permute-start.53 = (bf16[176,2304]{1,0:T(8,128)(2,1)S(1)}, bf16[176,2304]{1,0:T(8,128)(2,1)S(1)}, u32[]{:S(2)}, u32[]{:S(2)}) collective-permute-start(bf16[176,2304]{1,0:T(8,128)(2,1)S(1)} %get-tuple-element.167), channel_id=1, source_target_pairs={{0,1},{1,0},{2,3},{3,2},{4,5},{5,4},{6,7},{7,6},{8,9},{9,8},{10,11... | collective-permute-start | bytes 2433032 | tf_op jit(solution)/shard_map/ppermute | solution.py:64
  536.9 13.5 %collective-permute-start.54 = (bf16[176,2304]{1,0:T(8,128)(2,1)S(1)}, bf16[176,2304]{1,0:T(8,128)(2,1)S(1)}, u32[]{:S(2)}, u32[]{:S(2)}) collective-permute-start(bf16[176,2304]{1,0:T(8,128)(2,1)S(1)} %get-tuple-element.166), channel_id=1, source_target_pairs={{0,1},{1,0},{2,3},{3,2},{4,5},{5,4},{6,7},{7,6},{8,9},{9,8},{10,11... | collective-permute-start | bytes 2433032 | tf_op jit(solution)/shard_map/ppermute | solution.py:64
  544.1 13.6 %collective-permute-start.43 = (bf16[176,2304]{1,0:T(8,128)(2,1)S(1)}, bf16[176,2304]{1,0:T(8,128)(2,1)S(1)}, u32[]{:S(2)}, u32[]{:S(2)}) collective-permute-start(bf16[176,2304]{1,0:T(8,128)(2,1)S(1)} %get-tuple-element.169), channel_id=1, source_target_pairs={{0,1},{1,0},{2,3},{3,2},{4,5},{5,4},{6,7},{7,6},{8,9},{9,8},{10,11... | collective-permute-start | bytes 2433032 | tf_op jit(solution)/shard_map/ppermute | solution.py:64
  556.4 20.9 %collective-permute-start.55 = (bf16[2,88,2304]{2,1,0:T(8,128)(2,1)S(1)}, bf16[2,88,2304]{2,1,0:T(8,128)(2,1)S(1)}, u32[]{:S(2)}, u32[]{:S(2)}) collective-permute-start(bf16[2,88,2304]{2,1,0:T(8,128)(2,1)S(1)} %slice_bitcast_fusion.11), channel_id=1, source_target_pairs={{0,4},{4,0},{1,5},{5,1},{2,6},{6,2},{3,7},{7,3},{8,12},{12,8},{9,1... | collective-permute-start | bytes 2433032 | tf_op jit(solution)/shard_map/ppermute | solution.py:52
  557.7 21.0 %collective-permute-start.57 = (bf16[2,88,2304]{2,1,0:T(8,128)(2,1)S(1)}, bf16[2,88,2304]{2,1,0:T(8,128)(2,1)S(1)}, u32[]{:S(2)}, u32[]{:S(2)}) collective-permute-start(bf16[2,88,2304]{2,1,0:T(8,128)(2,1)S(1)} %slice_bitcast_fusion.9), channel_id=1, source_target_pairs={{0,2},{2,0},{1,3},{3,1},{4,6},{6,4},{5,7},{7,5},{8,10},{10,8},{9,1... | collective-permute-start | bytes 2433032 | tf_op jit(solution)/shard_map/ppermute | solution.py:56
  564.7 30.0 %collective-permute-start.47 = (bf16[2,88,2304]{2,1,0:T(8,128)(2,1)S(1)}, bf16[2,88,2304]{2,1,0:T(8,128)(2,1)S(1)}, u32[]{:S(2)}, u32[]{:S(2)}) collective-permute-start(bf16[2,88,2304]{2,1,0:T(8,128)(2,1)S(1)} %slice_bitcast_fusion.15), channel_id=1, source_target_pairs={{0,4},{4,0},{1,5},{5,1},{2,6},{6,2},{3,7},{7,3},{8,12},{12,8},{9,1... | collective-permute-start | bytes 2433032 | tf_op jit(solution)/shard_map/ppermute | solution.py:52
  565.4 30.7 %collective-permute-start.49 = (bf16[2,88,2304]{2,1,0:T(8,128)(2,1)S(1)}, bf16[2,88,2304]{2,1,0:T(8,128)(2,1)S(1)}, u32[]{:S(2)}, u32[]{:S(2)}) collective-permute-start(bf16[2,88,2304]{2,1,0:T(8,128)(2,1)S(1)} %slice_bitcast_fusion.13), channel_id=1, source_target_pairs={{0,2},{2,0},{1,3},{3,1},{4,6},{6,4},{5,7},{7,5},{8,10},{10,8},{9,1... | collective-permute-start | bytes 2433032 | tf_op jit(solution)/shard_map/ppermute | solution.py:56
  579.1 25.6 %collective-permute-start.56 = (bf16[88,2304]{1,0:T(8,128)(2,1)S(1)}, bf16[88,2304]{1,0:T(8,128)(2,1)S(1)}, u32[]{:S(2)}, u32[]{:S(2)}) collective-permute-start(bf16[88,2304]{1,0:T(8,128)(2,1)S(1)} %fusion.54), channel_id=1, source_target_pairs={{0,2},{2,0},{1,3},{3,1},{4,6},{6,4},{5,7},{7,5},{8,10},{10,8},{9,1... | collective-permute-start | bytes 1216520 | tf_op jit(solution)/shard_map/ppermute | solution.py:56
  580.7 24.1 %collective-permute-start.58 = (bf16[88,2304]{1,0:T(8,128)(2,1)S(1)}, bf16[88,2304]{1,0:T(8,128)(2,1)S(1)}, u32[]{:S(2)}, u32[]{:S(2)}) collective-permute-start(bf16[88,2304]{1,0:T(8,128)(2,1)S(1)} %fusion.55), channel_id=1, source_target_pairs={{0,4},{4,0},{1,5},{5,1},{2,6},{6,2},{3,7},{7,3},{8,12},{12,8},{9,1... | collective-permute-start | bytes 1216520 | tf_op jit(solution)/shard_map/ppermute | solution.py:52
  596.6 17.5 %collective-permute-start.48 = (bf16[88,2304]{1,0:T(8,128)(2,1)S(1)}, bf16[88,2304]{1,0:T(8,128)(2,1)S(1)}, u32[]{:S(2)}, u32[]{:S(2)}) collective-permute-start(bf16[88,2304]{1,0:T(8,128)(2,1)S(1)} %fusion.52), channel_id=1, source_target_pairs={{0,2},{2,0},{1,3},{3,1},{4,6},{6,4},{5,7},{7,5},{8,10},{10,8},{9,1... | collective-permute-start | bytes 1216520 | tf_op jit(solution)/shard_map/ppermute | solution.py:56
  598.2 20.3 %collective-permute-start.50 = (bf16[88,2304]{1,0:T(8,128)(2,1)S(1)}, bf16[88,2304]{1,0:T(8,128)(2,1)S(1)}, u32[]{:S(2)}, u32[]{:S(2)}) collective-permute-start(bf16[88,2304]{1,0:T(8,128)(2,1)S(1)} %fusion.53), channel_id=1, source_target_pairs={{0,4},{4,0},{1,5},{5,1},{2,6},{6,2},{3,7},{7,3},{8,12},{12,8},{9,1... | collective-permute-start | bytes 1216520 | tf_op jit(solution)/shard_map/ppermute | solution.py:52
  630.9 18.3 %collective-permute-start.63 = (bf16[288,1280]{1,0:T(8,128)(2,1)S(1)}, bf16[288,1280]{1,0:T(8,128)(2,1)S(1)}, u32[]{:S(2)}, u32[]{:S(2)}) collective-permute-start(bf16[288,1280]{1,0:T(8,128)(2,1)S(1)} %get-tuple-element.186), channel_id=1, source_target_pairs={{0,4},{4,0},{1,5},{5,1},{2,6},{6,2},{3,7},{7,3},{8,12},{12,8},{9,1... | collective-permute-start | bytes 2211848 | tf_op jit(solution)/shard_map/ppermute | solution.py:52
  (76 other events, 597.2 us)
Sparse Core Ops, SparseCore 0:
  43.0 86.6 all-gather.8
  131.8 142.9 all-gather.4
  277.0 58.4 all-gather.6
  337.6 55.8 reduce-scatter.3
  395.8 123.3 reduce-scatter.5
  524.2 105.2 reduce-scatter.7

commit v7 on v6

--- a/solution.py
+++ b/solution.py
@@ -757,7 +757,7 @@
     grad_attn, grad_gu, d_qkv, hidden = after(grad_attn, grad_gu, d_qkv, hidden)
     grad_attn = lax.psum_scatter(grad_attn, "dp", scatter_dimension=0, tiled=True)
     tail_mine, tail_got = rows_of_x(grad_gu[:, 2 * ff_main :])
-    tail_got, d_qkv, hidden = after(tail_got, d_qkv, hidden)
+    tail_got, d_qkv, hidden, grad_gu = after(tail_got, d_qkv, hidden, grad_gu)
     gu_mine, gu_got = rows_of_x(grad_gu[:, : 2 * ff_main])
     d_normed_attn = sum_rows(d_qkv, qkv_w, NT, pieces=4)
     back_attn, gain_attn_part = norm_back(inputs, gain_a, d_normed_attn)

time: 668 us -> 666 us (level)
  transfers between devices with their start and end apart: 73 -> 73, of which waited for: 38 -> 39; matrix products, arithmetic and copies ran while one was open for 23% -> 23% of each run, Pallas kernels for 23% -> 23%
where the time goes in v7:
time: 666 us; the launch traced here: 658 us
  waiting for transfers between devices  256 us (38%)
  Pallas kernels  152 us (23%)
  local copies, waits for them, and re-layouts  63 us (9%)
  starting transfers between devices  62.1 us (9%)
  matrix products  58.2 us (9%)
  other arithmetic  50.6 us (8%)
  between operations  15.7 us (2%)
    ppermute x24, waiting for transfers between devices, flip_x(): return lax.ppermute(field, 'ctx', [(0, 1), (1, 0)])  125 us
    dot_general x10, matrix products, dot(): return lax.dot_general(left, right, dims, preferred_element_type=f32)  58.2 us
    ppermute x17, waiting for transfers between devices, flip_y(): return lax.ppermute(field, 'mp', [(0, 2), (2, 0), (1, 3), (3, 1)])  44.8 us
    pallas_call x3, Pallas kernels, weight_grads(): pl.pallas_call(functools.partial(grads_kernel, place, counts), grid=(dept...  43.1 us
    pallas_call x4, Pallas kernels, gate_blocks(): pl.pallas_call(functools.partial(gate_kernel, size), grid=(2,), out_shape...  30.2 us
    ppermute x24, starting transfers between devices, flip_x(): return lax.ppermute(field, 'ctx', [(0, 1), (1, 0)])  26.7 us
    unnamed x115, local copies, waits for them, and re-layouts  26.4 us
    pallas_call x1, Pallas kernels, attention_backward(): pl.pallas_call(backward_kernel, out_shape=jax.ShapeDtypeStruct((slot, 8 *...  25.7 us
  transfers between devices with their start and end apart: 73, of which 39 were waited for; matrix products, arithmetic and copies ran while one was open for 23% of the time, Pallas kernels for 23%

profile of v7, /device:TPU:0, one launch (start us, length us, event | category | flops | bytes accessed | tf_op | source)
XLA Modules:
  0.0 657.8 jit_solution(17762538741309756989)
XLA Ops:
  21.3 3.8 fusion.56
  25.1 6.2 fusion.1.bias_ref
  42.9 4.5 pad_maximum_fusion.9
  48.3 20.7 %collective-permute-done.4 = bf16[288,1280]{1,0:T(8,128)(2,1)} collective-permute-done((bf16[288,1280]{1,0:T(8,128)(2,1)S(1)}, bf16[288,1280]{1,0:T(8,128)(2,1)}, u32[]{:S(2)}, u32[]{:S(2)}) %collective-permute-start.4) | collective-permute-done | bytes 737312 | tf_op jit(solution)/shard_map/ppermute | solution.py:681
  93.4 7.5 %collective-permute-done.8 = bf16[288,1536]{1,0:T(8,128)(2,1)} collective-permute-done((bf16[288,1536]{1,0:T(8,128)(2,1)}, bf16[288,1536]{1,0:T(8,128)(2,1)}, u32[]{:S(2)}, u32[]{:S(2)}) %collective-permute-start.8) | collective-permute-done | bytes 884768 | tf_op jit(solution)/shard_map/ppermute | solution.py:52
  100.9 3.2 maximum_select_fusion
  104.1 25.6 %all-gather.9.cloned.1.call-done = bf16[1152,1280]{1,0:T(8,128)(2,1)} async-done(((bf16[288,1280]{1,0:T(8,128)(2,1)}), bf16[1152,1280]{1,0:T(8,128)(2,1)}) %all-gather.9.cloned.1.call-update) | async-done | bytes 2949136 | tf_op jit(solution)/shard_map/all_gather | solution.py:697
  132.6 3.7 bitcast_dynamic-update-slice_fusion
  136.3 8.0 %project_half.2.refs_0_ = f32[1408,1024]{1,0:T(8,128)} custom-call(bf16[704,2304]{1,0:T(8,128)(2,1)} %constant_dynamic-update-slice_fusion.rows_ref.refs_0_, bf16[2304,1280]{1,0:T(8,128)(2,1)} %bitcast.24.w_ref), custom_call_target="tpu_custom_call" | custom-call | bytes 1024 | tf_op jit(solution)/shard_map/project_half/pallas_call | solution.py:535
  144.3 8.0 %project_half.3.qkv_ref = f32[1408,1024]{1,0:T(8,128)} custom-call(bf16[704,2304]{1,0:T(8,128)(2,1)} %collective-permute-done.9.rows_ref.refs_1_, bf16[2304,1280]{1,0:T(8,128)(2,1)} %bitcast.24.w_ref, f32[1408,1024]{1,0:T(8,128)} %project_half.2.refs_0_), custom_call_target="tpu_custom_call", output_to_operand_aliasing={{}: (2, {})} | custom-call | bytes 1024 | tf_op jit(solution)/shard_map/project_half/pallas_call | solution.py:535
  155.7 22.2 %attention_forward.1 = (bf16[1408,1024]{1,0:T(8,128)(2,1)S(1)}, bf16[1408,384]{1,0:T(8,128)(2,1)S(1)}, f32[3,8,2816]{2,1,0:T(8,128)S(1)}) custom-call(s32[17]{0:T(128)S(1)} %stack.80.info, f32[1408,1024]{1,0:T(8,128)} %project_half.3.qkv_ref, f32[1408,128]{1,0:T(8,128)S(1)} %get-tuple-element.93.cos_ref, f32[1408,128]{1,0:T(8,128)S(1)} %get-tuple-element.94.sin_ref, ...), custom_call_target="tpu_custom_call" | custom-call | bytes 1024 | tf_op jit(solution)/shard_map/attention_forward/pallas_call | solution.py:350
  177.9 4.7 convolution_convert_fusion
  192.4 4.8 convert_add_fusion.3
  197.4 13.0 %collective-permute-done.18 = bf16[176,2304]{1,0:T(8,128)(2,1)S(1)} collective-permute-done((bf16[176,2304]{1,0:T(8,128)(2,1)}, bf16[176,2304]{1,0:T(8,128)(2,1)S(1)}, u32[]{:S(2)}, u32[]{:S(2)}) %collective-permute-start.18) | collective-permute-done | bytes 811040 | tf_op jit(solution)/shard_map/ppermute | solution.py:56
  223.6 13.9 %collective-permute-done.14 = bf16[2,88,2304]{2,1,0:T(8,128)(2,1)S(1)} collective-permute-done((bf16[2,88,2304]{2,1,0:T(8,128)(2,1)S(1)}, bf16[2,88,2304]{2,1,0:T(8,128)(2,1)S(1)}, u32[]{:S(2)}, u32[]{:S(2)}) %collective-permute-start.14) | collective-permute-done | bytes 811040 | tf_op jit(solution)/shard_map/ppermute | solution.py:52
  240.2 6.6 %collective-permute-done.15 = bf16[88,2304]{1,0:T(8,128)(2,1)S(1)} collective-permute-done((bf16[88,2304]{1,0:T(8,128)(2,1)S(1)}, bf16[88,2304]{1,0:T(8,128)(2,1)S(1)}, u32[]{:S(2)}, u32[]{:S(2)}) %collective-permute-start.15) | collective-permute-done | bytes 405536 | tf_op jit(solution)/shard_map/ppermute | solution.py:56
  253.7 21.1 %all-gather.5.cloned.1.call-done.w_ref.tail_w_ref = bf16[2304,1536]{1,0:T(8,128)(2,1)} async-done(((bf16[576,1536]{1,0:T(8,128)(2,1)}), bf16[2304,1536]{1,0:T(8,128)(2,1)}) %all-gather.5.cloned.1.call-update) | async-done | bytes 7077904 | tf_op jit(solution)/shard_map/all_gather | solution.py:704
  278.7 7.6 %gate_blocks.4 = (f32[1408,1536]{1,0:T(8,128)}, bf16[1408,640]{1,0:T(8,128)(2,1)}, bf16[1408,256]{1,0:T(8,128)(2,1)S(1)}) custom-call(bf16[176,2304]{1,0:T(8,128)(2,1)S(1)} %multiply_convert_fusion.2.first_ref.refs_0_, bf16[176,2304]{1,0:T(8,128)(2,1)} %copy-done.39, bf16[2304,1536]{1,0:T(8,128)(2,1)} %all-gather.5.cloned.1.call-done.w_ref.tail_w_ref), custom_call_target="tpu_custom_call" | custom-call | flops 4982833152 | bytes 1024 | tf_op jit(solution)/shard_map/gate_blocks/pallas_call | solution.py:463
  286.3 9.0 %collective-permute-done.24.second_ref.refs_2_ = bf16[176,2304]{1,0:T(8,128)(2,1)S(1)} collective-permute-done((bf16[176,2304]{1,0:T(8,128)(2,1)S(1)}, bf16[176,2304]{1,0:T(8,128)(2,1)S(1)}, u32[]{:S(2)}, u32[]{:S(2)}) %collective-permute-start.24) | collective-permute-done | bytes 811040 | tf_op jit(solution)/shard_map/ppermute | solution.py:52
  299.2 7.5 %gate_blocks.5 = (f32[1408,1536]{1,0:T(8,128)}, bf16[1408,640]{1,0:T(8,128)(2,1)}, bf16[1408,256]{1,0:T(8,128)(2,1)S(1)}) custom-call(bf16[176,2304]{1,0:T(8,128)(2,1)S(1)} %collective-permute-done.25.first_ref.refs_1_, bf16[176,2304]{1,0:T(8,128)(2,1)} %copy-done.26, ...), custom_call_target="tpu_custom_call", output_to_operand_aliasing={{0}: (3, {}), {1}: (4, {}), {2}: (5, {})} | custom-call | flops 4982833152 | bytes 1024 | tf_op jit(solution)/shard_map/gate_blocks/pallas_call | solution.py:463
  311.0 7.6 %gate_blocks.6 = (f32[1408,1536]{1,0:T(8,128)}, bf16[1408,640]{1,0:T(8,128)(2,1)}, bf16[1408,256]{1,0:T(8,128)(2,1)S(1)}) custom-call(bf16[176,2304]{1,0:T(8,128)(2,1)S(1)} %collective-permute-done.30.first_ref.refs_5_, bf16[176,2304]{1,0:T(8,128)(2,1)} %copy-done.29, ...), custom_call_target="tpu_custom_call", output_to_operand_aliasing={{0}: (3, {}), {1}: (4, {}), {2}: (5, {})} | custom-call | flops 4982833152 | bytes 1024 | tf_op jit(solution)/shard_map/gate_blocks/pallas_call | solution.py:463
  319.5 7.5 %gate_blocks.7 = (f32[1408,1536]{1,0:T(8,128)}, bf16[1408,640]{1,0:T(8,128)(2,1)}, bf16[1408,256]{1,0:T(8,128)(2,1)S(1)}) custom-call(bf16[176,2304]{1,0:T(8,128)(2,1)S(1)} %pad_maximum_fusion.5.first_ref.refs_3_, bf16[176,2304]{1,0:T(8,128)(2,1)} %copy-done.30, ...), custom_call_target="tpu_custom_call", output_to_operand_aliasing={{0}: (3, {}), {1}: (4, {}), {2}: (5, {})} | custom-call | flops 4982833152 | bytes 1024 | tf_op jit(solution)/shard_map/gate_blocks/pallas_call | solution.py:463
  328.5 8.5 %weight_grads.3 = bf16[2304,640]{1,0:T(8,128)(2,1)} custom-call(bf16[704,2304]{1,0:T(8,128)(2,1)} %copy-done.21, bf16[704,2304]{1,0:T(8,128)(2,1)} %copy-done.16, bf16[1408,640]{1,0:T(8,128)(2,1)S(1)} %copy-done), custom_call_target="tpu_custom_call" | custom-call | bytes 1024 | tf_op jit(solution)/shard_map/weight_grads/pallas_call | solution.py:587
  337.1 14.1 %hidden_back.1.refs_8_ = bf16[1408,1536]{1,0:T(8,128)(2,1)} custom-call(bf16[1408,2304]{1,0:T(8,128)(2,1)} %constant_dynamic-update-slice_fusion.10.rows_ref, bf16[2304,640]{1,0:T(8,128)(2,1)} %all-gather.7.cloned.1.call-done.w_ref, bf16[2304,1536]{1,0:T(8,128)(2,1)} %all-gather.5.cloned.1.call-done.w_ref.tail_w_ref, f32[1408,1536]{1,0:T(8,128)} %get-tuple-element.125.gate_up_ref), custom_call_target="tpu_custom_call" | custom-call | bytes 1024 | tf_op jit(solution)/shard_map/hidden_back/pallas_call | solution.py:509
  351.3 18.5 %weight_grads.4 = bf16[2304,1536]{1,0:T(8,128)(2,1)} custom-call(bf16[176,2304]{1,0:T(8,128)(2,1)S(1)} %copy-done.7, bf16[176,2304]{1,0:T(8,128)(2,1)} %copy-done.3, bf16[176,2304]{1,0:T(8,128)(2,1)} %copy-done.26, bf16[176,2304]{1,0:T(8,128)(2,1)} %copy-done.2, bf16[176,2304]{1,0:T(8,128)(2,1)} %copy-done.39, bf16[176,2304]{1,0:T(8,128)(2,1)} %copy-done.8, ...), custom_call_target="tpu_custom_call" | custom-call | bytes 1024 | tf_op jit(solution)/shard_map/weight_grads/pallas_call | solution.py:587
  369.8 10.0 %convolution_convert_fusion.3 = bf16[704,2304]{1,0:T(8,128)(2,1)} fusion(bf16[2304,1536]{1,0:T(8,128)(2,1)} %all-gather.5.cloned.1.call-done.w_ref.tail_w_ref, bf16[1408,1536]{1,0:T(8,128)(2,1)} %hidden_back.1.refs_8_), kind=kOutput, calls=%fused_computation.16 | convolution fusion | flops 4984455168 | bytes 12484608 | tf_op jit(solution)/shard_map/dot_general | solution.py:30
  380.3 5.7 collective-permute-done.32
  385.9 9.5 %convert_add_fusion.2 = f32[704,2304]{1,0:T(8,128)S(1)} fusion(bf16[704,2304]{1,0:T(8,128)(2,1)} %collective-permute-done.32, bf16[2304,1536]{1,0:T(8,128)(2,1)} %all-gather.5.cloned.1.call-done.w_ref.tail_w_ref, bf16[1408,1536]{1,0:T(8,128)(2,1)} %hidden_back.1.refs_8_), kind=kOutput, calls=%fused_computation.11 | convolution fusion | flops 4986077184 | bytes 18972672 | tf_op jit(solution)/shard_map/dot_general | solution.py:30
  396.9 19.2 %collective-permute-done.33 = bf16[2,88,2304]{2,1,0:T(8,128)(2,1)S(1)} collective-permute-done((bf16[2,88,2304]{2,1,0:T(8,128)(2,1)S(1)}, bf16[2,88,2304]{2,1,0:T(8,128)(2,1)S(1)}, u32[]{:S(2)}, u32[]{:S(2)}) %collective-permute-start.33) | collective-permute-done | bytes 811040 | tf_op jit(solution)/shard_map/ppermute | solution.py:52
  422.5 7.5 %collective-permute-done.36 = bf16[88,2304]{1,0:T(8,128)(2,1)S(1)} collective-permute-done((bf16[88,2304]{1,0:T(8,128)(2,1)S(1)}, bf16[88,2304]{1,0:T(8,128)(2,1)S(1)}, u32[]{:S(2)}, u32[]{:S(2)}) %collective-permute-start.36) | collective-permute-done | bytes 405536 | tf_op jit(solution)/shard_map/ppermute | solution.py:52
  437.0 17.4 %collective-permute-done.38 = bf16[176,2304]{1,0:T(8,128)(2,1)S(1)} collective-permute-done((bf16[176,2304]{1,0:T(8,128)(2,1)S(1)}, bf16[176,2304]{1,0:T(8,128)(2,1)S(1)}, u32[]{:S(2)}, u32[]{:S(2)}) %collective-permute-start.38) | collective-permute-done | bytes 811040 | tf_op jit(solution)/shard_map/ppermute | solution.py:52
  456.8 6.7 %collective-permute-done.39 = bf16[88,2304]{1,0:T(8,128)(2,1)S(1)} collective-permute-done((bf16[88,2304]{1,0:T(8,128)(2,1)S(1)}, bf16[88,2304]{1,0:T(8,128)(2,1)S(1)}, u32[]{:S(2)}, u32[]{:S(2)}) %collective-permute-start.39) | collective-permute-done | bytes 405536 | tf_op jit(solution)/shard_map/ppermute | solution.py:56
  463.7 3.3 slice.448
  468.4 3.4 convolution_convert_fusion.5.near_ref
  471.8 4.5 convolution_convert_fusion.4.far_ref
  476.4 25.7 %attention_backward.1.refs_2_ = bf16[1408,1024]{1,0:T(8,128)(2,1)} custom-call(s32[17]{0:T(128)S(1)} %stack.80.info, bf16[1408,1024]{1,0:T(8,128)(2,1)} %copy-done.9, f32[1408,128]{1,0:T(8,128)S(1)} %get-tuple-element.93.cos_ref, f32[1408,128]{1,0:T(8,128)S(1)} %get-tuple-element.94.sin_ref, f32[1408,1408]{1,0:T(8,128)} %fusion.1.bias_ref, ...), custom_call_target="tpu_custom_call" | custom-call | bytes 1024 | tf_op jit(solution)/shard_map/attention_backward/pallas_call | solution.py:373
  502.1 16.0 %weight_grads.5 = bf16[2304,1280]{1,0:T(8,128)(2,1)} custom-call(bf16[704,2304]{1,0:T(8,128)(2,1)} %constant_dynamic-update-slice_fusion.rows_ref.refs_0_, bf16[704,2304]{1,0:T(8,128)(2,1)} %collective-permute-done.9.rows_ref.refs_1_, bf16[1408,1024]{1,0:T(8,128)(2,1)} %attention_backward.1.refs_2_, bf16[704,2304]{1,0:T(8,128)(2,1)} %copy-done.27, ...), custom_call_target="tpu_custom_call" | custom-call | bytes 1024 | tf_op jit(solution)/shard_map/weight_grads/pallas_call | solution.py:587
  522.0 3.9 collective-permute-done.42
  528.9 6.3 convolution_convert_fusion.1
  540.1 3.8 convolution_convert_fusion.2
  549.7 5.9 convert_add_fusion
  558.9 5.3 convert_add_fusion.1
  565.6 11.1 %collective-permute-done.55 = bf16[2,88,2304]{2,1,0:T(8,128)(2,1)S(1)} collective-permute-done((bf16[2,88,2304]{2,1,0:T(8,128)(2,1)S(1)}, bf16[2,88,2304]{2,1,0:T(8,128)(2,1)S(1)}, u32[]{:S(2)}, u32[]{:S(2)}) %collective-permute-start.55) | collective-permute-done | bytes 811040 | tf_op jit(solution)/shard_map/ppermute | solution.py:52
  581.0 13.0 %collective-permute-done.47 = bf16[2,88,2304]{2,1,0:T(8,128)(2,1)S(1)} collective-permute-done((bf16[2,88,2304]{2,1,0:T(8,128)(2,1)S(1)}, bf16[2,88,2304]{2,1,0:T(8,128)(2,1)S(1)}, u32[]{:S(2)}, u32[]{:S(2)}) %collective-permute-start.47) | collective-permute-done | bytes 811040 | tf_op jit(solution)/shard_map/ppermute | solution.py:52
  598.5 5.9 collective-permute-done.56
  613.1 3.1 collective-permute-done.61
  617.8 6.3 collective-permute-done.62
  636.2 10.4 %collective-permute-done.63 = bf16[288,1280]{1,0:T(8,128)(2,1)S(1)} collective-permute-done((bf16[288,1280]{1,0:T(8,128)(2,1)S(1)}, bf16[288,1280]{1,0:T(8,128)(2,1)S(1)}, u32[]{:S(2)}, u32[]{:S(2)}) %collective-permute-start.63) | collective-permute-done | bytes 737312 | tf_op jit(solution)/shard_map/ppermute | solution.py:52
  (375 shorter events, 180.6 us)
Async XLA Ops:
  7.2 122.4 %all-gather.9.cloned.1.call-start = ((), (), s32[]{:S(2)}) async-start(), calls=%async_computation.8 | async-start | bytes 3686400 | tf_op jit(solution)/shard_map/all_gather | solution.py:697
  12.5 35.9 %collective-permute-start.3 = (bf16[288,1280]{1,0:T(8,128)(2,1)S(1)}, bf16[288,1280]{1,0:T(8,128)(2,1)}, u32[]{:S(2)}, u32[]{:S(2)}) collective-permute-start(bf16[288,1280]{1,0:T(8,128)(2,1)S(1)} %get-tuple-element.79), channel_id=1, source_target_pairs={{0,8},{8,0},{16,24},{24,16},{1,9},{9,1},{17,25},{25,17},{2,10},{10... | collective-permute-start | bytes 2211848 | tf_op jit(solution)/shard_map/ppermute | solution.py:681
  15.5 53.5 %collective-permute-start.4 = (bf16[288,1280]{1,0:T(8,128)(2,1)S(1)}, bf16[288,1280]{1,0:T(8,128)(2,1)}, u32[]{:S(2)}, u32[]{:S(2)}) collective-permute-start(bf16[288,1280]{1,0:T(8,128)(2,1)S(1)} %get-tuple-element.79), channel_id=1, source_target_pairs={{0,16},{8,24},{16,0},{24,8},{1,17},{9,25},{17,1},{25,9},{2,18},{10... | collective-permute-start | bytes 2211848 | tf_op jit(solution)/shard_map/ppermute | solution.py:681
  18.1 63.9 %collective-permute-start.7 = (bf16[288,1280]{1,0:T(8,128)(2,1)S(1)}, bf16[288,1280]{1,0:T(8,128)(2,1)}, u32[]{:S(2)}, u32[]{:S(2)}) collective-permute-start(bf16[288,1280]{1,0:T(8,128)(2,1)S(1)} %get-tuple-element.79), channel_id=1, source_target_pairs={{0,24},{8,16},{16,8},{24,0},{1,25},{9,17},{17,9},{25,1},{2,26},{10... | collective-permute-start | bytes 2211848 | tf_op jit(solution)/shard_map/ppermute | solution.py:681
  18.1 17.8 %collective-permute-start = (bf16[288,1280]{1,0:T(8,128)(2,1)S(1)}, bf16[288,1280]{1,0:T(8,128)(2,1)}, u32[]{:S(2)}, u32[]{:S(2)}) collective-permute-start(bf16[288,1280]{1,0:T(8,128)(2,1)S(1)} %get-tuple-element.77), channel_id=1, source_target_pairs={{0,4},{4,0},{1,5},{5,1},{2,6},{6,2},{3,7},{7,3},{8,12},{12,8},{9,1... | collective-permute-start | bytes 2211848 | tf_op jit(solution)/shard_map/ppermute | solution.py:52
  35.9 33.1 %collective-permute-start.1 = (bf16[176,2304]{1,0:T(8,128)(2,1)}, bf16[176,2304]{1,0:T(8,128)(2,1)}, u32[]{:S(2)}, u32[]{:S(2)}) collective-permute-start(bf16[176,2304]{1,0:T(8,128)(2,1)} %fusion.10), channel_id=1, source_target_pairs={{0,4},{4,0},{1,5},{5,1},{2,6},{6,2},{3,7},{7,3},{8,12},{12,8},{9,1... | collective-permute-start | bytes 2433032 | tf_op jit(solution)/shard_map/ppermute | solution.py:52
  37.4 31.6 %collective-permute-start.2 = (bf16[176,2304]{1,0:T(8,128)(2,1)}, bf16[176,2304]{1,0:T(8,128)(2,1)}, u32[]{:S(2)}, u32[]{:S(2)}) collective-permute-start(bf16[176,2304]{1,0:T(8,128)(2,1)} %fusion.10), channel_id=1, source_target_pairs={{0,2},{2,0},{1,3},{3,1},{4,6},{6,4},{5,7},{7,5},{8,10},{10,8},{9,1... | collective-permute-start | bytes 2433032 | tf_op jit(solution)/shard_map/ppermute | solution.py:56
  42.9 232.0 %all-gather.5.cloned.1.call-start = ((), (), s32[]{:S(2)}) async-start(), calls=%async_computation.3 | async-start | bytes 8847360 | tf_op jit(solution)/shard_map/all_gather | solution.py:704
  86.4 14.5 %collective-permute-start.8 = (bf16[288,1536]{1,0:T(8,128)(2,1)}, bf16[288,1536]{1,0:T(8,128)(2,1)}, u32[]{:S(2)}, u32[]{:S(2)}) collective-permute-start(bf16[288,1536]{1,0:T(8,128)(2,1)} %concatenate.141), channel_id=1, source_target_pairs={{0,4},{4,0},{1,5},{5,1},{2,6},{6,2},{3,7},{7,3},{8,12},{12,8},{9,1... | collective-permute-start | bytes 2654216 | tf_op jit(solution)/shard_map/ppermute | solution.py:52
  129.7 207.5 %all-gather.7.cloned.1.call-start = ((), (), s32[]{:S(2)}) async-start(), calls=%async_computation.4 | async-start | bytes 3686400 | tf_op jit(solution)/shard_map/all_gather | solution.py:717
  129.9 14.4 %collective-permute-start.9 = (bf16[704,2304]{1,0:T(8,128)(2,1)}, bf16[704,2304]{1,0:T(8,128)(2,1)}, u32[]{:S(2)}, u32[]{:S(2)}) collective-permute-start(bf16[704,2304]{1,0:T(8,128)(2,1)} %constant_dynamic-update-slice_fusion.rows_ref.refs_0_), channel_id=1, source_target_pairs={{0,1},{1,0},{2,3},{3,2},{4,5},{5,4},{6,7},{7,6},{8,9},{9,8},{10,11... | collective-permute-start | bytes 9732104 | tf_op jit(solution)/shard_map/ppermute | solution.py:64
  153.7 35.5 %collective-permute-start.19 = (bf16[176,2304]{1,0:T(8,128)(2,1)}, bf16[176,2304]{1,0:T(8,128)(2,1)}, u32[]{:S(2)}, u32[]{:S(2)}) collective-permute-start(bf16[176,2304]{1,0:T(8,128)(2,1)} %get-tuple-element.156), channel_id=1, source_target_pairs={{0,4},{4,0},{1,5},{5,1},{2,6},{6,2},{3,7},{7,3},{8,12},{12,8},{9,1... | collective-permute-start | bytes 2433032 | tf_op jit(solution)/shard_map/ppermute | solution.py:52
  155.1 29.9 %collective-permute-start.23 = (bf16[288,640]{1,0:T(8,128)(2,1)S(1)}, bf16[288,640]{1,0:T(8,128)(2,1)S(1)}, u32[]{:S(2)}, u32[]{:S(2)}) collective-permute-start(bf16[288,640]{1,0:T(8,128)(2,1)S(1)} %slice.524), channel_id=1, source_target_pairs={{0,4},{4,0},{1,5},{5,1},{2,6},{6,2},{3,7},{7,3},{8,12},{12,8},{9,1... | collective-permute-start | bytes 1105928 | tf_op jit(solution)/shard_map/ppermute | solution.py:52
  188.7 231.9 %reduce-scatter.4.cloned.1.call-start = ((), (), s32[]{:S(2)}) async-start(), calls=%async_computation.5 | async-start | bytes 3686400 | tf_op jit(solution)/shard_map/reduce_scatter | solution.py:734
  189.2 21.2 %collective-permute-start.18 = (bf16[176,2304]{1,0:T(8,128)(2,1)}, bf16[176,2304]{1,0:T(8,128)(2,1)S(1)}, u32[]{:S(2)}, u32[]{:S(2)}) collective-permute-start(bf16[176,2304]{1,0:T(8,128)(2,1)} %get-tuple-element.156), channel_id=1, source_target_pairs={{0,2},{2,0},{1,3},{3,1},{4,6},{6,4},{5,7},{7,5},{8,10},{10,8},{9,1... | collective-permute-start | bytes 2433032 | tf_op jit(solution)/shard_map/ppermute | solution.py:56
  191.9 27.2 %collective-permute-start.20 = (bf16[88,2304]{1,0:T(8,128)(2,1)S(1)}, bf16[88,2304]{1,0:T(8,128)(2,1)S(1)}, u32[]{:S(2)}, u32[]{:S(2)}) collective-permute-start(bf16[88,2304]{1,0:T(8,128)(2,1)S(1)} %slice.538), channel_id=1, source_target_pairs={{0,2},{2,0},{1,3},{3,1},{4,6},{6,4},{5,7},{7,5},{8,10},{10,8},{9,1... | collective-permute-start | bytes 1216520 | tf_op jit(solution)/shard_map/ppermute | solution.py:56
  210.4 12.4 %collective-permute-start.21 = (bf16[88,2304]{1,0:T(8,128)(2,1)S(1)}, bf16[88,2304]{1,0:T(8,128)(2,1)S(1)}, u32[]{:S(2)}, u32[]{:S(2)}) collective-permute-start(bf16[88,2304]{1,0:T(8,128)(2,1)S(1)} %slice.539), channel_id=1, source_target_pairs={{0,4},{4,0},{1,5},{5,1},{2,6},{6,2},{3,7},{7,3},{8,12},{12,8},{9,1... | collective-permute-start | bytes 1216520 | tf_op jit(solution)/shard_map/ppermute | solution.py:52
  211.1 26.4 %collective-permute-start.14 = (bf16[2,88,2304]{2,1,0:T(8,128)(2,1)S(1)}, bf16[2,88,2304]{2,1,0:T(8,128)(2,1)S(1)}, u32[]{:S(2)}, u32[]{:S(2)}) collective-permute-start(bf16[2,88,2304]{2,1,0:T(8,128)(2,1)S(1)} %slice_bitcast_fusion.22), channel_id=1, source_target_pairs={{0,4},{4,0},{1,5},{5,1},{2,6},{6,2},{3,7},{7,3},{8,12},{12,8},{9,1... | collective-permute-start | bytes 2433032 | tf_op jit(solution)/shard_map/ppermute | solution.py:52
  212.5 25.0 %collective-permute-start.16 = (bf16[2,88,2304]{2,1,0:T(8,128)(2,1)S(1)}, bf16[2,88,2304]{2,1,0:T(8,128)(2,1)S(1)}, u32[]{:S(2)}, u32[]{:S(2)}) collective-permute-start(bf16[2,88,2304]{2,1,0:T(8,128)(2,1)S(1)} %slice_bitcast_fusion.20), channel_id=1, source_target_pairs={{0,2},{2,0},{1,3},{3,1},{4,6},{6,4},{5,7},{7,5},{8,10},{10,8},{9,1... | collective-permute-start | bytes 2433032 | tf_op jit(solution)/shard_map/ppermute | solution.py:56
  223.6 26.5 %collective-permute-start.22 = (bf16[704,2304]{1,0:T(8,128)(2,1)S(1)}, bf16[704,2304]{1,0:T(8,128)(2,1)S(1)}, u32[]{:S(2)}, u32[]{:S(2)}) collective-permute-start(bf16[704,2304]{1,0:T(8,128)(2,1)S(1)} %get-tuple-element.213.refs_0_.refs_9_), channel_id=1, source_target_pairs={{0,1},{1,0},{2,3},{3,2},{4,5},{5,4},{6,7},{7,6},{8,9},{9,8},{10,11... | collective-permute-start | bytes 9732104 | tf_op jit(solution)/shard_map/ppermute | solution.py:64
  274.9 20.4 %collective-permute-start.24 = (bf16[176,2304]{1,0:T(8,128)(2,1)S(1)}, bf16[176,2304]{1,0:T(8,128)(2,1)S(1)}, u32[]{:S(2)}, u32[]{:S(2)}) collective-permute-start(bf16[176,2304]{1,0:T(8,128)(2,1)S(1)} %multiply_convert_fusion.2.first_ref.refs_0_), channel_id=1, source_target_pairs={{0,4},{4,0},{1,5},{5,1},{2,6},{6,2},{3,7},{7,3},{8,12},{12,8},{9,1... | collective-permute-start | bytes 2433032 | tf_op jit(solution)/shard_map/ppermute | solution.py:52
  276.3 20.1 %collective-permute-start.25 = (bf16[176,2304]{1,0:T(8,128)(2,1)S(1)}, bf16[176,2304]{1,0:T(8,128)(2,1)S(1)}, u32[]{:S(2)}, u32[]{:S(2)}) collective-permute-start(bf16[176,2304]{1,0:T(8,128)(2,1)S(1)} %multiply_convert_fusion.2.first_ref.refs_0_), channel_id=1, source_target_pairs={{0,2},{2,0},{1,3},{3,1},{4,6},{6,4},{5,7},{7,5},{8,10},{10,8},{9,1... | collective-permute-start | bytes 2433032 | tf_op jit(solution)/shard_map/ppermute | solution.py:56
  296.5 13.4 %collective-permute-start.30 = (bf16[176,2304]{1,0:T(8,128)(2,1)S(1)}, bf16[176,2304]{1,0:T(8,128)(2,1)S(1)}, u32[]{:S(2)}, u32[]{:S(2)}) collective-permute-start(bf16[176,2304]{1,0:T(8,128)(2,1)S(1)} %collective-permute-done.25.first_ref.refs_1_), channel_id=1, source_target_pairs={{0,1},{1,0},{2,3},{3,2},{4,5},{5,4},{6,7},{7,6},{8,9},{9,8},{10,11... | collective-permute-start | bytes 2433032 | tf_op jit(solution)/shard_map/ppermute | solution.py:64
  296.6 13.3 %collective-permute-start.31 = (bf16[176,2304]{1,0:T(8,128)(2,1)S(1)}, bf16[176,2304]{1,0:T(8,128)(2,1)S(1)}, u32[]{:S(2)}, u32[]{:S(2)}) collective-permute-start(bf16[176,2304]{1,0:T(8,128)(2,1)S(1)} %collective-permute-done.24.second_ref.refs_2_), channel_id=1, source_target_pairs={{0,1},{1,0},{2,3},{3,2},{4,5},{5,4},{6,7},{7,6},{8,9},{9,8},{10,11... | collective-permute-start | bytes 2433032 | tf_op jit(solution)/shard_map/ppermute | solution.py:64
  297.2 11.4 %collective-permute-start.27 = (bf16[88,2304]{1,0:T(8,128)(2,1)S(1)}, bf16[88,2304]{1,0:T(8,128)(2,1)S(1)}, u32[]{:S(2)}, u32[]{:S(2)}) collective-permute-start(bf16[88,2304]{1,0:T(8,128)(2,1)S(1)} %slice.431), channel_id=1, source_target_pairs={{0,2},{2,0},{1,3},{3,1},{4,6},{6,4},{5,7},{7,5},{8,10},{10,8},{9,1... | collective-permute-start | bytes 1216520 | tf_op jit(solution)/shard_map/ppermute | solution.py:56
  298.7 11.1 %collective-permute-start.28 = (bf16[88,2304]{1,0:T(8,128)(2,1)S(1)}, bf16[88,2304]{1,0:T(8,128)(2,1)S(1)}, u32[]{:S(2)}, u32[]{:S(2)}) collective-permute-start(bf16[88,2304]{1,0:T(8,128)(2,1)S(1)} %slice.432), channel_id=1, source_target_pairs={{0,4},{4,0},{1,5},{5,1},{2,6},{6,2},{3,7},{7,3},{8,12},{12,8},{9,1... | collective-permute-start | bytes 1216520 | tf_op jit(solution)/shard_map/ppermute | solution.py:52
  337.1 182.2 %reduce-scatter.6.cloned.1.call-start = ((), (), s32[]{:S(2)}) async-start(), calls=%async_computation.6 | async-start | bytes 8847360 | tf_op jit(solution)/shard_map/reduce_scatter | solution.py:744
  380.2 246.6 %reduce-scatter.8.cloned.1.call-start = ((), (), s32[]{:S(2)}) async-start(), calls=%async_computation.7 | async-start | bytes 7372800 | tf_op jit(solution)/shard_map/reduce_scatter | solution.py:758
  395.7 20.5 %collective-permute-start.33 = (bf16[2,88,2304]{2,1,0:T(8,128)(2,1)S(1)}, bf16[2,88,2304]{2,1,0:T(8,128)(2,1)S(1)}, u32[]{:S(2)}, u32[]{:S(2)}) collective-permute-start(bf16[2,88,2304]{2,1,0:T(8,128)(2,1)S(1)} %slice_bitcast_fusion.18), channel_id=1, source_target_pairs={{0,4},{4,0},{1,5},{5,1},{2,6},{6,2},{3,7},{7,3},{8,12},{12,8},{9,1... | collective-permute-start | bytes 2433032 | tf_op jit(solution)/shard_map/ppermute | solution.py:52
  396.3 20.0 %collective-permute-start.35 = (bf16[2,88,2304]{2,1,0:T(8,128)(2,1)S(1)}, bf16[2,88,2304]{2,1,0:T(8,128)(2,1)S(1)}, u32[]{:S(2)}, u32[]{:S(2)}) collective-permute-start(bf16[2,88,2304]{2,1,0:T(8,128)(2,1)S(1)} %slice_bitcast_fusion.17), channel_id=1, source_target_pairs={{0,2},{2,0},{1,3},{3,1},{4,6},{6,4},{5,7},{7,5},{8,10},{10,8},{9,1... | collective-permute-start | bytes 2433032 | tf_op jit(solution)/shard_map/ppermute | solution.py:56
  436.0 18.3 %collective-permute-start.38 = (bf16[176,2304]{1,0:T(8,128)(2,1)S(1)}, bf16[176,2304]{1,0:T(8,128)(2,1)S(1)}, u32[]{:S(2)}, u32[]{:S(2)}) collective-permute-start(bf16[176,2304]{1,0:T(8,128)(2,1)S(1)} %get-tuple-element.153), channel_id=1, source_target_pairs={{0,4},{4,0},{1,5},{5,1},{2,6},{6,2},{3,7},{7,3},{8,12},{12,8},{9,1... | collective-permute-start | bytes 2433032 | tf_op jit(solution)/shard_map/ppermute | solution.py:52
  436.6 18.4 %collective-permute-start.37 = (bf16[176,2304]{1,0:T(8,128)(2,1)S(1)}, bf16[176,2304]{1,0:T(8,128)(2,1)S(1)}, u32[]{:S(2)}, u32[]{:S(2)}) collective-permute-start(bf16[176,2304]{1,0:T(8,128)(2,1)S(1)} %get-tuple-element.153), channel_id=1, source_target_pairs={{0,2},{2,0},{1,3},{3,1},{4,6},{6,4},{5,7},{7,5},{8,10},{10,8},{9,1... | collective-permute-start | bytes 2433032 | tf_op jit(solution)/shard_map/ppermute | solution.py:56
  467.1 70.0 %collective-permute-start.66 = (bf16[288,640]{1,0:T(8,128)(2,1)S(1)}, bf16[288,640]{1,0:T(8,128)(2,1)S(1)}, u32[]{:S(2)}, u32[]{:S(2)}) collective-permute-start(bf16[288,640]{1,0:T(8,128)(2,1)S(1)} %get-tuple-element.200), channel_id=1, source_target_pairs={{0,4},{4,0},{1,5},{5,1},{2,6},{6,2},{3,7},{7,3},{8,12},{12,8},{9,1... | collective-permute-start | bytes 1105928 | tf_op jit(solution)/shard_map/ppermute | solution.py:52
  527.4 17.5 %collective-permute-start.65 = (bf16[288,1280]{1,0:T(8,128)(2,1)S(1)}, bf16[288,1280]{1,0:T(8,128)(2,1)S(1)}, u32[]{:S(2)}, u32[]{:S(2)}) collective-permute-start(bf16[288,1280]{1,0:T(8,128)(2,1)S(1)} %get-tuple-element.180), channel_id=1, source_target_pairs={{0,4},{4,0},{1,5},{5,1},{2,6},{6,2},{3,7},{7,3},{8,12},{12,8},{9,1... | collective-permute-start | bytes 2211848 | tf_op jit(solution)/shard_map/ppermute | solution.py:52
  535.4 13.3 %collective-permute-start.51 = (bf16[176,2304]{1,0:T(8,128)(2,1)S(1)}, bf16[176,2304]{1,0:T(8,128)(2,1)S(1)}, u32[]{:S(2)}, u32[]{:S(2)}) collective-permute-start(bf16[176,2304]{1,0:T(8,128)(2,1)S(1)} %get-tuple-element.167), channel_id=1, source_target_pairs={{0,1},{1,0},{2,3},{3,2},{4,5},{5,4},{6,7},{7,6},{8,9},{9,8},{10,11... | collective-permute-start | bytes 2433032 | tf_op jit(solution)/shard_map/ppermute | solution.py:64
  535.5 13.7 %collective-permute-start.52 = (bf16[176,2304]{1,0:T(8,128)(2,1)S(1)}, bf16[176,2304]{1,0:T(8,128)(2,1)S(1)}, u32[]{:S(2)}, u32[]{:S(2)}) collective-permute-start(bf16[176,2304]{1,0:T(8,128)(2,1)S(1)} %get-tuple-element.170), channel_id=1, source_target_pairs={{0,1},{1,0},{2,3},{3,2},{4,5},{5,4},{6,7},{7,6},{8,9},{9,8},{10,11... | collective-permute-start | bytes 2433032 | tf_op jit(solution)/shard_map/ppermute | solution.py:64
  536.0 13.3 %collective-permute-start.53 = (bf16[176,2304]{1,0:T(8,128)(2,1)S(1)}, bf16[176,2304]{1,0:T(8,128)(2,1)S(1)}, u32[]{:S(2)}, u32[]{:S(2)}) collective-permute-start(bf16[176,2304]{1,0:T(8,128)(2,1)S(1)} %get-tuple-element.169), channel_id=1, source_target_pairs={{0,1},{1,0},{2,3},{3,2},{4,5},{5,4},{6,7},{7,6},{8,9},{9,8},{10,11... | collective-permute-start | bytes 2433032 | tf_op jit(solution)/shard_map/ppermute | solution.py:64
  537.1 12.6 %collective-permute-start.54 = (bf16[176,2304]{1,0:T(8,128)(2,1)S(1)}, bf16[176,2304]{1,0:T(8,128)(2,1)S(1)}, u32[]{:S(2)}, u32[]{:S(2)}) collective-permute-start(bf16[176,2304]{1,0:T(8,128)(2,1)S(1)} %get-tuple-element.168), channel_id=1, source_target_pairs={{0,1},{1,0},{2,3},{3,2},{4,5},{5,4},{6,7},{7,6},{8,9},{9,8},{10,11... | collective-permute-start | bytes 2433032 | tf_op jit(solution)/shard_map/ppermute | solution.py:64
  544.8 12.4 %collective-permute-start.43 = (bf16[176,2304]{1,0:T(8,128)(2,1)S(1)}, bf16[176,2304]{1,0:T(8,128)(2,1)S(1)}, u32[]{:S(2)}, u32[]{:S(2)}) collective-permute-start(bf16[176,2304]{1,0:T(8,128)(2,1)S(1)} %get-tuple-element.171), channel_id=1, source_target_pairs={{0,1},{1,0},{2,3},{3,2},{4,5},{5,4},{6,7},{7,6},{8,9},{9,8},{10,11... | collective-permute-start | bytes 2433032 | tf_op jit(solution)/shard_map/ppermute | solution.py:64
  555.7 21.0 %collective-permute-start.55 = (bf16[2,88,2304]{2,1,0:T(8,128)(2,1)S(1)}, bf16[2,88,2304]{2,1,0:T(8,128)(2,1)S(1)}, u32[]{:S(2)}, u32[]{:S(2)}) collective-permute-start(bf16[2,88,2304]{2,1,0:T(8,128)(2,1)S(1)} %slice_bitcast_fusion.11), channel_id=1, source_target_pairs={{0,4},{4,0},{1,5},{5,1},{2,6},{6,2},{3,7},{7,3},{8,12},{12,8},{9,1... | collective-permute-start | bytes 2433032 | tf_op jit(solution)/shard_map/ppermute | solution.py:52
  557.3 21.0 %collective-permute-start.57 = (bf16[2,88,2304]{2,1,0:T(8,128)(2,1)S(1)}, bf16[2,88,2304]{2,1,0:T(8,128)(2,1)S(1)}, u32[]{:S(2)}, u32[]{:S(2)}) collective-permute-start(bf16[2,88,2304]{2,1,0:T(8,128)(2,1)S(1)} %slice_bitcast_fusion.9), channel_id=1, source_target_pairs={{0,2},{2,0},{1,3},{3,1},{4,6},{6,4},{5,7},{7,5},{8,10},{10,8},{9,1... | collective-permute-start | bytes 2433032 | tf_op jit(solution)/shard_map/ppermute | solution.py:56
  564.3 29.8 %collective-permute-start.47 = (bf16[2,88,2304]{2,1,0:T(8,128)(2,1)S(1)}, bf16[2,88,2304]{2,1,0:T(8,128)(2,1)S(1)}, u32[]{:S(2)}, u32[]{:S(2)}) collective-permute-start(bf16[2,88,2304]{2,1,0:T(8,128)(2,1)S(1)} %slice_bitcast_fusion.15), channel_id=1, source_target_pairs={{0,4},{4,0},{1,5},{5,1},{2,6},{6,2},{3,7},{7,3},{8,12},{12,8},{9,1... | collective-permute-start | bytes 2433032 | tf_op jit(solution)/shard_map/ppermute | solution.py:52
  565.0 30.7 %collective-permute-start.49 = (bf16[2,88,2304]{2,1,0:T(8,128)(2,1)S(1)}, bf16[2,88,2304]{2,1,0:T(8,128)(2,1)S(1)}, u32[]{:S(2)}, u32[]{:S(2)}) collective-permute-start(bf16[2,88,2304]{2,1,0:T(8,128)(2,1)S(1)} %slice_bitcast_fusion.13), channel_id=1, source_target_pairs={{0,2},{2,0},{1,3},{3,1},{4,6},{6,4},{5,7},{7,5},{8,10},{10,8},{9,1... | collective-permute-start | bytes 2433032 | tf_op jit(solution)/shard_map/ppermute | solution.py:56
  578.8 25.6 %collective-permute-start.56 = (bf16[88,2304]{1,0:T(8,128)(2,1)S(1)}, bf16[88,2304]{1,0:T(8,128)(2,1)S(1)}, u32[]{:S(2)}, u32[]{:S(2)}) collective-permute-start(bf16[88,2304]{1,0:T(8,128)(2,1)S(1)} %fusion.54), channel_id=1, source_target_pairs={{0,2},{2,0},{1,3},{3,1},{4,6},{6,4},{5,7},{7,5},{8,10},{10,8},{9,1... | collective-permute-start | bytes 1216520 | tf_op jit(solution)/shard_map/ppermute | solution.py:56
  580.4 24.1 %collective-permute-start.58 = (bf16[88,2304]{1,0:T(8,128)(2,1)S(1)}, bf16[88,2304]{1,0:T(8,128)(2,1)S(1)}, u32[]{:S(2)}, u32[]{:S(2)}) collective-permute-start(bf16[88,2304]{1,0:T(8,128)(2,1)S(1)} %fusion.55), channel_id=1, source_target_pairs={{0,4},{4,0},{1,5},{5,1},{2,6},{6,2},{3,7},{7,3},{8,12},{12,8},{9,1... | collective-permute-start | bytes 1216520 | tf_op jit(solution)/shard_map/ppermute | solution.py:52
  596.2 16.8 %collective-permute-start.48 = (bf16[88,2304]{1,0:T(8,128)(2,1)S(1)}, bf16[88,2304]{1,0:T(8,128)(2,1)S(1)}, u32[]{:S(2)}, u32[]{:S(2)}) collective-permute-start(bf16[88,2304]{1,0:T(8,128)(2,1)S(1)} %fusion.52), channel_id=1, source_target_pairs={{0,2},{2,0},{1,3},{3,1},{4,6},{6,4},{5,7},{7,5},{8,10},{10,8},{9,1... | collective-permute-start | bytes 1216520 | tf_op jit(solution)/shard_map/ppermute | solution.py:56
  597.8 19.9 %collective-permute-start.50 = (bf16[88,2304]{1,0:T(8,128)(2,1)S(1)}, bf16[88,2304]{1,0:T(8,128)(2,1)S(1)}, u32[]{:S(2)}, u32[]{:S(2)}) collective-permute-start(bf16[88,2304]{1,0:T(8,128)(2,1)S(1)} %fusion.53), channel_id=1, source_target_pairs={{0,4},{4,0},{1,5},{5,1},{2,6},{6,2},{3,7},{7,3},{8,12},{12,8},{9,1... | collective-permute-start | bytes 1216520 | tf_op jit(solution)/shard_map/ppermute | solution.py:52
  628.3 18.4 %collective-permute-start.63 = (bf16[288,1280]{1,0:T(8,128)(2,1)S(1)}, bf16[288,1280]{1,0:T(8,128)(2,1)S(1)}, u32[]{:S(2)}, u32[]{:S(2)}) collective-permute-start(bf16[288,1280]{1,0:T(8,128)(2,1)S(1)} %get-tuple-element.188), channel_id=1, source_target_pairs={{0,4},{4,0},{1,5},{5,1},{2,6},{6,2},{3,7},{7,3},{8,12},{12,8},{9,1... | collective-permute-start | bytes 2211848 | tf_op jit(solution)/shard_map/ppermute | solution.py:52
  (76 other events, 599.2 us)
Sparse Core Ops, SparseCore 0:
  43.0 86.6 all-gather.8
  131.8 142.9 all-gather.4
  277.0 58.4 all-gather.6
  337.6 55.8 reduce-scatter.3
  395.8 123.3 reduce-scatter.5
  522.0 104.7 reduce-scatter.7
